TPU v7x, 32 devices: a whole 2x2x4 slice. The times are simulated.
32 devices in a mesh: groups: 2 (over x), vir: 16 (over z, y, core).
Axes of the slice: x: 2, y: 2, z: 4, core: 2. Of those that a mesh axis runs over, the one named last changes fastest.
Arguments:
- amps: bfloat16 [16, 8, 640, 640], P('groups', None, 'vir'), parts along dimension 0, may hold values from -6 to 6
- fock_vir: bfloat16 [1280, 640], P('groups'), parts along dimension 0, may hold values from -0.25 to 0.25
- fock_occ: bfloat16 [16, 8], P('groups'), parts along dimension 0, may hold values from -2 to 2
- ladder_ints: bfloat16 [640, 1280, 128], P('vir', 'groups'), parts along dimension 1, may hold values from -0.75 to 0.75
- cycle_ints: bfloat16 [640, 16, 128], P('vir', 'groups'), parts along dimension 1, may hold values from -0.5 to 0.5
- occ_irrep: int32 [16], P('groups'), parts along dimension 0, may hold values from 0 to 3, as said below
- vir_irrep: int32 [1280], P('groups'), parts along dimension 0, may hold values from 0 to 3
Outputs:
- residual: float32 [16, 8, 640, 640], P('groups', None, 'vir'), parts along dimension 0
There are 2 independent parts, one for each index of `groups`. A program takes and returns all parts, laid end to end along the dimension named above; each array names one. Nothing has to cross between parts.
Inputs may be any that keep to these rules, and one draw needn't show every extreme that they name: `occ_irrep`: labels of the four irreps of the point group, each labelling exactly 2 occupied orbitals; irreps multiply as the exclusive or of labels. `vir_irrep`: labels of the four irreps of the point group.
All inputs are finite; a program needn't handle non-finite values.
Results may differ from a plain program's by a relative error of at most 0.0003.
Values may be sent and summed in bfloat16 or wider, within the bound.
No kernel may reach another device: no remote copies, remote signals or barrier semaphores. Data moves between devices by JAX's collectives and lax.ppermute only.
A program may use at most 128 MiB of HBM per device.

v0:
```python
import jax
import jax.numpy as jnp
from jax import lax
from jax.sharding import PartitionSpec as P

DW = 8
CW = 16


def contract_last(left_side, right_side):
    return lax.dot_general(
        left_side, right_side, (((1,), (1,)), ((), ())), preferred_element_type=jnp.float32
    )


def body(amps, fock_vir, fock_occ, ladder_ints, cycle_ints, occ_irrep, vir_irrep):
    occupied = amps.shape[0]
    per_device = amps.shape[2]
    virtuals = amps.shape[3]
    pair_count = occupied * occupied
    position = lax.axis_index("vir")
    fock_term = jnp.dot(
        amps.reshape(pair_count * per_device, virtuals),
        fock_vir,
        preferred_element_type=jnp.float32,
    ).reshape(occupied, occupied, per_device, virtuals)
    occ_term = jnp.einsum("ikab,kj->ijab", amps, fock_occ, preferred_element_type=jnp.float32)
    flat_ints = ladder_ints.reshape(per_device * virtuals, ladder_ints.shape[2])
    local_window = amps[:, :, 0:1, :DW]
    local_cycle = amps[:, :, :, :CW]
    segment = lax.all_gather(local_window, "vir", axis=2, tiled=True)
    width = segment.shape[2] * DW
    ladder = contract_last(segment.reshape(pair_count, width), flat_ints)
    left_side = jnp.transpose(local_cycle, (0, 2, 1, 3)).reshape(
        occupied * per_device, occupied * CW
    )
    segment = lax.all_gather(cycle_ints, "vir", axis=0, tiled=True)
    right_side = segment.reshape(segment.shape[0] * occupied, occupied * CW)
    cycle_block = contract_last(left_side, right_side).reshape(
        occupied, per_device, segment.shape[0], occupied
    )
    cycle_part = jnp.transpose(cycle_block, (0, 3, 1, 2))
    half_sum = (
        fock_term - occ_term + ladder.reshape(occupied, occupied, per_device, virtuals) + cycle_part
    )
    vir_local = lax.dynamic_slice_in_dim(vir_irrep, position * per_device, per_device)
    occ_pair = jnp.bitwise_xor(occ_irrep[:, None], occ_irrep[None, :])
    vir_pair = jnp.bitwise_xor(vir_local[:, None], vir_irrep[None, :])
    received = lax.all_to_all(half_sum, "vir", split_axis=3, concat_axis=2, tiled=True)
    mirrored = jnp.transpose(received, (1, 0, 3, 2))
    product_irrep = jnp.bitwise_xor(occ_pair[:, :, None, None], vir_pair[None, None, :, :])
    allowed = jnp.where(product_irrep == 0, jnp.float32(1.0), jnp.float32(0.0))
    return allowed * (half_sum + mirrored)


def solution(mesh):
    return jax.shard_map(
        body,
        mesh=mesh,
        in_specs=(
            P("groups", None, "vir", None),
            P("groups", None),
            P("groups", None),
            P("vir", "groups", None),
            P("vir", "groups", None),
            P("groups"),
            P("groups"),
        ),
        out_specs=P("groups", None, "vir", None),
        check_vma=False,
    )
```

profile of v0, /device:TPU:13, one launch (start us, length us, event | category | flops | bytes accessed | tf_op | source)
XLA Modules:
  0.0 408.6 jit_solution(13577680956433998548)
XLA Ops:
  6.5 0.0 copy-start
  6.5 1.6 copy.30
  8.1 0.0 all-gather.2.cloned.1.call-update
  8.2 0.9 slice.6
  9.1 16.5 %all_gather.6 = bf16[8,8,16,8]{3,1,0,2:T(8,128)(2,1)S(1)} all-gather(bf16[8,8,1,8]{3,1,0,2:T(8,128)(2,1)S(1)} %copy.41), channel_id=1, replica_groups=mesh['groups'=2,'vir'=16] {'vir'}, dimensions={2}, use_global_device_ids=true | all-gather | bytes 17408 | tf_op jit(solution)/shard_map/all_gather | solution.py:31
  25.6 0.2 copy.27
  25.8 0.2 reshape.74
  26.0 1.1 slice_bitcast_fusion
  27.2 0.3 copy.29
  27.5 0.0 copy-start.2
  27.5 0.0 slice-start
  27.5 5.5 %fusion.4 = f32[8,8,40,640]{3,0,2,1:T(8,128)} fusion(bf16[8,8,40,640]{3,2,1,0:T(8,128)(2,1)} %param.7, bf16[8,8]{1,0:T(8,128)(2,1)} %param.9), kind=kOutput, calls=%fused_computation.9 | convolution fusion | flops 26214400 | bytes 9830528 | tf_op jit(solution)/shard_map/ikab,kj->ijab/dot_general | solution.py:27
  33.0 0.0 copy-done
  33.0 5.2 %fusion.7 = f32[8,8,40,640]{3,2,1,0:T(8,128)} fusion(bf16[8,8,40,640]{3,2,1,0:T(8,128)(2,1)S(1)} %copy-done.2, bf16[640,640]{1,0:T(8,128)(2,1)S(1)} %copy-done), kind=kOutput, calls=%fused_computation.12 | convolution fusion | flops 2097152000 | bytes 10649600 | tf_op jit(solution)/shard_map/dot_general | solution.py:22
  38.2 0.0 slice-done
  38.2 5.1 %fusion.1 = f32[8,8,40,640]{3,1,2,0:T(8,128)} fusion(bf16[40,640,128]{2,1,0:T(8,128)(2,1)S(1)} %bitcast.55, bf16[8,8,128,1]{2,1,0,3:T(8,128)(2,1)S(1)} %reshape.74), kind=kOutput, calls=%fused_computation.4 | convolution fusion | flops 419430400 | bytes 13123584 | tf_op jit(solution)/shard_map/dot_general | solution.py:11
  43.4 5.1 %all-gather.2.cloned.1.call-done = bf16[640,8,128]{2,0,1:T(8,128)(2,1)} async-done(((bf16[40,8,128]{2,0,1:T(8,128)(2,1)}), bf16[640,8,128]{2,0,1:T(8,128)(2,1)}) %all-gather.2.cloned.1.call-update) | async-done | bytes 1310736 | tf_op jit(solution)/shard_map/all_gather | solution.py:37
  48.5 13.6 %bitcast_add_fusion.1 = f32[8,8,40,640]{3,2,1,0:T(8,128)} fusion(f32[8,8,40,640]{3,2,1,0:T(8,128)} %fusion.7, f32[8,8,40,640]{3,1,2,0:T(8,128)} %fusion.1, f32[8,8,40,640]{3,0,2,1:T(8,128)} %fusion.4, bf16[8,40,128,1]{1,2,3,0:T(8,128)(2,1)S(1)} %bitcast.53, bf16[640,8,128]{2,0,1:T(8,128)(2,1)} %all-gather.2.cloned.1.call-done), kind=kOutput, calls=%fused_computation.3 | convolution fusion | flops 424345600 | bytes 27607040 | tf_op jit(solution)/shard_map/dot_general | solution.py:11
  62.1 17.8 %copy.32 = f32[8,8,40,640]{2,1,0,3:T(8,128)} copy(f32[8,8,40,640]{3,2,1,0:T(8,128)} %bitcast_add_fusion.1) | data formatting | bytes 13107200 | tf_op jit(solution)/shard_map/add | solution.py:44
  79.9 24.3 %reshape.79 = f32[16,1,102400]{2,1,0:T(1,128)} reshape(f32[640,8,8,40]{3,2,1,0:T(8,128)} %bitcast.52) | data formatting | bytes 13107200
  104.2 6.5 %all-to-all-start = ((f32[16,1,102400]{2,1,0:T(1,128)}), f32[16,1,102400]{2,1,0:T(1,128)}, u32[]{:S(2)}, u32[]{:S(2)}) async-start(f32[16,1,102400]{2,1,0:T(1,128)} %reshape.79), calls=%async_computation | async-start | bytes 13107200 | tf_op jit(solution)/shard_map/all_to_all | solution.py:49
  110.7 0.0 copy-done.3
  110.7 0.1 dynamic_slice.3
  110.8 0.1 broadcast_xor_fusion.1
  110.8 0.1 broadcast_xor_fusion
  110.9 142.8 %all-to-all-done = f32[16,1,102400]{2,1,0:T(1,128)} async-done(((f32[16,1,102400]{2,1,0:T(1,128)}), f32[16,1,102400]{2,1,0:T(1,128)}, u32[]{:S(2)}, u32[]{:S(2)}) %all-to-all-start) | async-done | bytes 6553632 | tf_op jit(solution)/shard_map/all_to_all | solution.py:49
  253.7 0.5 broadcast.38
  254.2 71.2 %reduce = f32[16,102400]{1,0:T(8,128)} reduce(f32[16,1,102400]{2,1,0:T(1,128)} %all-to-all-done, f32[]{:T(128)} %broadcast.38), dimensions={1}, to_apply=%all_to_all.13.reduce_sub_computation | reduce | bytes 13107204 | tf_op jit(solution)/shard_map/all_to_all | solution.py:49
  325.4 28.5 %reshape.80 = f32[640,8,8,40]{3,2,1,0:T(8,128)} reshape(f32[16,102400]{1,0:T(8,128)} %reduce) | data formatting | bytes 13107200
  353.9 21.3 %copy.47 = f32[8,8,40,16,40]{2,3,4,0,1:T(8,128)} copy(f32[8,8,40,16,40]{2,1,0,4,3:T(8,128)} %bitcast.50) | data formatting | bytes 13107200 | tf_op jit(solution)/shard_map/all_to_all | solution.py:49
  375.3 17.7 %all_to_all.16 = f32[8,8,640,40]{2,3,0,1:T(8,128)} reshape(f32[8,8,16,40,40]{3,2,4,0,1:T(8,128)} %bitcast.51) | data formatting | bytes 13107200 | tf_op jit(solution)/shard_map/all_to_all | solution.py:49
  393.0 8.8 %fusion = f32[8,8,40,640]{3,2,1,0:T(8,128)} fusion(f32[8,8,40,640]{3,2,1,0:T(8,128)} %bitcast_add_fusion.1, f32[8,8,640,40]{2,3,0,1:T(8,128)} %all_to_all.16, s32[40,640]{1,0:T(8,128)S(1)} %broadcast_xor_fusion, s32[8,8]{1,0:T(8,128)S(1)} %broadcast_xor_fusion.1), kind=kLoop, calls=%fused_computation.2 | loop fusion | flops 8192000 | bytes 19763456 | tf_op jit(solution)/shard_map/mul | solution.py:53
  (11 shorter events, 0.0 us)
Async XLA Ops:
  6.5 26.5 %copy-start = (bf16[640,640]{1,0:T(8,128)(2,1)S(1)}, bf16[640,640]{1,0:T(8,128)(2,1)}, u32[]{:S(2)}) copy-start(bf16[640,640]{1,0:T(8,128)(2,1)} %param.8) | copy-start | bytes 2457604
  6.5 42.0 %all-gather.2.cloned.1.call-start = ((), (), s32[]{:S(2)}) async-start(), calls=%async_computation.1 | async-start | bytes 1392640 | tf_op jit(solution)/shard_map/all_gather | solution.py:37
  27.5 5.5 %copy-start.2 = (bf16[8,8,40,640]{3,2,1,0:T(8,128)(2,1)S(1)}, bf16[8,8,40,640]{3,2,1,0:T(8,128)(2,1)}, u32[]{:S(2)}) copy-start(bf16[8,8,40,640]{3,2,1,0:T(8,128)(2,1)} %param.7) | copy-start | bytes 9830404
  27.5 10.8 %slice-start = ((s8[6553600]{0:T(1024)(128)(4,1)}), s8[4194304]{0:T(1024)(128)(4,1)S(1)}, s32[]{:S(2)}) async-start(s8[6553600]{0:T(1024)(128)(4,1)} %bitcast.54), calls=%async_computation.2 | async-start | bytes 8388608
  33.0 5.3 %slice-start.1 = ((s8[6553600]{0:T(1024)(128)(4,1)}), s8[2359296]{0:T(1024)(128)(4,1)S(1)}, s32[]{:S(2)}) async-start(s8[6553600]{0:T(1024)(128)(4,1)} %bitcast.54), calls=%async_computation.3 | async-start | bytes 4718592
  104.2 6.5 %copy-start.3 = (s32[640]{0:T(1024)S(1)}, s32[640]{0:T(1024)}, u32[]{:S(2)}) copy-start(s32[640]{0:T(1024)} %param.13) | copy-start | bytes 7684
  104.2 6.6 %copy-start.4 = (s32[8]{0:T(128)S(1)}, s32[8]{0:T(128)}, u32[]{:S(2)}) copy-start(s32[8]{0:T(128)} %param.12) | copy-start | bytes 100
  104.2 149.6 %all-to-all-start = ((f32[16,1,102400]{2,1,0:T(1,128)}), f32[16,1,102400]{2,1,0:T(1,128)}, u32[]{:S(2)}, u32[]{:S(2)}) async-start(f32[16,1,102400]{2,1,0:T(1,128)} %reshape.79), calls=%async_computation | async-start | bytes 13107200 | tf_op jit(solution)/shard_map/all_to_all | solution.py:49
  375.3 26.5 %copy-start.1 = (bf16[640,640]{1,0:T(8,128)(2,1)S(1)}, bf16[640,640]{1,0:T(8,128)(2,1)}, u32[]{:S(2)}) copy-start(bf16[640,640]{1,0:T(8,128)(2,1)} %param.8) | copy-start | bytes 2457604
Sparse Core Ops, SparseCore 0:
  9.7 38.7 all-gather.1
where the time goes:
time: 410 us; the launch traced here: 409 us
  waiting for transfers between devices  148 us (36%)
  local copies, waits for them, and re-layouts  115 us (28%)
  other arithmetic  80.1 us (20%)
  matrix products  29.4 us (7%)
  blocking collectives  16.5 us (4%)
  between operations  13.5 us (3%)
  starting transfers between devices  6.51 us (2%)
    all_to_all x1, waiting for transfers between devices, body(): lax.all_to_all(half_sum, 'vir', split_axis=3, concat_axis=2, tiled=True)  143 us
    all_to_all x1, other arithmetic, body(): lax.all_to_all(half_sum, 'vir', split_axis=3, concat_axis=2, tiled=True)  71.2 us
    unnamed x18, local copies, waits for them, and re-layouts  54.4 us
    all_to_all x3, local copies, waits for them, and re-layouts, body(): lax.all_to_all(half_sum, 'vir', split_axis=3, concat_axis=2, tiled=True)  39.5 us
    dot_general x2, matrix products, contract_last(): lax.dot_general(left_side, right_side, (((1,), (1,)), ((), ())), preferre...  18.7 us
    add x1, local copies, waits for them, and re-layouts, body(): fock_term - occ_term  17.8 us
    all_gather x1, blocking collectives, body(): segment = lax.all_gather(local_window, 'vir', axis=2, tiled=True)  16.5 us
    mul x1, other arithmetic, body(): return allowed * (half_sum + mirrored)  8.8 us
  transfers between devices with their start and end apart: 2, of which 2 were waited for; matrix products, arithmetic and copies ran while one was open for 5% of the time, Pallas kernels for 0%

commit v1 on v0

--- a/solution.py
+++ b/solution.py
@@ -1,10 +1,17 @@
+import functools
+
 import jax
 import jax.numpy as jnp
 from jax import lax
+from jax.experimental import pallas as pl
+from jax.experimental.pallas import tpu as pltpu
 from jax.sharding import PartitionSpec as P
 
 DW = 8
 CW = 16
+LANES = 128
+POWER = 9
+TOP_EXPONENT = 13
 
 
 def contract_last(left_side, right_side):
@@ -13,7 +20,7 @@
     )
 
 
-def body(amps, fock_vir, fock_occ, ladder_ints, cycle_ints, occ_irrep, vir_irrep):
+def plain_body(amps, fock_vir, fock_occ, ladder_ints, cycle_ints, occ_irrep, vir_irrep):
     occupied = amps.shape[0]
     per_device = amps.shape[2]
     virtuals = amps.shape[3]
@@ -53,9 +60,336 @@
     return allowed * (half_sum + mirrored)
 
 
+def labels_and_copies(occ_ref, occupied):
+    labels = [occ_ref[j] for j in range(occupied)]
+    copies = []
+    for j in range(occupied):
+        s = jnp.int32(0)
+        for k in range(j):
+            s = s + (labels[k] == labels[j]).astype(jnp.int32)
+        copies.append(s)
+    return labels, copies
+
+
+def prep_kernel(pos_ref, cyc_ref, amps_ref, out_ref):
+    per_device, occupied, _ = cyc_ref.shape
+    cyc = jnp.swapaxes(cyc_ref[...].astype(jnp.float32), 0, 1)
+    rows = occupied * per_device
+    out_ref[0:rows, :] = cyc.reshape(rows, LANES).astype(jnp.bfloat16)
+    win = amps_ref[:, :, 0, :].astype(jnp.float32).reshape(occupied * occupied, LANES)
+    lane = lax.broadcasted_iota(jnp.int32, win.shape, 1)
+    win = jnp.where(lane < DW, win, 0.0)
+    win = pltpu.roll(win, pos_ref[0] * DW, axis=1)
+    out_ref[rows:, :] = win.astype(jnp.bfloat16)
+
+
+def fock_kernel(occ_ref, amps_ref, fock_ref, mix_ref, u_ref, half_ref, cyc_ref, hs_ref):
+    i = pl.program_id(0)
+    _, per_device, virtuals = half_ref.shape
+    occupied = occ_ref.shape[0]
+    labels, copies = labels_and_copies(occ_ref, occupied)
+    a = amps_ref[0]
+    h = jnp.dot(a, fock_ref[...], preferred_element_type=jnp.float32)
+    h = h - jnp.dot(mix_ref[...], a, preferred_element_type=jnp.float32)
+    hs_ref[...] = h.reshape(occupied, per_device, virtuals)
+    own = occ_ref[i]
+    u = u_ref[...]
+    for j in range(occupied):
+        s = copies[j]
+        half_ref[s] = jnp.where(u == (own ^ labels[j]), hs_ref[j], half_ref[s])
+    head = a[:, :LANES].astype(jnp.float32)
+    lane = lax.broadcasted_iota(jnp.int32, (per_device, LANES), 1)
+    acc = jnp.zeros((per_device, LANES), jnp.float32)
+    for k in range(occupied):
+        piece = jnp.where(lane < CW, head[k * per_device : (k + 1) * per_device], 0.0)
+        acc = acc + (pltpu.roll(piece, k * CW, axis=1) if k else piece)
+    cyc_ref[0] = acc.astype(jnp.bfloat16)
+
+
+def payload_pieces(per_device, pairs, dests):
+    out = {}
+    for q in range(dests):
+        for e in range(pairs):
+            start = 0
+            while start < per_device:
+                src = q * per_device + start
+                dst = e * per_device + start
+                length = min(LANES - src % LANES, LANES - dst % LANES, per_device - start)
+                out.setdefault((q, dst // LANES), []).append(
+                    (dst % LANES, e, src // LANES, (dst - src) % LANES)
+                )
+                start += length
+    return out
+
+
+def half_kernel(
+    pos_ref, occ_ref, own_ref, mate_ref, cyc_ref, half_ref, u_ref, lad_ref,
+    out_ref, send_ref, xs_ref, w1_ref, w2_ref, hs_ref, ls_ref, pay_ref, max_ref,
+):
+    step = pl.program_id(0)
+    steps = pl.num_programs(0)
+    occupied = occ_ref.shape[0]
+    pairs, per_device, virtuals = hs_ref.shape
+    dests = send_ref.shape[0]
+    rows = occupied * per_device
+    labels, copies = labels_and_copies(occ_ref, occupied)
+
+    @pl.when(step == 0)
+    def _():
+        win = jnp.zeros((occupied * occupied, LANES), jnp.float32)
+        for r in range(dests):
+            ref = mate_ref if r & 1 else own_ref
+            block = ref[((r >> 1) & 1) * (dests // 4) + (r >> 2)].astype(jnp.float32)
+            win = win + block[rows:]
+            p = jnp.int32(r) ^ pos_ref[0]
+            at = pl.ds(pl.multiple_of(p * per_device, 8), per_device)
+            for j in range(occupied):
+                xs_ref[j, at, :] = block[j * per_device : (j + 1) * per_device]
+        w1_ref[...] = win
+        for i in range(occupied):
+            for j in range(occupied):
+                row = (labels[i] ^ labels[j]) * pairs + 2 * i + copies[j]
+                w2_ref[pl.ds(row, 1), :] = w1_ref[i * occupied + j : i * occupied + j + 1, :]
+        hs_ref[...] = half_ref[...]
+        u = u_ref[...]
+        for j in range(occupied):
+            c = contract_last(cyc_ref[...], xs_ref[j].astype(jnp.bfloat16))
+            for i in range(occupied):
+                e = 2 * i + copies[j]
+                part = c[i * per_device : (i + 1) * per_device]
+                hs_ref[e] = hs_ref[e] + jnp.where(u == (labels[i] ^ labels[j]), part, 0.0)
+        max_ref[...] = jnp.zeros_like(max_ref)
+
+    w2 = w2_ref[...].astype(jnp.bfloat16)
+    group = pl.ds(pl.multiple_of(step * 8, 8), 8)
+    u8 = u_ref[group, :]
+    for a in range(8):
+        ladder = contract_last(w2, lad_ref[a])
+        ua = u8[a : a + 1, :]
+        sel = ladder[0:pairs]
+        for v in range(1, 4):
+            sel = jnp.where(ua == v, ladder[v * pairs : (v + 1) * pairs], sel)
+        ls_ref[:, a, :] = sel
+    top = max_ref[...]
+    lane = lax.broadcasted_iota(jnp.int32, (8, LANES), 1)
+    tiles = {}
+    for e in range(pairs):
+        for v in range(virtuals // LANES):
+            at = slice(v * LANES, (v + 1) * LANES)
+            x = hs_ref[e, group, at] + ls_ref[e, :, at]
+            out_ref[e, :, at] = x
+            top = jnp.maximum(top, jnp.abs(x))
+            tiles[e, v] = x
+    max_ref[...] = top
+    rolled = {}
+    for (q, t), pieces in payload_pieces(per_device, pairs, dests).items():
+        acc = None
+        for first, e, v, shift in pieces:
+            if (e, v, shift) not in rolled:
+                x = tiles[e, v]
+                rolled[e, v, shift] = pltpu.roll(x, shift, axis=1) if shift else x
+            x = rolled[e, v, shift]
+            acc = x if acc is None else jnp.where(lane >= first, x, acc)
+        at = pl.ds(pl.multiple_of(t * per_device + step * 8, 8), 8)
+        pay_ref[q, at, :] = acc
+
+    @pl.when(step == steps - 1)
+    def _():
+        top = jnp.max(jnp.max(max_ref[...], axis=0, keepdims=True), axis=1, keepdims=True)
+        k = jnp.floor(TOP_EXPONENT - jnp.log2(jnp.maximum(top, 1e-30)))
+        scale = jnp.exp2(k)
+        count = pay_ref.shape[1]
+        row = lax.broadcasted_iota(jnp.int32, (count, LANES), 0)
+        data_rows = (virtuals // LANES) * per_device
+        for q in range(dests):
+            z = pay_ref[q] * scale
+            z2 = z * z
+            z4 = z2 * z2
+            y = jnp.where(row >= data_rows, k, z4 * z4 * z)
+            send_ref[q] = y.astype(jnp.bfloat16)
+
+
+def join_kernel(occ_ref, half_ref, recv_ref, u_ref, out_ref, dec_ref, mir_ref):
+    i = pl.program_id(0)
+    occupied = occ_ref.shape[0]
+    _, per_device, virtuals = half_ref.shape
+    dests = recv_ref.shape[0]
+    tiles = virtuals // LANES
+    labels, copies = labels_and_copies(occ_ref, occupied)
+
+    @pl.when(i == 0)
+    def _():
+        for p in range(dests):
+            block = recv_ref[p].astype(jnp.float32)
+            k = block[tiles * per_device : tiles * per_device + 1, 0:1]
+            y = block[: tiles * per_device]
+            size = jnp.exp2(jnp.log2(jnp.maximum(jnp.abs(y), 2.0**-126)) * (1.0 / POWER) - k)
+            x = jnp.where(y < 0, -size, jnp.where(y > 0, size, 0.0))
+            for t in range(tiles):
+                dec_ref[t, p * per_device : (p + 1) * per_device, :] = x[
+                    t * per_device : (t + 1) * per_device
+                ]
+        for t in range(tiles):
+            mir_ref[t * LANES : (t + 1) * LANES, :] = dec_ref[t].T
+
+    own = occ_ref[i]
+    copy = jnp.int32(0)
+    for k in range(occupied):
+        copy = copy + jnp.logical_and(labels[k] == own, k < i).astype(jnp.int32)
+    u = u_ref[...]
+    for j in range(occupied):
+        at = pl.ds(pl.multiple_of((2 * j + copy) * per_device, 8), per_device)
+        total = half_ref[copies[j]] + mir_ref[at, :]
+        out_ref[0, j] = jnp.where(u == (own ^ labels[j]), total, 0.0)
+
+
+def permute(x, flip, size):
+    return lax.ppermute(x, "vir", [(n, n ^ flip) for n in range(size)])
+
+
+def body(dests, amps, fock_vir, fock_occ, ladder_ints, cycle_ints, occ_irrep, vir_irrep):
+    occupied, _, per_device, virtuals = amps.shape
+    pairs = 2 * occupied
+    tiles = virtuals // LANES
+    rows = occupied * per_device
+    kw = ladder_ints.shape[2]
+    f32, bf16 = jnp.float32, jnp.bfloat16
+    position = lax.axis_index("vir").astype(jnp.int32)
+    pos = position.reshape(1)
+    vir_local = lax.dynamic_slice_in_dim(vir_irrep, position * per_device, per_device)
+    u = jnp.bitwise_xor(vir_local[:, None], vir_irrep[None, :])
+    smem = pl.BlockSpec(memory_space=pltpu.SMEM)
+    limit = 40 * 2**20
+
+    def whole(shape):
+        return pl.BlockSpec(shape, lambda n: (0,) * len(shape))
+
+    gather_rows = rows + occupied * occupied
+    block = pl.pallas_call(
+        prep_kernel,
+        grid=(1,),
+        out_shape=jax.ShapeDtypeStruct((gather_rows, LANES), bf16),
+        in_specs=[
+            smem,
+            whole(cycle_ints.shape),
+            pl.BlockSpec((occupied, occupied, 16, LANES), lambda n: (0, 0, 0, 0)),
+        ],
+        out_specs=whole((gather_rows, LANES)),
+        compiler_params=pltpu.CompilerParams(vmem_limit_bytes=limit),
+        cost_estimate=pl.CostEstimate(flops=0, bytes_accessed=600000, transcendentals=0),
+    )(pos, cycle_ints, amps)
+
+    along_z = [block] + [permute(block, m << 2, dests) for m in range(1, dests // 4)]
+    along_y = [permute(b, 2, dests) for b in along_z]
+    own_blocks = jnp.stack(along_z + along_y)
+    mate_blocks = permute(own_blocks, 1, dests)
+
+    mix = jnp.kron(fock_occ.T, jnp.eye(per_device, dtype=bf16))
+    half, cyc = pl.pallas_call(
+        fock_kernel,
+        grid=(occupied,),
+        out_shape=(
+            jax.ShapeDtypeStruct((pairs, per_device, virtuals), f32),
+            jax.ShapeDtypeStruct((occupied, per_device, LANES), bf16),
+        ),
+        in_specs=[
+            smem,
+            pl.BlockSpec((1, rows, virtuals), lambda n: (n, 0, 0)),
+            whole(fock_vir.shape),
+            whole(mix.shape),
+            whole(u.shape),
+        ],
+        out_specs=(
+            pl.BlockSpec((2, per_device, virtuals), lambda n: (n, 0, 0)),
+            pl.BlockSpec((1, per_device, LANES), lambda n: (n, 0, 0)),
+        ),
+        scratch_shapes=[pltpu.VMEM((occupied, per_device, virtuals), f32)],
+        compiler_params=pltpu.CompilerParams(vmem_limit_bytes=limit),
+        cost_estimate=pl.CostEstimate(
+            flops=3 * occupied * rows * virtuals * virtuals,
+            bytes_accessed=6 * 10**6,
+            transcendentals=0,
+        ),
+    )(occ_irrep, amps.reshape(occupied, rows, virtuals), fock_vir, mix, u)
+
+    send_rows = tiles * per_device + 8
+    half, send = pl.pallas_call(
+        half_kernel,
+        grid=(per_device // 8,),
+        out_shape=(
+            jax.ShapeDtypeStruct((pairs, per_device, virtuals), f32),
+            jax.ShapeDtypeStruct((dests, send_rows, LANES), bf16),
+        ),
+        in_specs=[
+            smem,
+            smem,
+            whole(own_blocks.shape),
+            whole(mate_blocks.shape),
+            whole((rows, LANES)),
+            whole(half.shape),
+            whole(u.shape),
+            pl.BlockSpec((8, virtuals, kw), lambda n: (n, 0, 0)),
+        ],
+        out_specs=(
+            pl.BlockSpec((pairs, 8, virtuals), lambda n: (0, n, 0)),
+            whole((dests, send_rows, LANES)),
+        ),
+        scratch_shapes=[
+            pltpu.VMEM((occupied, virtuals, LANES), f32),
+            pltpu.VMEM((occupied * occupied, LANES), f32),
+            pltpu.VMEM((occupied * occupied, LANES), f32),
+            pltpu.VMEM((pairs, per_device, virtuals), f32),
+            pltpu.VMEM((pairs, 8, virtuals), f32),
+            pltpu.VMEM((dests, send_rows, LANES), f32),
+            pltpu.VMEM((8, LANES), f32),
+        ],
+        compiler_params=pltpu.CompilerParams(vmem_limit_bytes=limit),
+        cost_estimate=pl.CostEstimate(
+            flops=4 * occupied * rows * virtuals * LANES,
+            bytes_accessed=12 * 10**6,
+            transcendentals=0,
+        ),
+    )(pos, occ_irrep, own_blocks, mate_blocks, cyc.reshape(rows, LANES), half, u, ladder_ints)
+
+    recv = lax.all_to_all(send, "vir", split_axis=0, concat_axis=0, tiled=True)
+
+    return pl.pallas_call(
+        join_kernel,
+        grid=(occupied,),
+        out_shape=jax.ShapeDtypeStruct((occupied, occupied, per_device, virtuals), f32),
+        in_specs=[
+            smem,
+            pl.BlockSpec((2, per_device, virtuals), lambda n: (n, 0, 0)),
+            whole(recv.shape),
+            whole(u.shape),
+        ],
+        out_specs=pl.BlockSpec((1, occupied, per_device, virtuals), lambda n: (n, 0, 0, 0)),
+        scratch_shapes=[
+            pltpu.VMEM((tiles, virtuals, LANES), f32),
+            pltpu.VMEM((tiles * LANES, virtuals), f32),
+        ],
+        compiler_params=pltpu.CompilerParams(vmem_limit_bytes=limit),
+        cost_estimate=pl.CostEstimate(flops=10**6, bytes_accessed=10**7, transcendentals=0),
+    )(occ_irrep, half, recv, u)
+
+
 def solution(mesh):
+    dests = mesh.shape["vir"]
+
+    def run(amps, *rest):
+        occupied, _, per_device, virtuals = amps.shape
+        tiled = (
+            dests == 16
+            and per_device % 8 == 0
+            and virtuals % LANES == 0
+            and 2 * occupied * per_device == virtuals
+            and rest[2].shape[2] == LANES
+            and rest[3].shape[2] == LANES
+        )
+        return body(dests, amps, *rest) if tiled else plain_body(amps, *rest)
+
     return jax.shard_map(
-        body,
+        run,
         mesh=mesh,
         in_specs=(
             P("groups", None, "vir", None),

time: 410 us -> 78.1 us (0.19)
  the two profiles are of different devices: /device:TPU:13 before, /device:TPU:1 now
where the time goes in v1:
time: 78.1 us; the launch traced here: 77.7 us
  blocking collectives  25.5 us (33%)
  Pallas kernels  22.5 us (29%)
  waiting for transfers between devices  10.9 us (14%)
  starting transfers between devices  9.71 us (12%)
  local copies, waits for them, and re-layouts  7.92 us (10%)
  other arithmetic  1.04 us (1%)
    all_to_all x1, blocking collectives, body(): recv = lax.all_to_all(send, 'vir', split_axis=0, concat_axis=0, tiled=True)  25.5 us
    ppermute x8, waiting for transfers between devices, permute(): return lax.ppermute(x, 'vir', [(n, n ^ flip) for n in range(size)])  10.9 us
    ppermute x8, starting transfers between devices, permute(): return lax.ppermute(x, 'vir', [(n, n ^ flip) for n in range(size)])  9.71 us
    pallas_call x1, Pallas kernels, body(): pl.pallas_call(half_kernel, grid=(per_device // 8,), out_shape=(jax.Shape...  8.95 us
    pallas_call x1, Pallas kernels, body(): pl.pallas_call(fock_kernel, grid=(occupied,), out_shape=(jax.ShapeDtypeSt...  7.6 us
    unnamed x25, local copies, waits for them, and re-layouts  6.01 us
    pallas_call x1, Pallas kernels, body(): pl.pallas_call(join_kernel, grid=(occupied,), out_shape=jax.ShapeDtypeStr...  5.8 us
    mul x1, local copies, waits for them, and re-layouts, body(): mix = jnp.kron(fock_occ.T, jnp.eye(per_device, dtype=bf16))  1.73 us
  transfers between devices with their start and end apart: 8, of which 3 were waited for; matrix products, arithmetic and copies ran while one was open for 4% of the time, Pallas kernels for 10%

profile of v1, /device:TPU:1, one launch (start us, length us, event | category | flops | bytes accessed | tf_op | source)
XLA Modules:
  0.0 77.7 jit_solution(1899844405784612408)
XLA Ops:
  0.0 1.9 %copy-done = bf16[8,8,40,640]{3,2,1,0:T(8,128)(2,1)S(1)} copy-done((bf16[8,8,40,640]{3,2,1,0:T(8,128)(2,1)S(1)}, bf16[8,8,40,640]{3,2,1,0:T(8,128)(2,1)}, u32[]{:S(2)}) %copy-start) | copy-done | bytes 3276824
  1.9 0.9 %copy-done.2 = bf16[40,8,128]{2,1,0:T(8,128)(2,1)S(1)} copy-done((bf16[40,8,128]{2,1,0:T(8,128)(2,1)S(1)}, bf16[40,8,128]{2,1,0:T(8,128)(2,1)}, u32[]{:S(2)}) %copy-start.2) | copy-done | bytes 81944
  2.8 0.1 shard_map.73
  3.0 2.1 %collective-permute-start.3 = (bf16[384,128]{1,0:T(8,128)(2,1)S(1)}, bf16[384,128]{1,0:T(8,128)(2,1)S(1)}, u32[]{:S(2)}, u32[]{:S(2)}) collective-permute-start(bf16[384,128]{1,0:T(8,128)(2,1)S(1)} %shard_map.73), channel_id=1, source_target_pairs={{0,2},{1,3},{2,0},{3,1},{4,6},{5,7},{6,4},{7,5},{8,10},{9,11},{10,... | collective-permute-start | bytes 294920 | tf_op jit(solution)/shard_map/ppermute | solution.py:247
  5.1 3.3 %collective-permute-start.2 = (bf16[384,128]{1,0:T(8,128)(2,1)S(1)}, bf16[384,128]{1,0:T(8,128)(2,1)S(1)}, u32[]{:S(2)}, u32[]{:S(2)}) collective-permute-start(bf16[384,128]{1,0:T(8,128)(2,1)S(1)} %shard_map.73), channel_id=1, source_target_pairs={{0,12},{1,13},{2,14},{3,15},{4,8},{5,9},{6,10},{7,11},{8,4},{9,5},... | collective-permute-start | bytes 294920 | tf_op jit(solution)/shard_map/ppermute | solution.py:247
  8.4 0.0 collective-permute-start.1
  8.4 0.3 collective-permute-start
  8.7 1.8 %collective-permute-done.2 = bf16[384,128]{1,0:T(8,128)(2,1)S(1)} collective-permute-done((bf16[384,128]{1,0:T(8,128)(2,1)S(1)}, bf16[384,128]{1,0:T(8,128)(2,1)S(1)}, u32[]{:S(2)}, u32[]{:S(2)}) %collective-permute-start.2) | collective-permute-done | bytes 98336 | tf_op jit(solution)/shard_map/ppermute | solution.py:247
  10.5 0.2 collective-permute-start.6
  10.7 5.6 %collective-permute-done.1 = bf16[384,128]{1,0:T(8,128)(2,1)S(1)} collective-permute-done((bf16[384,128]{1,0:T(8,128)(2,1)S(1)}, bf16[384,128]{1,0:T(8,128)(2,1)S(1)}, u32[]{:S(2)}, u32[]{:S(2)}) %collective-permute-start.1) | collective-permute-done | bytes 98336 | tf_op jit(solution)/shard_map/ppermute | solution.py:247
  16.3 0.1 collective-permute-start.5
  16.4 0.0 collective-permute-done
  16.4 1.3 %collective-permute-start.4 = (bf16[384,128]{1,0:T(8,128)(2,1)S(1)}, bf16[384,128]{1,0:T(8,128)(2,1)S(1)}, u32[]{:S(2)}, u32[]{:S(2)}) collective-permute-start(bf16[384,128]{1,0:T(8,128)(2,1)S(1)} %collective-permute-done), channel_id=1, source_target_pairs={{0,2},{1,3},{2,0},{3,1},{4,6},{5,7},{6,4},{7,5},{8,10},{9,11},{10,... | collective-permute-start | bytes 294920 | tf_op jit(solution)/shard_map/ppermute | solution.py:247
  17.8 0.0 collective-permute-done.3
  17.9 3.5 %collective-permute-done.4 = bf16[384,128]{1,0:T(8,128)(2,1)S(1)} collective-permute-done((bf16[384,128]{1,0:T(8,128)(2,1)S(1)}, bf16[384,128]{1,0:T(8,128)(2,1)S(1)}, u32[]{:S(2)}, u32[]{:S(2)}) %collective-permute-start.4) | collective-permute-done | bytes 98336 | tf_op jit(solution)/shard_map/ppermute | solution.py:247
  21.4 0.0 collective-permute-done.5
  21.4 0.0 collective-permute-done.6
  21.5 2.3 %collective-permute-start.7 = (bf16[8,384,128]{2,1,0:T(8,128)(2,1)S(1)}, bf16[8,384,128]{2,1,0:T(8,128)(2,1)}, u32[]{:S(2)}, u32[]{:S(2)}) collective-permute-start(bf16[8,384,128]{2,1,0:T(8,128)(2,1)S(1)} %bitcast_dynamic-update-slice_fusion.own_ref), channel_id=1, source_target_pairs={{0,1},{1,0},{2,3},{3,2},{4,5},{5,4},{6,7},{7,6},{8,9},{9,8},{10,11... | collective-permute-start | bytes 2359304 | tf_op jit(solution)/shard_map/ppermute | solution.py:247
  23.8 0.0 copy-done.6
  23.8 0.1 copy.8
  23.9 1.0 %broadcast_multiply_fusion = bf16[8,40,8,40]{3,2,1,0:T(8,128)(2,1)} fusion(bf16[40,40]{1,0:T(8,128)(2,1)S(1)} %fusion, bf16[8,8]{1,0:T(8,128)(2,1)S(1)} %copy.8), kind=kLoop, calls=%fused_computation | loop fusion | flops 102400 | bytes 208128 | tf_op jit(solution)/shard_map/jit(kron)/mul | solution.py:287
  24.8 1.7 %mul.30.mix_ref = bf16[320,320]{1,0:T(8,128)(2,1)S(1)} reshape(bf16[8,40,8,40]{3,2,1,0:T(8,128)(2,1)} %broadcast_multiply_fusion) | data formatting | bytes 409600 | tf_op jit(solution)/shard_map/jit(kron)/mul | solution.py:287
  26.6 0.1 dynamic_slice.3
  26.6 0.1 broadcast_xor_fusion.u_ref
  26.7 0.0 copy-start.1
  26.7 1.9 %copy-done.1 = bf16[8,8,40,640]{3,2,1,0:T(8,128)(2,1)S(1)} copy-done((bf16[8,8,40,640]{3,2,1,0:T(8,128)(2,1)S(1)}, bf16[8,8,40,640]{3,2,1,0:T(8,128)(2,1)}, u32[]{:S(2)}) %copy-start.1) | copy-done | bytes 3276824
  28.7 1.1 %copy-done.4 = bf16[640,640]{1,0:T(8,128)(2,1)S(1)} copy-done((bf16[640,640]{1,0:T(8,128)(2,1)S(1)}, bf16[640,640]{1,0:T(8,128)(2,1)}, u32[]{:S(2)}) %copy-start.4) | copy-done | bytes 819224
  29.8 7.6 %shard_map.74 = (f32[16,40,640]{2,1,0:T(8,128)S(1)}, bf16[8,40,128]{2,1,0:T(8,128)(2,1)S(1)}) custom-call(s32[8]{0:T(128)S(1)} %copy-done.3, bf16[8,320,640]{2,1,0:T(8,128)(2,1)S(1)} %bitcast.24, bf16[640,640]{1,0:T(8,128)(2,1)S(1)} %copy-done.4, bf16[320,320]{1,0:T(8,128)(2,1)S(1)} %mul.30.mix_ref, s32[40,640]{1,0:T(8,128)S(1)} %broadcast_xor_fusion.u_ref), custom_call_target="tpu_custom_call" | custom-call | flops 3145728000 | bytes 6000000 | tf_op jit(solution)/shard_map/pallas_call | solution.py:288
  37.4 0.0 collective-permute-done.7.mate_ref
  37.5 8.9 %shard_map.75 = (f32[16,40,640]{2,1,0:T(8,128)S(1)}, bf16[16,208,128]{2,1,0:T(8,128)(2,1)S(1)}) custom-call(s32[1]{0:T(128)} %bitcast.pos_ref, s32[8]{0:T(128)S(1)} %copy-done.3, bf16[8,384,128]{2,1,0:T(8,128)(2,1)S(1)} %bitcast_dynamic-update-slice_fusion.own_ref, bf16[8,384,128]{2,1,0:T(8,128)(2,1)} %collective-permute-done.7.mate_ref, ...), custom_call_target="tpu_custom_call" | custom-call | flops 838860800 | bytes 12000000 | tf_op jit(solution)/shard_map/pallas_call | solution.py:316
  46.4 25.5 %all_to_all.5.recv_ref = bf16[16,208,128]{2,1,0:T(8,128)(2,1)S(1)} all-to-all(bf16[16,208,128]{2,1,0:T(8,128)(2,1)S(1)} %get-tuple-element.12), channel_id=1, replica_groups=mesh['groups'=2,'vir'=16] {'vir'}, dimensions={0} | all-to-all | bytes 1703936 | tf_op jit(solution)/shard_map/all_to_all | solution.py:354
  71.9 5.8 %shard_map.76 = f32[8,8,40,640]{3,2,1,0:T(8,128)} custom-call(s32[8]{0:T(128)S(1)} %copy-done.3, f32[16,40,640]{2,1,0:T(8,128)S(1)} %get-tuple-element.11.half_ref, bf16[16,208,128]{2,1,0:T(8,128)(2,1)S(1)} %all_to_all.5.recv_ref, s32[40,640]{1,0:T(8,128)S(1)} %broadcast_xor_fusion.u_ref), custom_call_target="tpu_custom_call" | custom-call | flops 1000000 | bytes 10000000 | tf_op jit(solution)/shard_map/pallas_call | solution.py:356
  (22 shorter events, 0.1 us)
Async XLA Ops:
  0.0 23.8 %copy-start.6 = (bf16[8,8]{1,0:T(8,128)(2,1)S(1)}, bf16[8,8]{1,0:T(8,128)(2,1)}, u32[]{:S(2)}) copy-start(bf16[8,8]{1,0:T(8,128)(2,1)} %param.9) | copy-start | bytes 388
  0.0 1.9 %copy-start = (bf16[8,8,40,640]{3,2,1,0:T(8,128)(2,1)S(1)}, bf16[8,8,40,640]{3,2,1,0:T(8,128)(2,1)}, u32[]{:S(2)}) copy-start(bf16[8,8,40,640]{3,2,1,0:T(8,128)(2,1)} %amps_ref.1) | copy-start | bytes 9830404
  1.9 0.9 %copy-start.2 = (bf16[40,8,128]{2,1,0:T(8,128)(2,1)S(1)}, bf16[40,8,128]{2,1,0:T(8,128)(2,1)}, u32[]{:S(2)}) copy-start(bf16[40,8,128]{2,1,0:T(8,128)(2,1)} %cyc_ref.1) | copy-start | bytes 245764
  2.8 23.7 %copy-start.5 = (s32[640]{0:T(1024)S(1)}, s32[640]{0:T(1024)}, u32[]{:S(2)}) copy-start(s32[640]{0:T(1024)} %param.13) | copy-start | bytes 7684
  2.8 23.9 %copy-start.3 = (s32[8]{0:T(128)S(1)}, s32[8]{0:T(128)}, u32[]{:S(2)}) copy-start(s32[8]{0:T(128)} %occ_ref.5) | copy-start | bytes 100
  3.0 14.9 %collective-permute-start.3 = (bf16[384,128]{1,0:T(8,128)(2,1)S(1)}, bf16[384,128]{1,0:T(8,128)(2,1)S(1)}, u32[]{:S(2)}, u32[]{:S(2)}) collective-permute-start(bf16[384,128]{1,0:T(8,128)(2,1)S(1)} %shard_map.73), channel_id=1, source_target_pairs={{0,2},{1,3},{2,0},{3,1},{4,6},{5,7},{6,4},{7,5},{8,10},{9,11},{10,... | collective-permute-start | bytes 294920 | tf_op jit(solution)/shard_map/ppermute | solution.py:247
  5.1 5.4 %collective-permute-start.2 = (bf16[384,128]{1,0:T(8,128)(2,1)S(1)}, bf16[384,128]{1,0:T(8,128)(2,1)S(1)}, u32[]{:S(2)}, u32[]{:S(2)}) collective-permute-start(bf16[384,128]{1,0:T(8,128)(2,1)S(1)} %shard_map.73), channel_id=1, source_target_pairs={{0,12},{1,13},{2,14},{3,15},{4,8},{5,9},{6,10},{7,11},{8,4},{9,5},... | collective-permute-start | bytes 294920 | tf_op jit(solution)/shard_map/ppermute | solution.py:247
  8.4 7.9 %collective-permute-start.1 = (bf16[384,128]{1,0:T(8,128)(2,1)S(1)}, bf16[384,128]{1,0:T(8,128)(2,1)S(1)}, u32[]{:S(2)}, u32[]{:S(2)}) collective-permute-start(bf16[384,128]{1,0:T(8,128)(2,1)S(1)} %shard_map.73), channel_id=1, source_target_pairs={{0,8},{1,9},{2,10},{3,11},{4,12},{5,13},{6,14},{7,15},{8,0},{9,1},... | collective-permute-start | bytes 294920 | tf_op jit(solution)/shard_map/ppermute | solution.py:247
  8.4 8.0 %collective-permute-start = (bf16[384,128]{1,0:T(8,128)(2,1)S(1)}, bf16[384,128]{1,0:T(8,128)(2,1)S(1)}, u32[]{:S(2)}, u32[]{:S(2)}) collective-permute-start(bf16[384,128]{1,0:T(8,128)(2,1)S(1)} %shard_map.73), channel_id=1, source_target_pairs={{0,4},{1,5},{2,6},{3,7},{4,0},{5,1},{6,2},{7,3},{8,12},{9,13},{10,... | collective-permute-start | bytes 294920 | tf_op jit(solution)/shard_map/ppermute | solution.py:247
  10.5 10.9 %collective-permute-start.6 = (bf16[384,128]{1,0:T(8,128)(2,1)S(1)}, bf16[384,128]{1,0:T(8,128)(2,1)S(1)}, u32[]{:S(2)}, u32[]{:S(2)}) collective-permute-start(bf16[384,128]{1,0:T(8,128)(2,1)S(1)} %collective-permute-done.2), channel_id=1, source_target_pairs={{0,2},{1,3},{2,0},{3,1},{4,6},{5,7},{6,4},{7,5},{8,10},{9,11},{10,... | collective-permute-start | bytes 294920 | tf_op jit(solution)/shard_map/ppermute | solution.py:247
  16.3 5.1 %collective-permute-start.5 = (bf16[384,128]{1,0:T(8,128)(2,1)S(1)}, bf16[384,128]{1,0:T(8,128)(2,1)S(1)}, u32[]{:S(2)}, u32[]{:S(2)}) collective-permute-start(bf16[384,128]{1,0:T(8,128)(2,1)S(1)} %collective-permute-done.1), channel_id=1, source_target_pairs={{0,2},{1,3},{2,0},{3,1},{4,6},{5,7},{6,4},{7,5},{8,10},{9,11},{10,... | collective-permute-start | bytes 294920 | tf_op jit(solution)/shard_map/ppermute | solution.py:247
  16.4 4.9 %collective-permute-start.4 = (bf16[384,128]{1,0:T(8,128)(2,1)S(1)}, bf16[384,128]{1,0:T(8,128)(2,1)S(1)}, u32[]{:S(2)}, u32[]{:S(2)}) collective-permute-start(bf16[384,128]{1,0:T(8,128)(2,1)S(1)} %collective-permute-done), channel_id=1, source_target_pairs={{0,2},{1,3},{2,0},{3,1},{4,6},{5,7},{6,4},{7,5},{8,10},{9,11},{10,... | collective-permute-start | bytes 294920 | tf_op jit(solution)/shard_map/ppermute | solution.py:247
  21.5 15.9 %collective-permute-start.7 = (bf16[8,384,128]{2,1,0:T(8,128)(2,1)S(1)}, bf16[8,384,128]{2,1,0:T(8,128)(2,1)}, u32[]{:S(2)}, u32[]{:S(2)}) collective-permute-start(bf16[8,384,128]{2,1,0:T(8,128)(2,1)S(1)} %bitcast_dynamic-update-slice_fusion.own_ref), channel_id=1, source_target_pairs={{0,1},{1,0},{2,3},{3,2},{4,5},{5,4},{6,7},{7,6},{8,9},{9,8},{10,11... | collective-permute-start | bytes 2359304 | tf_op jit(solution)/shard_map/ppermute | solution.py:247
  24.8 12.6 %slice-start = ((s8[6553600]{0:T(1024)(128)(4,1)}), s8[2359296]{0:T(1024)(128)(4,1)S(1)}, s32[]{:S(2)}) async-start(s8[6553600]{0:T(1024)(128)(4,1)} %bitcast.22), calls=%async_computation.1 | async-start | bytes 4718592
  26.7 1.9 %copy-start.1 = (bf16[8,8,40,640]{3,2,1,0:T(8,128)(2,1)S(1)}, bf16[8,8,40,640]{3,2,1,0:T(8,128)(2,1)}, u32[]{:S(2)}) copy-start(bf16[8,8,40,640]{3,2,1,0:T(8,128)(2,1)} %amps_ref.1) | copy-start | bytes 9830404
  28.7 1.1 %copy-start.4 = (bf16[640,640]{1,0:T(8,128)(2,1)S(1)}, bf16[640,640]{1,0:T(8,128)(2,1)}, u32[]{:S(2)}) copy-start(bf16[640,640]{1,0:T(8,128)(2,1)} %fock_ref.1) | copy-start | bytes 2457604
  29.8 7.6 %slice-start.1 = ((s8[6553600]{0:T(1024)(128)(4,1)}), s8[4194304]{0:T(1024)(128)(4,1)S(1)}, s32[]{:S(2)}) async-start(s8[6553600]{0:T(1024)(128)(4,1)} %bitcast.22), calls=%async_computation.2 | async-start | bytes 8388608

commit v2 on v0

--- a/solution.py
+++ b/solution.py
@@ -1,10 +1,17 @@
+import functools
+
 import jax
 import jax.numpy as jnp
 from jax import lax
+from jax.experimental import pallas as pl
+from jax.experimental.pallas import tpu as pltpu
 from jax.sharding import PartitionSpec as P
 
 DW = 8
 CW = 16
+LANES = 128
+POWER = 9
+TOP_EXPONENT = 13
 
 
 def contract_last(left_side, right_side):
@@ -13,7 +20,7 @@
     )
 
 
-def body(amps, fock_vir, fock_occ, ladder_ints, cycle_ints, occ_irrep, vir_irrep):
+def plain_body(amps, fock_vir, fock_occ, ladder_ints, cycle_ints, occ_irrep, vir_irrep):
     occupied = amps.shape[0]
     per_device = amps.shape[2]
     virtuals = amps.shape[3]
@@ -53,9 +60,394 @@
     return allowed * (half_sum + mirrored)
 
 
+def labels_and_copies(occ_ref, occupied):
+    labels = [occ_ref[j] for j in range(occupied)]
+    copies = []
+    for j in range(occupied):
+        s = jnp.int32(0)
+        for k in range(j):
+            s = s + (labels[k] == labels[j]).astype(jnp.int32)
+        copies.append(s)
+    return labels, copies
+
+
+def prep_kernel(pos_ref, occ_vals_ref, amps_ref, win_ref, mix_ref):
+    occupied, _, _, _ = amps_ref.shape
+    rows = mix_ref.shape[0]
+    per_device = rows // occupied
+    win = amps_ref[:, :, 0, :].astype(jnp.float32).reshape(occupied * occupied, LANES)
+    lane = lax.broadcasted_iota(jnp.int32, win.shape, 1)
+    win = jnp.where(lane < DW, win, 0.0)
+    win_ref[...] = pltpu.roll(win, pos_ref[0] * DW, axis=1).astype(jnp.bfloat16)
+    r = lax.broadcasted_iota(jnp.int32, (rows, rows), 0)
+    c = lax.broadcasted_iota(jnp.int32, (rows, rows), 1)
+    mix = jnp.zeros((rows, rows), jnp.float32)
+    one = lax.broadcasted_iota(jnp.int32, (rows, occupied), 0)
+    col = lax.broadcasted_iota(jnp.int32, (rows, occupied), 1) * per_device
+    pick = jnp.logical_and(one >= col, one < col + per_device).astype(jnp.bfloat16)
+    left = lax.dot_general(
+        pick, occ_vals_ref[...], (((1,), (1,)), ((), ())), preferred_element_type=jnp.float32
+    ).astype(jnp.bfloat16)
+    mix = contract_last(left, pick)
+    gap = r - c
+    same = gap == 0
+    for n in range(1, occupied):
+        same = jnp.logical_or(same, jnp.abs(gap) == n * per_device)
+    mix_ref[...] = jnp.where(same, mix, 0.0).astype(jnp.bfloat16)
+
+
+def fock_kernel(first, occ_ref, amps_ref, fock_ref, mix_ref, u_ref, after_ref, half_ref, cyc_ref, hs_ref):
+    i = pl.program_id(0) + first
+    _, per_device, virtuals = half_ref.shape
+    occupied = occ_ref.shape[0]
+    labels, copies = labels_and_copies(occ_ref, occupied)
+    a = amps_ref[0]
+    h = jnp.dot(a, fock_ref[...], preferred_element_type=jnp.float32)
+    h = h - jnp.dot(mix_ref[...], a, preferred_element_type=jnp.float32)
+    hs_ref[...] = h.reshape(occupied, per_device, virtuals)
+    own = occ_ref[i]
+    u = u_ref[...]
+    for j in range(occupied):
+        s = copies[j]
+        half_ref[s] = jnp.where(u == (own ^ labels[j]), hs_ref[j], half_ref[s])
+    head = a[:, :LANES].astype(jnp.float32)
+    lane = lax.broadcasted_iota(jnp.int32, (per_device, LANES), 1)
+    acc = jnp.zeros((per_device, LANES), jnp.float32)
+    for k in range(occupied):
+        piece = jnp.where(lane < CW, head[k * per_device : (k + 1) * per_device], 0.0)
+        acc = acc + (pltpu.roll(piece, k * CW, axis=1) if k else piece)
+    cyc_ref[0] = acc.astype(jnp.bfloat16)
+
+
+def tie(blocks, windows, after):
+    count = len(blocks)
+
+    def kernel(*refs):
+        ins, outs = refs[: count + len(windows) + 1], refs[count + len(windows) + 1 :]
+        if windows:
+            total = ins[count][...]
+            for ref in ins[count + 1 : count + len(windows)]:
+                total = total + ref[...]
+            outs[count][...] = total
+
+    anywhere = pl.BlockSpec(memory_space=pl.ANY)
+    vmem = pl.BlockSpec(memory_space=pltpu.VMEM)
+    return pl.pallas_call(
+        kernel,
+        out_shape=tuple(jax.ShapeDtypeStruct(b.shape, b.dtype) for b in blocks)
+        + tuple(jax.ShapeDtypeStruct(w.shape, w.dtype) for w in windows[:1]),
+        in_specs=[anywhere] * count + [vmem] * len(windows) + [anywhere],
+        out_specs=(anywhere,) * count + (vmem,) * len(windows[:1]),
+        input_output_aliases={n: n for n in range(count)},
+        cost_estimate=pl.CostEstimate(flops=0, bytes_accessed=0, transcendentals=0),
+    )(*blocks, *windows, after)
+
+
+def payload_pieces(per_device, pairs, dests):
+    out = {}
+    for q in range(dests):
+        for e in range(pairs):
+            start = 0
+            while start < per_device:
+                src = q * per_device + start
+                dst = e * per_device + start
+                length = min(LANES - src % LANES, LANES - dst % LANES, per_device - start)
+                out.setdefault((q, dst // LANES), []).append(
+                    (dst % LANES, e, src // LANES, (dst - src) % LANES)
+                )
+                start += length
+    return out
+
+
+def ladder_kernel(occ_ref, win0_ref, win1_ref, half0, half1, half2, half3, u_ref, lad_ref, out_ref, w1_ref, w2_ref, ls_ref):
+    step = pl.program_id(0)
+    occupied = occ_ref.shape[0]
+    pairs, _, virtuals = out_ref.shape
+    labels, copies = labels_and_copies(occ_ref, occupied)
+
+    @pl.when(step == 0)
+    def _():
+        w1_ref[...] = win0_ref[...].astype(jnp.float32) + win1_ref[...].astype(jnp.float32)
+        for i in range(occupied):
+            for j in range(occupied):
+                row = (labels[i] ^ labels[j]) * pairs + 2 * i + copies[j]
+                w2_ref[pl.ds(row, 1), :] = w1_ref[i * occupied + j : i * occupied + j + 1, :]
+
+    w2 = w2_ref[...].astype(jnp.bfloat16)
+    u8 = u_ref[pl.ds(pl.multiple_of(step * 8, 8), 8), :]
+    for a in range(8):
+        ladder = contract_last(w2, lad_ref[a])
+        ua = u8[a : a + 1, :]
+        sel = ladder[0:pairs]
+        for v in range(1, 4):
+            sel = jnp.where(ua == v, ladder[v * pairs : (v + 1) * pairs], sel)
+        ls_ref[:, a, :] = sel
+    parts = (half0, half1, half2, half3)
+    per = pairs // len(parts)
+    for n, part in enumerate(parts):
+        out_ref[n * per : (n + 1) * per] = part[...] + ls_ref[n * per : (n + 1) * per]
+
+
+def cycle_kernel(dests, pos_ref, occ_ref, *refs):
+    own_ref, mate_ref, cyc0, cyc1, cyc2, cyc3, half_ref, u_ref, out_ref = refs[:9]
+    send_refs = refs[9 : 9 + dests]
+    xs_ref, pay_ref = refs[9 + dests :]
+    occupied = occ_ref.shape[0]
+    pairs, per_device, virtuals = half_ref.shape
+    labels, copies = labels_and_copies(occ_ref, occupied)
+    pos = pos_ref[0]
+    for r in range(dests):
+        ref = mate_ref if r & 1 else own_ref
+        block = ref[((r >> 1) & 1) * (dests // 4) + (r >> 2)].astype(jnp.float32)
+        xs_ref[pl.ds((pos ^ r) * per_device, per_device)] = block
+    u = u_ref[...]
+    out_ref[...] = half_ref[...]
+    left = jnp.concatenate([ref[...] for ref in (cyc0, cyc1, cyc2, cyc3)], axis=0)
+    left = left.astype(jnp.float32).reshape(occupied * per_device, LANES).astype(jnp.bfloat16)
+    for j in range(occupied):
+        c = contract_last(left, xs_ref[:, j, :].astype(jnp.bfloat16))
+        for i in range(occupied):
+            e = 2 * i + copies[j]
+            part = c[i * per_device : (i + 1) * per_device]
+            out_ref[e] = out_ref[e] + jnp.where(u == (labels[i] ^ labels[j]), part, 0.0)
+
+    pieces_of = payload_pieces(per_device, pairs, dests)
+    lane = lax.broadcasted_iota(jnp.int32, (8, LANES), 1)
+
+    def group(g, top):
+        rows = pl.ds(pl.multiple_of(g * 8, 8), 8)
+        tiles = {}
+        for e in range(pairs):
+            for v in range(virtuals // LANES):
+                x = out_ref[e, rows, v * LANES : (v + 1) * LANES]
+                top = jnp.maximum(top, jnp.abs(x))
+                tiles[e, v] = x
+        rolled = {}
+        for (q, t), pieces in pieces_of.items():
+            acc = None
+            for first, e, v, shift in pieces:
+                if (e, v, shift) not in rolled:
+                    x = tiles[e, v]
+                    rolled[e, v, shift] = pltpu.roll(x, shift, axis=1) if shift else x
+                x = rolled[e, v, shift]
+                acc = x if acc is None else jnp.where(lane >= first, x, acc)
+            at = pl.ds(pl.multiple_of(t * per_device + g * 8, 8), 8)
+            pay_ref[pos ^ q, at, :] = acc
+        return top
+
+    top = lax.fori_loop(0, per_device // 8, group, jnp.zeros((8, LANES), jnp.float32))
+    top = jnp.max(jnp.max(top, axis=0, keepdims=True), axis=1, keepdims=True)
+    k = jnp.floor(TOP_EXPONENT - jnp.log2(jnp.maximum(top, 1e-30)))
+    scale = jnp.exp2(k)
+    count = pay_ref.shape[1]
+    row = lax.broadcasted_iota(jnp.int32, (count, LANES), 0)
+    data_rows = (virtuals // LANES) * per_device
+    for r in range(dests):
+        z = pay_ref[r] * scale
+        z2 = z * z
+        z4 = z2 * z2
+        y = jnp.where(row >= data_rows, k, z4 * z4 * z)
+        send_refs[r][...] = y.astype(jnp.bfloat16)
+
+
+def join_kernel(dests, pos_ref, occ_ref, half_ref, u_ref, *refs):
+    recv_refs = refs[:dests]
+    out_ref, dec_ref, mir_ref = refs[dests:]
+    i = pl.program_id(0)
+    occupied = occ_ref.shape[0]
+    _, per_device, virtuals = half_ref.shape
+    tiles = virtuals // LANES
+    labels, copies = labels_and_copies(occ_ref, occupied)
+
+    @pl.when(i == 0)
+    def _():
+        for r in range(dests):
+            block = recv_refs[r][...].astype(jnp.float32)
+            k = block[tiles * per_device : tiles * per_device + 1, 0:1]
+            y = block[: tiles * per_device]
+            size = jnp.exp2(jnp.log2(jnp.maximum(jnp.abs(y), 2.0**-126)) * (1.0 / POWER) - k)
+            x = jnp.where(y < 0, -size, jnp.where(y > 0, size, 0.0))
+            at = pl.ds(pl.multiple_of((pos_ref[0] ^ r) * per_device, 8), per_device)
+            for t in range(tiles):
+                dec_ref[t, at, :] = x[t * per_device : (t + 1) * per_device]
+        for t in range(tiles):
+            mir_ref[t * LANES : (t + 1) * LANES, :] = dec_ref[t].T
+
+    own = occ_ref[i]
+    copy = jnp.int32(0)
+    for k in range(occupied):
+        copy = copy + jnp.logical_and(labels[k] == own, k < i).astype(jnp.int32)
+    u = u_ref[...]
+    for j in range(occupied):
+        at = pl.ds(pl.multiple_of((2 * j + copy) * per_device, 8), per_device)
+        total = half_ref[copies[j]] + mir_ref[at, :]
+        out_ref[0, j] = jnp.where(u == (own ^ labels[j]), total, 0.0)
+
+
+def permute(x, flip, size):
+    return lax.ppermute(x, "vir", [(n, n ^ flip) for n in range(size)])
+
+
+def body(dests, amps, fock_vir, fock_occ, ladder_ints, cycle_ints, occ_irrep, vir_irrep):
+    occupied, _, per_device, virtuals = amps.shape
+    pairs = 2 * occupied
+    tiles = virtuals // LANES
+    rows = occupied * per_device
+    kw = ladder_ints.shape[2]
+    f32, bf16 = jnp.float32, jnp.bfloat16
+    position = lax.axis_index("vir").astype(jnp.int32)
+    pos = position.reshape(1)
+    vir_local = lax.dynamic_slice_in_dim(vir_irrep, position * per_device, per_device)
+    u = jnp.bitwise_xor(vir_local[:, None], vir_irrep[None, :])
+    smem = pl.BlockSpec(memory_space=pltpu.SMEM)
+    limit = 40 * 2**20
+
+    def whole(shape):
+        return pl.BlockSpec(shape, lambda n: (0,) * len(shape))
+
+    def params():
+        return pltpu.CompilerParams(vmem_limit_bytes=limit)
+
+    def cost(flops, size):
+        return pl.CostEstimate(flops=flops, bytes_accessed=size, transcendentals=0)
+
+    anywhere = pl.BlockSpec(memory_space=pl.ANY)
+    quarter = dests // 4
+    x_z = [cycle_ints] + [permute(cycle_ints, m << 2, dests) for m in range(1, quarter)]
+    x_y = [permute(cycle_ints, 2, dests)]
+    corner = amps[:, :, :16, :LANES]
+    win, mix = pl.pallas_call(
+        prep_kernel,
+        out_shape=(
+            jax.ShapeDtypeStruct((occupied * occupied, LANES), bf16),
+            jax.ShapeDtypeStruct((rows, rows), bf16),
+        ),
+        in_specs=[smem] + [pl.BlockSpec(memory_space=pltpu.VMEM)] * 2,
+        compiler_params=params(),
+        cost_estimate=cost(0, 500000),
+    )(pos, fock_occ, corner)
+    wins = [win] + [permute(win, m << 2, dests) for m in range(1, quarter)]
+
+    flat_amps = amps.reshape(occupied, rows, virtuals)
+    parts = 4
+    per_part = occupied // parts
+
+    def fock_part(n, after):
+        first = n * per_part
+        return pl.pallas_call(
+            functools.partial(fock_kernel, first),
+            grid=(per_part,),
+            out_shape=(
+                jax.ShapeDtypeStruct((2 * per_part, per_device, virtuals), f32),
+                jax.ShapeDtypeStruct((per_part, per_device, LANES), bf16),
+            ),
+            in_specs=[
+                smem,
+                pl.BlockSpec((1, rows, virtuals), lambda i: (i + first, 0, 0)),
+                whole(fock_vir.shape),
+                whole(mix.shape),
+                whole(u.shape),
+                anywhere,
+            ],
+            out_specs=(
+                pl.BlockSpec((2, per_device, virtuals), lambda i: (i, 0, 0)),
+                pl.BlockSpec((1, per_device, LANES), lambda i: (i, 0, 0)),
+            ),
+            scratch_shapes=[pltpu.VMEM((occupied, per_device, virtuals), f32)],
+            compiler_params=params(),
+            cost_estimate=cost(3 * per_part * rows * virtuals * virtuals, 2 * 10**6),
+        )(occ_irrep, flat_amps, fock_vir, mix, u, after)
+
+    half0, cyc0 = fock_part(0, mix)
+    (x_z[1],) = tie([x_z[1]], [], half0)
+    x_y.append(permute(x_z[1], 2, dests))
+    half1, cyc1 = fock_part(1, x_z[1])
+    *x_z[2:], win = tie(x_z[2:], wins, half1)
+    x_y.extend(permute(b, 2, dests) for b in x_z[2:])
+    win_y = permute(win, 2, dests)
+    half2, cyc2 = fock_part(2, x_z[2])
+    *x_y, win = tie(x_y, [win, win_y], half2)
+    own_blocks = jnp.stack(x_z + list(x_y))
+    mate_blocks = permute(own_blocks, 1, dests)
+    win_mate = permute(win, 1, dests)
+    half3, cyc3 = fock_part(3, x_y[0])
+
+    half = pl.pallas_call(
+        ladder_kernel,
+        grid=(per_device // 8,),
+        out_shape=jax.ShapeDtypeStruct((pairs, per_device, virtuals), f32),
+        in_specs=[smem, whole(win.shape), whole(win.shape)]
+        + [pl.BlockSpec((2 * per_part, 8, virtuals), lambda n: (0, n, 0))] * parts
+        + [whole(u.shape), pl.BlockSpec((8, virtuals, kw), lambda n: (n, 0, 0))],
+        out_specs=pl.BlockSpec((pairs, 8, virtuals), lambda n: (0, n, 0)),
+        scratch_shapes=[
+            pltpu.VMEM((occupied * occupied, LANES), f32),
+            pltpu.VMEM((occupied * occupied, LANES), f32),
+            pltpu.VMEM((pairs, 8, virtuals), f32),
+        ],
+        compiler_params=params(),
+        cost_estimate=cost(4 * occupied * rows * virtuals * LANES, 9 * 10**6),
+    )(occ_irrep, win, win_mate, half0, half1, half2, half3, u, ladder_ints)
+
+    send_rows = tiles * per_device + 8
+    piece = jax.ShapeDtypeStruct((send_rows, LANES), bf16)
+    vmem = pl.BlockSpec(memory_space=pltpu.VMEM)
+    half, *sends = pl.pallas_call(
+        functools.partial(cycle_kernel, dests),
+        out_shape=(jax.ShapeDtypeStruct(half.shape, f32),) + (piece,) * dests,
+        in_specs=[smem, smem] + [vmem] * 8,
+        out_specs=(vmem,) * (1 + dests),
+        scratch_shapes=[
+            pltpu.VMEM((virtuals, occupied, LANES), f32),
+            pltpu.VMEM((dests, send_rows, LANES), f32),
+        ],
+        compiler_params=params(),
+        cost_estimate=cost(2 * occupied * rows * virtuals * LANES, 8 * 10**6),
+    )(pos, occ_irrep, own_blocks, mate_blocks, cyc0, cyc1, cyc2, cyc3, half, u)
+
+    recv = [None] * dests
+    recv[0] = sends[0]
+    for r in reversed(range(1, dests)):
+        recv[r] = permute(sends[r], r, dests)
+
+    return pl.pallas_call(
+        functools.partial(join_kernel, dests),
+        grid=(occupied,),
+        out_shape=jax.ShapeDtypeStruct((occupied, occupied, per_device, virtuals), f32),
+        in_specs=[
+            smem,
+            smem,
+            pl.BlockSpec((2, per_device, virtuals), lambda n: (n, 0, 0)),
+            whole(u.shape),
+        ]
+        + [whole(piece.shape)] * dests,
+        out_specs=pl.BlockSpec((1, occupied, per_device, virtuals), lambda n: (n, 0, 0, 0)),
+        scratch_shapes=[
+            pltpu.VMEM((tiles, virtuals, LANES), f32),
+            pltpu.VMEM((tiles * LANES, virtuals), f32),
+        ],
+        compiler_params=params(),
+        cost_estimate=cost(10**6, 10**7),
+    )(pos, occ_irrep, half, u, *recv)
+
+
 def solution(mesh):
+    dests = mesh.shape["vir"]
+
+    def run(amps, *rest):
+        occupied, _, per_device, virtuals = amps.shape
+        tiled = (
+            dests == 16
+            and per_device % 8 == 0
+            and virtuals % LANES == 0
+            and 2 * occupied * per_device == virtuals
+            and rest[2].shape[2] == LANES
+            and rest[3].shape[2] == LANES
+        )
+        return body(dests, amps, *rest) if tiled else plain_body(amps, *rest)
+
     return jax.shard_map(
-        body,
+        run,
         mesh=mesh,
         in_specs=(
             P("groups", None, "vir", None),

time: 410 us -> 114 us (0.28)
  the two profiles are of different devices: /device:TPU:13 before, /device:TPU:1 now
where the time goes in v2:
time: 114 us; the launch traced here: 113 us
  starting transfers between devices  40.7 us (36%)
  local copies, waits for them, and re-layouts  35.6 us (31%)
  Pallas kernels  31 us (27%)
  waiting for transfers between devices  4.14 us (4%)
    ppermute x28, starting transfers between devices, permute(): return lax.ppermute(x, 'vir', [(n, n ^ flip) for n in range(size)])  40.7 us
    unnamed x71, local copies, waits for them, and re-layouts  32.4 us
    pallas_call x4, Pallas kernels, fock_part(): pl.pallas_call(functools.partial(fock_kernel, first), grid=(per_part,), o...  8.99 us
    pallas_call x1, Pallas kernels, body(): pl.pallas_call(functools.partial(cycle_kernel, dests), out_shape=(jax.Sha...  7.26 us
    pallas_call x1, Pallas kernels, body(): pl.pallas_call(functools.partial(join_kernel, dests), grid=(occupied,), o...  6.3 us
    pallas_call x1, Pallas kernels, body(): pl.pallas_call(ladder_kernel, grid=(per_device // 8,), out_shape=jax.Shap...  4.73 us
    ppermute x28, waiting for transfers between devices, permute(): return lax.ppermute(x, 'vir', [(n, n ^ flip) for n in range(size)])  4.14 us
    pallas_call x3, Pallas kernels, tie(): pl.pallas_call(kernel, out_shape=tuple((jax.ShapeDtypeStruct(b.shape, b.d...  2.72 us
  transfers between devices with their start and end apart: 28, of which 1 were waited for; matrix products, arithmetic and copies ran while one was open for 8% of the time, Pallas kernels for 14%

profile of v2, /device:TPU:1, one launch (start us, length us, event | category | flops | bytes accessed | tf_op | source)
XLA Modules:
  0.0 112.5 jit_solution(3335545424848674941)
XLA Ops:
  0.0 3.1 %collective-permute-start.1 = (bf16[40,8,128]{2,1,0:T(8,128)(2,1)}, bf16[40,8,128]{2,1,0:T(8,128)(2,1)S(1)}, u32[]{:S(2)}, u32[]{:S(2)}) collective-permute-start(bf16[40,8,128]{2,1,0:T(8,128)(2,1)} %param.11), channel_id=1, source_target_pairs={{0,8},{1,9},{2,10},{3,11},{4,12},{5,13},{6,14},{7,15},{8,0},{9,1},... | collective-permute-start | bytes 245768 | tf_op jit(solution)/shard_map/ppermute | solution.py:288
  3.1 1.3 %collective-permute-start = (bf16[40,8,128]{2,1,0:T(8,128)(2,1)}, bf16[40,8,128]{2,1,0:T(8,128)(2,1)}, u32[]{:S(2)}, u32[]{:S(2)}) collective-permute-start(bf16[40,8,128]{2,1,0:T(8,128)(2,1)} %param.11), channel_id=1, source_target_pairs={{0,4},{1,5},{2,6},{3,7},{4,0},{5,1},{6,2},{7,3},{8,12},{9,13},{10,... | collective-permute-start | bytes 245768 | tf_op jit(solution)/shard_map/ppermute | solution.py:288
  7.8 3.3 %collective-permute-start.5 = (bf16[64,128]{1,0:T(8,128)(2,1)}, bf16[64,128]{1,0:T(8,128)(2,1)}, u32[]{:S(2)}, u32[]{:S(2)}) collective-permute-start(bf16[64,128]{1,0:T(8,128)(2,1)} %get-tuple-element.42.refs_2_), channel_id=1, source_target_pairs={{0,12},{1,13},{2,14},{3,15},{4,8},{5,9},{6,10},{7,11},{8,4},{9,5},... | collective-permute-start | bytes 49160 | tf_op jit(solution)/shard_map/ppermute | solution.py:288
  11.1 1.5 %bitcast_dynamic-update-slice_fusion.7 = bf16[8,40,8,128]{3,2,1,0:T(8,128)(2,1)} fusion(bf16[40,8,128]{2,1,0:T(8,128)(2,1)} %param.11), kind=kLoop, calls=%fused_computation.7 | loop fusion | bytes 163840
  14.1 1.9 %copy-done = bf16[8,8,40,640]{3,2,1,0:T(8,128)(2,1)S(1)} copy-done((bf16[8,8,40,640]{3,2,1,0:T(8,128)(2,1)S(1)}, bf16[8,8,40,640]{3,2,1,0:T(8,128)(2,1)}, u32[]{:S(2)}) %copy-start) | copy-done | bytes 3276824
  18.8 2.2 %shard_map.74 = (f32[4,40,640]{2,1,0:T(8,128)S(1)}, bf16[2,40,128]{2,1,0:T(8,128)(2,1)S(1)}) custom-call(s32[8]{0:T(128)S(1)} %copy-done.23, bf16[8,320,640]{2,1,0:T(8,128)(2,1)S(1)} %bitcast.18, bf16[640,640]{1,0:T(8,128)(2,1)S(1)} %copy-done.2, bf16[320,320]{1,0:T(8,128)(2,1)S(1)} %copy-done.8, s32[40,640]{1,0:T(8,128)S(1)} %broadcast_xor_fusion.u_ref.refs_7_, ...), custom_call_target="tpu_custom_call" | custom-call | flops 786432000 | bytes 2000000 | tf_op jit(solution)/shard_map/pallas_call | solution.py:337
  24.8 2.2 %shard_map.76 = (f32[4,40,640]{2,1,0:T(8,128)S(1)}, bf16[2,40,128]{2,1,0:T(8,128)(2,1)S(1)}) custom-call(s32[8]{0:T(128)S(1)} %copy-done.24, bf16[8,320,640]{2,1,0:T(8,128)(2,1)S(1)} %bitcast.19, bf16[640,640]{1,0:T(8,128)(2,1)S(1)} %copy-done.3, bf16[320,320]{1,0:T(8,128)(2,1)S(1)} %copy-done.9, s32[40,640]{1,0:T(8,128)S(1)} %broadcast_xor_fusion.u_ref.refs_7_, ...), custom_call_target="tpu_custom_call" | custom-call | flops 786432000 | bytes 2000000 | tf_op jit(solution)/shard_map/pallas_call | solution.py:337
  30.5 1.4 %shard_map.77 = (bf16[40,8,128]{2,1,0:T(8,128)(2,1)}, bf16[40,8,128]{2,1,0:T(8,128)(2,1)}, bf16[64,128]{1,0:T(8,128)(2,1)}) custom-call(bf16[40,8,128]{2,1,0:T(8,128)(2,1)} %copy-done.19, bf16[40,8,128]{2,1,0:T(8,128)(2,1)} %collective-permute-done.2.refs_1_, ...), custom_call_target="tpu_custom_call", output_to_operand_aliasing={{0}: (0, {}), {1}: (1, {})} | custom-call | tf_op jit(solution)/shard_map/pallas_call | solution.py:135
  34.6 1.5 %bitcast_dynamic-update-slice_fusion.6 = bf16[8,40,8,128]{3,2,1,0:T(8,128)(2,1)} fusion(bf16[8,40,8,128]{3,2,1,0:T(8,128)(2,1)} %bitcast_dynamic-update-slice_fusion.7, bf16[40,8,128]{2,1,0:T(8,128)(2,1)} %shard_map.75.after_ref), kind=kLoop, calls=%fused_computation.6 | loop fusion | bytes 163840
  36.2 1.5 %bitcast_dynamic-update-slice_fusion.5 = bf16[8,40,8,128]{3,2,1,0:T(8,128)(2,1)} fusion(bf16[8,40,8,128]{3,2,1,0:T(8,128)(2,1)} %bitcast_dynamic-update-slice_fusion.6, bf16[40,8,128]{2,1,0:T(8,128)(2,1)} %get-tuple-element.44.after_ref), kind=kLoop, calls=%fused_computation.5 | loop fusion | bytes 163840
  37.7 1.5 %bitcast_dynamic-update-slice_fusion.4 = bf16[8,40,8,128]{3,2,1,0:T(8,128)(2,1)} fusion(bf16[8,40,8,128]{3,2,1,0:T(8,128)(2,1)} %bitcast_dynamic-update-slice_fusion.5, bf16[40,8,128]{2,1,0:T(8,128)(2,1)} %get-tuple-element.45), kind=kLoop, calls=%fused_computation.4 | loop fusion | bytes 163840
  42.2 2.2 %shard_map.78 = (f32[4,40,640]{2,1,0:T(8,128)S(1)}, bf16[2,40,128]{2,1,0:T(8,128)(2,1)S(1)}) custom-call(s32[8]{0:T(128)S(1)} %copy-done.24, bf16[8,320,640]{2,1,0:T(8,128)(2,1)S(1)} %bitcast.20, bf16[640,640]{1,0:T(8,128)(2,1)S(1)} %copy-done.4, bf16[320,320]{1,0:T(8,128)(2,1)S(1)} %copy-done.10, s32[40,640]{1,0:T(8,128)S(1)} %broadcast_xor_fusion.u_ref.refs_7_, ...), custom_call_target="tpu_custom_call" | custom-call | flops 786432000 | bytes 2000000 | tf_op jit(solution)/shard_map/pallas_call | solution.py:337
  45.8 1.3 %shard_map.79 = (bf16[40,8,128]{2,1,0:T(8,128)(2,1)}, bf16[40,8,128]{2,1,0:T(8,128)(2,1)}, bf16[40,8,128]{2,1,0:T(8,128)(2,1)}, bf16[40,8,128]{2,1,0:T(8,128)(2,1)}, bf16[64,128]{1,0:T(8,128)(2,1)}) custom-call(bf16[40,8,128]{2,1,0:T(8,128)(2,1)} %copy-done.21, ...), custom_call_target="tpu_custom_call", output_to_operand_aliasing={{0}: (0, {}), {1}: (1, {}), {2}: (2, {}), {3}: (3, {})} | custom-call | tf_op jit(solution)/shard_map/pallas_call | solution.py:135
  47.2 1.6 %bitcast_dynamic-update-slice_fusion.3 = bf16[8,40,8,128]{3,2,1,0:T(8,128)(2,1)} fusion(bf16[8,40,8,128]{3,2,1,0:T(8,128)(2,1)} %bitcast_dynamic-update-slice_fusion.4, bf16[40,8,128]{2,1,0:T(8,128)(2,1)} %get-tuple-element.48.after_ref), kind=kLoop, calls=%fused_computation.3 | loop fusion | bytes 163840
  48.8 1.5 %bitcast_dynamic-update-slice_fusion.2 = bf16[8,40,8,128]{3,2,1,0:T(8,128)(2,1)} fusion(bf16[8,40,8,128]{3,2,1,0:T(8,128)(2,1)} %bitcast_dynamic-update-slice_fusion.3, bf16[40,8,128]{2,1,0:T(8,128)(2,1)} %get-tuple-element.49), kind=kLoop, calls=%fused_computation.2 | loop fusion | bytes 163840
  50.3 1.5 %bitcast_dynamic-update-slice_fusion.1 = bf16[8,40,8,128]{3,2,1,0:T(8,128)(2,1)} fusion(bf16[8,40,8,128]{3,2,1,0:T(8,128)(2,1)} %bitcast_dynamic-update-slice_fusion.2, bf16[40,8,128]{2,1,0:T(8,128)(2,1)} %get-tuple-element.50), kind=kLoop, calls=%fused_computation.1 | loop fusion | bytes 163840
  51.8 1.5 %bitcast_dynamic-update-slice_fusion.refs_0_ = bf16[8,40,8,128]{3,2,1,0:T(8,128)(2,1)} fusion(bf16[8,40,8,128]{3,2,1,0:T(8,128)(2,1)} %bitcast_dynamic-update-slice_fusion.1, bf16[40,8,128]{2,1,0:T(8,128)(2,1)} %get-tuple-element.51), kind=kLoop, calls=%fused_computation | loop fusion | bytes 163840 | tf_op jit(solution)/shard_map/stack | solution.py:370
  53.3 3.7 %collective-permute-start.11 = (bf16[8,40,8,128]{3,2,1,0:T(8,128)(2,1)}, bf16[8,40,8,128]{3,2,1,0:T(8,128)(2,1)S(1)}, u32[]{:S(2)}, u32[]{:S(2)}) collective-permute-start(bf16[8,40,8,128]{3,2,1,0:T(8,128)(2,1)} %bitcast_dynamic-update-slice_fusion.refs_0_), channel_id=1, source_target_pairs={{0,1},{1,0},{2,3},{3,2},{4,5},{5,4},{6,7},{7,6},{8,9},{9,8},{10,11... | collective-permute-start | bytes 1966088 | tf_op jit(solution)/shard_map/ppermute | solution.py:288
  60.0 2.3 %shard_map.80 = (f32[4,40,640]{2,1,0:T(8,128)S(1)}, bf16[2,40,128]{2,1,0:T(8,128)(2,1)S(1)}) custom-call(s32[8]{0:T(128)S(1)} %copy-done.24, bf16[8,320,640]{2,1,0:T(8,128)(2,1)S(1)} %bitcast.21, bf16[640,640]{1,0:T(8,128)(2,1)S(1)} %copy-done.5, bf16[320,320]{1,0:T(8,128)(2,1)S(1)} %copy-done.11, s32[40,640]{1,0:T(8,128)S(1)} %broadcast_xor_fusion.u_ref.refs_7_, ...), custom_call_target="tpu_custom_call" | custom-call | flops 786432000 | bytes 2000000 | tf_op jit(solution)/shard_map/pallas_call | solution.py:337
  62.3 2.9 %copy-done.6 = bf16[40,640,128]{2,1,0:T(8,128)(2,1)S(1)} copy-done((bf16[40,640,128]{2,1,0:T(8,128)(2,1)S(1)}, bf16[40,640,128]{2,1,0:T(8,128)(2,1)}, u32[]{:S(2)}) %copy-start.6) | copy-done | bytes 6553624
  65.2 4.7 %shard_map.81.refs_6_ = f32[16,40,640]{2,1,0:T(8,128)S(1)} custom-call(s32[8]{0:T(128)S(1)} %copy-done.24, bf16[64,128]{1,0:T(8,128)(2,1)S(1)} %copy-done.29, bf16[64,128]{1,0:T(8,128)(2,1)S(1)} %collective-permute-done.12.win1_ref, f32[4,40,640]{2,1,0:T(8,128)S(1)} %copy-done.13, f32[4,40,640]{2,1,0:T(8,128)S(1)} %copy-done.15, ...), custom_call_target="tpu_custom_call" | custom-call | flops 838860800 | bytes 9000000 | tf_op jit(solution)/shard_map/pallas_call | solution.py:375
  70.0 7.3 %shard_map.82 = (f32[16,40,640]{2,1,0:T(8,128)S(1)}, bf16[208,128]{1,0:T(8,128)(2,1)S(1)}, bf16[208,128]{1,0:T(8,128)(2,1)S(1)}, bf16[208,128]{1,0:T(8,128)(2,1)...) custom-call(s32[1]{0:T(128)} %bitcast.pos_ref, ...), custom_call_target="tpu_custom_call" | custom-call | flops 419430400 | bytes 8000000 | tf_op jit(solution)/shard_map/pallas_call | solution.py:395
  77.9 1.7 %collective-permute-start.15 = (bf16[208,128]{1,0:T(8,128)(2,1)S(1)}, bf16[208,128]{1,0:T(8,128)(2,1)S(1)}, u32[]{:S(2)}, u32[]{:S(2)}) collective-permute-start(bf16[208,128]{1,0:T(8,128)(2,1)S(1)} %get-tuple-element.62), channel_id=1, source_target_pairs={{0,3},{1,2},{2,1},{3,0},{4,7},{5,6},{6,5},{7,4},{8,11},{9,10},{10,... | collective-permute-start | bytes 159752 | tf_op jit(solution)/shard_map/ppermute | solution.py:288
  82.2 1.7 %collective-permute-start.19 = (bf16[208,128]{1,0:T(8,128)(2,1)S(1)}, bf16[208,128]{1,0:T(8,128)(2,1)S(1)}, u32[]{:S(2)}, u32[]{:S(2)}) collective-permute-start(bf16[208,128]{1,0:T(8,128)(2,1)S(1)} %get-tuple-element.66), channel_id=1, source_target_pairs={{0,7},{1,6},{2,5},{3,4},{4,3},{5,2},{6,1},{7,0},{8,15},{9,14},{10,... | collective-permute-start | bytes 159752 | tf_op jit(solution)/shard_map/ppermute | solution.py:288
  83.9 2.2 %collective-permute-start.20 = (bf16[208,128]{1,0:T(8,128)(2,1)S(1)}, bf16[208,128]{1,0:T(8,128)(2,1)S(1)}, u32[]{:S(2)}, u32[]{:S(2)}) collective-permute-start(bf16[208,128]{1,0:T(8,128)(2,1)S(1)} %get-tuple-element.67), channel_id=1, source_target_pairs={{0,8},{1,9},{2,10},{3,11},{4,12},{5,13},{6,14},{7,15},{8,0},{9,1},... | collective-permute-start | bytes 159752 | tf_op jit(solution)/shard_map/ppermute | solution.py:288
  86.6 2.2 %collective-permute-start.22 = (bf16[208,128]{1,0:T(8,128)(2,1)S(1)}, bf16[208,128]{1,0:T(8,128)(2,1)S(1)}, u32[]{:S(2)}, u32[]{:S(2)}) collective-permute-start(bf16[208,128]{1,0:T(8,128)(2,1)S(1)} %get-tuple-element.69), channel_id=1, source_target_pairs={{0,10},{1,11},{2,8},{3,9},{4,14},{5,15},{6,12},{7,13},{8,2},{9,3},... | collective-permute-start | bytes 159752 | tf_op jit(solution)/shard_map/ppermute | solution.py:288
  90.1 3.3 %collective-permute-start.24 = (bf16[208,128]{1,0:T(8,128)(2,1)S(1)}, bf16[208,128]{1,0:T(8,128)(2,1)S(1)}, u32[]{:S(2)}, u32[]{:S(2)}) collective-permute-start(bf16[208,128]{1,0:T(8,128)(2,1)S(1)} %get-tuple-element.71), channel_id=1, source_target_pairs={{0,12},{1,13},{2,14},{3,15},{4,8},{5,9},{6,10},{7,11},{8,4},{9,5},... | collective-permute-start | bytes 159752 | tf_op jit(solution)/shard_map/ppermute | solution.py:288
  93.5 1.5 %collective-permute-start.25 = (bf16[208,128]{1,0:T(8,128)(2,1)S(1)}, bf16[208,128]{1,0:T(8,128)(2,1)S(1)}, u32[]{:S(2)}, u32[]{:S(2)}) collective-permute-start(bf16[208,128]{1,0:T(8,128)(2,1)S(1)} %get-tuple-element.72), channel_id=1, source_target_pairs={{0,13},{1,12},{2,15},{3,14},{4,9},{5,8},{6,11},{7,10},{8,5},{9,4},... | collective-permute-start | bytes 159752 | tf_op jit(solution)/shard_map/ppermute | solution.py:288
  95.0 4.9 %collective-permute-start.26 = (bf16[208,128]{1,0:T(8,128)(2,1)S(1)}, bf16[208,128]{1,0:T(8,128)(2,1)S(1)}, u32[]{:S(2)}, u32[]{:S(2)}) collective-permute-start(bf16[208,128]{1,0:T(8,128)(2,1)S(1)} %get-tuple-element.73), channel_id=1, source_target_pairs={{0,14},{1,15},{2,12},{3,13},{4,10},{5,11},{6,8},{7,9},{8,6},{9,7},... | collective-permute-start | bytes 159752 | tf_op jit(solution)/shard_map/ppermute | solution.py:288
  99.9 2.3 %collective-permute-start.27 = (bf16[208,128]{1,0:T(8,128)(2,1)S(1)}, bf16[208,128]{1,0:T(8,128)(2,1)S(1)}, u32[]{:S(2)}, u32[]{:S(2)}) collective-permute-start(bf16[208,128]{1,0:T(8,128)(2,1)S(1)} %get-tuple-element.74), channel_id=1, source_target_pairs={{0,15},{1,14},{2,13},{3,12},{4,11},{5,10},{6,9},{7,8},{8,7},{9,6},... | collective-permute-start | bytes 159752 | tf_op jit(solution)/shard_map/ppermute | solution.py:288
  102.2 4.1 %collective-permute-done.27.refs_15_ = bf16[208,128]{1,0:T(8,128)(2,1)S(1)} collective-permute-done((bf16[208,128]{1,0:T(8,128)(2,1)S(1)}, bf16[208,128]{1,0:T(8,128)(2,1)S(1)}, u32[]{:S(2)}, u32[]{:S(2)}) %collective-permute-start.27) | collective-permute-done | bytes 53280 | tf_op jit(solution)/shard_map/ppermute | solution.py:288
  106.2 6.3 %shard_map.83 = f32[8,8,40,640]{3,2,1,0:T(8,128)} custom-call(s32[1]{0:T(128)} %bitcast.pos_ref, s32[8]{0:T(128)S(1)} %copy-done.24, f32[16,40,640]{2,1,0:T(8,128)S(1)} %get-tuple-element.58.half_ref, s32[40,640]{1,0:T(8,128)S(1)} %broadcast_xor_fusion.u_ref.refs_7_, bf16[208,128]{1,0:T(8,128)(2,1)S(1)} %get-tuple-element.59.refs_0_, ...), custom_call_target="tpu_custom_call" | custom-call | flops 1000000 | bytes 10000000 | tf_op jit(solution)/shard_map/pallas_call | solution.py:413
  (110 shorter events, 30.0 us)
Async XLA Ops:
  0.0 22.7 %copy-start.24 = (s32[8]{0:T(128)S(1)}, s32[8]{0:T(128)}, u32[]{:S(2)}) copy-start(s32[8]{0:T(128)} %occ_ref.13) | copy-start | bytes 100
  0.0 29.9 %collective-permute-start.1 = (bf16[40,8,128]{2,1,0:T(8,128)(2,1)}, bf16[40,8,128]{2,1,0:T(8,128)(2,1)S(1)}, u32[]{:S(2)}, u32[]{:S(2)}) collective-permute-start(bf16[40,8,128]{2,1,0:T(8,128)(2,1)} %param.11), channel_id=1, source_target_pairs={{0,8},{1,9},{2,10},{3,11},{4,12},{5,13},{6,14},{7,15},{8,0},{9,1},... | collective-permute-start | bytes 245768 | tf_op jit(solution)/shard_map/ppermute | solution.py:288
  3.1 19.3 %collective-permute-start = (bf16[40,8,128]{2,1,0:T(8,128)(2,1)}, bf16[40,8,128]{2,1,0:T(8,128)(2,1)}, u32[]{:S(2)}, u32[]{:S(2)}) collective-permute-start(bf16[40,8,128]{2,1,0:T(8,128)(2,1)} %param.11), channel_id=1, source_target_pairs={{0,4},{1,5},{2,6},{3,7},{4,0},{5,1},{6,2},{7,3},{8,12},{9,13},{10,... | collective-permute-start | bytes 245768 | tf_op jit(solution)/shard_map/ppermute | solution.py:288
  4.4 25.5 %collective-permute-start.2 = (bf16[40,8,128]{2,1,0:T(8,128)(2,1)}, bf16[40,8,128]{2,1,0:T(8,128)(2,1)}, u32[]{:S(2)}, u32[]{:S(2)}) collective-permute-start(bf16[40,8,128]{2,1,0:T(8,128)(2,1)} %param.11), channel_id=1, source_target_pairs={{0,12},{1,13},{2,14},{3,15},{4,8},{5,9},{6,10},{7,11},{8,4},{9,5},... | collective-permute-start | bytes 245768 | tf_op jit(solution)/shard_map/ppermute | solution.py:288
  7.8 20.6 %collective-permute-start.5 = (bf16[64,128]{1,0:T(8,128)(2,1)}, bf16[64,128]{1,0:T(8,128)(2,1)}, u32[]{:S(2)}, u32[]{:S(2)}) collective-permute-start(bf16[64,128]{1,0:T(8,128)(2,1)} %get-tuple-element.42.refs_2_), channel_id=1, source_target_pairs={{0,12},{1,13},{2,14},{3,15},{4,8},{5,9},{6,10},{7,11},{8,4},{9,5},... | collective-permute-start | bytes 49160 | tf_op jit(solution)/shard_map/ppermute | solution.py:288
  11.1 18.6 %collective-permute-start.4 = (bf16[64,128]{1,0:T(8,128)(2,1)}, bf16[64,128]{1,0:T(8,128)(2,1)}, u32[]{:S(2)}, u32[]{:S(2)}) collective-permute-start(bf16[64,128]{1,0:T(8,128)(2,1)} %get-tuple-element.42.refs_2_), channel_id=1, source_target_pairs={{0,8},{1,9},{2,10},{3,11},{4,12},{5,13},{6,14},{7,15},{8,0},{9,1},... | collective-permute-start | bytes 49160 | tf_op jit(solution)/shard_map/ppermute | solution.py:288
  22.4 7.5 %collective-permute-start.3 = (bf16[64,128]{1,0:T(8,128)(2,1)}, bf16[64,128]{1,0:T(8,128)(2,1)}, u32[]{:S(2)}, u32[]{:S(2)}) collective-permute-start(bf16[64,128]{1,0:T(8,128)(2,1)} %get-tuple-element.42.refs_2_), channel_id=1, source_target_pairs={{0,4},{1,5},{2,6},{3,7},{4,0},{5,1},{6,2},{7,3},{8,12},{9,13},{10,... | collective-permute-start | bytes 49160 | tf_op jit(solution)/shard_map/ppermute | solution.py:288
  28.4 16.8 %collective-permute-start.6 = (bf16[40,8,128]{2,1,0:T(8,128)(2,1)}, bf16[40,8,128]{2,1,0:T(8,128)(2,1)S(1)}, u32[]{:S(2)}, u32[]{:S(2)}) collective-permute-start(bf16[40,8,128]{2,1,0:T(8,128)(2,1)} %param.11), channel_id=1, source_target_pairs={{0,2},{1,3},{2,0},{3,1},{4,6},{5,7},{6,4},{7,5},{8,10},{9,11},{10,... | collective-permute-start | bytes 245768 | tf_op jit(solution)/shard_map/ppermute | solution.py:288
  29.7 15.6 %collective-permute-start.7 = (bf16[40,8,128]{2,1,0:T(8,128)(2,1)}, bf16[40,8,128]{2,1,0:T(8,128)(2,1)}, u32[]{:S(2)}, u32[]{:S(2)}) collective-permute-start(bf16[40,8,128]{2,1,0:T(8,128)(2,1)} %shard_map.75.after_ref), channel_id=1, source_target_pairs={{0,2},{1,3},{2,0},{3,1},{4,6},{5,7},{6,4},{7,5},{8,10},{9,11},{10,... | collective-permute-start | bytes 245768 | tf_op jit(solution)/shard_map/ppermute | solution.py:288
  31.9 13.3 %collective-permute-start.10 = (bf16[64,128]{1,0:T(8,128)(2,1)}, bf16[64,128]{1,0:T(8,128)(2,1)S(1)}, u32[]{:S(2)}, u32[]{:S(2)}) collective-permute-start(bf16[64,128]{1,0:T(8,128)(2,1)} %get-tuple-element.46.refs_4_), channel_id=1, source_target_pairs={{0,2},{1,3},{2,0},{3,1},{4,6},{5,7},{6,4},{7,5},{8,10},{9,11},{10,... | collective-permute-start | bytes 49160 | tf_op jit(solution)/shard_map/ppermute | solution.py:288
  33.2 12.1 %collective-permute-start.9 = (bf16[40,8,128]{2,1,0:T(8,128)(2,1)}, bf16[40,8,128]{2,1,0:T(8,128)(2,1)}, u32[]{:S(2)}, u32[]{:S(2)}) collective-permute-start(bf16[40,8,128]{2,1,0:T(8,128)(2,1)} %get-tuple-element.45), channel_id=1, source_target_pairs={{0,2},{1,3},{2,0},{3,1},{4,6},{5,7},{6,4},{7,5},{8,10},{9,11},{10,... | collective-permute-start | bytes 245768 | tf_op jit(solution)/shard_map/ppermute | solution.py:288
  33.4 11.9 %collective-permute-start.8 = (bf16[40,8,128]{2,1,0:T(8,128)(2,1)}, bf16[40,8,128]{2,1,0:T(8,128)(2,1)}, u32[]{:S(2)}, u32[]{:S(2)}) collective-permute-start(bf16[40,8,128]{2,1,0:T(8,128)(2,1)} %get-tuple-element.44.after_ref), channel_id=1, source_target_pairs={{0,2},{1,3},{2,0},{3,1},{4,6},{5,7},{6,4},{7,5},{8,10},{9,11},{10,... | collective-permute-start | bytes 245768 | tf_op jit(solution)/shard_map/ppermute | solution.py:288
  47.2 15.1 %copy-start.13 = (f32[4,40,640]{2,1,0:T(8,128)S(1)}, f32[4,40,640]{2,1,0:T(8,128)}, u32[]{:S(2)}) copy-start(f32[4,40,640]{2,1,0:T(8,128)} %copy-done.12) | copy-start | bytes 1228804
  47.2 15.1 %copy-start.29 = (bf16[64,128]{1,0:T(8,128)(2,1)S(1)}, bf16[64,128]{1,0:T(8,128)(2,1)}, u32[]{:S(2)}) copy-start(bf16[64,128]{1,0:T(8,128)(2,1)} %get-tuple-element.56.win0_ref) | copy-start | bytes 49156
  53.3 16.6 %collective-permute-start.11 = (bf16[8,40,8,128]{3,2,1,0:T(8,128)(2,1)}, bf16[8,40,8,128]{3,2,1,0:T(8,128)(2,1)S(1)}, u32[]{:S(2)}, u32[]{:S(2)}) collective-permute-start(bf16[8,40,8,128]{3,2,1,0:T(8,128)(2,1)} %bitcast_dynamic-update-slice_fusion.refs_0_), channel_id=1, source_target_pairs={{0,1},{1,0},{2,3},{3,2},{4,5},{5,4},{6,7},{7,6},{8,9},{9,8},{10,11... | collective-permute-start | bytes 1966088 | tf_op jit(solution)/shard_map/ppermute | solution.py:288
  57.0 5.2 %collective-permute-start.12 = (bf16[64,128]{1,0:T(8,128)(2,1)}, bf16[64,128]{1,0:T(8,128)(2,1)S(1)}, u32[]{:S(2)}, u32[]{:S(2)}) collective-permute-start(bf16[64,128]{1,0:T(8,128)(2,1)} %get-tuple-element.56.win0_ref), channel_id=1, source_target_pairs={{0,1},{1,0},{2,3},{3,2},{4,5},{5,4},{6,7},{7,6},{8,9},{9,8},{10,11... | collective-permute-start | bytes 49160 | tf_op jit(solution)/shard_map/ppermute | solution.py:288
  65.2 4.8 %copy-start.28 = (bf16[2,40,128]{2,1,0:T(8,128)(2,1)S(1)}, bf16[2,40,128]{2,1,0:T(8,128)(2,1)}, u32[]{:S(2)}) copy-start(bf16[2,40,128]{2,1,0:T(8,128)(2,1)} %copy-done.27) | copy-start | bytes 61444
  77.2 4.1 %collective-permute-start.13 = (bf16[208,128]{1,0:T(8,128)(2,1)S(1)}, bf16[208,128]{1,0:T(8,128)(2,1)S(1)}, u32[]{:S(2)}, u32[]{:S(2)}) collective-permute-start(bf16[208,128]{1,0:T(8,128)(2,1)S(1)} %get-tuple-element.60), channel_id=1, source_target_pairs={{0,1},{1,0},{2,3},{3,2},{4,5},{5,4},{6,7},{7,6},{8,9},{9,8},{10,11... | collective-permute-start | bytes 159752 | tf_op jit(solution)/shard_map/ppermute | solution.py:288
  77.8 4.4 %collective-permute-start.14 = (bf16[208,128]{1,0:T(8,128)(2,1)S(1)}, bf16[208,128]{1,0:T(8,128)(2,1)S(1)}, u32[]{:S(2)}, u32[]{:S(2)}) collective-permute-start(bf16[208,128]{1,0:T(8,128)(2,1)S(1)} %get-tuple-element.61), channel_id=1, source_target_pairs={{0,2},{1,3},{2,0},{3,1},{4,6},{5,7},{6,4},{7,5},{8,10},{9,11},{10,... | collective-permute-start | bytes 159752 | tf_op jit(solution)/shard_map/ppermute | solution.py:288
  77.9 6.1 %collective-permute-start.15 = (bf16[208,128]{1,0:T(8,128)(2,1)S(1)}, bf16[208,128]{1,0:T(8,128)(2,1)S(1)}, u32[]{:S(2)}, u32[]{:S(2)}) collective-permute-start(bf16[208,128]{1,0:T(8,128)(2,1)S(1)} %get-tuple-element.62), channel_id=1, source_target_pairs={{0,3},{1,2},{2,1},{3,0},{4,7},{5,6},{6,5},{7,4},{8,11},{9,10},{10,... | collective-permute-start | bytes 159752 | tf_op jit(solution)/shard_map/ppermute | solution.py:288
  79.5 6.6 %collective-permute-start.16 = (bf16[208,128]{1,0:T(8,128)(2,1)S(1)}, bf16[208,128]{1,0:T(8,128)(2,1)S(1)}, u32[]{:S(2)}, u32[]{:S(2)}) collective-permute-start(bf16[208,128]{1,0:T(8,128)(2,1)S(1)} %get-tuple-element.63), channel_id=1, source_target_pairs={{0,4},{1,5},{2,6},{3,7},{4,0},{5,1},{6,2},{7,3},{8,12},{9,13},{10,... | collective-permute-start | bytes 159752 | tf_op jit(solution)/shard_map/ppermute | solution.py:288
  80.5 6.1 %collective-permute-start.17 = (bf16[208,128]{1,0:T(8,128)(2,1)S(1)}, bf16[208,128]{1,0:T(8,128)(2,1)S(1)}, u32[]{:S(2)}, u32[]{:S(2)}) collective-permute-start(bf16[208,128]{1,0:T(8,128)(2,1)S(1)} %get-tuple-element.64), channel_id=1, source_target_pairs={{0,5},{1,4},{2,7},{3,6},{4,1},{5,0},{6,3},{7,2},{8,13},{9,12},{10,... | collective-permute-start | bytes 159752 | tf_op jit(solution)/shard_map/ppermute | solution.py:288
  81.3 7.5 %collective-permute-start.18 = (bf16[208,128]{1,0:T(8,128)(2,1)S(1)}, bf16[208,128]{1,0:T(8,128)(2,1)S(1)}, u32[]{:S(2)}, u32[]{:S(2)}) collective-permute-start(bf16[208,128]{1,0:T(8,128)(2,1)S(1)} %get-tuple-element.65), channel_id=1, source_target_pairs={{0,6},{1,7},{2,4},{3,5},{4,2},{5,3},{6,0},{7,1},{8,14},{9,15},{10,... | collective-permute-start | bytes 159752 | tf_op jit(solution)/shard_map/ppermute | solution.py:288
  82.2 7.9 %collective-permute-start.19 = (bf16[208,128]{1,0:T(8,128)(2,1)S(1)}, bf16[208,128]{1,0:T(8,128)(2,1)S(1)}, u32[]{:S(2)}, u32[]{:S(2)}) collective-permute-start(bf16[208,128]{1,0:T(8,128)(2,1)S(1)} %get-tuple-element.66), channel_id=1, source_target_pairs={{0,7},{1,6},{2,5},{3,4},{4,3},{5,2},{6,1},{7,0},{8,15},{9,14},{10,... | collective-permute-start | bytes 159752 | tf_op jit(solution)/shard_map/ppermute | solution.py:288
  83.9 9.5 %collective-permute-start.20 = (bf16[208,128]{1,0:T(8,128)(2,1)S(1)}, bf16[208,128]{1,0:T(8,128)(2,1)S(1)}, u32[]{:S(2)}, u32[]{:S(2)}) collective-permute-start(bf16[208,128]{1,0:T(8,128)(2,1)S(1)} %get-tuple-element.67), channel_id=1, source_target_pairs={{0,8},{1,9},{2,10},{3,11},{4,12},{5,13},{6,14},{7,15},{8,0},{9,1},... | collective-permute-start | bytes 159752 | tf_op jit(solution)/shard_map/ppermute | solution.py:288
  86.1 8.8 %collective-permute-start.21 = (bf16[208,128]{1,0:T(8,128)(2,1)S(1)}, bf16[208,128]{1,0:T(8,128)(2,1)S(1)}, u32[]{:S(2)}, u32[]{:S(2)}) collective-permute-start(bf16[208,128]{1,0:T(8,128)(2,1)S(1)} %get-tuple-element.68), channel_id=1, source_target_pairs={{0,9},{1,8},{2,11},{3,10},{4,13},{5,12},{6,15},{7,14},{8,1},{9,0},... | collective-permute-start | bytes 159752 | tf_op jit(solution)/shard_map/ppermute | solution.py:288
  86.6 13.2 %collective-permute-start.22 = (bf16[208,128]{1,0:T(8,128)(2,1)S(1)}, bf16[208,128]{1,0:T(8,128)(2,1)S(1)}, u32[]{:S(2)}, u32[]{:S(2)}) collective-permute-start(bf16[208,128]{1,0:T(8,128)(2,1)S(1)} %get-tuple-element.69), channel_id=1, source_target_pairs={{0,10},{1,11},{2,8},{3,9},{4,14},{5,15},{6,12},{7,13},{8,2},{9,3},... | collective-permute-start | bytes 159752 | tf_op jit(solution)/shard_map/ppermute | solution.py:288
  88.9 13.3 %collective-permute-start.23 = (bf16[208,128]{1,0:T(8,128)(2,1)S(1)}, bf16[208,128]{1,0:T(8,128)(2,1)S(1)}, u32[]{:S(2)}, u32[]{:S(2)}) collective-permute-start(bf16[208,128]{1,0:T(8,128)(2,1)S(1)} %get-tuple-element.70), channel_id=1, source_target_pairs={{0,11},{1,10},{2,9},{3,8},{4,15},{5,14},{6,13},{7,12},{8,3},{9,2},... | collective-permute-start | bytes 159752 | tf_op jit(solution)/shard_map/ppermute | solution.py:288
  90.1 12.0 %collective-permute-start.24 = (bf16[208,128]{1,0:T(8,128)(2,1)S(1)}, bf16[208,128]{1,0:T(8,128)(2,1)S(1)}, u32[]{:S(2)}, u32[]{:S(2)}) collective-permute-start(bf16[208,128]{1,0:T(8,128)(2,1)S(1)} %get-tuple-element.71), channel_id=1, source_target_pairs={{0,12},{1,13},{2,14},{3,15},{4,8},{5,9},{6,10},{7,11},{8,4},{9,5},... | collective-permute-start | bytes 159752 | tf_op jit(solution)/shard_map/ppermute | solution.py:288
  93.5 8.7 %collective-permute-start.25 = (bf16[208,128]{1,0:T(8,128)(2,1)S(1)}, bf16[208,128]{1,0:T(8,128)(2,1)S(1)}, u32[]{:S(2)}, u32[]{:S(2)}) collective-permute-start(bf16[208,128]{1,0:T(8,128)(2,1)S(1)} %get-tuple-element.72), channel_id=1, source_target_pairs={{0,13},{1,12},{2,15},{3,14},{4,9},{5,8},{6,11},{7,10},{8,5},{9,4},... | collective-permute-start | bytes 159752 | tf_op jit(solution)/shard_map/ppermute | solution.py:288
  95.0 7.2 %collective-permute-start.26 = (bf16[208,128]{1,0:T(8,128)(2,1)S(1)}, bf16[208,128]{1,0:T(8,128)(2,1)S(1)}, u32[]{:S(2)}, u32[]{:S(2)}) collective-permute-start(bf16[208,128]{1,0:T(8,128)(2,1)S(1)} %get-tuple-element.73), channel_id=1, source_target_pairs={{0,14},{1,15},{2,12},{3,13},{4,10},{5,11},{6,8},{7,9},{8,6},{9,7},... | collective-permute-start | bytes 159752 | tf_op jit(solution)/shard_map/ppermute | solution.py:288
  99.9 6.4 %collective-permute-start.27 = (bf16[208,128]{1,0:T(8,128)(2,1)S(1)}, bf16[208,128]{1,0:T(8,128)(2,1)S(1)}, u32[]{:S(2)}, u32[]{:S(2)}) collective-permute-start(bf16[208,128]{1,0:T(8,128)(2,1)S(1)} %get-tuple-element.74), channel_id=1, source_target_pairs={{0,15},{1,14},{2,13},{3,12},{4,11},{5,10},{6,9},{7,8},{8,7},{9,6},... | collective-permute-start | bytes 159752 | tf_op jit(solution)/shard_map/ppermute | solution.py:288
  (28 other events, 40.4 us)

commit v3 on v2

--- a/solution.py
+++ b/solution.py
@@ -12,6 +12,7 @@
 LANES = 128
 POWER = 9
 TOP_EXPONENT = 13
+LIMIT = 60 * 2**20
 
 
 def contract_last(left_side, right_side):
@@ -71,14 +72,18 @@
     return labels, copies
 
 
-def prep_kernel(pos_ref, occ_vals_ref, amps_ref, win_ref, mix_ref):
+def prep_kernel(pos_ref, occ_vals_ref, cyc_ref, amps_ref, block_ref, mix_ref):
     occupied, _, _, _ = amps_ref.shape
     rows = mix_ref.shape[0]
     per_device = rows // occupied
-    win = amps_ref[:, :, 0, :].astype(jnp.float32).reshape(occupied * occupied, LANES)
-    lane = lax.broadcasted_iota(jnp.int32, win.shape, 1)
-    win = jnp.where(lane < DW, win, 0.0)
-    win_ref[...] = pltpu.roll(win, pos_ref[0] * DW, axis=1).astype(jnp.bfloat16)
+    block_ref[:rows, :] = cyc_ref[...].astype(jnp.float32).reshape(rows, LANES).astype(jnp.bfloat16)
+    lane = lax.broadcasted_iota(jnp.int32, (occupied, LANES), 1)
+    packed = jnp.zeros((occupied, LANES), jnp.float32)
+    for j in range(occupied):
+        w = jnp.where(lane < DW, amps_ref[:, j, 0, :].astype(jnp.float32), 0.0)
+        packed = packed + (pltpu.roll(w, j * DW, axis=1) if j else w)
+    packed = jnp.concatenate([packed, jnp.zeros_like(packed)], axis=0)
+    block_ref[rows:, :] = packed.astype(jnp.bfloat16)
     r = lax.broadcasted_iota(jnp.int32, (rows, rows), 0)
     c = lax.broadcasted_iota(jnp.int32, (rows, rows), 1)
     mix = jnp.zeros((rows, rows), jnp.float32)
@@ -119,28 +124,54 @@
     cyc_ref[0] = acc.astype(jnp.bfloat16)
 
 
-def tie(blocks, windows, after):
+def stack(blocks, after):
+    heads = [b.shape[0] for b in blocks]
     count = len(blocks)
 
     def kernel(*refs):
-        ins, outs = refs[: count + len(windows) + 1], refs[count + len(windows) + 1 :]
-        if windows:
-            total = ins[count][...]
-            for ref in ins[count + 1 : count + len(windows)]:
-                total = total + ref[...]
-            outs[count][...] = total
+        out, sems = refs[count + 1], refs[count + 2]
+        copies = []
+        at = 0
+        for n in range(count):
+            copies.append(
+                pltpu.make_async_copy(refs[n], out.at[at : at + heads[n]], sems.at[n])
+            )
+            at += heads[n]
+        for copy in copies:
+            copy.start()
+        for copy in copies:
+            copy.wait()
 
     anywhere = pl.BlockSpec(memory_space=pl.ANY)
-    vmem = pl.BlockSpec(memory_space=pltpu.VMEM)
+    shape = (sum(heads),) + blocks[0].shape[1:]
     return pl.pallas_call(
         kernel,
-        out_shape=tuple(jax.ShapeDtypeStruct(b.shape, b.dtype) for b in blocks)
-        + tuple(jax.ShapeDtypeStruct(w.shape, w.dtype) for w in windows[:1]),
-        in_specs=[anywhere] * count + [vmem] * len(windows) + [anywhere],
-        out_specs=(anywhere,) * count + (vmem,) * len(windows[:1]),
-        input_output_aliases={n: n for n in range(count)},
-        cost_estimate=pl.CostEstimate(flops=0, bytes_accessed=0, transcendentals=0),
-    )(*blocks, *windows, after)
+        out_shape=jax.ShapeDtypeStruct(shape, blocks[0].dtype),
+        in_specs=[anywhere] * (count + 1),
+        out_specs=anywhere,
+        scratch_shapes=[pltpu.SemaphoreType.DMA((count,))],
+        compiler_params=pltpu.CompilerParams(vmem_limit_bytes=LIMIT),
+        cost_estimate=pl.CostEstimate(flops=0, bytes_accessed=10**6, transcendentals=0),
+    )(*blocks, after)
+
+
+def unpack_kernel(pos_ref, blocks_ref, after_ref, win_ref):
+    count, _, lanes = blocks_ref.shape
+    occupied = win_ref.shape[0] // 8
+    lane = lax.broadcasted_iota(jnp.int32, (8, lanes), 1)
+    quarter = count // 2
+    parts = []
+    for j in range(occupied):
+        total = jnp.zeros((8, lanes), jnp.float32)
+        for n in range(count):
+            flip = ((n // quarter) << 1) | ((n % quarter) << 2)
+            p = pos_ref[0] ^ flip
+            w = blocks_ref[n][:8].astype(jnp.float32)
+            shift = lax.rem(p * DW - j * DW + lanes, lanes)
+            w = jnp.where(jnp.logical_and(lane >= j * DW, lane < (j + 1) * DW), w, 0.0)
+            total = total + pltpu.roll(w, shift, axis=1)
+        parts.append(total)
+    win_ref[...] = jnp.concatenate(parts, axis=0).astype(jnp.bfloat16)
 
 
 def payload_pieces(per_device, pairs, dests):
@@ -159,7 +190,9 @@
     return out
 
 
-def ladder_kernel(occ_ref, win0_ref, win1_ref, half0, half1, half2, half3, u_ref, lad_ref, out_ref, w1_ref, w2_ref, ls_ref):
+def ladder_kernel(parts, occ_ref, win0_ref, win1_ref, *refs):
+    halves = refs[: len(parts)]
+    u_ref, lad_ref, out_ref, w1_ref, w2_ref, ls_ref = refs[len(parts) :]
     step = pl.program_id(0)
     occupied = occ_ref.shape[0]
     pairs, _, virtuals = out_ref.shape
@@ -171,7 +204,7 @@
         for i in range(occupied):
             for j in range(occupied):
                 row = (labels[i] ^ labels[j]) * pairs + 2 * i + copies[j]
-                w2_ref[pl.ds(row, 1), :] = w1_ref[i * occupied + j : i * occupied + j + 1, :]
+                w2_ref[pl.ds(row, 1), :] = w1_ref[j * occupied + i : j * occupied + i + 1, :]
 
     w2 = w2_ref[...].astype(jnp.bfloat16)
     u8 = u_ref[pl.ds(pl.multiple_of(step * 8, 8), 8), :]
@@ -182,34 +215,41 @@
         for v in range(1, 4):
             sel = jnp.where(ua == v, ladder[v * pairs : (v + 1) * pairs], sel)
         ls_ref[:, a, :] = sel
-    parts = (half0, half1, half2, half3)
-    per = pairs // len(parts)
-    for n, part in enumerate(parts):
-        out_ref[n * per : (n + 1) * per] = part[...] + ls_ref[n * per : (n + 1) * per]
-
-
-def cycle_kernel(dests, pos_ref, occ_ref, *refs):
-    own_ref, mate_ref, cyc0, cyc1, cyc2, cyc3, half_ref, u_ref, out_ref = refs[:9]
-    send_refs = refs[9 : 9 + dests]
-    xs_ref, pay_ref = refs[9 + dests :]
+    at = 0
+    for part, count in zip(halves, parts):
+        out_ref[at : at + 2 * count] = part[...] + ls_ref[at : at + 2 * count]
+        at += 2 * count
+
+
+def cycle_kernel(parts, pos_ref, occ_ref, own_ref, mate_ref, *refs):
+    cycs = refs[: len(parts)]
+    half_ref, u_ref, out_ref, send_ref, xs_ref, acc_ref, pay_ref, sems = refs[len(parts) :]
     occupied = occ_ref.shape[0]
-    pairs, per_device, virtuals = half_ref.shape
+    pairs, per_device, virtuals = acc_ref.shape
+    dests = send_ref.shape[0]
+    rows = occupied * per_device
+    load = pltpu.make_async_copy(half_ref, acc_ref, sems.at[0])
+    load.start()
     labels, copies = labels_and_copies(occ_ref, occupied)
     pos = pos_ref[0]
     for r in range(dests):
         ref = mate_ref if r & 1 else own_ref
-        block = ref[((r >> 1) & 1) * (dests // 4) + (r >> 2)].astype(jnp.float32)
-        xs_ref[pl.ds((pos ^ r) * per_device, per_device)] = block
+        block = ref[((r >> 1) & 1) * (dests // 4) + (r >> 2)][:rows].astype(jnp.float32)
+        xs_ref[pl.ds((pos ^ r) * per_device, per_device)] = block.reshape(
+            per_device, occupied, LANES
+        )
     u = u_ref[...]
-    out_ref[...] = half_ref[...]
-    left = jnp.concatenate([ref[...] for ref in (cyc0, cyc1, cyc2, cyc3)], axis=0)
-    left = left.astype(jnp.float32).reshape(occupied * per_device, LANES).astype(jnp.bfloat16)
+    left = jnp.concatenate([ref[...].astype(jnp.float32) for ref in cycs], axis=0)
+    left = left.reshape(rows, LANES).astype(jnp.bfloat16)
+    load.wait()
     for j in range(occupied):
         c = contract_last(left, xs_ref[:, j, :].astype(jnp.bfloat16))
         for i in range(occupied):
             e = 2 * i + copies[j]
             part = c[i * per_device : (i + 1) * per_device]
-            out_ref[e] = out_ref[e] + jnp.where(u == (labels[i] ^ labels[j]), part, 0.0)
+            acc_ref[e] = acc_ref[e] + jnp.where(u == (labels[i] ^ labels[j]), part, 0.0)
+    store = pltpu.make_async_copy(acc_ref, out_ref, sems.at[0])
+    store.start()
 
     pieces_of = payload_pieces(per_device, pairs, dests)
     lane = lax.broadcasted_iota(jnp.int32, (8, LANES), 1)
@@ -219,7 +259,7 @@
         tiles = {}
         for e in range(pairs):
             for v in range(virtuals // LANES):
-                x = out_ref[e, rows, v * LANES : (v + 1) * LANES]
+                x = acc_ref[e, rows, v * LANES : (v + 1) * LANES]
                 top = jnp.maximum(top, jnp.abs(x))
                 tiles[e, v] = x
         rolled = {}
@@ -232,7 +272,7 @@
                 x = rolled[e, v, shift]
                 acc = x if acc is None else jnp.where(lane >= first, x, acc)
             at = pl.ds(pl.multiple_of(t * per_device + g * 8, 8), 8)
-            pay_ref[pos ^ q, at, :] = acc
+            pay_ref[q, at, :] = acc
         return top
 
     top = lax.fori_loop(0, per_device // 8, group, jnp.zeros((8, LANES), jnp.float32))
@@ -242,34 +282,35 @@
     count = pay_ref.shape[1]
     row = lax.broadcasted_iota(jnp.int32, (count, LANES), 0)
     data_rows = (virtuals // LANES) * per_device
-    for r in range(dests):
-        z = pay_ref[r] * scale
+    for q in range(dests):
+        z = pay_ref[q] * scale
         z2 = z * z
         z4 = z2 * z2
         y = jnp.where(row >= data_rows, k, z4 * z4 * z)
-        send_refs[r][...] = y.astype(jnp.bfloat16)
-
-
-def join_kernel(dests, pos_ref, occ_ref, half_ref, u_ref, *refs):
-    recv_refs = refs[:dests]
-    out_ref, dec_ref, mir_ref = refs[dests:]
+        send_ref[q] = y.astype(jnp.bfloat16)
+    store.wait()
+
+
+def join_kernel(occ_ref, half_ref, recv_ref, u_ref, out_ref, dec_ref, mir_ref):
     i = pl.program_id(0)
     occupied = occ_ref.shape[0]
     _, per_device, virtuals = half_ref.shape
+    dests = recv_ref.shape[0]
     tiles = virtuals // LANES
     labels, copies = labels_and_copies(occ_ref, occupied)
 
     @pl.when(i == 0)
     def _():
-        for r in range(dests):
-            block = recv_refs[r][...].astype(jnp.float32)
+        for p in range(dests):
+            block = recv_ref[p].astype(jnp.float32)
             k = block[tiles * per_device : tiles * per_device + 1, 0:1]
             y = block[: tiles * per_device]
             size = jnp.exp2(jnp.log2(jnp.maximum(jnp.abs(y), 2.0**-126)) * (1.0 / POWER) - k)
             x = jnp.where(y < 0, -size, jnp.where(y > 0, size, 0.0))
-            at = pl.ds(pl.multiple_of((pos_ref[0] ^ r) * per_device, 8), per_device)
             for t in range(tiles):
-                dec_ref[t, at, :] = x[t * per_device : (t + 1) * per_device]
+                dec_ref[t, p * per_device : (p + 1) * per_device, :] = x[
+                    t * per_device : (t + 1) * per_device
+                ]
         for t in range(tiles):
             mir_ref[t * LANES : (t + 1) * LANES, :] = dec_ref[t].T
 
@@ -300,46 +341,49 @@
     vir_local = lax.dynamic_slice_in_dim(vir_irrep, position * per_device, per_device)
     u = jnp.bitwise_xor(vir_local[:, None], vir_irrep[None, :])
     smem = pl.BlockSpec(memory_space=pltpu.SMEM)
-    limit = 40 * 2**20
 
     def whole(shape):
         return pl.BlockSpec(shape, lambda n: (0,) * len(shape))
 
     def params():
-        return pltpu.CompilerParams(vmem_limit_bytes=limit)
+        return pltpu.CompilerParams(vmem_limit_bytes=LIMIT)
 
     def cost(flops, size):
         return pl.CostEstimate(flops=flops, bytes_accessed=size, transcendentals=0)
 
     anywhere = pl.BlockSpec(memory_space=pl.ANY)
     quarter = dests // 4
-    x_z = [cycle_ints] + [permute(cycle_ints, m << 2, dests) for m in range(1, quarter)]
-    x_y = [permute(cycle_ints, 2, dests)]
-    corner = amps[:, :, :16, :LANES]
-    win, mix = pl.pallas_call(
+    block_rows = rows + 16
+    block, mix = pl.pallas_call(
         prep_kernel,
+        grid=(1,),
         out_shape=(
-            jax.ShapeDtypeStruct((occupied * occupied, LANES), bf16),
+            jax.ShapeDtypeStruct((block_rows, LANES), bf16),
             jax.ShapeDtypeStruct((rows, rows), bf16),
         ),
-        in_specs=[smem] + [pl.BlockSpec(memory_space=pltpu.VMEM)] * 2,
+        in_specs=[
+            smem,
+            whole(fock_occ.shape),
+            whole(cycle_ints.shape),
+            pl.BlockSpec((occupied, occupied, 16, LANES), lambda n: (0, 0, 0, 0)),
+        ],
+        out_specs=(whole((block_rows, LANES)), whole((rows, rows))),
         compiler_params=params(),
         cost_estimate=cost(0, 500000),
-    )(pos, fock_occ, corner)
-    wins = [win] + [permute(win, m << 2, dests) for m in range(1, quarter)]
+    )(pos, fock_occ, cycle_ints, amps)
+    block = block.reshape(1, block_rows, LANES)
 
     flat_amps = amps.reshape(occupied, rows, virtuals)
-    parts = 4
-    per_part = occupied // parts
+    parts = (3, 3, 2)
 
     def fock_part(n, after):
-        first = n * per_part
+        first, count = sum(parts[:n]), parts[n]
         return pl.pallas_call(
             functools.partial(fock_kernel, first),
-            grid=(per_part,),
+            grid=(count,),
             out_shape=(
-                jax.ShapeDtypeStruct((2 * per_part, per_device, virtuals), f32),
-                jax.ShapeDtypeStruct((per_part, per_device, LANES), bf16),
+                jax.ShapeDtypeStruct((2 * count, per_device, virtuals), f32),
+                jax.ShapeDtypeStruct((count, per_device, LANES), bf16),
             ),
             in_specs=[
                 smem,
@@ -355,29 +399,40 @@
             ),
             scratch_shapes=[pltpu.VMEM((occupied, per_device, virtuals), f32)],
             compiler_params=params(),
-            cost_estimate=cost(3 * per_part * rows * virtuals * virtuals, 2 * 10**6),
+            cost_estimate=cost(3 * count * rows * virtuals * virtuals, 2 * 10**6),
         )(occ_irrep, flat_amps, fock_vir, mix, u, after)
 
+    z1, z2, z3 = [permute(block, m << 2, dests) for m in range(1, quarter)]
     half0, cyc0 = fock_part(0, mix)
-    (x_z[1],) = tie([x_z[1]], [], half0)
-    x_y.append(permute(x_z[1], 2, dests))
-    half1, cyc1 = fock_part(1, x_z[1])
-    *x_z[2:], win = tie(x_z[2:], wins, half1)
-    x_y.extend(permute(b, 2, dests) for b in x_z[2:])
-    win_y = permute(win, 2, dests)
-    half2, cyc2 = fock_part(2, x_z[2])
-    *x_y, win = tie(x_y, [win, win_y], half2)
-    own_blocks = jnp.stack(x_z + list(x_y))
+    near = stack([block, z1], half0)
+    near_y = permute(near, 2, dests)
+    half1, cyc1 = fock_part(1, near)
+    far = stack([z2, z3], half1)
+    far_y = permute(far, 2, dests)
+    half2, cyc2 = fock_part(2, far)
+    own_blocks = stack([near, far, near_y, far_y], half2)
+    win = pl.pallas_call(
+        unpack_kernel,
+        grid=(1,),
+        out_shape=jax.ShapeDtypeStruct((occupied * occupied, LANES), bf16),
+        in_specs=[
+            smem,
+            pl.BlockSpec((dests // 2, 16, LANES), lambda n: (0, rows // 16, 0)),
+            anywhere,
+        ],
+        out_specs=whole((occupied * occupied, LANES)),
+        compiler_params=params(),
+        cost_estimate=cost(0, 10**5),
+    )(pos, own_blocks, own_blocks)
+    win_mate = permute(win, 1, dests)
     mate_blocks = permute(own_blocks, 1, dests)
-    win_mate = permute(win, 1, dests)
-    half3, cyc3 = fock_part(3, x_y[0])
 
     half = pl.pallas_call(
-        ladder_kernel,
+        functools.partial(ladder_kernel, parts),
         grid=(per_device // 8,),
         out_shape=jax.ShapeDtypeStruct((pairs, per_device, virtuals), f32),
         in_specs=[smem, whole(win.shape), whole(win.shape)]
-        + [pl.BlockSpec((2 * per_part, 8, virtuals), lambda n: (0, n, 0))] * parts
+        + [pl.BlockSpec((2 * count, 8, virtuals), lambda n: (0, n, 0)) for count in parts]
         + [whole(u.shape), pl.BlockSpec((8, virtuals, kw), lambda n: (n, 0, 0))],
         out_specs=pl.BlockSpec((pairs, 8, virtuals), lambda n: (0, n, 0)),
         scratch_shapes=[
@@ -387,40 +442,40 @@
         ],
         compiler_params=params(),
         cost_estimate=cost(4 * occupied * rows * virtuals * LANES, 9 * 10**6),
-    )(occ_irrep, win, win_mate, half0, half1, half2, half3, u, ladder_ints)
+    )(occ_irrep, win, win_mate, half0, half1, half2, u, ladder_ints)
 
     send_rows = tiles * per_device + 8
-    piece = jax.ShapeDtypeStruct((send_rows, LANES), bf16)
     vmem = pl.BlockSpec(memory_space=pltpu.VMEM)
-    half, *sends = pl.pallas_call(
-        functools.partial(cycle_kernel, dests),
-        out_shape=(jax.ShapeDtypeStruct(half.shape, f32),) + (piece,) * dests,
-        in_specs=[smem, smem] + [vmem] * 8,
-        out_specs=(vmem,) * (1 + dests),
+    half, send = pl.pallas_call(
+        functools.partial(cycle_kernel, parts),
+        out_shape=(
+            jax.ShapeDtypeStruct(half.shape, f32),
+            jax.ShapeDtypeStruct((dests, send_rows, LANES), bf16),
+        ),
+        in_specs=[smem, smem] + [vmem] * 5 + [anywhere, vmem],
+        out_specs=(anywhere, vmem),
         scratch_shapes=[
             pltpu.VMEM((virtuals, occupied, LANES), f32),
+            pltpu.VMEM(half.shape, f32),
             pltpu.VMEM((dests, send_rows, LANES), f32),
+            pltpu.SemaphoreType.DMA((1,)),
         ],
         compiler_params=params(),
         cost_estimate=cost(2 * occupied * rows * virtuals * LANES, 8 * 10**6),
-    )(pos, occ_irrep, own_blocks, mate_blocks, cyc0, cyc1, cyc2, cyc3, half, u)
-
-    recv = [None] * dests
-    recv[0] = sends[0]
-    for r in reversed(range(1, dests)):
-        recv[r] = permute(sends[r], r, dests)
+    )(pos, occ_irrep, own_blocks, mate_blocks, cyc0, cyc1, cyc2, half, u)
+
+    recv = lax.all_to_all(send, "vir", split_axis=0, concat_axis=0, tiled=True)
 
     return pl.pallas_call(
-        functools.partial(join_kernel, dests),
+        join_kernel,
         grid=(occupied,),
         out_shape=jax.ShapeDtypeStruct((occupied, occupied, per_device, virtuals), f32),
         in_specs=[
             smem,
-            smem,
             pl.BlockSpec((2, per_device, virtuals), lambda n: (n, 0, 0)),
+            whole(recv.shape),
             whole(u.shape),
-        ]
-        + [whole(piece.shape)] * dests,
+        ],
         out_specs=pl.BlockSpec((1, occupied, per_device, virtuals), lambda n: (n, 0, 0, 0)),
         scratch_shapes=[
             pltpu.VMEM((tiles, virtuals, LANES), f32),
@@ -428,7 +483,7 @@
         ],
         compiler_params=params(),
         cost_estimate=cost(10**6, 10**7),
-    )(pos, occ_irrep, half, u, *recv)
+    )(occ_irrep, half, recv, u)
 
 
 def solution(mesh):

time: 114 us -> 121 us (1.061)
  Pallas kernels: 31 us -> 77.8 us
  local copies, waits for them, and re-layouts: 35.6 us -> 3.45 us
  starting transfers between devices: 40.7 us -> 9 us
  blocking collectives: 0 us -> 26.9 us
  waiting for transfers between devices: 4.14 us -> 1.81 us
    pallas_call x11, Pallas kernels: 31 us -> 77.8 us  [the longest x3 34.6 us: stack(): pl.pallas_call(kernel, out_shape=jax.ShapeDtypeStruct(shape, blocks[0].dt...]
    ppermute x28 -> x7, starting transfers between devices: 40.7 us -> 9 us  [permute(): return lax.ppermute(x, 'vir', [(n, n ^ flip) for n in range(size)])]
    unnamed x71 -> x16, local copies, waits for them, and re-layouts: 32.4 us -> 3.38 us
    all_to_all x0 -> x1, blocking collectives: none -> 26.9 us  [body(): recv = lax.all_to_all(send, 'vir', split_axis=0, concat_axis=0, tiled=True)]
    ppermute x28 -> x7, waiting for transfers between devices: 4.14 us -> 1.81 us  [permute(): return lax.ppermute(x, 'vir', [(n, n ^ flip) for n in range(size)])]
    another operation x1 -> x0, local copies, waits for them, and re-layouts: 1.53 us -> none  [body(): own_blocks = jnp.stack(x_z + list(x_y))]
  transfers between devices with their start and end apart: 28 -> 7, of which waited for: 1 -> 2; matrix products, arithmetic and copies ran while one was open for 8% -> 1% of each run, Pallas kernels for 14% -> 30%
where the time goes in v3:
time: 121 us; the launch traced here: 120 us
  Pallas kernels  77.8 us (64%)
  blocking collectives  26.9 us (22%)
  starting transfers between devices  9 us (7%)
  local copies, waits for them, and re-layouts  3.45 us (3%)
  waiting for transfers between devices  1.81 us (1%)
    pallas_call x3, Pallas kernels, stack(): pl.pallas_call(kernel, out_shape=jax.ShapeDtypeStruct(shape, blocks[0].dt...  34.6 us
    all_to_all x1, blocking collectives, body(): recv = lax.all_to_all(send, 'vir', split_axis=0, concat_axis=0, tiled=True)  26.9 us
    pallas_call x3, Pallas kernels, fock_part(): pl.pallas_call(functools.partial(fock_kernel, first), grid=(count,), out_...  13.6 us
    pallas_call x1, Pallas kernels, body(): pl.pallas_call(functools.partial(cycle_kernel, parts), out_shape=(jax.Sha...  10.1 us
    ppermute x7, starting transfers between devices, permute(): return lax.ppermute(x, 'vir', [(n, n ^ flip) for n in range(size)])  9 us
    pallas_call x1, Pallas kernels, body(): pl.pallas_call(join_kernel, grid=(occupied,), out_shape=jax.ShapeDtypeStr...  7.98 us
    pallas_call x1, Pallas kernels, body(): pl.pallas_call(functools.partial(ladder_kernel, parts), grid=(per_device...  7.72 us
    unnamed x16, local copies, waits for them, and re-layouts  3.38 us
  transfers between devices with their start and end apart: 7, of which 2 were waited for; matrix products, arithmetic and copies ran while one was open for 1% of the time, Pallas kernels for 30%

profile of v3, /device:TPU:1, one launch (start us, length us, event | category | flops | bytes accessed | tf_op | source)
XLA Modules:
  0.0 119.8 jit_solution(6049430903734504190)
XLA Ops:
  0.0 2.2 %shard_map.73 = (bf16[336,128]{1,0:T(8,128)(2,1)}, bf16[320,320]{1,0:T(8,128)(2,1)}) custom-call(s32[1]{0:T(128)} %bitcast.pos_ref, bf16[8,8]{1,0:T(8,128)(2,1)} %occ_vals_ref.1, bf16[40,8,128]{2,1,0:T(8,128)(2,1)} %cyc_ref.1, bf16[8,8,40,640]{3,2,1,0:T(8,128)(2,1)} %amps_ref.1), custom_call_target="tpu_custom_call" | custom-call | bytes 500000 | tf_op jit(solution)/shard_map/pallas_call | solution.py:357
  2.2 4.2 %collective-permute-start.2 = (bf16[1,336,128]{2,1,0:T(8,128)(2,1)}, bf16[1,336,128]{2,1,0:T(8,128)(2,1)S(1)}, u32[]{:S(2)}, u32[]{:S(2)}) collective-permute-start(bf16[1,336,128]{2,1,0:T(8,128)(2,1)} %bitcast.6), channel_id=1, source_target_pairs={{0,12},{1,13},{2,14},{3,15},{4,8},{5,9},{6,10},{7,11},{8,4},{9,5},... | collective-permute-start | bytes 258056 | tf_op jit(solution)/shard_map/ppermute | solution.py:329
  6.4 0.0 collective-permute-start.1
  6.4 0.3 collective-permute-start
  6.6 0.1 dynamic_slice.3
  6.7 0.7 broadcast_xor_fusion.u_ref.refs_3_.refs_4_
  7.4 4.9 %shard_map.74 = (f32[6,40,640]{2,1,0:T(8,128)}, bf16[3,40,128]{2,1,0:T(8,128)(2,1)}) custom-call(s32[8]{0:T(128)} %occ_ref.11, bf16[8,320,640]{2,1,0:T(8,128)(2,1)} %bitcast.3, bf16[640,640]{1,0:T(8,128)(2,1)} %fock_ref.5, bf16[320,320]{1,0:T(8,128)(2,1)} %get-tuple-element.16.mix_ref.after_ref, s32[40,640]{1,0:T(8,128)} %broadcast_xor_fusion.u_ref.refs_3_.refs_4_, ...), custom_call_target="tpu_custom_call" | custom-call | flops 1179648000 | bytes 2000000 | tf_op jit(solution)/shard_map/pallas_call | solution.py:381
  12.4 0.6 copy-done.5
  13.0 6.3 %shard_map.75.after_ref.refs_0_ = bf16[2,336,128]{2,1,0:T(8,128)(2,1)} custom-call(bf16[1,336,128]{2,1,0:T(8,128)(2,1)} %bitcast.9, bf16[1,336,128]{2,1,0:T(8,128)(2,1)} %copy-done.5, f32[6,40,640]{2,1,0:T(8,128)} %get-tuple-element.17.refs_2_.refs_0_), custom_call_target="tpu_custom_call" | custom-call | bytes 1000000 | tf_op jit(solution)/shard_map/pallas_call | solution.py:147
  19.3 1.3 %collective-permute-start.3 = (bf16[2,336,128]{2,1,0:T(8,128)(2,1)}, bf16[2,336,128]{2,1,0:T(8,128)(2,1)S(1)}, u32[]{:S(2)}, u32[]{:S(2)}) collective-permute-start(bf16[2,336,128]{2,1,0:T(8,128)(2,1)} %shard_map.75.after_ref.refs_0_), channel_id=1, source_target_pairs={{0,2},{1,3},{2,0},{3,1},{4,6},{5,7},{6,4},{7,5},{8,10},{9,11},{10,... | collective-permute-start | bytes 516104 | tf_op jit(solution)/shard_map/ppermute | solution.py:329
  20.6 4.9 %shard_map.76 = (f32[6,40,640]{2,1,0:T(8,128)}, bf16[3,40,128]{2,1,0:T(8,128)(2,1)}) custom-call(s32[8]{0:T(128)} %occ_ref.11, bf16[8,320,640]{2,1,0:T(8,128)(2,1)} %bitcast.4, bf16[640,640]{1,0:T(8,128)(2,1)} %fock_ref.5, bf16[320,320]{1,0:T(8,128)(2,1)} %get-tuple-element.16.mix_ref.after_ref, s32[40,640]{1,0:T(8,128)} %broadcast_xor_fusion.u_ref.refs_3_.refs_4_, ...), custom_call_target="tpu_custom_call" | custom-call | flops 1179648000 | bytes 2000000 | tf_op jit(solution)/shard_map/pallas_call | solution.py:381
  25.5 0.0 collective-permute-done.2.refs_1_
  25.6 0.6 copy-done.3
  26.1 0.0 copy-done.4
  26.2 6.3 %shard_map.77.after_ref.refs_1_ = bf16[2,336,128]{2,1,0:T(8,128)(2,1)} custom-call(bf16[1,336,128]{2,1,0:T(8,128)(2,1)} %copy-done.4, bf16[1,336,128]{2,1,0:T(8,128)(2,1)} %copy-done.3, f32[6,40,640]{2,1,0:T(8,128)} %get-tuple-element.18.refs_2_.refs_1_), custom_call_target="tpu_custom_call" | custom-call | bytes 1000000 | tf_op jit(solution)/shard_map/pallas_call | solution.py:147
  32.5 0.3 collective-permute-start.4
  32.8 3.8 %shard_map.78 = (f32[4,40,640]{2,1,0:T(8,128)}, bf16[2,40,128]{2,1,0:T(8,128)(2,1)}) custom-call(s32[8]{0:T(128)} %occ_ref.11, bf16[8,320,640]{2,1,0:T(8,128)(2,1)} %bitcast.5, bf16[640,640]{1,0:T(8,128)(2,1)} %fock_ref.5, bf16[320,320]{1,0:T(8,128)(2,1)} %get-tuple-element.16.mix_ref.after_ref, s32[40,640]{1,0:T(8,128)} %broadcast_xor_fusion.u_ref.refs_3_.refs_4_, ...), custom_call_target="tpu_custom_call" | custom-call | flops 786432000 | bytes 2000000 | tf_op jit(solution)/shard_map/pallas_call | solution.py:381
  36.6 0.0 copy-start.1
  36.6 0.4 collective-permute-done.4.refs_3_
  37.1 0.2 copy-done.1
  37.3 0.4 copy-done.2
  37.7 22.0 %shard_map.79.blocks_ref.after_ref.own_ref = bf16[8,336,128]{2,1,0:T(8,128)(2,1)} custom-call(bf16[2,336,128]{2,1,0:T(8,128)(2,1)} %shard_map.75.after_ref.refs_0_, bf16[2,336,128]{2,1,0:T(8,128)(2,1)} %shard_map.77.after_ref.refs_1_, bf16[2,336,128]{2,1,0:T(8,128)(2,1)} %copy-done.1, bf16[2,336,128]{2,1,0:T(8,128)(2,1)} %copy-done.2, ...), custom_call_target="tpu_custom_call" | custom-call | bytes 1000000 | tf_op jit(solution)/shard_map/pallas_call | solution.py:147
  59.7 2.9 %collective-permute-start.5 = (bf16[8,336,128]{2,1,0:T(8,128)(2,1)}, bf16[8,336,128]{2,1,0:T(8,128)(2,1)S(1)}, u32[]{:S(2)}, u32[]{:S(2)}) collective-permute-start(bf16[8,336,128]{2,1,0:T(8,128)(2,1)} %shard_map.79.blocks_ref.after_ref.own_ref), channel_id=1, source_target_pairs={{0,1},{1,0},{2,3},{3,2},{4,5},{5,4},{6,7},{7,6},{8,9},{9,8},{10,11... | collective-permute-start | bytes 2064392 | tf_op jit(solution)/shard_map/ppermute | solution.py:329
  62.7 1.6 %shard_map.80.win0_ref = bf16[64,128]{1,0:T(8,128)(2,1)} custom-call(s32[1]{0:T(128)} %bitcast.pos_ref, bf16[8,336,128]{2,1,0:T(8,128)(2,1)} %shard_map.79.blocks_ref.after_ref.own_ref, bf16[8,336,128]{2,1,0:T(8,128)(2,1)} %shard_map.79.blocks_ref.after_ref.own_ref), custom_call_target="tpu_custom_call" | custom-call | bytes 100000 | tf_op jit(solution)/shard_map/pallas_call | solution.py:414
  64.2 0.0 collective-permute-start.6
  64.2 1.4 %collective-permute-done.6.win1_ref = bf16[64,128]{1,0:T(8,128)(2,1)S(1)} collective-permute-done((bf16[64,128]{1,0:T(8,128)(2,1)}, bf16[64,128]{1,0:T(8,128)(2,1)S(1)}, u32[]{:S(2)}, u32[]{:S(2)}) %collective-permute-start.6) | collective-permute-done | bytes 16416 | tf_op jit(solution)/shard_map/ppermute | solution.py:329
  65.6 0.6 copy-done.6
  66.2 7.7 %shard_map.81.refs_3_ = f32[16,40,640]{2,1,0:T(8,128)} custom-call(s32[8]{0:T(128)} %occ_ref.11, bf16[64,128]{1,0:T(8,128)(2,1)} %shard_map.80.win0_ref, bf16[64,128]{1,0:T(8,128)(2,1)} %copy-done.6, f32[6,40,640]{2,1,0:T(8,128)} %get-tuple-element.17.refs_2_.refs_0_, f32[6,40,640]{2,1,0:T(8,128)} %get-tuple-element.18.refs_2_.refs_1_, ...), custom_call_target="tpu_custom_call" | custom-call | flops 838860800 | bytes 9000000 | tf_op jit(solution)/shard_map/pallas_call | solution.py:430
  74.0 0.9 copy-done
  74.8 10.1 %shard_map.82 = (f32[16,40,640]{2,1,0:T(8,128)}, bf16[16,208,128]{2,1,0:T(8,128)(2,1)}) custom-call(s32[1]{0:T(128)} %bitcast.pos_ref, s32[8]{0:T(128)} %occ_ref.11, bf16[8,336,128]{2,1,0:T(8,128)(2,1)} %shard_map.79.blocks_ref.after_ref.own_ref, bf16[8,336,128]{2,1,0:T(8,128)(2,1)} %copy-done, bf16[3,40,128]{2,1,0:T(8,128)(2,1)} %get-tuple-element.20.refs_0_, ...), custom_call_target="tpu_custom_call" | custom-call | flops 419430400 | bytes 8000000 | tf_op jit(solution)/shard_map/pallas_call | solution.py:449
  84.9 26.9 %all_to_all.5.recv_ref = bf16[16,208,128]{2,1,0:T(8,128)(2,1)} all-to-all(bf16[16,208,128]{2,1,0:T(8,128)(2,1)} %get-tuple-element.24), channel_id=1, replica_groups=mesh['groups'=2,'vir'=16] {'vir'}, dimensions={0} | all-to-all | bytes 1703936 | tf_op jit(solution)/shard_map/all_to_all | solution.py:467
  111.8 8.0 %shard_map.83 = f32[8,8,40,640]{3,2,1,0:T(8,128)} custom-call(s32[8]{0:T(128)} %occ_ref.11, f32[16,40,640]{2,1,0:T(8,128)} %get-tuple-element.23.half_ref, bf16[16,208,128]{2,1,0:T(8,128)(2,1)} %all_to_all.5.recv_ref, s32[40,640]{1,0:T(8,128)} %broadcast_xor_fusion.u_ref.refs_3_.refs_4_), custom_call_target="tpu_custom_call" | custom-call | flops 1000000 | bytes 10000000 | tf_op jit(solution)/shard_map/pallas_call | solution.py:469
  (12 shorter events, 0.0 us)
Async XLA Ops:
  0.0 6.6 %copy-start.7 = (s32[640]{0:T(1024)S(1)}, s32[640]{0:T(1024)}, u32[]{:S(2)}) copy-start(s32[640]{0:T(1024)} %param.13) | copy-start | bytes 7684
  2.2 23.3 %collective-permute-start.2 = (bf16[1,336,128]{2,1,0:T(8,128)(2,1)}, bf16[1,336,128]{2,1,0:T(8,128)(2,1)S(1)}, u32[]{:S(2)}, u32[]{:S(2)}) collective-permute-start(bf16[1,336,128]{2,1,0:T(8,128)(2,1)} %bitcast.6), channel_id=1, source_target_pairs={{0,12},{1,13},{2,14},{3,15},{4,8},{5,9},{6,10},{7,11},{8,4},{9,5},... | collective-permute-start | bytes 258056 | tf_op jit(solution)/shard_map/ppermute | solution.py:329
  6.4 19.2 %collective-permute-start.1 = (bf16[1,336,128]{2,1,0:T(8,128)(2,1)}, bf16[1,336,128]{2,1,0:T(8,128)(2,1)S(1)}, u32[]{:S(2)}, u32[]{:S(2)}) collective-permute-start(bf16[1,336,128]{2,1,0:T(8,128)(2,1)} %bitcast.7), channel_id=1, source_target_pairs={{0,8},{1,9},{2,10},{3,11},{4,12},{5,13},{6,14},{7,15},{8,0},{9,1},... | collective-permute-start | bytes 258056 | tf_op jit(solution)/shard_map/ppermute | solution.py:329
  6.4 6.0 %collective-permute-start = (bf16[1,336,128]{2,1,0:T(8,128)(2,1)}, bf16[1,336,128]{2,1,0:T(8,128)(2,1)S(1)}, u32[]{:S(2)}, u32[]{:S(2)}) collective-permute-start(bf16[1,336,128]{2,1,0:T(8,128)(2,1)} %bitcast.8), channel_id=1, source_target_pairs={{0,4},{1,5},{2,6},{3,7},{4,0},{5,1},{6,2},{7,3},{8,12},{9,13},{10,... | collective-permute-start | bytes 258056 | tf_op jit(solution)/shard_map/ppermute | solution.py:329
  12.4 0.6 copy-start.5
  19.3 17.3 %collective-permute-start.3 = (bf16[2,336,128]{2,1,0:T(8,128)(2,1)}, bf16[2,336,128]{2,1,0:T(8,128)(2,1)S(1)}, u32[]{:S(2)}, u32[]{:S(2)}) collective-permute-start(bf16[2,336,128]{2,1,0:T(8,128)(2,1)} %shard_map.75.after_ref.refs_0_), channel_id=1, source_target_pairs={{0,2},{1,3},{2,0},{3,1},{4,6},{5,7},{6,4},{7,5},{8,10},{9,11},{10,... | collective-permute-start | bytes 516104 | tf_op jit(solution)/shard_map/ppermute | solution.py:329
  25.5 0.6 copy-start.3
  25.5 0.6 copy-start.4
  32.5 4.5 %collective-permute-start.4 = (bf16[2,336,128]{2,1,0:T(8,128)(2,1)}, bf16[2,336,128]{2,1,0:T(8,128)(2,1)S(1)}, u32[]{:S(2)}, u32[]{:S(2)}) collective-permute-start(bf16[2,336,128]{2,1,0:T(8,128)(2,1)} %shard_map.77.after_ref.refs_1_), channel_id=1, source_target_pairs={{0,2},{1,3},{2,0},{3,1},{4,6},{5,7},{6,4},{7,5},{8,10},{9,11},{10,... | collective-permute-start | bytes 516104 | tf_op jit(solution)/shard_map/ppermute | solution.py:329
  36.6 0.7 copy-start.1
  37.1 0.7 copy-start.2
  59.7 14.2 %collective-permute-start.5 = (bf16[8,336,128]{2,1,0:T(8,128)(2,1)}, bf16[8,336,128]{2,1,0:T(8,128)(2,1)S(1)}, u32[]{:S(2)}, u32[]{:S(2)}) collective-permute-start(bf16[8,336,128]{2,1,0:T(8,128)(2,1)} %shard_map.79.blocks_ref.after_ref.own_ref), channel_id=1, source_target_pairs={{0,1},{1,0},{2,3},{3,2},{4,5},{5,4},{6,7},{7,6},{8,9},{9,8},{10,11... | collective-permute-start | bytes 2064392 | tf_op jit(solution)/shard_map/ppermute | solution.py:329
  64.2 1.4 %collective-permute-start.6 = (bf16[64,128]{1,0:T(8,128)(2,1)}, bf16[64,128]{1,0:T(8,128)(2,1)S(1)}, u32[]{:S(2)}, u32[]{:S(2)}) collective-permute-start(bf16[64,128]{1,0:T(8,128)(2,1)} %shard_map.80.win0_ref), channel_id=1, source_target_pairs={{0,1},{1,0},{2,3},{3,2},{4,5},{5,4},{6,7},{7,6},{8,9},{9,8},{10,11... | collective-permute-start | bytes 49160 | tf_op jit(solution)/shard_map/ppermute | solution.py:329
  65.6 0.6 copy-start.6
  74.0 0.9 copy-start

commit v4 on v3

--- a/solution.py
+++ b/solution.py
@@ -12,7 +12,6 @@
 LANES = 128
 POWER = 9
 TOP_EXPONENT = 13
-LIMIT = 60 * 2**20
 
 
 def contract_last(left_side, right_side):
@@ -61,6 +60,10 @@
     return allowed * (half_sum + mirrored)
 
 
+def params(mib):
+    return pltpu.CompilerParams(vmem_limit_bytes=mib * 2**20)
+
+
 def labels_and_copies(occ_ref, occupied):
     labels = [occ_ref[j] for j in range(occupied)]
     copies = []
@@ -102,55 +105,52 @@
 
 
 def fock_kernel(first, occ_ref, amps_ref, fock_ref, mix_ref, u_ref, after_ref, half_ref, cyc_ref, hs_ref):
-    i = pl.program_id(0) + first
-    _, per_device, virtuals = half_ref.shape
+    wide, rows, virtuals = amps_ref.shape
+    _, per_device, _ = half_ref.shape
     occupied = occ_ref.shape[0]
     labels, copies = labels_and_copies(occ_ref, occupied)
-    a = amps_ref[0]
-    h = jnp.dot(a, fock_ref[...], preferred_element_type=jnp.float32)
-    h = h - jnp.dot(mix_ref[...], a, preferred_element_type=jnp.float32)
-    hs_ref[...] = h.reshape(occupied, per_device, virtuals)
-    own = occ_ref[i]
     u = u_ref[...]
-    for j in range(occupied):
-        s = copies[j]
-        half_ref[s] = jnp.where(u == (own ^ labels[j]), hs_ref[j], half_ref[s])
-    head = a[:, :LANES].astype(jnp.float32)
-    lane = lax.broadcasted_iota(jnp.int32, (per_device, LANES), 1)
-    acc = jnp.zeros((per_device, LANES), jnp.float32)
-    for k in range(occupied):
-        piece = jnp.where(lane < CW, head[k * per_device : (k + 1) * per_device], 0.0)
-        acc = acc + (pltpu.roll(piece, k * CW, axis=1) if k else piece)
-    cyc_ref[0] = acc.astype(jnp.bfloat16)
+    h = jnp.dot(
+        amps_ref[...].reshape(wide * rows, virtuals),
+        fock_ref[...],
+        preferred_element_type=jnp.float32,
+    )
+    for w in range(wide):
+        a = amps_ref[w]
+        mixed = jnp.dot(mix_ref[...], a, preferred_element_type=jnp.float32)
+        hs_ref[...] = (h[w * rows : (w + 1) * rows] - mixed).reshape(hs_ref.shape)
+        own = occ_ref[pl.program_id(0) * wide + w + first]
+        for j in range(occupied):
+            at = 2 * w + copies[j]
+            half_ref[at] = jnp.where(u == (own ^ labels[j]), hs_ref[j], half_ref[at])
+        head = a[:, :LANES].astype(jnp.float32)
+        lane = lax.broadcasted_iota(jnp.int32, (per_device, LANES), 1)
+        acc = jnp.zeros((per_device, LANES), jnp.float32)
+        for k in range(occupied):
+            piece = jnp.where(lane < CW, head[k * per_device : (k + 1) * per_device], 0.0)
+            acc = acc + (pltpu.roll(piece, k * CW, axis=1) if k else piece)
+        cyc_ref[w] = acc.astype(jnp.bfloat16)
 
 
 def stack(blocks, after):
-    heads = [b.shape[0] for b in blocks]
     count = len(blocks)
 
     def kernel(*refs):
-        out, sems = refs[count + 1], refs[count + 2]
-        copies = []
+        out = refs[count + 1]
         at = 0
         for n in range(count):
-            copies.append(
-                pltpu.make_async_copy(refs[n], out.at[at : at + heads[n]], sems.at[n])
-            )
-            at += heads[n]
-        for copy in copies:
-            copy.start()
-        for copy in copies:
-            copy.wait()
-
-    anywhere = pl.BlockSpec(memory_space=pl.ANY)
-    shape = (sum(heads),) + blocks[0].shape[1:]
+            head = blocks[n].shape[0]
+            out[at : at + head] = refs[n][...]
+            at += head
+
+    vmem = pl.BlockSpec(memory_space=pltpu.VMEM)
+    shape = (sum(b.shape[0] for b in blocks),) + blocks[0].shape[1:]
     return pl.pallas_call(
         kernel,
         out_shape=jax.ShapeDtypeStruct(shape, blocks[0].dtype),
-        in_specs=[anywhere] * (count + 1),
-        out_specs=anywhere,
-        scratch_shapes=[pltpu.SemaphoreType.DMA((count,))],
-        compiler_params=pltpu.CompilerParams(vmem_limit_bytes=LIMIT),
+        in_specs=[vmem] * count + [pl.BlockSpec(memory_space=pl.ANY)],
+        out_specs=vmem,
+        compiler_params=params(4),
         cost_estimate=pl.CostEstimate(flops=0, bytes_accessed=10**6, transcendentals=0),
     )(*blocks, after)
 
@@ -345,9 +345,6 @@
     def whole(shape):
         return pl.BlockSpec(shape, lambda n: (0,) * len(shape))
 
-    def params():
-        return pltpu.CompilerParams(vmem_limit_bytes=LIMIT)
-
     def cost(flops, size):
         return pl.CostEstimate(flops=flops, bytes_accessed=size, transcendentals=0)
 
@@ -368,37 +365,38 @@
             pl.BlockSpec((occupied, occupied, 16, LANES), lambda n: (0, 0, 0, 0)),
         ],
         out_specs=(whole((block_rows, LANES)), whole((rows, rows))),
-        compiler_params=params(),
+        compiler_params=params(8),
         cost_estimate=cost(0, 500000),
     )(pos, fock_occ, cycle_ints, amps)
     block = block.reshape(1, block_rows, LANES)
 
     flat_amps = amps.reshape(occupied, rows, virtuals)
-    parts = (3, 3, 2)
+    parts = (2, 4, 2)
+    wide = 2
 
     def fock_part(n, after):
         first, count = sum(parts[:n]), parts[n]
         return pl.pallas_call(
             functools.partial(fock_kernel, first),
-            grid=(count,),
+            grid=(count // wide,),
             out_shape=(
                 jax.ShapeDtypeStruct((2 * count, per_device, virtuals), f32),
                 jax.ShapeDtypeStruct((count, per_device, LANES), bf16),
             ),
             in_specs=[
                 smem,
-                pl.BlockSpec((1, rows, virtuals), lambda i: (i + first, 0, 0)),
+                pl.BlockSpec((wide, rows, virtuals), lambda i: (i + first // wide, 0, 0)),
                 whole(fock_vir.shape),
                 whole(mix.shape),
                 whole(u.shape),
                 anywhere,
             ],
             out_specs=(
-                pl.BlockSpec((2, per_device, virtuals), lambda i: (i, 0, 0)),
-                pl.BlockSpec((1, per_device, LANES), lambda i: (i, 0, 0)),
+                pl.BlockSpec((2 * wide, per_device, virtuals), lambda i: (i, 0, 0)),
+                pl.BlockSpec((wide, per_device, LANES), lambda i: (i, 0, 0)),
             ),
             scratch_shapes=[pltpu.VMEM((occupied, per_device, virtuals), f32)],
-            compiler_params=params(),
+            compiler_params=params(12),
             cost_estimate=cost(3 * count * rows * virtuals * virtuals, 2 * 10**6),
         )(occ_irrep, flat_amps, fock_vir, mix, u, after)
 
@@ -421,7 +419,7 @@
             anywhere,
         ],
         out_specs=whole((occupied * occupied, LANES)),
-        compiler_params=params(),
+        compiler_params=params(4),
         cost_estimate=cost(0, 10**5),
     )(pos, own_blocks, own_blocks)
     win_mate = permute(win, 1, dests)
@@ -440,7 +438,7 @@
             pltpu.VMEM((occupied * occupied, LANES), f32),
             pltpu.VMEM((pairs, 8, virtuals), f32),
         ],
-        compiler_params=params(),
+        compiler_params=params(16),
         cost_estimate=cost(4 * occupied * rows * virtuals * LANES, 9 * 10**6),
     )(occ_irrep, win, win_mate, half0, half1, half2, u, ladder_ints)
 
@@ -460,7 +458,7 @@
             pltpu.VMEM((dests, send_rows, LANES), f32),
             pltpu.SemaphoreType.DMA((1,)),
         ],
-        compiler_params=params(),
+        compiler_params=params(24),
         cost_estimate=cost(2 * occupied * rows * virtuals * LANES, 8 * 10**6),
     )(pos, occ_irrep, own_blocks, mate_blocks, cyc0, cyc1, cyc2, half, u)
 
@@ -481,7 +479,7 @@
             pltpu.VMEM((tiles, virtuals, LANES), f32),
             pltpu.VMEM((tiles * LANES, virtuals), f32),
         ],
-        compiler_params=params(),
+        compiler_params=params(16),
         cost_estimate=cost(10**6, 10**7),
     )(occ_irrep, half, recv, u)
 

time: 121 us -> 74.6 us (0.62)
  Pallas kernels: 77.8 us -> 28.9 us
  waiting for transfers between devices: 1.81 us -> 5.15 us
  local copies, waits for them, and re-layouts: 3.45 us -> 4.75 us
    pallas_call x3, Pallas kernels: 34.6 us -> 1.93 us  [stack(): pl.pallas_call(kernel, out_shape=jax.ShapeDtypeStruct(shape, blocks[0].dt...]
    pallas_call x3, Pallas kernels: 13.6 us -> 7.74 us  [fock_part(): pl.pallas_call(functools.partial(fock_kernel, first), grid=(count // wide...]
    ppermute x7, waiting for transfers between devices: 1.81 us -> 5.15 us  [permute(): return lax.ppermute(x, 'vir', [(n, n ^ flip) for n in range(size)])]
    pallas_call x1, Pallas kernels: 7.72 us -> 4.69 us  [body(): pl.pallas_call(functools.partial(ladder_kernel, parts), grid=(per_device...]
    pallas_call x1, Pallas kernels: 10.1 us -> 7.45 us  [body(): pl.pallas_call(functools.partial(cycle_kernel, parts), out_shape=(jax.Sha...]
    pallas_call x1, Pallas kernels: 7.98 us -> 5.8 us  [body(): pl.pallas_call(join_kernel, grid=(occupied,), out_shape=jax.ShapeDtypeStr...]
    pallas_call x1, Pallas kernels: 1.56 us -> 0.2 us  [body(): pl.pallas_call(unpack_kernel, grid=(1,), out_shape=jax.ShapeDtypeStruct((...]
    unnamed x16 -> x18, local copies, waits for them, and re-layouts: 3.38 us -> 4.68 us
  transfers between devices with their start and end apart: 7 -> 7, of which waited for: 2 -> 3; matrix products, arithmetic and copies ran while one was open for 1% -> 0% of each run, Pallas kernels for 30% -> 20%
where the time goes in v4:
time: 74.6 us; the launch traced here: 74.2 us
  Pallas kernels  28.9 us (39%)
  blocking collectives  26.1 us (35%)
  starting transfers between devices  9.12 us (12%)
  waiting for transfers between devices  5.15 us (7%)
  local copies, waits for them, and re-layouts  4.75 us (6%)
    all_to_all x1, blocking collectives, body(): recv = lax.all_to_all(send, 'vir', split_axis=0, concat_axis=0, tiled=True)  26.1 us
    ppermute x7, starting transfers between devices, permute(): return lax.ppermute(x, 'vir', [(n, n ^ flip) for n in range(size)])  9.12 us
    pallas_call x3, Pallas kernels, fock_part(): pl.pallas_call(functools.partial(fock_kernel, first), grid=(count // wide...  7.74 us
    pallas_call x1, Pallas kernels, body(): pl.pallas_call(functools.partial(cycle_kernel, parts), out_shape=(jax.Sha...  7.45 us
    pallas_call x1, Pallas kernels, body(): pl.pallas_call(join_kernel, grid=(occupied,), out_shape=jax.ShapeDtypeStr...  5.8 us
    ppermute x7, waiting for transfers between devices, permute(): return lax.ppermute(x, 'vir', [(n, n ^ flip) for n in range(size)])  5.15 us
    pallas_call x1, Pallas kernels, body(): pl.pallas_call(functools.partial(ladder_kernel, parts), grid=(per_device...  4.69 us
    unnamed x18, local copies, waits for them, and re-layouts  4.68 us
  transfers between devices with their start and end apart: 7, of which 3 were waited for; matrix products, arithmetic and copies ran while one was open for 0% of the time, Pallas kernels for 20%

profile of v4, /device:TPU:1, one launch (start us, length us, event | category | flops | bytes accessed | tf_op | source)
XLA Modules:
  0.0 74.2 jit_solution(6625497413346823969)
XLA Ops:
  0.0 1.9 %copy-done = bf16[8,8,40,640]{3,2,1,0:T(8,128)(2,1)S(1)} copy-done((bf16[8,8,40,640]{3,2,1,0:T(8,128)(2,1)S(1)}, bf16[8,8,40,640]{3,2,1,0:T(8,128)(2,1)}, u32[]{:S(2)}) %copy-start) | copy-done | bytes 3276824
  2.0 0.9 %copy-done.3 = bf16[40,8,128]{2,1,0:T(8,128)(2,1)S(1)} copy-done((bf16[40,8,128]{2,1,0:T(8,128)(2,1)S(1)}, bf16[40,8,128]{2,1,0:T(8,128)(2,1)}, u32[]{:S(2)}) %copy-start.3) | copy-done | bytes 81944
  2.8 0.7 copy-done.5
  3.5 1.1 %shard_map.73 = (bf16[336,128]{1,0:T(8,128)(2,1)}, bf16[320,320]{1,0:T(8,128)(2,1)S(1)}) custom-call(s32[1]{0:T(128)} %bitcast.pos_ref, bf16[8,8]{1,0:T(8,128)(2,1)S(1)} %copy-done.5, bf16[40,8,128]{2,1,0:T(8,128)(2,1)S(1)} %copy-done.3, bf16[8,8,40,640]{3,2,1,0:T(8,128)(2,1)S(1)} %copy-done), custom_call_target="tpu_custom_call" | custom-call | bytes 500000 | tf_op jit(solution)/shard_map/pallas_call | solution.py:354
  4.6 4.2 %collective-permute-start.2 = (bf16[1,336,128]{2,1,0:T(8,128)(2,1)}, bf16[1,336,128]{2,1,0:T(8,128)(2,1)}, u32[]{:S(2)}, u32[]{:S(2)}) collective-permute-start(bf16[1,336,128]{2,1,0:T(8,128)(2,1)} %bitcast.1.refs_0_), channel_id=1, source_target_pairs={{0,12},{1,13},{2,14},{3,15},{4,8},{5,9},{6,10},{7,11},{8,4},{9,5},... | collective-permute-start | bytes 258056 | tf_op jit(solution)/shard_map/ppermute | solution.py:329
  8.8 0.0 collective-permute-start.1
  8.8 0.3 collective-permute-start
  9.0 0.1 dynamic_slice.3
  9.1 0.1 broadcast_xor_fusion.u_ref.refs_3_.refs_4_
  9.2 0.0 copy-start.2
  9.2 1.1 %copy-done.2 = bf16[640,640]{1,0:T(8,128)(2,1)S(1)} copy-done((bf16[640,640]{1,0:T(8,128)(2,1)S(1)}, bf16[640,640]{1,0:T(8,128)(2,1)}, u32[]{:S(2)}) %copy-start.2) | copy-done | bytes 819224
  10.4 2.0 %shard_map.74 = (f32[4,40,640]{2,1,0:T(8,128)S(1)}, bf16[2,40,128]{2,1,0:T(8,128)(2,1)S(1)}) custom-call(s32[8]{0:T(128)S(1)} %copy-done.4, bf16[8,320,640]{2,1,0:T(8,128)(2,1)S(1)} %bitcast.3, bf16[640,640]{1,0:T(8,128)(2,1)S(1)} %copy-done.2, bf16[320,320]{1,0:T(8,128)(2,1)S(1)} %get-tuple-element.16.mix_ref.after_ref, ...), custom_call_target="tpu_custom_call" | custom-call | flops 786432000 | bytes 2000000 | tf_op jit(solution)/shard_map/pallas_call | solution.py:379
  12.4 1.6 %collective-permute-done.refs_1_ = bf16[1,336,128]{2,1,0:T(8,128)(2,1)} collective-permute-done((bf16[1,336,128]{2,1,0:T(8,128)(2,1)}, bf16[1,336,128]{2,1,0:T(8,128)(2,1)}, u32[]{:S(2)}, u32[]{:S(2)}) %collective-permute-start) | collective-permute-done | bytes 86048 | tf_op jit(solution)/shard_map/ppermute | solution.py:329
  14.0 0.9 %shard_map.75.after_ref.refs_0_ = bf16[2,336,128]{2,1,0:T(8,128)(2,1)S(1)} custom-call(bf16[1,336,128]{2,1,0:T(8,128)(2,1)} %bitcast.1.refs_0_, bf16[1,336,128]{2,1,0:T(8,128)(2,1)} %collective-permute-done.refs_1_, f32[4,40,640]{2,1,0:T(8,128)S(1)} %get-tuple-element.17.refs_2_.refs_0_), custom_call_target="tpu_custom_call" | custom-call | bytes 1000000 | tf_op jit(solution)/shard_map/pallas_call | solution.py:148
  15.0 1.3 %collective-permute-start.3 = (bf16[2,336,128]{2,1,0:T(8,128)(2,1)S(1)}, bf16[2,336,128]{2,1,0:T(8,128)(2,1)S(1)}, u32[]{:S(2)}, u32[]{:S(2)}) collective-permute-start(bf16[2,336,128]{2,1,0:T(8,128)(2,1)S(1)} %shard_map.75.after_ref.refs_0_), channel_id=1, source_target_pairs={{0,2},{1,3},{2,0},{3,1},{4,6},{5,7},{6,4},{7,5},{8,10},{9,11},{10,... | collective-permute-start | bytes 516104 | tf_op jit(solution)/shard_map/ppermute | solution.py:329
  16.3 3.7 %shard_map.76 = (f32[8,40,640]{2,1,0:T(8,128)S(1)}, bf16[4,40,128]{2,1,0:T(8,128)(2,1)S(1)}) custom-call(s32[8]{0:T(128)S(1)} %copy-done.4, bf16[8,320,640]{2,1,0:T(8,128)(2,1)S(1)} %bitcast.4, bf16[640,640]{1,0:T(8,128)(2,1)S(1)} %copy-done.2, bf16[320,320]{1,0:T(8,128)(2,1)S(1)} %get-tuple-element.16.mix_ref.after_ref, ...), custom_call_target="tpu_custom_call" | custom-call | flops 1572864000 | bytes 2000000 | tf_op jit(solution)/shard_map/pallas_call | solution.py:379
  20.0 0.0 collective-permute-done.2.refs_1_
  20.0 0.9 %shard_map.77.after_ref.refs_1_ = bf16[2,336,128]{2,1,0:T(8,128)(2,1)S(1)} custom-call(bf16[1,336,128]{2,1,0:T(8,128)(2,1)} %collective-permute-done.1.refs_0_, bf16[1,336,128]{2,1,0:T(8,128)(2,1)} %collective-permute-done.2.refs_1_, f32[8,40,640]{2,1,0:T(8,128)S(1)} %get-tuple-element.18.refs_2_.refs_1_), custom_call_target="tpu_custom_call" | custom-call | bytes 1000000 | tf_op jit(solution)/shard_map/pallas_call | solution.py:148
  20.9 0.0 slice-start.1
  21.0 0.3 collective-permute-start.4
  21.3 2.0 %shard_map.78 = (f32[4,40,640]{2,1,0:T(8,128)S(1)}, bf16[2,40,128]{2,1,0:T(8,128)(2,1)S(1)}) custom-call(s32[8]{0:T(128)S(1)} %copy-done.4, bf16[8,320,640]{2,1,0:T(8,128)(2,1)S(1)} %bitcast.5, bf16[640,640]{1,0:T(8,128)(2,1)S(1)} %copy-done.2, bf16[320,320]{1,0:T(8,128)(2,1)S(1)} %get-tuple-element.16.mix_ref.after_ref, ...), custom_call_target="tpu_custom_call" | custom-call | flops 786432000 | bytes 2000000 | tf_op jit(solution)/shard_map/pallas_call | solution.py:379
  23.3 0.0 collective-permute-done.3.refs_2_
  23.3 2.0 %collective-permute-done.4.refs_3_ = bf16[2,336,128]{2,1,0:T(8,128)(2,1)S(1)} collective-permute-done((bf16[2,336,128]{2,1,0:T(8,128)(2,1)S(1)}, bf16[2,336,128]{2,1,0:T(8,128)(2,1)S(1)}, u32[]{:S(2)}, u32[]{:S(2)}) %collective-permute-start.4) | collective-permute-done | bytes 172064 | tf_op jit(solution)/shard_map/ppermute | solution.py:329
  25.3 3.0 %collective-permute-start.5 = (bf16[8,336,128]{2,1,0:T(8,128)(2,1)S(1)}, bf16[8,336,128]{2,1,0:T(8,128)(2,1)S(1)}, u32[]{:S(2)}, u32[]{:S(2)}) collective-permute-start(bf16[8,336,128]{2,1,0:T(8,128)(2,1)S(1)} %shard_map.79.blocks_ref.after_ref.own_ref), channel_id=1, source_target_pairs={{0,1},{1,0},{2,3},{3,2},{4,5},{5,4},{6,7},{7,6},{8,9},{9,8},{10,11... | collective-permute-start | bytes 2064392 | tf_op jit(solution)/shard_map/ppermute | solution.py:329
  28.3 0.2 shard_map.80.win0_ref
  28.5 0.1 collective-permute-start.6
  28.6 1.5 %collective-permute-done.6.win1_ref = bf16[64,128]{1,0:T(8,128)(2,1)S(1)} collective-permute-done((bf16[64,128]{1,0:T(8,128)(2,1)S(1)}, bf16[64,128]{1,0:T(8,128)(2,1)S(1)}, u32[]{:S(2)}, u32[]{:S(2)}) %collective-permute-start.6) | collective-permute-done | bytes 16416 | tf_op jit(solution)/shard_map/ppermute | solution.py:329
  30.1 4.7 %shard_map.81.refs_3_ = f32[16,40,640]{2,1,0:T(8,128)S(1)} custom-call(s32[8]{0:T(128)S(1)} %copy-done.4, bf16[64,128]{1,0:T(8,128)(2,1)S(1)} %shard_map.80.win0_ref, bf16[64,128]{1,0:T(8,128)(2,1)S(1)} %collective-permute-done.6.win1_ref, f32[4,40,640]{2,1,0:T(8,128)S(1)} %get-tuple-element.17.refs_2_.refs_0_, ...), custom_call_target="tpu_custom_call" | custom-call | flops 838860800 | bytes 9000000 | tf_op jit(solution)/shard_map/pallas_call | solution.py:428
  34.8 0.0 collective-permute-done.5.mate_ref
  34.8 7.5 %shard_map.82 = (f32[16,40,640]{2,1,0:T(8,128)S(1)}, bf16[16,208,128]{2,1,0:T(8,128)(2,1)S(1)}) custom-call(s32[1]{0:T(128)} %bitcast.pos_ref, s32[8]{0:T(128)S(1)} %copy-done.4, bf16[8,336,128]{2,1,0:T(8,128)(2,1)S(1)} %shard_map.79.blocks_ref.after_ref.own_ref, bf16[8,336,128]{2,1,0:T(8,128)(2,1)S(1)} %collective-permute-done.5.mate_ref, ...), custom_call_target="tpu_custom_call" | custom-call | flops 419430400 | bytes 8000000 | tf_op jit(solution)/shard_map/pallas_call | solution.py:447
  42.3 26.1 %all_to_all.5.recv_ref = bf16[16,208,128]{2,1,0:T(8,128)(2,1)S(1)} all-to-all(bf16[16,208,128]{2,1,0:T(8,128)(2,1)S(1)} %get-tuple-element.24), channel_id=1, replica_groups=mesh['groups'=2,'vir'=16] {'vir'}, dimensions={0} | all-to-all | bytes 1703936 | tf_op jit(solution)/shard_map/all_to_all | solution.py:465
  68.4 5.8 %shard_map.83 = f32[8,8,40,640]{3,2,1,0:T(8,128)} custom-call(s32[8]{0:T(128)S(1)} %copy-done.4, f32[16,40,640]{2,1,0:T(8,128)S(1)} %get-tuple-element.23.half_ref, bf16[16,208,128]{2,1,0:T(8,128)(2,1)S(1)} %all_to_all.5.recv_ref, s32[40,640]{1,0:T(8,128)S(1)} %broadcast_xor_fusion.u_ref.refs_3_.refs_4_), custom_call_target="tpu_custom_call" | custom-call | flops 1000000 | bytes 10000000 | tf_op jit(solution)/shard_map/pallas_call | solution.py:467
  (15 shorter events, 0.1 us)
Async XLA Ops:
  0.0 9.0 %copy-start.6 = (s32[640]{0:T(1024)S(1)}, s32[640]{0:T(1024)}, u32[]{:S(2)}) copy-start(s32[640]{0:T(1024)} %param.13) | copy-start | bytes 7684
  0.0 9.2 %copy-start.4 = (s32[8]{0:T(128)S(1)}, s32[8]{0:T(128)}, u32[]{:S(2)}) copy-start(s32[8]{0:T(128)} %occ_ref.11) | copy-start | bytes 100
  0.0 2.0 %copy-start = (bf16[8,8,40,640]{3,2,1,0:T(8,128)(2,1)S(1)}, bf16[8,8,40,640]{3,2,1,0:T(8,128)(2,1)}, u32[]{:S(2)}) copy-start(bf16[8,8,40,640]{3,2,1,0:T(8,128)(2,1)} %amps_ref.1) | copy-start | bytes 9830404
  2.0 0.9 %copy-start.3 = (bf16[40,8,128]{2,1,0:T(8,128)(2,1)S(1)}, bf16[40,8,128]{2,1,0:T(8,128)(2,1)}, u32[]{:S(2)}) copy-start(bf16[40,8,128]{2,1,0:T(8,128)(2,1)} %cyc_ref.1) | copy-start | bytes 245764
  2.8 0.7 copy-start.5
  3.5 5.7 %copy-start.1 = (bf16[8,8,40,640]{3,2,1,0:T(8,128)(2,1)S(1)}, bf16[8,8,40,640]{3,2,1,0:T(8,128)(2,1)}, u32[]{:S(2)}) copy-start(bf16[8,8,40,640]{3,2,1,0:T(8,128)(2,1)} %amps_ref.1) | copy-start | bytes 9830404
  4.6 15.4 %collective-permute-start.2 = (bf16[1,336,128]{2,1,0:T(8,128)(2,1)}, bf16[1,336,128]{2,1,0:T(8,128)(2,1)}, u32[]{:S(2)}, u32[]{:S(2)}) collective-permute-start(bf16[1,336,128]{2,1,0:T(8,128)(2,1)} %bitcast.1.refs_0_), channel_id=1, source_target_pairs={{0,12},{1,13},{2,14},{3,15},{4,8},{5,9},{6,10},{7,11},{8,4},{9,5},... | collective-permute-start | bytes 258056 | tf_op jit(solution)/shard_map/ppermute | solution.py:329
  8.8 11.2 %collective-permute-start.1 = (bf16[1,336,128]{2,1,0:T(8,128)(2,1)}, bf16[1,336,128]{2,1,0:T(8,128)(2,1)}, u32[]{:S(2)}, u32[]{:S(2)}) collective-permute-start(bf16[1,336,128]{2,1,0:T(8,128)(2,1)} %bitcast.1.refs_0_), channel_id=1, source_target_pairs={{0,8},{1,9},{2,10},{3,11},{4,12},{5,13},{6,14},{7,15},{8,0},{9,1},... | collective-permute-start | bytes 258056 | tf_op jit(solution)/shard_map/ppermute | solution.py:329
  8.8 5.3 %collective-permute-start = (bf16[1,336,128]{2,1,0:T(8,128)(2,1)}, bf16[1,336,128]{2,1,0:T(8,128)(2,1)}, u32[]{:S(2)}, u32[]{:S(2)}) collective-permute-start(bf16[1,336,128]{2,1,0:T(8,128)(2,1)} %bitcast.1.refs_0_), channel_id=1, source_target_pairs={{0,4},{1,5},{2,6},{3,7},{4,0},{5,1},{6,2},{7,3},{8,12},{9,13},{10,... | collective-permute-start | bytes 258056 | tf_op jit(solution)/shard_map/ppermute | solution.py:329
  9.2 1.1 %copy-start.2 = (bf16[640,640]{1,0:T(8,128)(2,1)S(1)}, bf16[640,640]{1,0:T(8,128)(2,1)}, u32[]{:S(2)}) copy-start(bf16[640,640]{1,0:T(8,128)(2,1)} %fock_ref.5) | copy-start | bytes 2457604
  15.0 8.3 %collective-permute-start.3 = (bf16[2,336,128]{2,1,0:T(8,128)(2,1)S(1)}, bf16[2,336,128]{2,1,0:T(8,128)(2,1)S(1)}, u32[]{:S(2)}, u32[]{:S(2)}) collective-permute-start(bf16[2,336,128]{2,1,0:T(8,128)(2,1)S(1)} %shard_map.75.after_ref.refs_0_), channel_id=1, source_target_pairs={{0,2},{1,3},{2,0},{3,1},{4,6},{5,7},{6,4},{7,5},{8,10},{9,11},{10,... | collective-permute-start | bytes 516104 | tf_op jit(solution)/shard_map/ppermute | solution.py:329
  16.3 13.8 %slice-start = ((s8[6553600]{0:T(1024)(128)(4,1)}), s8[4194304]{0:T(1024)(128)(4,1)S(1)}, s32[]{:S(2)}) async-start(s8[6553600]{0:T(1024)(128)(4,1)} %bitcast.6), calls=%async_computation.1 | async-start | bytes 8388608
  20.9 9.2 %slice-start.1 = ((s8[6553600]{0:T(1024)(128)(4,1)}), s8[2359296]{0:T(1024)(128)(4,1)S(1)}, s32[]{:S(2)}) async-start(s8[6553600]{0:T(1024)(128)(4,1)} %bitcast.6), calls=%async_computation.2 | async-start | bytes 4718592
  21.0 4.3 %collective-permute-start.4 = (bf16[2,336,128]{2,1,0:T(8,128)(2,1)S(1)}, bf16[2,336,128]{2,1,0:T(8,128)(2,1)S(1)}, u32[]{:S(2)}, u32[]{:S(2)}) collective-permute-start(bf16[2,336,128]{2,1,0:T(8,128)(2,1)S(1)} %shard_map.77.after_ref.refs_1_), channel_id=1, source_target_pairs={{0,2},{1,3},{2,0},{3,1},{4,6},{5,7},{6,4},{7,5},{8,10},{9,11},{10,... | collective-permute-start | bytes 516104 | tf_op jit(solution)/shard_map/ppermute | solution.py:329
  25.3 9.5 %collective-permute-start.5 = (bf16[8,336,128]{2,1,0:T(8,128)(2,1)S(1)}, bf16[8,336,128]{2,1,0:T(8,128)(2,1)S(1)}, u32[]{:S(2)}, u32[]{:S(2)}) collective-permute-start(bf16[8,336,128]{2,1,0:T(8,128)(2,1)S(1)} %shard_map.79.blocks_ref.after_ref.own_ref), channel_id=1, source_target_pairs={{0,1},{1,0},{2,3},{3,2},{4,5},{5,4},{6,7},{7,6},{8,9},{9,8},{10,11... | collective-permute-start | bytes 2064392 | tf_op jit(solution)/shard_map/ppermute | solution.py:329
  28.5 1.6 %collective-permute-start.6 = (bf16[64,128]{1,0:T(8,128)(2,1)S(1)}, bf16[64,128]{1,0:T(8,128)(2,1)S(1)}, u32[]{:S(2)}, u32[]{:S(2)}) collective-permute-start(bf16[64,128]{1,0:T(8,128)(2,1)S(1)} %shard_map.80.win0_ref), channel_id=1, source_target_pairs={{0,1},{1,0},{2,3},{3,2},{4,5},{5,4},{6,7},{7,6},{8,9},{9,8},{10,11... | collective-permute-start | bytes 49160 | tf_op jit(solution)/shard_map/ppermute | solution.py:329

commit v5 on v4

--- a/solution.py
+++ b/solution.py
@@ -75,11 +75,10 @@
     return labels, copies
 
 
-def prep_kernel(pos_ref, occ_vals_ref, cyc_ref, amps_ref, block_ref, mix_ref):
-    occupied, _, _, _ = amps_ref.shape
-    rows = mix_ref.shape[0]
-    per_device = rows // occupied
-    block_ref[:rows, :] = cyc_ref[...].astype(jnp.float32).reshape(rows, LANES).astype(jnp.bfloat16)
+def prep_kernel(cyc_ref, amps_ref, block_ref):
+    occupied = amps_ref.shape[0]
+    rows = cyc_ref.shape[0]
+    block_ref[:rows, :] = cyc_ref[...]
     lane = lax.broadcasted_iota(jnp.int32, (occupied, LANES), 1)
     packed = jnp.zeros((occupied, LANES), jnp.float32)
     for j in range(occupied):
@@ -87,21 +86,24 @@
         packed = packed + (pltpu.roll(w, j * DW, axis=1) if j else w)
     packed = jnp.concatenate([packed, jnp.zeros_like(packed)], axis=0)
     block_ref[rows:, :] = packed.astype(jnp.bfloat16)
-    r = lax.broadcasted_iota(jnp.int32, (rows, rows), 0)
-    c = lax.broadcasted_iota(jnp.int32, (rows, rows), 1)
-    mix = jnp.zeros((rows, rows), jnp.float32)
-    one = lax.broadcasted_iota(jnp.int32, (rows, occupied), 0)
-    col = lax.broadcasted_iota(jnp.int32, (rows, occupied), 1) * per_device
-    pick = jnp.logical_and(one >= col, one < col + per_device).astype(jnp.bfloat16)
-    left = lax.dot_general(
-        pick, occ_vals_ref[...], (((1,), (1,)), ((), ())), preferred_element_type=jnp.float32
-    ).astype(jnp.bfloat16)
-    mix = contract_last(left, pick)
-    gap = r - c
-    same = gap == 0
+
+
+def mix_kernel(occ_vals_ref, after_ref, mix_ref):
+    rows = mix_ref.shape[0]
+    occupied = occ_vals_ref.shape[0]
+    per_device = rows // occupied
+    row = lax.broadcasted_iota(jnp.int32, (rows, occupied), 0)
+    start = lax.broadcasted_iota(jnp.int32, (rows, occupied), 1) * per_device
+    in_block = jnp.logical_and(row >= start, row < start + per_device).astype(jnp.bfloat16)
+    row = lax.broadcasted_iota(jnp.int32, (rows, per_device), 0)
+    at = lax.broadcasted_iota(jnp.int32, (rows, per_device), 1)
+    same = row == at
     for n in range(1, occupied):
-        same = jnp.logical_or(same, jnp.abs(gap) == n * per_device)
-    mix_ref[...] = jnp.where(same, mix, 0.0).astype(jnp.bfloat16)
+        same = jnp.logical_or(same, row == at + n * per_device)
+    same = same.astype(jnp.bfloat16)
+    left = contract_last(in_block, occ_vals_ref[...]).astype(jnp.bfloat16)
+    mix = contract_last(left, in_block) * contract_last(same, same)
+    mix_ref[...] = mix.astype(jnp.bfloat16)
 
 
 def fock_kernel(first, occ_ref, amps_ref, fock_ref, mix_ref, u_ref, after_ref, half_ref, cyc_ref, hs_ref):
@@ -221,108 +223,145 @@
         at += 2 * count
 
 
-def cycle_kernel(parts, pos_ref, occ_ref, own_ref, mate_ref, *refs):
-    cycs = refs[: len(parts)]
-    half_ref, u_ref, out_ref, send_ref, xs_ref, acc_ref, pay_ref, sems = refs[len(parts) :]
+def cycle_kernel(chunk, before, parts, pos_ref, occ_ref, *refs):
+    i0, i1, t0, t1 = chunk
+    refs = list(refs)
+    if before is None:
+        own_ref, mate_ref = refs.pop(0), refs.pop(0)
+    else:
+        x_ref, prev_ref = refs.pop(0), refs.pop(0)
+    cycs = [refs.pop(0) for _ in parts]
+    half_ref, u_ref, out_ref, send_ref = (refs.pop(0) for _ in range(4))
+    if before is None:
+        x_ref = refs.pop(0)
+    orb_ref, cs_ref, hin_ref, pay_ref, sems = (refs.pop(0) for _ in range(5))
     occupied = occ_ref.shape[0]
-    pairs, per_device, virtuals = acc_ref.shape
+    pairs = 2 * occupied
+    _, per_device, virtuals = hin_ref.shape
     dests = send_ref.shape[0]
     rows = occupied * per_device
-    load = pltpu.make_async_copy(half_ref, acc_ref, sems.at[0])
+    tiles = virtuals // LANES
+    load = pltpu.make_async_copy(half_ref.at[2 * i0 : 2 * i1], hin_ref, sems.at[0])
     load.start()
     labels, copies = labels_and_copies(occ_ref, occupied)
-    pos = pos_ref[0]
-    for r in range(dests):
-        ref = mate_ref if r & 1 else own_ref
-        block = ref[((r >> 1) & 1) * (dests // 4) + (r >> 2)][:rows].astype(jnp.float32)
-        xs_ref[pl.ds((pos ^ r) * per_device, per_device)] = block.reshape(
-            per_device, occupied, LANES
-        )
-    u = u_ref[...]
-    left = jnp.concatenate([ref[...].astype(jnp.float32) for ref in cycs], axis=0)
-    left = left.reshape(rows, LANES).astype(jnp.bfloat16)
+    for j in range(occupied):
+        orb_ref[2 * labels[j] + copies[j]] = jnp.int32(j)
+    if before is None:
+        (xs_ref,) = refs
+        for r in range(dests):
+            ref = mate_ref if r & 1 else own_ref
+            block = ref[((r >> 1) & 1) * (dests // 4) + (r >> 2)][:rows].astype(jnp.float32)
+            xs_ref[pl.ds((pos_ref[0] ^ r) * per_device, per_device)] = block.reshape(
+                per_device, occupied, LANES
+            )
+        for j in range(occupied):
+            x_ref[j] = xs_ref[:, j, :].astype(jnp.bfloat16)
+    left = jnp.concatenate([ref[...].astype(jnp.float32) for ref in cycs], axis=0)[i0:i1]
+    left = left.reshape((i1 - i0) * per_device, LANES).astype(jnp.bfloat16)
+    for j in range(occupied):
+        cs_ref[j] = contract_last(left, x_ref[j]).reshape(i1 - i0, per_device, virtuals)
     load.wait()
-    for j in range(occupied):
-        c = contract_last(left, xs_ref[:, j, :].astype(jnp.bfloat16))
-        for i in range(occupied):
-            e = 2 * i + copies[j]
-            part = c[i * per_device : (i + 1) * per_device]
-            acc_ref[e] = acc_ref[e] + jnp.where(u == (labels[i] ^ labels[j]), part, 0.0)
-    store = pltpu.make_async_copy(acc_ref, out_ref, sems.at[0])
-    store.start()
 
     pieces_of = payload_pieces(per_device, pairs, dests)
     lane = lax.broadcasted_iota(jnp.int32, (8, LANES), 1)
+    choices = {
+        (i, s): [orb_ref[2 * (labels[i] ^ n) + s] for n in range(4)]
+        for i in range(i0, i1)
+        for s in range(2)
+    }
 
     def group(g, top):
         rows = pl.ds(pl.multiple_of(g * 8, 8), 8)
-        tiles = {}
-        for e in range(pairs):
-            for v in range(virtuals // LANES):
-                x = acc_ref[e, rows, v * LANES : (v + 1) * LANES]
+        found = {}
+
+        def fill(e):
+            nonlocal top
+            for v in range(tiles):
+                at = slice(v * LANES, (v + 1) * LANES)
+                if e < 2 * i0:
+                    x = prev_ref[e - 2 * before, rows, at]
+                else:
+                    js = choices[e // 2, e % 2]
+                    uv = u_ref[rows, at]
+                    x = cs_ref[js[0], e // 2 - i0, rows, at]
+                    for n in range(1, 4):
+                        x = jnp.where(uv == n, cs_ref[js[n], e // 2 - i0, rows, at], x)
+                    x = x + hin_ref[e - 2 * i0, rows, at]
+                    out_ref[e - 2 * i0, rows, at] = x
                 top = jnp.maximum(top, jnp.abs(x))
-                tiles[e, v] = x
-        rolled = {}
-        for (q, t), pieces in pieces_of.items():
-            acc = None
-            for first, e, v, shift in pieces:
-                if (e, v, shift) not in rolled:
-                    x = tiles[e, v]
-                    rolled[e, v, shift] = pltpu.roll(x, shift, axis=1) if shift else x
-                x = rolled[e, v, shift]
-                acc = x if acc is None else jnp.where(lane >= first, x, acc)
-            at = pl.ds(pl.multiple_of(t * per_device + g * 8, 8), 8)
-            pay_ref[q, at, :] = acc
+                found[e, v] = x
+
+        for t in range(t0, t1):
+            first_e = t * LANES // per_device
+            last_e = min(((t + 1) * LANES - 1) // per_device, pairs - 1)
+            for e in range(first_e, last_e + 1):
+                if (e, 0) not in found:
+                    fill(e)
+            for q in range(dests):
+                acc = None
+                for first, e, v, shift in pieces_of[q, t]:
+                    x = pltpu.roll(found[e, v], shift, axis=1) if shift else found[e, v]
+                    acc = x if acc is None else jnp.where(lane >= first, x, acc)
+                at = pl.ds(pl.multiple_of((t - t0) * per_device + g * 8, 8), 8)
+                pay_ref[q, at, :] = acc
         return top
 
     top = lax.fori_loop(0, per_device // 8, group, jnp.zeros((8, LANES), jnp.float32))
     top = jnp.max(jnp.max(top, axis=0, keepdims=True), axis=1, keepdims=True)
     k = jnp.floor(TOP_EXPONENT - jnp.log2(jnp.maximum(top, 1e-30)))
     scale = jnp.exp2(k)
-    count = pay_ref.shape[1]
-    row = lax.broadcasted_iota(jnp.int32, (count, LANES), 0)
-    data_rows = (virtuals // LANES) * per_device
+    row = lax.broadcasted_iota(jnp.int32, pay_ref.shape[1:], 0)
     for q in range(dests):
         z = pay_ref[q] * scale
         z2 = z * z
         z4 = z2 * z2
-        y = jnp.where(row >= data_rows, k, z4 * z4 * z)
+        y = jnp.where(row >= (t1 - t0) * per_device, k, z4 * z4 * z)
         send_ref[q] = y.astype(jnp.bfloat16)
-    store.wait()
-
-
-def join_kernel(occ_ref, half_ref, recv_ref, u_ref, out_ref, dec_ref, mir_ref):
-    i = pl.program_id(0)
+
+
+def join_kernel(chunks, first_j, occ_ref, u_ref, *refs):
+    count = len(chunks)
+    halves, recvs = refs[:count], refs[count : 2 * count]
+    out_ref, dec_ref, mir_ref = refs[-3:]
+    step = pl.program_id(0)
+    j = step + first_j
     occupied = occ_ref.shape[0]
-    _, per_device, virtuals = half_ref.shape
-    dests = recv_ref.shape[0]
-    tiles = virtuals // LANES
+    per_device, virtuals = u_ref.shape
     labels, copies = labels_and_copies(occ_ref, occupied)
-
-    @pl.when(i == 0)
-    def _():
-        for p in range(dests):
-            block = recv_ref[p].astype(jnp.float32)
-            k = block[tiles * per_device : tiles * per_device + 1, 0:1]
-            y = block[: tiles * per_device]
-            size = jnp.exp2(jnp.log2(jnp.maximum(jnp.abs(y), 2.0**-126)) * (1.0 / POWER) - k)
-            x = jnp.where(y < 0, -size, jnp.where(y > 0, size, 0.0))
-            for t in range(tiles):
-                dec_ref[t, p * per_device : (p + 1) * per_device, :] = x[
-                    t * per_device : (t + 1) * per_device
-                ]
-        for t in range(tiles):
-            mir_ref[t * LANES : (t + 1) * LANES, :] = dec_ref[t].T
-
-    own = occ_ref[i]
+    spread = 2 * per_device
+    for (_, _, t0, t1), recv_ref in zip(chunks, recvs):
+        dests = recv_ref.shape[0]
+        for t in range(t0, t1):
+            if (t + 1) * LANES <= first_j * spread:
+                continue
+            need = max(t * LANES // spread - first_j, 0)
+
+            @pl.when(step == need)
+            def _(t=t, t0=t0, t1=t1, recv_ref=recv_ref, dests=dests):
+                start = (t - t0) * per_device
+                low, high = start // 16 * 16, (start + per_device + 15) // 16 * 16
+                end = (t1 - t0) * per_device
+                for p in range(dests):
+                    tail = recv_ref[p, end // 16 * 16 : end // 16 * 16 + 16, :]
+                    k = tail.astype(jnp.float32)[end % 16 : end % 16 + 1, 0:1]
+                    y = recv_ref[p, low:high, :].astype(jnp.float32)
+                    y = y[start - low : start - low + per_device]
+                    size = jnp.log2(jnp.maximum(jnp.abs(y), 2.0**-126)) * (1.0 / POWER) - k
+                    size = jnp.exp2(size)
+                    x = jnp.where(y < 0, -size, jnp.where(y > 0, size, 0.0))
+                    dec_ref[p * per_device : (p + 1) * per_device, :] = x
+                mir_ref[t * LANES : (t + 1) * LANES, :] = dec_ref[...].T
+
+    own = occ_ref[j]
     copy = jnp.int32(0)
     for k in range(occupied):
-        copy = copy + jnp.logical_and(labels[k] == own, k < i).astype(jnp.int32)
+        copy = copy + jnp.logical_and(labels[k] == own, k < j).astype(jnp.int32)
     u = u_ref[...]
-    for j in range(occupied):
-        at = pl.ds(pl.multiple_of((2 * j + copy) * per_device, 8), per_device)
-        total = half_ref[copies[j]] + mir_ref[at, :]
-        out_ref[0, j] = jnp.where(u == (own ^ labels[j]), total, 0.0)
+    for (i0, i1, _, _), half_ref in zip(chunks, halves):
+        for i in range(i0, i1):
+            at = pl.ds(pl.multiple_of((2 * j + copies[i]) * per_device, 8), per_device)
+            total = half_ref[2 * (i - i0) + copy] + mir_ref[at, :]
+            out_ref[i, 0] = jnp.where(u == (own ^ labels[i]), total, 0.0)
 
 
 def permute(x, flip, size):
@@ -351,24 +390,28 @@
     anywhere = pl.BlockSpec(memory_space=pl.ANY)
     quarter = dests // 4
     block_rows = rows + 16
-    block, mix = pl.pallas_call(
+    block = pl.pallas_call(
         prep_kernel,
         grid=(1,),
-        out_shape=(
-            jax.ShapeDtypeStruct((block_rows, LANES), bf16),
-            jax.ShapeDtypeStruct((rows, rows), bf16),
-        ),
+        out_shape=jax.ShapeDtypeStruct((block_rows, LANES), bf16),
         in_specs=[
-            smem,
-            whole(fock_occ.shape),
-            whole(cycle_ints.shape),
+            whole((rows, LANES)),
             pl.BlockSpec((occupied, occupied, 16, LANES), lambda n: (0, 0, 0, 0)),
         ],
-        out_specs=(whole((block_rows, LANES)), whole((rows, rows))),
-        compiler_params=params(8),
+        out_specs=whole((block_rows, LANES)),
+        compiler_params=params(60),
         cost_estimate=cost(0, 500000),
-    )(pos, fock_occ, cycle_ints, amps)
+    )(cycle_ints.reshape(rows, LANES), amps)
     block = block.reshape(1, block_rows, LANES)
+    vmem = pl.BlockSpec(memory_space=pltpu.VMEM)
+    mix = pl.pallas_call(
+        mix_kernel,
+        out_shape=jax.ShapeDtypeStruct((rows, rows), bf16),
+        in_specs=[vmem, anywhere],
+        out_specs=vmem,
+        compiler_params=params(4),
+        cost_estimate=cost(10**7, 300000),
+    )(fock_occ, block)
 
     flat_amps = amps.reshape(occupied, rows, virtuals)
     parts = (2, 4, 2)
@@ -442,46 +485,72 @@
         cost_estimate=cost(4 * occupied * rows * virtuals * LANES, 9 * 10**6),
     )(occ_irrep, win, win_mate, half0, half1, half2, u, ladder_ints)
 
-    send_rows = tiles * per_device + 8
-    vmem = pl.BlockSpec(memory_space=pltpu.VMEM)
-    half, send = pl.pallas_call(
-        functools.partial(cycle_kernel, parts),
-        out_shape=(
-            jax.ShapeDtypeStruct(half.shape, f32),
+    chunks = ((0, occupied, 0, tiles),)
+    joins = ((0, occupied),)
+    cycs = (cyc0, cyc1, cyc2)
+    halves, recvs = [], []
+    x_shape = (occupied, virtuals, LANES)
+    for n, chunk in enumerate(chunks):
+        i0, i1, t0, t1 = chunk
+        wide_i = i1 - i0
+        send_rows = ((t1 - t0) * per_device + 8 + 15) // 16 * 16
+        half_shape = (2 * wide_i, per_device, virtuals)
+        out_shape = [
+            jax.ShapeDtypeStruct(half_shape, f32),
             jax.ShapeDtypeStruct((dests, send_rows, LANES), bf16),
-        ),
-        in_specs=[smem, smem] + [vmem] * 5 + [anywhere, vmem],
-        out_specs=(anywhere, vmem),
-        scratch_shapes=[
-            pltpu.VMEM((virtuals, occupied, LANES), f32),
-            pltpu.VMEM(half.shape, f32),
+        ]
+        scratch = [
+            pltpu.SMEM((occupied,), jnp.int32),
+            pltpu.VMEM((occupied, wide_i, per_device, virtuals), f32),
+            pltpu.VMEM(half_shape, f32),
             pltpu.VMEM((dests, send_rows, LANES), f32),
             pltpu.SemaphoreType.DMA((1,)),
-        ],
-        compiler_params=params(24),
-        cost_estimate=cost(2 * occupied * rows * virtuals * LANES, 8 * 10**6),
-    )(pos, occ_irrep, own_blocks, mate_blocks, cyc0, cyc1, cyc2, half, u)
-
-    recv = lax.all_to_all(send, "vir", split_axis=0, concat_axis=0, tiled=True)
-
-    return pl.pallas_call(
-        join_kernel,
-        grid=(occupied,),
-        out_shape=jax.ShapeDtypeStruct((occupied, occupied, per_device, virtuals), f32),
-        in_specs=[
-            smem,
-            pl.BlockSpec((2, per_device, virtuals), lambda n: (n, 0, 0)),
-            whole(recv.shape),
-            whole(u.shape),
-        ],
-        out_specs=pl.BlockSpec((1, occupied, per_device, virtuals), lambda n: (n, 0, 0, 0)),
-        scratch_shapes=[
-            pltpu.VMEM((tiles, virtuals, LANES), f32),
-            pltpu.VMEM((tiles * LANES, virtuals), f32),
-        ],
-        compiler_params=params(16),
-        cost_estimate=cost(10**6, 10**7),
-    )(occ_irrep, half, recv, u)
+        ]
+        if n == 0:
+            given = (own_blocks, mate_blocks)
+            out_shape.append(jax.ShapeDtypeStruct(x_shape, bf16))
+            scratch.append(pltpu.VMEM((virtuals, occupied, LANES), f32))
+        else:
+            given = (x_all, halves[-1])
+        got = pl.pallas_call(
+            functools.partial(cycle_kernel, chunk, chunks[n - 1][0] if n else None, parts),
+            out_shape=out_shape,
+            in_specs=[smem, smem] + [vmem] * 5 + [anywhere, vmem],
+            out_specs=[vmem] * len(out_shape),
+            scratch_shapes=scratch,
+            compiler_params=params(28),
+            cost_estimate=cost(2 * wide_i * rows * virtuals * LANES, 8 * 10**6),
+        )(pos, occ_irrep, *given, *cycs, half, u)
+        if n == 0:
+            x_all = got[2]
+        halves.append(got[0])
+        recvs.append(
+            lax.all_to_all(got[1], "vir", split_axis=0, concat_axis=0, tiled=True)
+        )
+
+    out = None
+    for n, (j0, j1) in enumerate(joins):
+        used = chunks if n + 1 == len(joins) else chunks
+        extra = () if out is None else (out,)
+        out = pl.pallas_call(
+            functools.partial(join_kernel, used, j0),
+            grid=(j1 - j0,),
+            out_shape=jax.ShapeDtypeStruct((occupied, occupied, per_device, virtuals), f32),
+            in_specs=[smem, whole(u.shape)]
+            + [whole(x.shape) for x in halves]
+            + [whole(x.shape) for x in recvs]
+            + [anywhere] * len(extra),
+            out_specs=pl.BlockSpec(
+                (occupied, 1, per_device, virtuals), lambda n, j0=j0: (0, n + j0, 0, 0)
+            ),
+            scratch_shapes=[
+                pltpu.VMEM((virtuals, LANES), f32),
+                pltpu.VMEM((tiles * LANES, virtuals), f32),
+            ],
+            compiler_params=params(16),
+            cost_estimate=cost(10**6, 10**7),
+        )(occ_irrep, u, *halves, *recvs, *extra)
+    return out
 
 
 def solution(mesh):

time: 74.6 us -> 71.2 us (0.954)
  local copies, waits for them, and re-layouts: 4.75 us -> 2.13 us
  waiting for transfers between devices: 5.15 us -> 3.83 us
    unnamed x18, local copies, waits for them, and re-layouts: 4.68 us -> 2.05 us
    ppermute x7, waiting for transfers between devices: 5.15 us -> 3.83 us  [permute(): return lax.ppermute(x, 'vir', [(n, n ^ flip) for n in range(size)])]
    pallas_call x3 -> x4, Pallas kernels: 14.3 us -> 15.5 us  [the longest x1 7.37 us: body(): pl.pallas_call(functools.partial(cycle_kernel, chunk, chunks[n - 1][0] if...]
    pallas_call x3, Pallas kernels: 1.93 us -> 0.96 us  [stack(): pl.pallas_call(kernel, out_shape=jax.ShapeDtypeStruct(shape, blocks[0].dt...]
where the time goes in v5:
time: 71.2 us; the launch traced here: 71 us
  Pallas kernels  29.2 us (41%)
  blocking collectives  26.5 us (37%)
  starting transfers between devices  9.11 us (13%)
  waiting for transfers between devices  3.83 us (5%)
  local copies, waits for them, and re-layouts  2.13 us (3%)
    all_to_all x1, blocking collectives, body(): lax.all_to_all(got[1], 'vir', split_axis=0, concat_axis=0, tiled=True)  26.5 us
    ppermute x7, starting transfers between devices, permute(): return lax.ppermute(x, 'vir', [(n, n ^ flip) for n in range(size)])  9.11 us
    pallas_call x3, Pallas kernels, fock_part(): pl.pallas_call(functools.partial(fock_kernel, first), grid=(count // wide...  7.83 us
    pallas_call x1, Pallas kernels, body(): pl.pallas_call(functools.partial(cycle_kernel, chunk, chunks[n - 1][0] if...  7.37 us
    pallas_call x1, Pallas kernels, body(): pl.pallas_call(functools.partial(join_kernel, used, j0), grid=(j1 - j0,),...  5.88 us
    pallas_call x1, Pallas kernels, body(): pl.pallas_call(functools.partial(ladder_kernel, parts), grid=(per_device...  4.68 us
    ppermute x7, waiting for transfers between devices, permute(): return lax.ppermute(x, 'vir', [(n, n ^ flip) for n in range(size)])  3.83 us
    unnamed x18, local copies, waits for them, and re-layouts  2.05 us
  transfers between devices with their start and end apart: 7, of which 3 were waited for; matrix products, arithmetic and copies ran while one was open for 0% of the time, Pallas kernels for 20%

profile of v5, /device:TPU:1, one launch (start us, length us, event | category | flops | bytes accessed | tf_op | source)
XLA Modules:
  0.0 71.0 jit_solution(3230264660815882462)
XLA Ops:
  0.0 1.9 %shard_map.73 = bf16[336,128]{1,0:T(8,128)(2,1)} custom-call(bf16[320,128]{1,0:T(8,128)(2,1)} %bitcast.14, bf16[8,8,40,640]{3,2,1,0:T(8,128)(2,1)} %amps_ref.1), custom_call_target="tpu_custom_call" | custom-call | bytes 500000 | tf_op jit(solution)/shard_map/pallas_call | solution.py:393
  1.9 4.2 %collective-permute-start.2 = (bf16[1,336,128]{2,1,0:T(8,128)(2,1)}, bf16[1,336,128]{2,1,0:T(8,128)(2,1)S(1)}, u32[]{:S(2)}, u32[]{:S(2)}) collective-permute-start(bf16[1,336,128]{2,1,0:T(8,128)(2,1)} %bitcast.9), channel_id=1, source_target_pairs={{0,12},{1,13},{2,14},{3,15},{4,8},{5,9},{6,10},{7,11},{8,4},{9,5},... | collective-permute-start | bytes 258056 | tf_op jit(solution)/shard_map/ppermute | solution.py:368
  6.1 0.0 collective-permute-start.1
  6.1 0.3 collective-permute-start
  6.4 0.1 dynamic_slice.3
  6.4 0.1 broadcast_xor_fusion.u_ref.refs_3_.refs_6_
  6.5 0.0 copy-start.2
  6.5 0.9 %copy-done.2 = bf16[336,128]{1,0:T(8,128)(2,1)S(1)} copy-done((bf16[336,128]{1,0:T(8,128)(2,1)S(1)}, bf16[336,128]{1,0:T(8,128)(2,1)}, u32[]{:S(2)}) %copy-start.2) | copy-done | bytes 86040
  7.4 0.4 shard_map.74.mix_ref.after_ref
  7.8 0.0 copy-start.1
  7.8 1.1 %copy-done.1 = bf16[640,640]{1,0:T(8,128)(2,1)S(1)} copy-done((bf16[640,640]{1,0:T(8,128)(2,1)S(1)}, bf16[640,640]{1,0:T(8,128)(2,1)}, u32[]{:S(2)}) %copy-start.1) | copy-done | bytes 819224
  9.0 2.0 %shard_map.75 = (f32[4,40,640]{2,1,0:T(8,128)S(1)}, bf16[2,40,128]{2,1,0:T(8,128)(2,1)S(1)}) custom-call(s32[8]{0:T(128)S(1)} %copy-done.4, bf16[8,320,640]{2,1,0:T(8,128)(2,1)S(1)} %bitcast.4, bf16[640,640]{1,0:T(8,128)(2,1)S(1)} %copy-done.1, bf16[320,320]{1,0:T(8,128)(2,1)S(1)} %shard_map.74.mix_ref.after_ref, ...), custom_call_target="tpu_custom_call" | custom-call | flops 786432000 | bytes 2000000 | tf_op jit(solution)/shard_map/pallas_call | solution.py:422
  11.0 0.3 collective-permute-done.refs_1_
  11.4 1.3 %collective-permute-start.3 = (bf16[2,336,128]{2,1,0:T(8,128)(2,1)S(1)}, bf16[2,336,128]{2,1,0:T(8,128)(2,1)S(1)}, u32[]{:S(2)}, u32[]{:S(2)}) collective-permute-start(bf16[2,336,128]{2,1,0:T(8,128)(2,1)S(1)} %shard_map.76.after_ref.refs_0_), channel_id=1, source_target_pairs={{0,2},{1,3},{2,0},{3,1},{4,6},{5,7},{6,4},{7,5},{8,10},{9,11},{10,... | collective-permute-start | bytes 516104 | tf_op jit(solution)/shard_map/ppermute | solution.py:368
  12.7 3.7 %shard_map.77 = (f32[8,40,640]{2,1,0:T(8,128)S(1)}, bf16[4,40,128]{2,1,0:T(8,128)(2,1)S(1)}) custom-call(s32[8]{0:T(128)S(1)} %copy-done.4, bf16[8,320,640]{2,1,0:T(8,128)(2,1)S(1)} %bitcast.5, bf16[640,640]{1,0:T(8,128)(2,1)S(1)} %copy-done.1, bf16[320,320]{1,0:T(8,128)(2,1)S(1)} %shard_map.74.mix_ref.after_ref, ...), custom_call_target="tpu_custom_call" | custom-call | flops 1572864000 | bytes 2000000 | tf_op jit(solution)/shard_map/pallas_call | solution.py:422
  16.4 0.0 collective-permute-done.2.refs_1_
  16.4 0.0 collective-permute-done.1.refs_0_
  16.4 0.9 %shard_map.78.after_ref.refs_1_ = bf16[2,336,128]{2,1,0:T(8,128)(2,1)S(1)} custom-call(bf16[1,336,128]{2,1,0:T(8,128)(2,1)} %collective-permute-done.1.refs_0_, bf16[1,336,128]{2,1,0:T(8,128)(2,1)S(1)} %collective-permute-done.2.refs_1_, f32[8,40,640]{2,1,0:T(8,128)S(1)} %get-tuple-element.14.refs_2_.refs_1_), custom_call_target="tpu_custom_call" | custom-call | bytes 1000000 | tf_op jit(solution)/shard_map/pallas_call | solution.py:150
  17.4 0.0 slice-start.1
  17.4 0.3 collective-permute-start.4
  17.7 2.0 %shard_map.79 = (f32[4,40,640]{2,1,0:T(8,128)S(1)}, bf16[2,40,128]{2,1,0:T(8,128)(2,1)S(1)}) custom-call(s32[8]{0:T(128)S(1)} %copy-done.4, bf16[8,320,640]{2,1,0:T(8,128)(2,1)S(1)} %bitcast.6, bf16[640,640]{1,0:T(8,128)(2,1)S(1)} %copy-done.1, bf16[320,320]{1,0:T(8,128)(2,1)S(1)} %shard_map.74.mix_ref.after_ref, ...), custom_call_target="tpu_custom_call" | custom-call | flops 786432000 | bytes 2000000 | tf_op jit(solution)/shard_map/pallas_call | solution.py:422
  19.7 0.0 collective-permute-done.3.refs_2_
  19.7 2.0 %collective-permute-done.4.refs_3_ = bf16[2,336,128]{2,1,0:T(8,128)(2,1)S(1)} collective-permute-done((bf16[2,336,128]{2,1,0:T(8,128)(2,1)S(1)}, bf16[2,336,128]{2,1,0:T(8,128)(2,1)S(1)}, u32[]{:S(2)}, u32[]{:S(2)}) %collective-permute-start.4) | collective-permute-done | bytes 172064 | tf_op jit(solution)/shard_map/ppermute | solution.py:368
  21.7 3.0 %collective-permute-start.5 = (bf16[8,336,128]{2,1,0:T(8,128)(2,1)S(1)}, bf16[8,336,128]{2,1,0:T(8,128)(2,1)S(1)}, u32[]{:S(2)}, u32[]{:S(2)}) collective-permute-start(bf16[8,336,128]{2,1,0:T(8,128)(2,1)S(1)} %shard_map.80.blocks_ref.after_ref.refs_0_), channel_id=1, source_target_pairs={{0,1},{1,0},{2,3},{3,2},{4,5},{5,4},{6,7},{7,6},{8,9},{9,8},{10,11... | collective-permute-start | bytes 2064392 | tf_op jit(solution)/shard_map/ppermute | solution.py:368
  24.7 0.2 shard_map.81.win0_ref
  24.9 0.1 collective-permute-start.6
  25.0 1.5 %collective-permute-done.6.win1_ref = bf16[64,128]{1,0:T(8,128)(2,1)S(1)} collective-permute-done((bf16[64,128]{1,0:T(8,128)(2,1)S(1)}, bf16[64,128]{1,0:T(8,128)(2,1)S(1)}, u32[]{:S(2)}, u32[]{:S(2)}) %collective-permute-start.6) | collective-permute-done | bytes 16416 | tf_op jit(solution)/shard_map/ppermute | solution.py:368
  26.5 4.7 %shard_map.82.refs_5_ = f32[16,40,640]{2,1,0:T(8,128)S(1)} custom-call(s32[8]{0:T(128)S(1)} %copy-done.4, bf16[64,128]{1,0:T(8,128)(2,1)S(1)} %shard_map.81.win0_ref, bf16[64,128]{1,0:T(8,128)(2,1)S(1)} %collective-permute-done.6.win1_ref, f32[4,40,640]{2,1,0:T(8,128)S(1)} %get-tuple-element.13.refs_2_.refs_0_, ...), custom_call_target="tpu_custom_call" | custom-call | flops 838860800 | bytes 9000000 | tf_op jit(solution)/shard_map/pallas_call | solution.py:471
  31.2 0.0 collective-permute-done.5.refs_1_
  31.2 7.4 %shard_map.83 = (f32[16,40,640]{2,1,0:T(8,128)S(1)}, bf16[16,208,128]{2,1,0:T(8,128)(2,1)S(1)}, bf16[8,640,128]{2,1,0:T(8,128)(2,1)}) custom-call(s32[1]{0:T(128)} %bitcast.pos_ref, s32[8]{0:T(128)S(1)} %copy-done.4, bf16[8,336,128]{2,1,0:T(8,128)(2,1)S(1)} %shard_map.80.blocks_ref.after_ref.refs_0_, ...), custom_call_target="tpu_custom_call" | custom-call | flops 419430400 | bytes 8000000 | tf_op jit(solution)/shard_map/pallas_call | solution.py:515
  38.6 26.5 %all_to_all.5.refs_1_ = bf16[16,208,128]{2,1,0:T(8,128)(2,1)S(1)} all-to-all(bf16[16,208,128]{2,1,0:T(8,128)(2,1)S(1)} %get-tuple-element.20), channel_id=1, replica_groups=mesh['groups'=2,'vir'=16] {'vir'}, dimensions={0} | all-to-all | bytes 1703936 | tf_op jit(solution)/shard_map/all_to_all | solution.py:528
  65.1 5.9 %shard_map.84 = f32[8,8,40,640]{3,2,1,0:T(8,128)} custom-call(s32[8]{0:T(128)S(1)} %copy-done.4, s32[40,640]{1,0:T(8,128)S(1)} %broadcast_xor_fusion.u_ref.refs_3_.refs_6_, f32[16,40,640]{2,1,0:T(8,128)S(1)} %get-tuple-element.19.refs_0_, bf16[16,208,128]{2,1,0:T(8,128)(2,1)S(1)} %all_to_all.5.refs_1_), custom_call_target="tpu_custom_call" | custom-call | flops 1000000 | bytes 10000000 | tf_op jit(solution)/shard_map/pallas_call | solution.py:535
  (16 shorter events, 0.1 us)
Async XLA Ops:
  0.0 7.8 %copy-start = (bf16[8,8,40,640]{3,2,1,0:T(8,128)(2,1)S(1)}, bf16[8,8,40,640]{3,2,1,0:T(8,128)(2,1)}, u32[]{:S(2)}) copy-start(bf16[8,8,40,640]{3,2,1,0:T(8,128)(2,1)} %amps_ref.1) | copy-start | bytes 9830404
  0.0 6.3 %copy-start.6 = (s32[640]{0:T(1024)S(1)}, s32[640]{0:T(1024)}, u32[]{:S(2)}) copy-start(s32[640]{0:T(1024)} %param.13) | copy-start | bytes 7684
  0.0 6.5 %copy-start.5 = (bf16[8,8]{1,0:T(8,128)(2,1)S(1)}, bf16[8,8]{1,0:T(8,128)(2,1)}, u32[]{:S(2)}) copy-start(bf16[8,8]{1,0:T(8,128)(2,1)} %occ_vals_ref.1) | copy-start | bytes 388
  0.0 7.8 %copy-start.4 = (s32[8]{0:T(128)S(1)}, s32[8]{0:T(128)}, u32[]{:S(2)}) copy-start(s32[8]{0:T(128)} %occ_ref.11) | copy-start | bytes 100
  1.9 9.4 %copy-start.3 = (bf16[336,128]{1,0:T(8,128)(2,1)S(1)}, bf16[336,128]{1,0:T(8,128)(2,1)}, u32[]{:S(2)}) copy-start(bf16[336,128]{1,0:T(8,128)(2,1)} %shard_map.73) | copy-start | bytes 258052
  1.9 14.5 %collective-permute-start.2 = (bf16[1,336,128]{2,1,0:T(8,128)(2,1)}, bf16[1,336,128]{2,1,0:T(8,128)(2,1)S(1)}, u32[]{:S(2)}, u32[]{:S(2)}) collective-permute-start(bf16[1,336,128]{2,1,0:T(8,128)(2,1)} %bitcast.9), channel_id=1, source_target_pairs={{0,12},{1,13},{2,14},{3,15},{4,8},{5,9},{6,10},{7,11},{8,4},{9,5},... | collective-permute-start | bytes 258056 | tf_op jit(solution)/shard_map/ppermute | solution.py:368
  6.1 10.4 %collective-permute-start.1 = (bf16[1,336,128]{2,1,0:T(8,128)(2,1)}, bf16[1,336,128]{2,1,0:T(8,128)(2,1)}, u32[]{:S(2)}, u32[]{:S(2)}) collective-permute-start(bf16[1,336,128]{2,1,0:T(8,128)(2,1)} %bitcast.10), channel_id=1, source_target_pairs={{0,8},{1,9},{2,10},{3,11},{4,12},{5,13},{6,14},{7,15},{8,0},{9,1},... | collective-permute-start | bytes 258056 | tf_op jit(solution)/shard_map/ppermute | solution.py:368
  6.1 5.3 %collective-permute-start = (bf16[1,336,128]{2,1,0:T(8,128)(2,1)}, bf16[1,336,128]{2,1,0:T(8,128)(2,1)S(1)}, u32[]{:S(2)}, u32[]{:S(2)}) collective-permute-start(bf16[1,336,128]{2,1,0:T(8,128)(2,1)} %bitcast.11), channel_id=1, source_target_pairs={{0,4},{1,5},{2,6},{3,7},{4,0},{5,1},{6,2},{7,3},{8,12},{9,13},{10,... | collective-permute-start | bytes 258056 | tf_op jit(solution)/shard_map/ppermute | solution.py:368
  6.5 0.9 %copy-start.2 = (bf16[336,128]{1,0:T(8,128)(2,1)S(1)}, bf16[336,128]{1,0:T(8,128)(2,1)}, u32[]{:S(2)}) copy-start(bf16[336,128]{1,0:T(8,128)(2,1)} %shard_map.73) | copy-start | bytes 258052
  7.8 1.1 %copy-start.1 = (bf16[640,640]{1,0:T(8,128)(2,1)S(1)}, bf16[640,640]{1,0:T(8,128)(2,1)}, u32[]{:S(2)}) copy-start(bf16[640,640]{1,0:T(8,128)(2,1)} %fock_ref.5) | copy-start | bytes 2457604
  11.4 8.3 %collective-permute-start.3 = (bf16[2,336,128]{2,1,0:T(8,128)(2,1)S(1)}, bf16[2,336,128]{2,1,0:T(8,128)(2,1)S(1)}, u32[]{:S(2)}, u32[]{:S(2)}) collective-permute-start(bf16[2,336,128]{2,1,0:T(8,128)(2,1)S(1)} %shard_map.76.after_ref.refs_0_), channel_id=1, source_target_pairs={{0,2},{1,3},{2,0},{3,1},{4,6},{5,7},{6,4},{7,5},{8,10},{9,11},{10,... | collective-permute-start | bytes 516104 | tf_op jit(solution)/shard_map/ppermute | solution.py:368
  12.7 13.9 %slice-start = ((s8[6553600]{0:T(1024)(128)(4,1)}), s8[4194304]{0:T(1024)(128)(4,1)S(1)}, s32[]{:S(2)}) async-start(s8[6553600]{0:T(1024)(128)(4,1)} %bitcast.7), calls=%async_computation.1 | async-start | bytes 8388608
  17.4 9.2 %slice-start.1 = ((s8[6553600]{0:T(1024)(128)(4,1)}), s8[2359296]{0:T(1024)(128)(4,1)S(1)}, s32[]{:S(2)}) async-start(s8[6553600]{0:T(1024)(128)(4,1)} %bitcast.7), calls=%async_computation.2 | async-start | bytes 4718592
  17.4 4.3 %collective-permute-start.4 = (bf16[2,336,128]{2,1,0:T(8,128)(2,1)S(1)}, bf16[2,336,128]{2,1,0:T(8,128)(2,1)S(1)}, u32[]{:S(2)}, u32[]{:S(2)}) collective-permute-start(bf16[2,336,128]{2,1,0:T(8,128)(2,1)S(1)} %shard_map.78.after_ref.refs_1_), channel_id=1, source_target_pairs={{0,2},{1,3},{2,0},{3,1},{4,6},{5,7},{6,4},{7,5},{8,10},{9,11},{10,... | collective-permute-start | bytes 516104 | tf_op jit(solution)/shard_map/ppermute | solution.py:368
  21.7 9.5 %collective-permute-start.5 = (bf16[8,336,128]{2,1,0:T(8,128)(2,1)S(1)}, bf16[8,336,128]{2,1,0:T(8,128)(2,1)S(1)}, u32[]{:S(2)}, u32[]{:S(2)}) collective-permute-start(bf16[8,336,128]{2,1,0:T(8,128)(2,1)S(1)} %shard_map.80.blocks_ref.after_ref.refs_0_), channel_id=1, source_target_pairs={{0,1},{1,0},{2,3},{3,2},{4,5},{5,4},{6,7},{7,6},{8,9},{9,8},{10,11... | collective-permute-start | bytes 2064392 | tf_op jit(solution)/shard_map/ppermute | solution.py:368
  24.9 1.6 %collective-permute-start.6 = (bf16[64,128]{1,0:T(8,128)(2,1)S(1)}, bf16[64,128]{1,0:T(8,128)(2,1)S(1)}, u32[]{:S(2)}, u32[]{:S(2)}) collective-permute-start(bf16[64,128]{1,0:T(8,128)(2,1)S(1)} %shard_map.81.win0_ref), channel_id=1, source_target_pairs={{0,1},{1,0},{2,3},{3,2},{4,5},{5,4},{6,7},{7,6},{8,9},{9,8},{10,11... | collective-permute-start | bytes 49160 | tf_op jit(solution)/shard_map/ppermute | solution.py:368

commit v6 on v5

--- a/solution.py
+++ b/solution.py
@@ -319,49 +319,51 @@
         send_ref[q] = y.astype(jnp.bfloat16)
 
 
-def join_kernel(chunks, first_j, occ_ref, u_ref, *refs):
-    count = len(chunks)
-    halves, recvs = refs[:count], refs[count : 2 * count]
-    out_ref, dec_ref, mir_ref = refs[-3:]
-    step = pl.program_id(0)
-    j = step + first_j
+def join_kernel(chunks, some, j0, j1, occ_ref, u_ref, *refs):
+    halves, recvs = refs[: len(chunks)], refs[len(chunks) : len(chunks) + some]
+    out_ref, dec_ref, mir_ref, res_ref, sems = refs[-5:]
     occupied = occ_ref.shape[0]
     per_device, virtuals = u_ref.shape
     labels, copies = labels_and_copies(occ_ref, occupied)
     spread = 2 * per_device
-    for (_, _, t0, t1), recv_ref in zip(chunks, recvs):
-        dests = recv_ref.shape[0]
-        for t in range(t0, t1):
-            if (t + 1) * LANES <= first_j * spread:
-                continue
-            need = max(t * LANES // spread - first_j, 0)
-
-            @pl.when(step == need)
-            def _(t=t, t0=t0, t1=t1, recv_ref=recv_ref, dests=dests):
-                start = (t - t0) * per_device
-                low, high = start // 16 * 16, (start + per_device + 15) // 16 * 16
-                end = (t1 - t0) * per_device
-                for p in range(dests):
-                    tail = recv_ref[p, end // 16 * 16 : end // 16 * 16 + 16, :]
-                    k = tail.astype(jnp.float32)[end % 16 : end % 16 + 1, 0:1]
-                    y = recv_ref[p, low:high, :].astype(jnp.float32)
-                    y = y[start - low : start - low + per_device]
-                    size = jnp.log2(jnp.maximum(jnp.abs(y), 2.0**-126)) * (1.0 / POWER) - k
-                    size = jnp.exp2(size)
-                    x = jnp.where(y < 0, -size, jnp.where(y > 0, size, 0.0))
-                    dec_ref[p * per_device : (p + 1) * per_device, :] = x
-                mir_ref[t * LANES : (t + 1) * LANES, :] = dec_ref[...].T
-
-    own = occ_ref[j]
-    copy = jnp.int32(0)
-    for k in range(occupied):
-        copy = copy + jnp.logical_and(labels[k] == own, k < j).astype(jnp.int32)
-    u = u_ref[...]
-    for (i0, i1, _, _), half_ref in zip(chunks, halves):
-        for i in range(i0, i1):
-            at = pl.ds(pl.multiple_of((2 * j + copies[i]) * per_device, 8), per_device)
-            total = half_ref[2 * (i - i0) + copy] + mir_ref[at, :]
-            out_ref[i, 0] = jnp.where(u == (own ^ labels[i]), total, 0.0)
+    ready = set()
+
+    def decode(t):
+        ready.add(t)
+        ((_, _, t0, t1), recv_ref), = [
+            (c, r) for c, r in zip(chunks, recvs) if c[2] <= t < c[3]
+        ]
+        start = (t - t0) * per_device
+        low, high = start // 16 * 16, (start + per_device + 15) // 16 * 16
+        end = (t1 - t0) * per_device
+        for p in range(recv_ref.shape[0]):
+            tail = recv_ref[p, end // 16 * 16 : end // 16 * 16 + 16, :]
+            k = tail.astype(jnp.float32)[end % 16 : end % 16 + 1, 0:1]
+            y = recv_ref[p, low:high, :].astype(jnp.float32)
+            y = y[start - low : start - low + per_device]
+            size = jnp.log2(jnp.maximum(jnp.abs(y), 2.0**-126)) * (1.0 / POWER) - k
+            size = jnp.exp2(size)
+            x = jnp.where(y < 0, -size, jnp.where(y > 0, size, 0.0))
+            dec_ref[p * per_device : (p + 1) * per_device, :] = x
+        mir_ref[t * LANES : (t + 1) * LANES, :] = dec_ref[...].T
+
+    stores = []
+    for j in range(j0, j1):
+        for t in range(j * spread // LANES, ((j + 1) * spread - 1) // LANES + 1):
+            if t not in ready:
+                decode(t)
+        u = u_ref[...]
+        for (i0, i1, _, _), half_ref in zip(chunks, halves):
+            for i in range(i0, i1):
+                at = pl.ds(pl.multiple_of((2 * j + copies[i]) * per_device, 8), per_device)
+                total = half_ref[2 * (i - i0) + copies[j]] + mir_ref[at, :]
+                n = (j - j0) * occupied + i
+                res_ref[n] = jnp.where(u == (labels[j] ^ labels[i]), total, 0.0)
+                store = pltpu.make_async_copy(res_ref.at[n], out_ref.at[i, j], sems.at[n])
+                store.start()
+                stores.append(store)
+    for store in stores:
+        store.wait()
 
 
 def permute(x, flip, size):
@@ -485,8 +487,12 @@
         cost_estimate=cost(4 * occupied * rows * virtuals * LANES, 9 * 10**6),
     )(occ_irrep, win, win_mate, half0, half1, half2, u, ladder_ints)
 
-    chunks = ((0, occupied, 0, tiles),)
-    joins = ((0, occupied),)
+    spread = 2 * per_device
+    t_mid = (3 * tiles + 4) // 5
+    i_mid = -(-t_mid * LANES // spread)
+    j_mid = t_mid * LANES // spread
+    chunks = ((0, i_mid, 0, t_mid), (i_mid, occupied, t_mid, tiles))
+    joins = ((0, j_mid), (j_mid, occupied))
     cycs = (cyc0, cyc1, cyc2)
     halves, recvs = [], []
     x_shape = (occupied, virtuals, LANES)
@@ -530,26 +536,24 @@
 
     out = None
     for n, (j0, j1) in enumerate(joins):
-        used = chunks if n + 1 == len(joins) else chunks
         extra = () if out is None else (out,)
+        some = n + 1
+        count = (j1 - j0) * occupied
         out = pl.pallas_call(
-            functools.partial(join_kernel, used, j0),
-            grid=(j1 - j0,),
+            functools.partial(join_kernel, chunks, some, j0, j1),
             out_shape=jax.ShapeDtypeStruct((occupied, occupied, per_device, virtuals), f32),
-            in_specs=[smem, whole(u.shape)]
-            + [whole(x.shape) for x in halves]
-            + [whole(x.shape) for x in recvs]
-            + [anywhere] * len(extra),
-            out_specs=pl.BlockSpec(
-                (occupied, 1, per_device, virtuals), lambda n, j0=j0: (0, n + j0, 0, 0)
-            ),
+            in_specs=[smem] + [vmem] * (1 + len(halves) + some) + [anywhere] * len(extra),
+            out_specs=anywhere,
+            input_output_aliases={2 + len(halves) + some: 0} if extra else {},
             scratch_shapes=[
                 pltpu.VMEM((virtuals, LANES), f32),
                 pltpu.VMEM((tiles * LANES, virtuals), f32),
+                pltpu.VMEM((count, per_device, virtuals), f32),
+                pltpu.SemaphoreType.DMA((count,)),
             ],
             compiler_params=params(16),
-            cost_estimate=cost(10**6, 10**7),
-        )(occ_irrep, u, *halves, *recvs, *extra)
+            cost_estimate=cost(10**6, 5 * 10**6),
+        )(occ_irrep, u, *halves, *recvs[:some], *extra)
     return out
 
 

time: 71.2 us -> 83.8 us (1.18)
  blocking collectives: 26.5 us -> 0 us
  waiting for transfers between devices: 3.83 us -> 19.8 us
  local copies, waits for them, and re-layouts: 2.13 us -> 12.8 us
  starting transfers between devices: 9.11 us -> 18.9 us
  Pallas kernels: 29.2 us -> 30.2 us
    all_to_all x1 -> x0, blocking collectives: 26.5 us -> none  [body(): lax.all_to_all(got[1], 'vir', split_axis=0, concat_axis=0, tiled=True)]
    all_to_all x0 -> x2, waiting for transfers between devices: none -> 16.3 us  [body(): lax.all_to_all(got[1], 'vir', split_axis=0, concat_axis=0, tiled=True)]
    unnamed x18 -> x32, local copies, waits for them, and re-layouts: 2.05 us -> 12 us
    all_to_all x0 -> x2, starting transfers between devices: none -> 9.88 us  [body(): lax.all_to_all(got[1], 'vir', split_axis=0, concat_axis=0, tiled=True)]
    pallas_call x1 -> x2, Pallas kernels: 7.37 us -> 9.04 us  [body(): pl.pallas_call(functools.partial(cycle_kernel, chunk, chunks[n - 1][0] if...]
    pallas_call x3, Pallas kernels: 0.96 us -> 0.07 us  [stack(): pl.pallas_call(kernel, out_shape=jax.ShapeDtypeStruct(shape, blocks[0].dt...]
    pallas_call x1 -> x2, Pallas kernels: 5.88 us -> 6.17 us  [body(): pl.pallas_call(functools.partial(join_kernel, chunks, some, j0, j1), out_...]
  transfers between devices with their start and end apart: 7 -> 9, of which waited for: 3 -> 4; matrix products, arithmetic and copies ran while one was open for 0% -> 2% of each run, Pallas kernels for 20% -> 23%
where the time goes in v6:
time: 83.8 us; the launch traced here: 82.8 us
  Pallas kernels  30.2 us (36%)
  waiting for transfers between devices  19.8 us (24%)
  starting transfers between devices  18.9 us (23%)
  local copies, waits for them, and re-layouts  12.8 us (15%)
    all_to_all x2, waiting for transfers between devices, body(): lax.all_to_all(got[1], 'vir', split_axis=0, concat_axis=0, tiled=True)  16.3 us
    unnamed x32, local copies, waits for them, and re-layouts  12 us
    all_to_all x2, starting transfers between devices, body(): lax.all_to_all(got[1], 'vir', split_axis=0, concat_axis=0, tiled=True)  9.88 us
    ppermute x7, starting transfers between devices, permute(): return lax.ppermute(x, 'vir', [(n, n ^ flip) for n in range(size)])  9.07 us
    pallas_call x2, Pallas kernels, body(): pl.pallas_call(functools.partial(cycle_kernel, chunk, chunks[n - 1][0] if...  9.04 us
    pallas_call x3, Pallas kernels, fock_part(): pl.pallas_call(functools.partial(fock_kernel, first), grid=(count // wide...  7.86 us
    pallas_call x2, Pallas kernels, body(): pl.pallas_call(functools.partial(join_kernel, chunks, some, j0, j1), out_...  6.17 us
    pallas_call x1, Pallas kernels, body(): pl.pallas_call(functools.partial(ladder_kernel, parts), grid=(per_device...  4.71 us
  transfers between devices with their start and end apart: 9, of which 4 were waited for; matrix products, arithmetic and copies ran while one was open for 2% of the time, Pallas kernels for 23%

profile of v6, /device:TPU:1, one launch (start us, length us, event | category | flops | bytes accessed | tf_op | source)
XLA Modules:
  0.0 82.8 jit_solution(12147281830883518314)
XLA Ops:
  0.0 1.8 %shard_map.73 = bf16[336,128]{1,0:T(8,128)(2,1)} custom-call(bf16[320,128]{1,0:T(8,128)(2,1)} %bitcast.14, bf16[8,8,40,640]{3,2,1,0:T(8,128)(2,1)} %amps_ref.1), custom_call_target="tpu_custom_call" | custom-call | bytes 500000 | tf_op jit(solution)/shard_map/pallas_call | solution.py:395
  1.8 4.2 %collective-permute-start.2 = (bf16[1,336,128]{2,1,0:T(8,128)(2,1)}, bf16[1,336,128]{2,1,0:T(8,128)(2,1)S(1)}, u32[]{:S(2)}, u32[]{:S(2)}) collective-permute-start(bf16[1,336,128]{2,1,0:T(8,128)(2,1)} %bitcast.9), channel_id=1, source_target_pairs={{0,12},{1,13},{2,14},{3,15},{4,8},{5,9},{6,10},{7,11},{8,4},{9,5},... | collective-permute-start | bytes 258056 | tf_op jit(solution)/shard_map/ppermute | solution.py:370
  6.2 0.8 dynamic_slice.3
  7.0 0.8 broadcast_xor_fusion.u_ref.refs_3_.refs_6_
  7.7 0.9 %copy-done.7 = bf16[336,128]{1,0:T(8,128)(2,1)S(1)} copy-done((bf16[336,128]{1,0:T(8,128)(2,1)S(1)}, bf16[336,128]{1,0:T(8,128)(2,1)}, u32[]{:S(2)}) %copy-start.7) | copy-done | bytes 86040
  8.6 0.7 copy-done.13
  9.7 1.9 %copy-done = bf16[8,8,40,640]{3,2,1,0:T(8,128)(2,1)S(1)} copy-done((bf16[8,8,40,640]{3,2,1,0:T(8,128)(2,1)S(1)}, bf16[8,8,40,640]{3,2,1,0:T(8,128)(2,1)}, u32[]{:S(2)}) %copy-start) | copy-done | bytes 3276824
  11.6 1.1 %copy-done.1 = bf16[640,640]{1,0:T(8,128)(2,1)S(1)} copy-done((bf16[640,640]{1,0:T(8,128)(2,1)S(1)}, bf16[640,640]{1,0:T(8,128)(2,1)}, u32[]{:S(2)}) %copy-start.1) | copy-done | bytes 819224
  12.8 0.7 copy-done.11
  13.4 2.1 %shard_map.75 = (f32[4,40,640]{2,1,0:T(8,128)S(1)}, bf16[2,40,128]{2,1,0:T(8,128)(2,1)S(1)}) custom-call(s32[8]{0:T(128)S(1)} %copy-done.11, bf16[8,320,640]{2,1,0:T(8,128)(2,1)S(1)} %bitcast.4, bf16[640,640]{1,0:T(8,128)(2,1)S(1)} %copy-done.1, bf16[320,320]{1,0:T(8,128)(2,1)S(1)} %shard_map.74.mix_ref.after_ref, ...), custom_call_target="tpu_custom_call" | custom-call | flops 786432000 | bytes 2000000 | tf_op jit(solution)/shard_map/pallas_call | solution.py:424
  15.5 0.9 %copy-done.8 = bf16[336,128]{1,0:T(8,128)(2,1)S(1)} copy-done((bf16[336,128]{1,0:T(8,128)(2,1)S(1)}, bf16[336,128]{1,0:T(8,128)(2,1)}, u32[]{:S(2)}) %copy-start.8) | copy-done | bytes 86040
  16.4 1.3 %collective-permute-start.3 = (bf16[2,336,128]{2,1,0:T(8,128)(2,1)S(1)}, bf16[2,336,128]{2,1,0:T(8,128)(2,1)S(1)}, u32[]{:S(2)}, u32[]{:S(2)}) collective-permute-start(bf16[2,336,128]{2,1,0:T(8,128)(2,1)S(1)} %shard_map.76.after_ref.refs_0_), channel_id=1, source_target_pairs={{0,2},{1,3},{2,0},{3,1},{4,6},{5,7},{6,4},{7,5},{8,10},{9,11},{10,... | collective-permute-start | bytes 516104 | tf_op jit(solution)/shard_map/ppermute | solution.py:370
  17.7 3.7 %shard_map.77 = (f32[8,40,640]{2,1,0:T(8,128)S(1)}, bf16[4,40,128]{2,1,0:T(8,128)(2,1)S(1)}) custom-call(s32[8]{0:T(128)S(1)} %copy-done.12, bf16[8,320,640]{2,1,0:T(8,128)(2,1)S(1)} %bitcast.5, bf16[640,640]{1,0:T(8,128)(2,1)S(1)} %copy-done.1, bf16[320,320]{1,0:T(8,128)(2,1)S(1)} %shard_map.74.mix_ref.after_ref, ...), custom_call_target="tpu_custom_call" | custom-call | flops 1572864000 | bytes 2000000 | tf_op jit(solution)/shard_map/pallas_call | solution.py:424
  21.8 2.1 %shard_map.79 = (f32[4,40,640]{2,1,0:T(8,128)S(1)}, bf16[2,40,128]{2,1,0:T(8,128)(2,1)S(1)}) custom-call(s32[8]{0:T(128)S(1)} %copy-done.12, bf16[8,320,640]{2,1,0:T(8,128)(2,1)S(1)} %bitcast.6, bf16[640,640]{1,0:T(8,128)(2,1)S(1)} %copy-done.1, bf16[320,320]{1,0:T(8,128)(2,1)S(1)} %shard_map.74.mix_ref.after_ref, ...), custom_call_target="tpu_custom_call" | custom-call | flops 786432000 | bytes 2000000 | tf_op jit(solution)/shard_map/pallas_call | solution.py:424
  23.9 2.0 %collective-permute-done.4.refs_3_ = bf16[2,336,128]{2,1,0:T(8,128)(2,1)S(1)} collective-permute-done((bf16[2,336,128]{2,1,0:T(8,128)(2,1)S(1)}, bf16[2,336,128]{2,1,0:T(8,128)(2,1)S(1)}, u32[]{:S(2)}, u32[]{:S(2)}) %collective-permute-start.4) | collective-permute-done | bytes 172064 | tf_op jit(solution)/shard_map/ppermute | solution.py:370
  25.9 3.0 %collective-permute-start.5 = (bf16[8,336,128]{2,1,0:T(8,128)(2,1)S(1)}, bf16[8,336,128]{2,1,0:T(8,128)(2,1)S(1)}, u32[]{:S(2)}, u32[]{:S(2)}) collective-permute-start(bf16[8,336,128]{2,1,0:T(8,128)(2,1)S(1)} %shard_map.80.blocks_ref.after_ref.refs_0_), channel_id=1, source_target_pairs={{0,1},{1,0},{2,3},{3,2},{4,5},{5,4},{6,7},{7,6},{8,9},{9,8},{10,11... | collective-permute-start | bytes 2064392 | tf_op jit(solution)/shard_map/ppermute | solution.py:370
  29.1 1.5 %collective-permute-done.6.win1_ref = bf16[64,128]{1,0:T(8,128)(2,1)S(1)} collective-permute-done((bf16[64,128]{1,0:T(8,128)(2,1)S(1)}, bf16[64,128]{1,0:T(8,128)(2,1)S(1)}, u32[]{:S(2)}, u32[]{:S(2)}) %collective-permute-start.6) | collective-permute-done | bytes 16416 | tf_op jit(solution)/shard_map/ppermute | solution.py:370
  30.6 4.7 %shard_map.82.refs_5_ = f32[16,40,640]{2,1,0:T(8,128)S(1)} custom-call(s32[8]{0:T(128)S(1)} %copy-done.12, bf16[64,128]{1,0:T(8,128)(2,1)S(1)} %shard_map.81.win0_ref, bf16[64,128]{1,0:T(8,128)(2,1)S(1)} %collective-permute-done.6.win1_ref, f32[4,40,640]{2,1,0:T(8,128)S(1)} %get-tuple-element.16.refs_2_.refs_0_, ...), custom_call_target="tpu_custom_call" | custom-call | flops 838860800 | bytes 9000000 | tf_op jit(solution)/shard_map/pallas_call | solution.py:473
  35.4 6.4 %shard_map.83 = (f32[10,40,640]{2,1,0:T(8,128)S(1)}, bf16[16,128,128]{2,1,0:T(8,128)(2,1)S(1)}, bf16[8,640,128]{2,1,0:T(8,128)(2,1)S(1)}) custom-call(s32[1]{0:T(128)} %bitcast.pos_ref, s32[8]{0:T(128)S(1)} %copy-done.12, bf16[8,336,128]{2,1,0:T(8,128)(2,1)S(1)} %shard_map.80.blocks_ref.after_ref.refs_0_, ...), custom_call_target="tpu_custom_call" | custom-call | flops 262144000 | bytes 8000000 | tf_op jit(solution)/shard_map/pallas_call | solution.py:521
  41.8 1.0 %copy-done.5 = bf16[8,640,128]{2,1,0:T(8,128)(2,1)} copy-done((bf16[8,640,128]{2,1,0:T(8,128)(2,1)}, bf16[8,640,128]{2,1,0:T(8,128)(2,1)S(1)}, u32[]{:S(2)}) %copy-start.5) | copy-done | bytes 1310744
  42.8 0.8 copy-done.9
  43.7 5.2 %all-to-all-start = ((bf16[16,128,128]{2,1,0:T(8,128)(2,1)}), bf16[16,128,128]{2,1,0:T(8,128)(2,1)S(1)}, u32[]{:S(2)}, u32[]{:S(2)}) async-start(bf16[16,128,128]{2,1,0:T(8,128)(2,1)} %copy-done.9), calls=%async_computation | async-start | bytes 1048576 | tf_op jit(solution)/shard_map/all_to_all | solution.py:534
  48.9 1.3 %copy-done.6 = bf16[8,640,128]{2,1,0:T(8,128)(2,1)S(1)} copy-done((bf16[8,640,128]{2,1,0:T(8,128)(2,1)S(1)}, bf16[8,640,128]{2,1,0:T(8,128)(2,1)}, u32[]{:S(2)}) %copy-start.6) | copy-done | bytes 1310744
  50.2 2.6 %shard_map.84 = (f32[6,40,640]{2,1,0:T(8,128)S(1)}, bf16[16,96,128]{2,1,0:T(8,128)(2,1)S(1)}) custom-call(s32[1]{0:T(128)} %bitcast.pos_ref, s32[8]{0:T(128)S(1)} %copy-done.12, bf16[8,640,128]{2,1,0:T(8,128)(2,1)S(1)} %copy-done.6, f32[10,40,640]{2,1,0:T(8,128)S(1)} %get-tuple-element.22.refs_1_.refs_0_, bf16[2,40,128]{2,1,0:T(8,128)(2,1)S(1)} %get-tuple-element.19.refs_2_, ...), custom_call_target="tpu_custom_call" | custom-call | flops 157286400 | bytes 8000000 | tf_op jit(solution)/shard_map/pallas_call | solution.py:521
  52.9 0.8 copy-done.2
  53.7 0.8 copy-done.10
  54.4 8.5 %all-to-all-done.refs_2_ = bf16[16,128,128]{2,1,0:T(8,128)(2,1)S(1)} async-done(((bf16[16,128,128]{2,1,0:T(8,128)(2,1)}), bf16[16,128,128]{2,1,0:T(8,128)(2,1)S(1)}, u32[]{:S(2)}, u32[]{:S(2)}) %all-to-all-start) | async-done | bytes 524320 | tf_op jit(solution)/shard_map/all_to_all | solution.py:534
  63.0 4.6 %all-to-all-start.1 = ((bf16[16,96,128]{2,1,0:T(8,128)(2,1)}), bf16[16,96,128]{2,1,0:T(8,128)(2,1)S(1)}, u32[]{:S(2)}, u32[]{:S(2)}) async-start(bf16[16,96,128]{2,1,0:T(8,128)(2,1)} %copy-done.10), calls=%async_computation.1 | async-start | bytes 786432 | tf_op jit(solution)/shard_map/all_to_all | solution.py:534
  67.6 1.1 %copy-done.3 = f32[6,40,640]{2,1,0:T(8,128)S(1)} copy-done((f32[6,40,640]{2,1,0:T(8,128)S(1)}, f32[6,40,640]{2,1,0:T(8,128)}, u32[]{:S(2)}) %copy-start.3) | copy-done | bytes 614424
  68.7 3.0 %shard_map.85.refs_4_ = f32[8,8,40,640]{3,2,1,0:T(8,128)} custom-call(s32[8]{0:T(128)S(1)} %copy-done.12, s32[40,640]{1,0:T(8,128)S(1)} %broadcast_xor_fusion.u_ref.refs_3_.refs_6_, f32[10,40,640]{2,1,0:T(8,128)S(1)} %get-tuple-element.22.refs_1_.refs_0_, f32[6,40,640]{2,1,0:T(8,128)S(1)} %copy-done.3, bf16[16,128,128]{2,1,0:T(8,128)(2,1)S(1)} %all-to-all-done.refs_2_), custom_call_target="tpu_custom_call" | custom-call | flops 1000000 | bytes 5000000 | tf_op jit(solution)/shard_map/pallas_call | solution.py:542
  71.7 7.8 %all-to-all-done.1.refs_3_ = bf16[16,96,128]{2,1,0:T(8,128)(2,1)S(1)} async-done(((bf16[16,96,128]{2,1,0:T(8,128)(2,1)}), bf16[16,96,128]{2,1,0:T(8,128)(2,1)S(1)}, u32[]{:S(2)}, u32[]{:S(2)}) %all-to-all-start.1) | async-done | bytes 393248 | tf_op jit(solution)/shard_map/all_to_all | solution.py:534
  79.5 3.1 %shard_map.86 = f32[8,8,40,640]{3,2,1,0:T(8,128)} custom-call(s32[8]{0:T(128)S(1)} %copy-done.12, s32[40,640]{1,0:T(8,128)S(1)} %broadcast_xor_fusion.u_ref.refs_3_.refs_6_, f32[10,40,640]{2,1,0:T(8,128)S(1)} %get-tuple-element.22.refs_1_.refs_0_, f32[6,40,640]{2,1,0:T(8,128)S(1)} %copy-done.4, ...), custom_call_target="tpu_custom_call", output_to_operand_aliasing={{}: (6, {})} | custom-call | flops 1000000 | bytes 5000000 | tf_op jit(solution)/shard_map/pallas_call | solution.py:542
  (35 shorter events, 1.4 us)
Async XLA Ops:
  0.0 17.7 %copy-start.12 = (s32[8]{0:T(128)S(1)}, s32[8]{0:T(128)}, u32[]{:S(2)}) copy-start(s32[8]{0:T(128)} %occ_ref.15) | copy-start | bytes 100
  1.8 19.7 %collective-permute-start.2 = (bf16[1,336,128]{2,1,0:T(8,128)(2,1)}, bf16[1,336,128]{2,1,0:T(8,128)(2,1)S(1)}, u32[]{:S(2)}, u32[]{:S(2)}) collective-permute-start(bf16[1,336,128]{2,1,0:T(8,128)(2,1)} %bitcast.9), channel_id=1, source_target_pairs={{0,12},{1,13},{2,14},{3,15},{4,8},{5,9},{6,10},{7,11},{8,4},{9,5},... | collective-permute-start | bytes 258056 | tf_op jit(solution)/shard_map/ppermute | solution.py:370
  5.9 15.6 %collective-permute-start.1 = (bf16[1,336,128]{2,1,0:T(8,128)(2,1)}, bf16[1,336,128]{2,1,0:T(8,128)(2,1)S(1)}, u32[]{:S(2)}, u32[]{:S(2)}) collective-permute-start(bf16[1,336,128]{2,1,0:T(8,128)(2,1)} %bitcast.10), channel_id=1, source_target_pairs={{0,8},{1,9},{2,10},{3,11},{4,12},{5,13},{6,14},{7,15},{8,0},{9,1},... | collective-permute-start | bytes 258056 | tf_op jit(solution)/shard_map/ppermute | solution.py:370
  5.9 9.6 %collective-permute-start = (bf16[1,336,128]{2,1,0:T(8,128)(2,1)}, bf16[1,336,128]{2,1,0:T(8,128)(2,1)S(1)}, u32[]{:S(2)}, u32[]{:S(2)}) collective-permute-start(bf16[1,336,128]{2,1,0:T(8,128)(2,1)} %bitcast.11), channel_id=1, source_target_pairs={{0,4},{1,5},{2,6},{3,7},{4,0},{5,1},{6,2},{7,3},{8,12},{9,13},{10,... | collective-permute-start | bytes 258056 | tf_op jit(solution)/shard_map/ppermute | solution.py:370
  7.7 0.9 %copy-start.7 = (bf16[336,128]{1,0:T(8,128)(2,1)S(1)}, bf16[336,128]{1,0:T(8,128)(2,1)}, u32[]{:S(2)}) copy-start(bf16[336,128]{1,0:T(8,128)(2,1)} %shard_map.73) | copy-start | bytes 258052
  8.6 0.7 copy-start.13
  9.7 1.9 %copy-start = (bf16[8,8,40,640]{3,2,1,0:T(8,128)(2,1)S(1)}, bf16[8,8,40,640]{3,2,1,0:T(8,128)(2,1)}, u32[]{:S(2)}) copy-start(bf16[8,8,40,640]{3,2,1,0:T(8,128)(2,1)} %amps_ref.1) | copy-start | bytes 9830404
  11.6 1.1 %copy-start.1 = (bf16[640,640]{1,0:T(8,128)(2,1)S(1)}, bf16[640,640]{1,0:T(8,128)(2,1)}, u32[]{:S(2)}) copy-start(bf16[640,640]{1,0:T(8,128)(2,1)} %fock_ref.5) | copy-start | bytes 2457604
  12.8 0.7 copy-start.11
  15.5 0.9 %copy-start.8 = (bf16[336,128]{1,0:T(8,128)(2,1)S(1)}, bf16[336,128]{1,0:T(8,128)(2,1)}, u32[]{:S(2)}) copy-start(bf16[336,128]{1,0:T(8,128)(2,1)} %shard_map.73) | copy-start | bytes 258052
  16.4 14.2 %slice-start = ((s8[6553600]{0:T(1024)(128)(4,1)}), s8[4194304]{0:T(1024)(128)(4,1)S(1)}, s32[]{:S(2)}) async-start(s8[6553600]{0:T(1024)(128)(4,1)} %bitcast.7), calls=%async_computation.2 | async-start | bytes 8388608
  16.4 7.5 %collective-permute-start.3 = (bf16[2,336,128]{2,1,0:T(8,128)(2,1)S(1)}, bf16[2,336,128]{2,1,0:T(8,128)(2,1)S(1)}, u32[]{:S(2)}, u32[]{:S(2)}) collective-permute-start(bf16[2,336,128]{2,1,0:T(8,128)(2,1)S(1)} %shard_map.76.after_ref.refs_0_), channel_id=1, source_target_pairs={{0,2},{1,3},{2,0},{3,1},{4,6},{5,7},{6,4},{7,5},{8,10},{9,11},{10,... | collective-permute-start | bytes 516104 | tf_op jit(solution)/shard_map/ppermute | solution.py:370
  21.5 9.1 %slice-start.1 = ((s8[6553600]{0:T(1024)(128)(4,1)}), s8[2359296]{0:T(1024)(128)(4,1)S(1)}, s32[]{:S(2)}) async-start(s8[6553600]{0:T(1024)(128)(4,1)} %bitcast.7), calls=%async_computation.3 | async-start | bytes 4718592
  21.5 4.3 %collective-permute-start.4 = (bf16[2,336,128]{2,1,0:T(8,128)(2,1)S(1)}, bf16[2,336,128]{2,1,0:T(8,128)(2,1)S(1)}, u32[]{:S(2)}, u32[]{:S(2)}) collective-permute-start(bf16[2,336,128]{2,1,0:T(8,128)(2,1)S(1)} %shard_map.78.after_ref.refs_1_), channel_id=1, source_target_pairs={{0,2},{1,3},{2,0},{3,1},{4,6},{5,7},{6,4},{7,5},{8,10},{9,11},{10,... | collective-permute-start | bytes 516104 | tf_op jit(solution)/shard_map/ppermute | solution.py:370
  25.9 9.5 %collective-permute-start.5 = (bf16[8,336,128]{2,1,0:T(8,128)(2,1)S(1)}, bf16[8,336,128]{2,1,0:T(8,128)(2,1)S(1)}, u32[]{:S(2)}, u32[]{:S(2)}) collective-permute-start(bf16[8,336,128]{2,1,0:T(8,128)(2,1)S(1)} %shard_map.80.blocks_ref.after_ref.refs_0_), channel_id=1, source_target_pairs={{0,1},{1,0},{2,3},{3,2},{4,5},{5,4},{6,7},{7,6},{8,9},{9,8},{10,11... | collective-permute-start | bytes 2064392 | tf_op jit(solution)/shard_map/ppermute | solution.py:370
  29.0 1.6 %collective-permute-start.6 = (bf16[64,128]{1,0:T(8,128)(2,1)S(1)}, bf16[64,128]{1,0:T(8,128)(2,1)S(1)}, u32[]{:S(2)}, u32[]{:S(2)}) collective-permute-start(bf16[64,128]{1,0:T(8,128)(2,1)S(1)} %shard_map.81.win0_ref), channel_id=1, source_target_pairs={{0,1},{1,0},{2,3},{3,2},{4,5},{5,4},{6,7},{7,6},{8,9},{9,8},{10,11... | collective-permute-start | bytes 49160 | tf_op jit(solution)/shard_map/ppermute | solution.py:370
  41.8 1.1 %copy-start.5 = (bf16[8,640,128]{2,1,0:T(8,128)(2,1)}, bf16[8,640,128]{2,1,0:T(8,128)(2,1)S(1)}, u32[]{:S(2)}) copy-start(bf16[8,640,128]{2,1,0:T(8,128)(2,1)S(1)} %get-tuple-element.23.refs_0_) | copy-start | bytes 3932164
  42.8 0.8 copy-start.9
  43.7 19.3 %all-to-all-start = ((bf16[16,128,128]{2,1,0:T(8,128)(2,1)}), bf16[16,128,128]{2,1,0:T(8,128)(2,1)S(1)}, u32[]{:S(2)}, u32[]{:S(2)}) async-start(bf16[16,128,128]{2,1,0:T(8,128)(2,1)} %copy-done.9), calls=%async_computation | async-start | bytes 1048576 | tf_op jit(solution)/shard_map/all_to_all | solution.py:534
  48.9 1.3 %copy-start.6 = (bf16[8,640,128]{2,1,0:T(8,128)(2,1)S(1)}, bf16[8,640,128]{2,1,0:T(8,128)(2,1)}, u32[]{:S(2)}) copy-start(bf16[8,640,128]{2,1,0:T(8,128)(2,1)} %copy-done.5) | copy-start | bytes 3932164
  52.9 0.8 copy-start.2
  53.7 0.8 copy-start.10
  63.0 16.5 %copy-start.4 = (f32[6,40,640]{2,1,0:T(8,128)S(1)}, f32[6,40,640]{2,1,0:T(8,128)}, u32[]{:S(2)}) copy-start(f32[6,40,640]{2,1,0:T(8,128)} %copy-done.2) | copy-start | bytes 1843204
  63.0 16.5 %all-to-all-start.1 = ((bf16[16,96,128]{2,1,0:T(8,128)(2,1)}), bf16[16,96,128]{2,1,0:T(8,128)(2,1)S(1)}, u32[]{:S(2)}, u32[]{:S(2)}) async-start(bf16[16,96,128]{2,1,0:T(8,128)(2,1)} %copy-done.10), calls=%async_computation.1 | async-start | bytes 786432 | tf_op jit(solution)/shard_map/all_to_all | solution.py:534
  67.6 1.1 %copy-start.3 = (f32[6,40,640]{2,1,0:T(8,128)S(1)}, f32[6,40,640]{2,1,0:T(8,128)}, u32[]{:S(2)}) copy-start(f32[6,40,640]{2,1,0:T(8,128)} %copy-done.2) | copy-start | bytes 1843204

commit v7 on v0

--- a/solution.py
+++ b/solution.py
@@ -1,10 +1,17 @@
+import functools
+
 import jax
 import jax.numpy as jnp
 from jax import lax
+from jax.experimental import pallas as pl
+from jax.experimental.pallas import tpu as pltpu
 from jax.sharding import PartitionSpec as P
 
 DW = 8
 CW = 16
+LANES = 128
+POWER = 9
+TOP_EXPONENT = 13
 
 
 def contract_last(left_side, right_side):
@@ -13,7 +20,7 @@
     )
 
 
-def body(amps, fock_vir, fock_occ, ladder_ints, cycle_ints, occ_irrep, vir_irrep):
+def plain_body(amps, fock_vir, fock_occ, ladder_ints, cycle_ints, occ_irrep, vir_irrep):
     occupied = amps.shape[0]
     per_device = amps.shape[2]
     virtuals = amps.shape[3]
@@ -53,9 +60,475 @@
     return allowed * (half_sum + mirrored)
 
 
+def params(mib):
+    return pltpu.CompilerParams(vmem_limit_bytes=mib * 2**20)
+
+
+def labels_and_copies(occ_ref, occupied):
+    labels = [occ_ref[j] for j in range(occupied)]
+    copies = []
+    for j in range(occupied):
+        s = jnp.int32(0)
+        for k in range(j):
+            s = s + (labels[k] == labels[j]).astype(jnp.int32)
+        copies.append(s)
+    return labels, copies
+
+
+def prep_kernel(cyc_ref, amps_ref, win_ref, xt_ref, t_ref):
+    occupied, _, per_device, _ = amps_ref.shape
+    xt_ref[0, 0] = cyc_ref[...]
+    lane = lax.broadcasted_iota(jnp.int32, (occupied, LANES), 1)
+    packed = jnp.zeros((occupied, LANES), jnp.float32)
+    for j in range(occupied):
+        w = jnp.where(lane < DW, amps_ref[:, j, 0, :].astype(jnp.float32), 0.0)
+        packed = packed + (pltpu.roll(w, j * DW, axis=1) if j else w)
+    packed = jnp.concatenate([packed, jnp.zeros_like(packed)], axis=0)
+    win_ref[...] = packed.astype(jnp.bfloat16)
+    lane = lax.broadcasted_iota(jnp.int32, (per_device, LANES), 1)
+    for i in range(occupied):
+        acc = jnp.zeros((per_device, LANES), jnp.float32)
+        for k in range(occupied):
+            piece = jnp.where(lane < CW, amps_ref[i, k].astype(jnp.float32), 0.0)
+            acc = acc + (pltpu.roll(piece, k * CW, axis=1) if k else piece)
+        t_ref[i * per_device : (i + 1) * per_device, :] = acc
+    xt_ref[0, 1] = t_ref[...].astype(jnp.bfloat16)
+
+
+def mix_kernel(occ_vals_ref, after_ref, mix_ref):
+    rows = mix_ref.shape[0]
+    occupied = occ_vals_ref.shape[0]
+    per_device = rows // occupied
+    row = lax.broadcasted_iota(jnp.int32, (rows, occupied), 0)
+    start = lax.broadcasted_iota(jnp.int32, (rows, occupied), 1) * per_device
+    in_block = jnp.logical_and(row >= start, row < start + per_device).astype(jnp.bfloat16)
+    row = lax.broadcasted_iota(jnp.int32, (rows, per_device), 0)
+    at = lax.broadcasted_iota(jnp.int32, (rows, per_device), 1)
+    same = row == at
+    for n in range(1, occupied):
+        same = jnp.logical_or(same, row == at + n * per_device)
+    same = same.astype(jnp.bfloat16)
+    left = contract_last(in_block, occ_vals_ref[...]).astype(jnp.bfloat16)
+    mix = contract_last(left, in_block) * contract_last(same, same)
+    mix_ref[...] = mix.astype(jnp.bfloat16)
+
+
+def fock_kernel(first, occ_ref, amps_ref, fock_ref, mix_ref, u_ref, after_ref, half_ref, hs_ref):
+    wide, rows, virtuals = amps_ref.shape
+    _, per_device, _ = half_ref.shape
+    occupied = occ_ref.shape[0]
+    labels, copies = labels_and_copies(occ_ref, occupied)
+    u = u_ref[...]
+    h = jnp.dot(
+        amps_ref[...].reshape(wide * rows, virtuals),
+        fock_ref[...],
+        preferred_element_type=jnp.float32,
+    )
+    for w in range(wide):
+        a = amps_ref[w]
+        mixed = jnp.dot(mix_ref[...], a, preferred_element_type=jnp.float32)
+        hs_ref[...] = (h[w * rows : (w + 1) * rows] - mixed).reshape(hs_ref.shape)
+        own = occ_ref[pl.program_id(0) * wide + w + first]
+        for j in range(occupied):
+            at = 2 * w + copies[j]
+            half_ref[at] = jnp.where(u == (own ^ labels[j]), hs_ref[j], half_ref[at])
+
+
+def stack(blocks, after):
+    count = len(blocks)
+
+    def kernel(*refs):
+        out = refs[count + 1]
+        at = 0
+        for n in range(count):
+            head = blocks[n].shape[0]
+            out[at : at + head] = refs[n][...]
+            at += head
+
+    vmem = pl.BlockSpec(memory_space=pltpu.VMEM)
+    shape = (sum(b.shape[0] for b in blocks),) + blocks[0].shape[1:]
+    return pl.pallas_call(
+        kernel,
+        out_shape=jax.ShapeDtypeStruct(shape, blocks[0].dtype),
+        in_specs=[vmem] * count + [pl.BlockSpec(memory_space=pl.ANY)],
+        out_specs=vmem,
+        compiler_params=params(4),
+        cost_estimate=pl.CostEstimate(flops=0, bytes_accessed=10**6, transcendentals=0),
+    )(*blocks, after)
+
+
+def unpack_kernel(pos_ref, *refs):
+    blocks, win_ref = refs[:-2], refs[-1]
+    occupied, _, lanes = win_ref.shape
+    lane = lax.broadcasted_iota(jnp.int32, (8, lanes), 1)
+    for j in range(occupied):
+        total = jnp.zeros((8, lanes), jnp.float32)
+        for m, block in enumerate(blocks):
+            p = pos_ref[0] ^ (m << 2)
+            w = block[...].astype(jnp.float32)[:8]
+            w = jnp.where(jnp.logical_and(lane >= j * DW, lane < (j + 1) * DW), w, 0.0)
+            total = total + pltpu.roll(w, lax.rem(p * DW - j * DW + lanes, lanes), axis=1)
+        win_ref[j] = total
+
+
+def add_kernel(a_ref, b_ref, after_ref, out_ref):
+    out_ref[...] = a_ref[...] + b_ref[...]
+
+
+def payload_pieces(per_device, pairs, dests):
+    out = {}
+    for q in range(dests):
+        for e in range(pairs):
+            start = 0
+            while start < per_device:
+                src = q * per_device + start
+                dst = e * per_device + start
+                length = min(LANES - src % LANES, LANES - dst % LANES, per_device - start)
+                out.setdefault((q, dst // LANES), []).append(
+                    (dst % LANES, e, src // LANES, (dst - src) % LANES)
+                )
+                start += length
+    return out
+
+
+def ladder_kernel(parts, occ_ref, win0_ref, win1_ref, *refs):
+    halves = refs[: len(parts)]
+    u_ref, lad_ref, out_ref, send_ref, w2_ref, ls_ref, pay_ref, max_ref = refs[len(parts) :]
+    step = pl.program_id(0)
+    occupied = occ_ref.shape[0]
+    pairs, _, virtuals = out_ref.shape
+    per_device = u_ref.shape[0]
+    dests = send_ref.shape[0]
+    tiles = virtuals // LANES
+    labels, copies = labels_and_copies(occ_ref, occupied)
+
+    @pl.when(step == 0)
+    def _():
+        for i in range(occupied):
+            for j in range(occupied):
+                row = (labels[i] ^ labels[j]) * pairs + 2 * i + copies[j]
+                w = win0_ref[j, i : i + 1, :].astype(jnp.float32)
+                w2_ref[pl.ds(row, 1), :] = w + win1_ref[j, i : i + 1, :].astype(jnp.float32)
+        max_ref[...] = jnp.zeros_like(max_ref)
+
+    w2 = w2_ref[...].astype(jnp.bfloat16)
+    u8 = u_ref[pl.ds(pl.multiple_of(step * 8, 8), 8), :]
+    for a in range(8):
+        ladder = contract_last(w2, lad_ref[a])
+        ua = u8[a : a + 1, :]
+        sel = ladder[0:pairs]
+        for v in range(1, 4):
+            sel = jnp.where(ua == v, ladder[v * pairs : (v + 1) * pairs], sel)
+        ls_ref[:, a, :] = sel
+    sources = [(part, n) for part, count in zip(halves, parts) for n in range(2 * count)]
+    pieces_of = payload_pieces(per_device, pairs, dests)
+    lane = lax.broadcasted_iota(jnp.int32, (8, LANES), 1)
+    top = max_ref[...]
+    found = {}
+    for t in range(tiles):
+        last_e = min(((t + 1) * LANES - 1) // per_device, pairs - 1)
+        for e in range(t * LANES // per_device, last_e + 1):
+            if (e, 0) in found:
+                continue
+            part, n = sources[e]
+            for v in range(tiles):
+                at = slice(v * LANES, (v + 1) * LANES)
+                x = part[n, :, at] + ls_ref[e, :, at]
+                out_ref[e, :, at] = x
+                top = jnp.maximum(top, jnp.abs(x))
+                found[e, v] = x
+        for q in range(dests):
+            acc = None
+            for first, e, v, shift in pieces_of[q, t]:
+                x = pltpu.roll(found[e, v], shift, axis=1) if shift else found[e, v]
+                acc = x if acc is None else jnp.where(lane >= first, x, acc)
+            at = pl.ds(pl.multiple_of(t * per_device + step * 8, 8), 8)
+            pay_ref[q, at, :] = acc
+    max_ref[...] = top
+
+    @pl.when(step == pl.num_programs(0) - 1)
+    def _():
+        most = jnp.max(jnp.max(max_ref[...], axis=0, keepdims=True), axis=1, keepdims=True)
+        k = jnp.floor(TOP_EXPONENT - jnp.log2(jnp.maximum(most, 1e-30)))
+        scale = jnp.exp2(k)
+        row = lax.broadcasted_iota(jnp.int32, pay_ref.shape[1:], 0)
+        for q in range(dests):
+            z = pay_ref[q] * scale
+            z2 = z * z
+            z4 = z2 * z2
+            y = jnp.where(row >= tiles * per_device, k, z4 * z4 * z)
+            send_ref[q] = y.astype(jnp.bfloat16)
+
+
+def cycle_kernel(pos_ref, occ_ref, own_ref, mate_ref, half_ref, u_ref, out_ref, orb_ref, cs_ref, xs_ref, ts_ref):
+    occupied = occ_ref.shape[0]
+    pairs, per_device, virtuals = half_ref.shape
+    quads, _, rows, _ = own_ref.shape
+    dests = 2 * quads
+    tiles = virtuals // LANES
+    labels, copies = labels_and_copies(occ_ref, occupied)
+    for j in range(occupied):
+        orb_ref[2 * labels[j] + copies[j]] = jnp.int32(j)
+    for r in range(dests):
+        ref = mate_ref if r & 1 else own_ref
+        n = ((r >> 1) & 1) * (dests // 4) + (r >> 2)
+        p = pos_ref[0] ^ r
+        x = ref[n, 0].astype(jnp.float32).reshape(per_device, occupied, LANES)
+        xs_ref[pl.ds(p * per_device, per_device)] = x
+        t = ref[n, 1].astype(jnp.float32)
+        at = pl.ds(pl.multiple_of(p * per_device, 8), per_device)
+        for j in range(occupied):
+            ts_ref[j, at, :] = t[j * per_device : (j + 1) * per_device]
+    here = pl.ds(pos_ref[0] * per_device, per_device)
+    x_left = jnp.concatenate([xs_ref[here, i, :] for i in range(occupied)], axis=0)
+    left = jnp.concatenate([own_ref[0, 1], x_left.astype(jnp.bfloat16)], axis=1)
+    for j in range(occupied):
+        right = jnp.concatenate([xs_ref[:, j, :], ts_ref[j]], axis=1).astype(jnp.bfloat16)
+        cs_ref[j] = contract_last(left, right).reshape(occupied, per_device, virtuals)
+    choices = [
+        [orb_ref[2 * (labels[e // 2] ^ n) + e % 2] for n in range(4)] for e in range(pairs)
+    ]
+
+    def group(g, carry):
+        rows = pl.ds(pl.multiple_of(g * 8, 8), 8)
+        for v in range(tiles):
+            at = slice(v * LANES, (v + 1) * LANES)
+            uv = u_ref[rows, at]
+            masks = [uv == n for n in range(1, 4)]
+            for e in range(pairs):
+                x = cs_ref[choices[e][0], e // 2, rows, at]
+                for n in range(1, 4):
+                    x = jnp.where(masks[n - 1], cs_ref[choices[e][n], e // 2, rows, at], x)
+                out_ref[e, rows, at] = half_ref[e, rows, at] + x
+        return carry
+
+    lax.fori_loop(0, per_device // 8, group, 0)
+
+
+def join_kernel(occ_ref, u_ref, half_ref, recv_ref, out_ref, dec_ref, mir_ref, res_ref, sems):
+    occupied = occ_ref.shape[0]
+    per_device, virtuals = u_ref.shape
+    labels, copies = labels_and_copies(occ_ref, occupied)
+    spread = 2 * per_device
+    ready = set()
+
+    def decode(t):
+        ready.add(t)
+        start = t * per_device
+        low, high = start // 16 * 16, (start + per_device + 15) // 16 * 16
+        end = virtuals // LANES * per_device
+        for p in range(recv_ref.shape[0]):
+            tail = recv_ref[p, end // 16 * 16 : end // 16 * 16 + 16, :]
+            k = tail.astype(jnp.float32)[end % 16 : end % 16 + 1, 0:1]
+            y = recv_ref[p, low:high, :].astype(jnp.float32)
+            y = y[start - low : start - low + per_device]
+            size = jnp.log2(jnp.maximum(jnp.abs(y), 2.0**-126)) * (1.0 / POWER) - k
+            size = jnp.exp2(size)
+            x = jnp.where(y < 0, -size, jnp.where(y > 0, size, 0.0))
+            dec_ref[p * per_device : (p + 1) * per_device, :] = x
+        mir_ref[t * LANES : (t + 1) * LANES, :] = dec_ref[...].T
+
+    stores = []
+    for j in range(occupied):
+        for t in range(j * spread // LANES, ((j + 1) * spread - 1) // LANES + 1):
+            if t not in ready:
+                decode(t)
+        u = u_ref[...]
+        for i in range(occupied):
+            at = pl.ds(pl.multiple_of((2 * j + copies[i]) * per_device, 8), per_device)
+            total = half_ref[2 * i + copies[j]] + mir_ref[at, :]
+            n = j * occupied + i
+            res_ref[n] = jnp.where(u == (labels[j] ^ labels[i]), total, 0.0)
+            store = pltpu.make_async_copy(res_ref.at[n], out_ref.at[i, j], sems.at[n])
+            store.start()
+            stores.append(store)
+    for store in stores:
+        store.wait()
+
+
+def permute(x, flip, size):
+    return lax.ppermute(x, "vir", [(n, n ^ flip) for n in range(size)])
+
+
+def body(dests, amps, fock_vir, fock_occ, ladder_ints, cycle_ints, occ_irrep, vir_irrep):
+    occupied, _, per_device, virtuals = amps.shape
+    pairs = 2 * occupied
+    tiles = virtuals // LANES
+    rows = occupied * per_device
+    kw = ladder_ints.shape[2]
+    f32, bf16 = jnp.float32, jnp.bfloat16
+    position = lax.axis_index("vir").astype(jnp.int32)
+    pos = position.reshape(1)
+    vir_local = lax.dynamic_slice_in_dim(vir_irrep, position * per_device, per_device)
+    u = jnp.bitwise_xor(vir_local[:, None], vir_irrep[None, :])
+    smem = pl.BlockSpec(memory_space=pltpu.SMEM)
+
+    def whole(shape):
+        return pl.BlockSpec(shape, lambda n: (0,) * len(shape))
+
+    def cost(flops, size):
+        return pl.CostEstimate(flops=flops, bytes_accessed=size, transcendentals=0)
+
+    anywhere = pl.BlockSpec(memory_space=pl.ANY)
+    quarter = dests // 4
+    win, xt = pl.pallas_call(
+        prep_kernel,
+        grid=(1,),
+        out_shape=(
+            jax.ShapeDtypeStruct((16, LANES), bf16),
+            jax.ShapeDtypeStruct((1, 2, rows, LANES), bf16),
+        ),
+        in_specs=[
+            whole((rows, LANES)),
+            pl.BlockSpec((occupied, occupied, per_device, LANES), lambda n: (0, 0, 0, 0)),
+        ],
+        out_specs=(whole((16, LANES)), whole((1, 2, rows, LANES))),
+        scratch_shapes=[pltpu.VMEM((rows, LANES), f32)],
+        compiler_params=params(60),
+        cost_estimate=cost(0, 500000),
+    )(cycle_ints.reshape(rows, LANES), amps)
+    vmem = pl.BlockSpec(memory_space=pltpu.VMEM)
+    mix = pl.pallas_call(
+        mix_kernel,
+        out_shape=jax.ShapeDtypeStruct((rows, rows), bf16),
+        in_specs=[vmem, anywhere],
+        out_specs=vmem,
+        compiler_params=params(4),
+        cost_estimate=cost(10**7, 300000),
+    )(fock_occ, win)
+
+    flat_amps = amps.reshape(occupied, rows, virtuals)
+    parts = (2, 2, 4)
+    wide = 2
+
+    def fock_part(n, after):
+        first, count = sum(parts[:n]), parts[n]
+        return pl.pallas_call(
+            functools.partial(fock_kernel, first),
+            grid=(count // wide,),
+            out_shape=jax.ShapeDtypeStruct((2 * count, per_device, virtuals), f32),
+            in_specs=[
+                smem,
+                pl.BlockSpec((wide, rows, virtuals), lambda i: (i + first // wide, 0, 0)),
+                whole(fock_vir.shape),
+                whole(mix.shape),
+                whole(u.shape),
+                anywhere,
+            ],
+            out_specs=pl.BlockSpec((2 * wide, per_device, virtuals), lambda i: (i, 0, 0)),
+            scratch_shapes=[pltpu.VMEM((occupied, per_device, virtuals), f32)],
+            compiler_params=params(12),
+            cost_estimate=cost(3 * count * rows * virtuals * virtuals, 2 * 10**6),
+        )(occ_irrep, flat_amps, fock_vir, mix, u, after)
+
+    flips = [m << 2 for m in range(1, quarter)]
+    win_shape = (occupied, occupied, LANES)
+    wins = [win] + [permute(win, flip, dests) for flip in flips]
+    blocks = [xt] + [permute(xt, flip, dests) for flip in flips]
+    half0 = fock_part(0, mix)
+    win = pl.pallas_call(
+        unpack_kernel,
+        out_shape=jax.ShapeDtypeStruct(win_shape, f32),
+        in_specs=[smem] + [vmem] * quarter + [anywhere],
+        out_specs=vmem,
+        compiler_params=params(4),
+        cost_estimate=cost(0, 10**5),
+    )(pos, *wins, half0)
+
+    def add(a, b, after):
+        return pl.pallas_call(
+            add_kernel,
+            out_shape=jax.ShapeDtypeStruct(a.shape, a.dtype),
+            in_specs=[vmem, vmem, anywhere],
+            out_specs=vmem,
+            compiler_params=params(4),
+            cost_estimate=cost(0, 10**5),
+        )(a, b, after)
+
+    win_y = permute(win, 2, dests)
+    half1 = fock_part(1, win)
+    win = add(win, win_y, half1)
+    win_mate = permute(win, 1, dests)
+    half2 = fock_part(2, win)
+
+    send_rows = tiles * per_device + 8
+    half, send = pl.pallas_call(
+        functools.partial(ladder_kernel, parts),
+        grid=(per_device // 8,),
+        out_shape=(
+            jax.ShapeDtypeStruct((pairs, per_device, virtuals), f32),
+            jax.ShapeDtypeStruct((dests, send_rows, LANES), bf16),
+        ),
+        in_specs=[smem, whole(win_shape), whole(win_shape)]
+        + [pl.BlockSpec((2 * count, 8, virtuals), lambda n: (0, n, 0)) for count in parts]
+        + [whole(u.shape), pl.BlockSpec((8, virtuals, kw), lambda n: (n, 0, 0))],
+        out_specs=(
+            pl.BlockSpec((pairs, 8, virtuals), lambda n: (0, n, 0)),
+            whole((dests, send_rows, LANES)),
+        ),
+        scratch_shapes=[
+            pltpu.VMEM((occupied * occupied, LANES), f32),
+            pltpu.VMEM((pairs, 8, virtuals), f32),
+            pltpu.VMEM((dests, send_rows, LANES), f32),
+            pltpu.VMEM((8, LANES), f32),
+        ],
+        compiler_params=params(16),
+        cost_estimate=cost(4 * occupied * rows * virtuals * LANES, 9 * 10**6),
+    )(occ_irrep, win, win_mate, half0, half1, half2, u, ladder_ints)
+
+    near = stack(blocks, half)
+    near_y = permute(near, 2, dests)
+    recv = lax.all_to_all(send, "vir", split_axis=0, concat_axis=0, tiled=True)
+    own_blocks = stack([near, near_y], send)
+    mate_blocks = permute(own_blocks, 1, dests)
+    half = pl.pallas_call(
+        cycle_kernel,
+        out_shape=jax.ShapeDtypeStruct((pairs, per_device, virtuals), f32),
+        in_specs=[smem, smem] + [vmem] * 4,
+        out_specs=vmem,
+        scratch_shapes=[
+            pltpu.SMEM((occupied,), jnp.int32),
+            pltpu.VMEM((occupied, occupied, per_device, virtuals), f32),
+            pltpu.VMEM((virtuals, occupied, LANES), f32),
+            pltpu.VMEM((occupied, virtuals, LANES), f32),
+        ],
+        compiler_params=params(28),
+        cost_estimate=cost(1000, 1000),
+    )(pos, occ_irrep, own_blocks, mate_blocks, half, u)
+
+    return pl.pallas_call(
+        join_kernel,
+        out_shape=jax.ShapeDtypeStruct((occupied, occupied, per_device, virtuals), f32),
+        in_specs=[smem, vmem, vmem, vmem],
+        out_specs=anywhere,
+        scratch_shapes=[
+            pltpu.VMEM((virtuals, LANES), f32),
+            pltpu.VMEM((tiles * LANES, virtuals), f32),
+            pltpu.VMEM((occupied * occupied, per_device, virtuals), f32),
+            pltpu.SemaphoreType.DMA((occupied * occupied,)),
+        ],
+        compiler_params=params(16),
+        cost_estimate=cost(10**6, 5 * 10**6),
+    )(occ_irrep, u, half, recv)
+
+
 def solution(mesh):
+    dests = mesh.shape["vir"]
+
+    def run(amps, *rest):
+        occupied, _, per_device, virtuals = amps.shape
+        tiled = (
+            dests == 16
+            and per_device % 8 == 0
+            and virtuals % LANES == 0
+            and 2 * occupied * per_device == virtuals
+            and rest[2].shape[2] == LANES
+            and rest[3].shape[2] == LANES
+        )
+        return body(dests, amps, *rest) if tiled else plain_body(amps, *rest)
+
     return jax.shard_map(
-        body,
+        run,
         mesh=mesh,
         in_specs=(
             P("groups", None, "vir", None),

time: 410 us -> 71.1 us (0.17)
  the two profiles are of different devices: /device:TPU:13 before, /device:TPU:1 now
where the time goes in v7:
time: 71.1 us; the launch traced here: 70.3 us
  Pallas kernels  28.7 us (40%)
  starting transfers between devices  20.1 us (28%)
  waiting for transfers between devices  17.3 us (24%)
  local copies, waits for them, and re-layouts  3.29 us (5%)
  other arithmetic  0.76 us (1%)
    ppermute x10, waiting for transfers between devices, permute(): return lax.ppermute(x, 'vir', [(n, n ^ flip) for n in range(size)])  17.3 us
    ppermute x10, starting transfers between devices, permute(): return lax.ppermute(x, 'vir', [(n, n ^ flip) for n in range(size)])  14.9 us
    pallas_call x1, Pallas kernels, body(): pl.pallas_call(functools.partial(ladder_kernel, parts), grid=(per_device...  7.82 us
    pallas_call x3, Pallas kernels, fock_part(): pl.pallas_call(functools.partial(fock_kernel, first), grid=(count // wide...  7.78 us
    all_to_all x1, starting transfers between devices, body(): recv = lax.all_to_all(send, 'vir', split_axis=0, concat_axis=0, tiled=True)  5.2 us
    pallas_call x1, Pallas kernels, body(): pl.pallas_call(join_kernel, out_shape=jax.ShapeDtypeStruct((occupied, occ...  5 us
    pallas_call x1, Pallas kernels, body(): pl.pallas_call(cycle_kernel, out_shape=jax.ShapeDtypeStruct((pairs, per_d...  3.63 us
    unnamed x18, local copies, waits for them, and re-layouts  2.53 us
  transfers between devices with their start and end apart: 11, of which 2 were waited for; matrix products, arithmetic and copies ran while one was open for 2% of the time, Pallas kernels for 29%

profile of v7, /device:TPU:1, one launch (start us, length us, event | category | flops | bytes accessed | tf_op | source)
XLA Modules:
  0.0 70.3 jit_solution(10591571312232121914)
XLA Ops:
  0.0 2.2 %shard_map.73 = (bf16[16,128]{1,0:T(8,128)(2,1)}, bf16[1,2,320,128]{3,2,1,0:T(8,128)(2,1)}) custom-call(bf16[320,128]{1,0:T(8,128)(2,1)} %bitcast.8, bf16[8,8,40,640]{3,2,1,0:T(8,128)(2,1)} %amps_ref.1), custom_call_target="tpu_custom_call" | custom-call | bytes 500000 | tf_op jit(solution)/shard_map/pallas_call | solution.py:374
  2.2 4.2 %collective-permute-start.5 = (bf16[16,128]{1,0:T(8,128)(2,1)}, bf16[16,128]{1,0:T(8,128)(2,1)S(1)}, u32[]{:S(2)}, u32[]{:S(2)}) collective-permute-start(bf16[16,128]{1,0:T(8,128)(2,1)} %get-tuple-element.10.after_ref.refs_0_), channel_id=1, source_target_pairs={{0,12},{1,13},{2,14},{3,15},{4,8},{5,9},{6,10},{7,11},{8,4},{9,5},... | collective-permute-start | bytes 12296 | tf_op jit(solution)/shard_map/ppermute | solution.py:350
  6.3 0.0 collective-permute-start.4
  6.3 0.3 collective-permute-start.3
  6.6 3.3 %collective-permute-start.2 = (bf16[1,2,320,128]{3,2,1,0:T(8,128)(2,1)}, bf16[1,2,320,128]{3,2,1,0:T(8,128)(2,1)S(1)}, u32[]{:S(2)}, u32[]{:S(2)}) collective-permute-start(bf16[1,2,320,128]{3,2,1,0:T(8,128)(2,1)} %get-tuple-element.9.refs_0_), channel_id=1, source_target_pairs={{0,12},{1,13},{2,14},{3,15},{4,8},{5,9},{6,10},{7,11},{8,4},{9,5},... | collective-permute-start | bytes 491528 | tf_op jit(solution)/shard_map/ppermute | solution.py:350
  9.9 0.0 collective-permute-start.1
  9.9 0.8 %dynamic_slice.3 = s32[40]{0:T(128)S(1)} dynamic-slice(s32[640]{0:T(1024)} %param.13, s32[]{:T(128)S(6)} %select_n.3), dynamic_slice_sizes={40} | dynamic-slice | bytes 324 | tf_op jit(solution)/shard_map/dynamic_slice | solution.py:362
  10.7 0.8 %broadcast_xor_fusion.u_ref.refs_3_ = s32[40,640]{1,0:T(8,128)S(1)} fusion(s32[640]{0:T(1024)} %param.13, s32[40]{0:T(128)S(1)} %dynamic_slice.3), kind=kLoop, calls=%fused_computation | loop fusion | flops 25600 | bytes 105120 | tf_op jit(solution)/shard_map/xor | solution.py:363
  11.4 0.7 copy-done.3
  12.1 0.7 copy-done.6
  12.8 0.4 shard_map.74.mix_ref.after_ref
  13.2 0.0 copy-start.1
  13.2 1.1 %copy-done.1 = bf16[640,640]{1,0:T(8,128)(2,1)S(1)} copy-done((bf16[640,640]{1,0:T(8,128)(2,1)S(1)}, bf16[640,640]{1,0:T(8,128)(2,1)}, u32[]{:S(2)}) %copy-start.1) | copy-done | bytes 819224
  14.4 2.0 %shard_map.75.refs_4_.refs_0_ = f32[4,40,640]{2,1,0:T(8,128)S(1)} custom-call(s32[8]{0:T(128)S(1)} %copy-done.5, bf16[8,320,640]{2,1,0:T(8,128)(2,1)S(1)} %bitcast.3, bf16[640,640]{1,0:T(8,128)(2,1)S(1)} %copy-done.1, bf16[320,320]{1,0:T(8,128)(2,1)S(1)} %shard_map.74.mix_ref.after_ref, s32[40,640]{1,0:T(8,128)S(1)} %broadcast_xor_fusion.u_ref.refs_3_, ...), custom_call_target="tpu_custom_call" | custom-call | flops 786432000 | bytes 2000000 | tf_op jit(solution)/shard_map/pallas_call | solution.py:406
  16.4 0.0 collective-permute-done.5.refs_3_
  16.4 0.3 collective-permute-start
  16.8 0.8 %shard_map.76.after_ref.a_ref = f32[8,8,128]{2,1,0:T(8,128)S(1)} custom-call(s32[1]{0:T(128)} %bitcast.pos_ref, bf16[16,128]{1,0:T(8,128)(2,1)S(1)} %copy-done.4, bf16[16,128]{1,0:T(8,128)(2,1)} %collective-permute-done.3.refs_1_, bf16[16,128]{1,0:T(8,128)(2,1)S(1)} %collective-permute-done.4.refs_2_, bf16[16,128]{1,0:T(8,128)(2,1)S(1)} %collective-permute-done.5.refs_3_, ...), custom_call_target="tpu_custom_call" | custom-call | bytes 100000 | tf_op jit(solution)/shard_map/pallas_call | solution.py:429
  17.6 0.0 slice-start.1
  17.6 1.3 %collective-permute-start.6 = (f32[8,8,128]{2,1,0:T(8,128)S(1)}, f32[8,8,128]{2,1,0:T(8,128)S(1)}, u32[]{:S(2)}, u32[]{:S(2)}) collective-permute-start(f32[8,8,128]{2,1,0:T(8,128)S(1)} %shard_map.76.after_ref.a_ref), channel_id=1, source_target_pairs={{0,2},{1,3},{2,0},{3,1},{4,6},{5,7},{6,4},{7,5},{8,10},{9,11},{10,... | collective-permute-start | bytes 98312 | tf_op jit(solution)/shard_map/ppermute | solution.py:350
  18.9 2.0 %shard_map.77.after_ref.refs_1_ = f32[4,40,640]{2,1,0:T(8,128)S(1)} custom-call(s32[8]{0:T(128)S(1)} %copy-done.5, bf16[8,320,640]{2,1,0:T(8,128)(2,1)S(1)} %bitcast.4, bf16[640,640]{1,0:T(8,128)(2,1)S(1)} %copy-done.1, bf16[320,320]{1,0:T(8,128)(2,1)S(1)} %shard_map.74.mix_ref.after_ref, s32[40,640]{1,0:T(8,128)S(1)} %broadcast_xor_fusion.u_ref.refs_3_, ...), custom_call_target="tpu_custom_call" | custom-call | flops 786432000 | bytes 2000000 | tf_op jit(solution)/shard_map/pallas_call | solution.py:406
  21.0 2.9 %collective-permute-start.7 = (f32[8,8,128]{2,1,0:T(8,128)S(1)}, f32[8,8,128]{2,1,0:T(8,128)S(1)}, u32[]{:S(2)}, u32[]{:S(2)}) collective-permute-start(f32[8,8,128]{2,1,0:T(8,128)S(1)} %shard_map.78.after_ref.win0_ref), channel_id=1, source_target_pairs={{0,1},{1,0},{2,3},{3,2},{4,5},{5,4},{6,7},{7,6},{8,9},{9,8},{10,11... | collective-permute-start | bytes 98312 | tf_op jit(solution)/shard_map/ppermute | solution.py:350
  23.8 3.7 %shard_map.79.refs_2_ = f32[8,40,640]{2,1,0:T(8,128)S(1)} custom-call(s32[8]{0:T(128)S(1)} %copy-done.5, bf16[8,320,640]{2,1,0:T(8,128)(2,1)S(1)} %bitcast.5, bf16[640,640]{1,0:T(8,128)(2,1)S(1)} %copy-done.1, bf16[320,320]{1,0:T(8,128)(2,1)S(1)} %shard_map.74.mix_ref.after_ref, s32[40,640]{1,0:T(8,128)S(1)} %broadcast_xor_fusion.u_ref.refs_3_, ...), custom_call_target="tpu_custom_call" | custom-call | flops 1572864000 | bytes 2000000 | tf_op jit(solution)/shard_map/pallas_call | solution.py:406
  27.6 7.8 %shard_map.80 = (f32[16,40,640]{2,1,0:T(8,128)S(1)}, bf16[16,208,128]{2,1,0:T(8,128)(2,1)}) custom-call(s32[8]{0:T(128)S(1)} %copy-done.5, f32[8,8,128]{2,1,0:T(8,128)S(1)} %shard_map.78.after_ref.win0_ref, f32[8,8,128]{2,1,0:T(8,128)S(1)} %collective-permute-done.7.win1_ref, f32[4,40,640]{2,1,0:T(8,128)S(1)} %shard_map.75.refs_4_.refs_0_, ...), custom_call_target="tpu_custom_call" | custom-call | flops 838860800 | bytes 9000000 | tf_op jit(solution)/shard_map/pallas_call | solution.py:455
  35.4 1.0 %shard_map.81.refs_0_ = bf16[4,2,320,128]{3,2,1,0:T(8,128)(2,1)S(1)} custom-call(bf16[1,2,320,128]{3,2,1,0:T(8,128)(2,1)S(1)} %copy-done.2, bf16[1,2,320,128]{3,2,1,0:T(8,128)(2,1)S(1)} %collective-permute-done.refs_1_, bf16[1,2,320,128]{3,2,1,0:T(8,128)(2,1)} %collective-permute-done.1.refs_2_, bf16[1,2,320,128]{3,2,1,0:T(8,128)(2,1)S(1)} %collective-permute-done.2.refs_3_, ...), custom_call_target="tpu_custom_call" | custom-call | bytes 1000000 | tf_op jit(solution)/shard_map/pallas_call | solution.py:150
  36.4 1.4 %collective-permute-start.8 = (bf16[4,2,320,128]{3,2,1,0:T(8,128)(2,1)S(1)}, bf16[4,2,320,128]{3,2,1,0:T(8,128)(2,1)S(1)}, u32[]{:S(2)}, u32[]{:S(2)}) collective-permute-start(bf16[4,2,320,128]{3,2,1,0:T(8,128)(2,1)S(1)} %shard_map.81.refs_0_), channel_id=1, source_target_pairs={{0,2},{1,3},{2,0},{3,1},{4,6},{5,7},{6,4},{7,5},{8,10},{9,11},{10,... | collective-permute-start | bytes 1966088 | tf_op jit(solution)/shard_map/ppermute | solution.py:350
  37.8 5.2 %all-to-all-start = ((bf16[16,208,128]{2,1,0:T(8,128)(2,1)}), bf16[16,208,128]{2,1,0:T(8,128)(2,1)}, u32[]{:S(2)}, u32[]{:S(2)}) async-start(bf16[16,208,128]{2,1,0:T(8,128)(2,1)} %get-tuple-element.12.refs_2_), calls=%async_computation | async-start | bytes 1703936 | tf_op jit(solution)/shard_map/all_to_all | solution.py:481
  43.0 14.6 %collective-permute-done.8.refs_1_ = bf16[4,2,320,128]{3,2,1,0:T(8,128)(2,1)S(1)} collective-permute-done((bf16[4,2,320,128]{3,2,1,0:T(8,128)(2,1)S(1)}, bf16[4,2,320,128]{3,2,1,0:T(8,128)(2,1)S(1)}, u32[]{:S(2)}, u32[]{:S(2)}) %collective-permute-start.8) | collective-permute-done | bytes 655392 | tf_op jit(solution)/shard_map/ppermute | solution.py:350
  57.6 0.1 shard_map.82.own_ref
  57.7 1.3 %collective-permute-start.9 = (bf16[8,2,320,128]{3,2,1,0:T(8,128)(2,1)S(1)}, bf16[8,2,320,128]{3,2,1,0:T(8,128)(2,1)S(1)}, u32[]{:S(2)}, u32[]{:S(2)}) collective-permute-start(bf16[8,2,320,128]{3,2,1,0:T(8,128)(2,1)S(1)} %shard_map.82.own_ref), channel_id=1, source_target_pairs={{0,1},{1,0},{2,3},{3,2},{4,5},{5,4},{6,7},{7,6},{8,9},{9,8},{10,11... | collective-permute-start | bytes 3932168 | tf_op jit(solution)/shard_map/ppermute | solution.py:350
  59.0 2.7 %collective-permute-done.9.mate_ref = bf16[8,2,320,128]{3,2,1,0:T(8,128)(2,1)S(1)} collective-permute-done((bf16[8,2,320,128]{3,2,1,0:T(8,128)(2,1)S(1)}, bf16[8,2,320,128]{3,2,1,0:T(8,128)(2,1)S(1)}, u32[]{:S(2)}, u32[]{:S(2)}) %collective-permute-start.9) | collective-permute-done | bytes 1310752 | tf_op jit(solution)/shard_map/ppermute | solution.py:350
  61.6 3.6 %shard_map.83.half_ref = f32[16,40,640]{2,1,0:T(8,128)S(1)} custom-call(s32[1]{0:T(128)} %bitcast.pos_ref, s32[8]{0:T(128)S(1)} %copy-done.5, bf16[8,2,320,128]{3,2,1,0:T(8,128)(2,1)S(1)} %shard_map.82.own_ref, bf16[8,2,320,128]{3,2,1,0:T(8,128)(2,1)S(1)} %collective-permute-done.9.mate_ref, f32[16,40,640]{2,1,0:T(8,128)S(1)} %get-tuple-element.11.refs_4_.half_ref, ...), custom_call_target="tpu_custom_call" | custom-call | flops 1000 | bytes 1000 | tf_op jit(solution)/shard_map/pallas_call | solution.py:484
  65.3 5.0 %shard_map.84 = f32[8,8,40,640]{3,2,1,0:T(8,128)} custom-call(s32[8]{0:T(128)S(1)} %copy-done.5, s32[40,640]{1,0:T(8,128)S(1)} %broadcast_xor_fusion.u_ref.refs_3_, f32[16,40,640]{2,1,0:T(8,128)S(1)} %shard_map.83.half_ref, bf16[16,208,128]{2,1,0:T(8,128)(2,1)} %all-to-all-done.recv_ref), custom_call_target="tpu_custom_call" | custom-call | flops 1000000 | bytes 5000000 | tf_op jit(solution)/shard_map/pallas_call | solution.py:499
  (23 shorter events, 0.1 us)
Async XLA Ops:
  0.0 13.2 %copy-start = (bf16[8,8,40,640]{3,2,1,0:T(8,128)(2,1)S(1)}, bf16[8,8,40,640]{3,2,1,0:T(8,128)(2,1)}, u32[]{:S(2)}) copy-start(bf16[8,8,40,640]{3,2,1,0:T(8,128)(2,1)} %amps_ref.1) | copy-start | bytes 9830404
  0.0 13.2 %copy-start.5 = (s32[8]{0:T(128)S(1)}, s32[8]{0:T(128)}, u32[]{:S(2)}) copy-start(s32[8]{0:T(128)} %occ_ref.11) | copy-start | bytes 100
  2.2 14.2 %collective-permute-start.5 = (bf16[16,128]{1,0:T(8,128)(2,1)}, bf16[16,128]{1,0:T(8,128)(2,1)S(1)}, u32[]{:S(2)}, u32[]{:S(2)}) collective-permute-start(bf16[16,128]{1,0:T(8,128)(2,1)} %get-tuple-element.10.after_ref.refs_0_), channel_id=1, source_target_pairs={{0,12},{1,13},{2,14},{3,15},{4,8},{5,9},{6,10},{7,11},{8,4},{9,5},... | collective-permute-start | bytes 12296 | tf_op jit(solution)/shard_map/ppermute | solution.py:350
  6.3 10.4 %collective-permute-start.4 = (bf16[16,128]{1,0:T(8,128)(2,1)}, bf16[16,128]{1,0:T(8,128)(2,1)S(1)}, u32[]{:S(2)}, u32[]{:S(2)}) collective-permute-start(bf16[16,128]{1,0:T(8,128)(2,1)} %get-tuple-element.10.after_ref.refs_0_), channel_id=1, source_target_pairs={{0,8},{1,9},{2,10},{3,11},{4,12},{5,13},{6,14},{7,15},{8,0},{9,1},... | collective-permute-start | bytes 12296 | tf_op jit(solution)/shard_map/ppermute | solution.py:350
  6.3 10.4 %collective-permute-start.3 = (bf16[16,128]{1,0:T(8,128)(2,1)}, bf16[16,128]{1,0:T(8,128)(2,1)}, u32[]{:S(2)}, u32[]{:S(2)}) collective-permute-start(bf16[16,128]{1,0:T(8,128)(2,1)} %get-tuple-element.10.after_ref.refs_0_), channel_id=1, source_target_pairs={{0,4},{1,5},{2,6},{3,7},{4,0},{5,1},{6,2},{7,3},{8,12},{9,13},{10,... | collective-permute-start | bytes 12296 | tf_op jit(solution)/shard_map/ppermute | solution.py:350
  6.6 28.8 %collective-permute-start.2 = (bf16[1,2,320,128]{3,2,1,0:T(8,128)(2,1)}, bf16[1,2,320,128]{3,2,1,0:T(8,128)(2,1)S(1)}, u32[]{:S(2)}, u32[]{:S(2)}) collective-permute-start(bf16[1,2,320,128]{3,2,1,0:T(8,128)(2,1)} %get-tuple-element.9.refs_0_), channel_id=1, source_target_pairs={{0,12},{1,13},{2,14},{3,15},{4,8},{5,9},{6,10},{7,11},{8,4},{9,5},... | collective-permute-start | bytes 491528 | tf_op jit(solution)/shard_map/ppermute | solution.py:350
  9.9 25.5 %collective-permute-start.1 = (bf16[1,2,320,128]{3,2,1,0:T(8,128)(2,1)}, bf16[1,2,320,128]{3,2,1,0:T(8,128)(2,1)}, u32[]{:S(2)}, u32[]{:S(2)}) collective-permute-start(bf16[1,2,320,128]{3,2,1,0:T(8,128)(2,1)} %get-tuple-element.9.refs_0_), channel_id=1, source_target_pairs={{0,8},{1,9},{2,10},{3,11},{4,12},{5,13},{6,14},{7,15},{8,0},{9,1},... | collective-permute-start | bytes 491528 | tf_op jit(solution)/shard_map/ppermute | solution.py:350
  11.4 0.7 copy-start.3
  12.1 0.7 copy-start.6
  13.2 1.1 %copy-start.1 = (bf16[640,640]{1,0:T(8,128)(2,1)S(1)}, bf16[640,640]{1,0:T(8,128)(2,1)}, u32[]{:S(2)}) copy-start(bf16[640,640]{1,0:T(8,128)(2,1)} %fock_ref.5) | copy-start | bytes 2457604
  14.4 2.0 %copy-start.2 = (bf16[1,2,320,128]{3,2,1,0:T(8,128)(2,1)S(1)}, bf16[1,2,320,128]{3,2,1,0:T(8,128)(2,1)}, u32[]{:S(2)}) copy-start(bf16[1,2,320,128]{3,2,1,0:T(8,128)(2,1)} %get-tuple-element.9.refs_0_) | copy-start | bytes 491524
  14.4 2.4 %copy-start.4 = (bf16[16,128]{1,0:T(8,128)(2,1)S(1)}, bf16[16,128]{1,0:T(8,128)(2,1)}, u32[]{:S(2)}) copy-start(bf16[16,128]{1,0:T(8,128)(2,1)} %get-tuple-element.10.after_ref.refs_0_) | copy-start | bytes 12292
  14.4 13.2 %slice-start = ((s8[6553600]{0:T(1024)(128)(4,1)}), s8[4194304]{0:T(1024)(128)(4,1)S(1)}, s32[]{:S(2)}) async-start(s8[6553600]{0:T(1024)(128)(4,1)} %bitcast.6), calls=%async_computation.1 | async-start | bytes 8388608
  16.4 19.0 %collective-permute-start = (bf16[1,2,320,128]{3,2,1,0:T(8,128)(2,1)S(1)}, bf16[1,2,320,128]{3,2,1,0:T(8,128)(2,1)S(1)}, u32[]{:S(2)}, u32[]{:S(2)}) collective-permute-start(bf16[1,2,320,128]{3,2,1,0:T(8,128)(2,1)S(1)} %copy-done.2), channel_id=1, source_target_pairs={{0,4},{1,5},{2,6},{3,7},{4,0},{5,1},{6,2},{7,3},{8,12},{9,13},{10,... | collective-permute-start | bytes 491528 | tf_op jit(solution)/shard_map/ppermute | solution.py:350
  17.6 10.0 %slice-start.1 = ((s8[6553600]{0:T(1024)(128)(4,1)}), s8[2359296]{0:T(1024)(128)(4,1)S(1)}, s32[]{:S(2)}) async-start(s8[6553600]{0:T(1024)(128)(4,1)} %bitcast.6), calls=%async_computation.2 | async-start | bytes 4718592
  17.6 3.3 %collective-permute-start.6 = (f32[8,8,128]{2,1,0:T(8,128)S(1)}, f32[8,8,128]{2,1,0:T(8,128)S(1)}, u32[]{:S(2)}, u32[]{:S(2)}) collective-permute-start(f32[8,8,128]{2,1,0:T(8,128)S(1)} %shard_map.76.after_ref.a_ref), channel_id=1, source_target_pairs={{0,2},{1,3},{2,0},{3,1},{4,6},{5,7},{6,4},{7,5},{8,10},{9,11},{10,... | collective-permute-start | bytes 98312 | tf_op jit(solution)/shard_map/ppermute | solution.py:350
  21.0 6.6 %collective-permute-start.7 = (f32[8,8,128]{2,1,0:T(8,128)S(1)}, f32[8,8,128]{2,1,0:T(8,128)S(1)}, u32[]{:S(2)}, u32[]{:S(2)}) collective-permute-start(f32[8,8,128]{2,1,0:T(8,128)S(1)} %shard_map.78.after_ref.win0_ref), channel_id=1, source_target_pairs={{0,1},{1,0},{2,3},{3,2},{4,5},{5,4},{6,7},{7,6},{8,9},{9,8},{10,11... | collective-permute-start | bytes 98312 | tf_op jit(solution)/shard_map/ppermute | solution.py:350
  36.4 21.2 %collective-permute-start.8 = (bf16[4,2,320,128]{3,2,1,0:T(8,128)(2,1)S(1)}, bf16[4,2,320,128]{3,2,1,0:T(8,128)(2,1)S(1)}, u32[]{:S(2)}, u32[]{:S(2)}) collective-permute-start(bf16[4,2,320,128]{3,2,1,0:T(8,128)(2,1)S(1)} %shard_map.81.refs_0_), channel_id=1, source_target_pairs={{0,2},{1,3},{2,0},{3,1},{4,6},{5,7},{6,4},{7,5},{8,10},{9,11},{10,... | collective-permute-start | bytes 1966088 | tf_op jit(solution)/shard_map/ppermute | solution.py:350
  37.8 27.5 %all-to-all-start = ((bf16[16,208,128]{2,1,0:T(8,128)(2,1)}), bf16[16,208,128]{2,1,0:T(8,128)(2,1)}, u32[]{:S(2)}, u32[]{:S(2)}) async-start(bf16[16,208,128]{2,1,0:T(8,128)(2,1)} %get-tuple-element.12.refs_2_), calls=%async_computation | async-start | bytes 1703936 | tf_op jit(solution)/shard_map/all_to_all | solution.py:481
  57.7 3.9 %collective-permute-start.9 = (bf16[8,2,320,128]{3,2,1,0:T(8,128)(2,1)S(1)}, bf16[8,2,320,128]{3,2,1,0:T(8,128)(2,1)S(1)}, u32[]{:S(2)}, u32[]{:S(2)}) collective-permute-start(bf16[8,2,320,128]{3,2,1,0:T(8,128)(2,1)S(1)} %shard_map.82.own_ref), channel_id=1, source_target_pairs={{0,1},{1,0},{2,3},{3,2},{4,5},{5,4},{6,7},{7,6},{8,9},{9,8},{10,11... | collective-permute-start | bytes 3932168 | tf_op jit(solution)/shard_map/ppermute | solution.py:350

commit v8 on v7

--- a/solution.py
+++ b/solution.py
@@ -95,7 +95,9 @@
     xt_ref[0, 1] = t_ref[...].astype(jnp.bfloat16)
 
 
-def mix_kernel(occ_vals_ref, after_ref, mix_ref):
+def setup_kernel(pos_ref, vir_ref, occ_vals_ref, row_ref, mix_ref, u_ref):
+    for a in range(u_ref.shape[0]):
+        u_ref[a : a + 1, :] = row_ref[...] ^ vir_ref[pos_ref[0] * u_ref.shape[0] + a]
     rows = mix_ref.shape[0]
     occupied = occ_vals_ref.shape[0]
     per_device = rows // occupied
@@ -193,7 +195,7 @@
 
 def ladder_kernel(parts, occ_ref, win0_ref, win1_ref, *refs):
     halves = refs[: len(parts)]
-    u_ref, lad_ref, out_ref, send_ref, w2_ref, ls_ref, pay_ref, max_ref = refs[len(parts) :]
+    u_ref, lad_ref, _, out_ref, send_ref, w2_ref, ls_ref, pay_ref, max_ref = refs[len(parts) :]
     step = pl.program_id(0)
     occupied = occ_ref.shape[0]
     pairs, _, virtuals = out_ref.shape
@@ -219,7 +221,8 @@
         sel = ladder[0:pairs]
         for v in range(1, 4):
             sel = jnp.where(ua == v, ladder[v * pairs : (v + 1) * pairs], sel)
-        ls_ref[:, a, :] = sel
+        for v in range(tiles):
+            ls_ref[v, pl.ds(a, pairs, stride=8), :] = sel[:, v * LANES : (v + 1) * LANES]
     sources = [(part, n) for part, count in zip(halves, parts) for n in range(2 * count)]
     pieces_of = payload_pieces(per_device, pairs, dests)
     lane = lax.broadcasted_iota(jnp.int32, (8, LANES), 1)
@@ -233,7 +236,7 @@
             part, n = sources[e]
             for v in range(tiles):
                 at = slice(v * LANES, (v + 1) * LANES)
-                x = part[n, :, at] + ls_ref[e, :, at]
+                x = part[n, :, at] + ls_ref[v, 8 * e : 8 * e + 8, :]
                 out_ref[e, :, at] = x
                 top = jnp.maximum(top, jnp.abs(x))
                 found[e, v] = x
@@ -359,8 +362,6 @@
     f32, bf16 = jnp.float32, jnp.bfloat16
     position = lax.axis_index("vir").astype(jnp.int32)
     pos = position.reshape(1)
-    vir_local = lax.dynamic_slice_in_dim(vir_irrep, position * per_device, per_device)
-    u = jnp.bitwise_xor(vir_local[:, None], vir_irrep[None, :])
     smem = pl.BlockSpec(memory_space=pltpu.SMEM)
 
     def whole(shape):
@@ -388,17 +389,20 @@
         cost_estimate=cost(0, 500000),
     )(cycle_ints.reshape(rows, LANES), amps)
     vmem = pl.BlockSpec(memory_space=pltpu.VMEM)
-    mix = pl.pallas_call(
-        mix_kernel,
-        out_shape=jax.ShapeDtypeStruct((rows, rows), bf16),
-        in_specs=[vmem, anywhere],
-        out_specs=vmem,
+    mix, u = pl.pallas_call(
+        setup_kernel,
+        out_shape=(
+            jax.ShapeDtypeStruct((rows, rows), bf16),
+            jax.ShapeDtypeStruct((per_device, virtuals), jnp.int32),
+        ),
+        in_specs=[smem, smem, vmem, vmem],
+        out_specs=(vmem, vmem),
         compiler_params=params(4),
         cost_estimate=cost(10**7, 300000),
-    )(fock_occ, win)
+    )(pos, vir_irrep, fock_occ, vir_irrep.reshape(1, virtuals))
 
     flat_amps = amps.reshape(occupied, rows, virtuals)
-    parts = (2, 2, 4)
+    parts = (4, 4)
     wide = 2
 
     def fock_part(n, after):
@@ -412,7 +416,7 @@
                 pl.BlockSpec((wide, rows, virtuals), lambda i: (i + first // wide, 0, 0)),
                 whole(fock_vir.shape),
                 whole(mix.shape),
-                whole(u.shape),
+                whole((per_device, virtuals)),
                 anywhere,
             ],
             out_specs=pl.BlockSpec((2 * wide, per_device, virtuals), lambda i: (i, 0, 0)),
@@ -449,7 +453,8 @@
     half1 = fock_part(1, win)
     win = add(win, win_y, half1)
     win_mate = permute(win, 1, dests)
-    half2 = fock_part(2, win)
+    near = stack(blocks, win)
+    near_y = permute(near, 2, dests)
 
     send_rows = tiles * per_device + 8
     half, send = pl.pallas_call(
@@ -461,23 +466,21 @@
         ),
         in_specs=[smem, whole(win_shape), whole(win_shape)]
         + [pl.BlockSpec((2 * count, 8, virtuals), lambda n: (0, n, 0)) for count in parts]
-        + [whole(u.shape), pl.BlockSpec((8, virtuals, kw), lambda n: (n, 0, 0))],
+        + [whole((per_device, virtuals)), pl.BlockSpec((8, virtuals, kw), lambda n: (n, 0, 0)), anywhere],
         out_specs=(
             pl.BlockSpec((pairs, 8, virtuals), lambda n: (0, n, 0)),
             whole((dests, send_rows, LANES)),
         ),
         scratch_shapes=[
             pltpu.VMEM((occupied * occupied, LANES), f32),
-            pltpu.VMEM((pairs, 8, virtuals), f32),
+            pltpu.VMEM((tiles, 8 * pairs, LANES), f32),
             pltpu.VMEM((dests, send_rows, LANES), f32),
             pltpu.VMEM((8, LANES), f32),
         ],
         compiler_params=params(16),
-        cost_estimate=cost(4 * occupied * rows * virtuals * LANES, 9 * 10**6),
-    )(occ_irrep, win, win_mate, half0, half1, half2, u, ladder_ints)
-
-    near = stack(blocks, half)
-    near_y = permute(near, 2, dests)
+        cost_estimate=cost(4 * occupied * rows * virtuals * LANES, 25 * 10**6),
+    )(occ_irrep, win, win_mate, half0, half1, u, ladder_ints, near)
+
     recv = lax.all_to_all(send, "vir", split_axis=0, concat_axis=0, tiled=True)
     own_blocks = stack([near, near_y], send)
     mate_blocks = permute(own_blocks, 1, dests)

time: 71.1 us -> 68.2 us (0.959)
  starting transfers between devices: 20.1 us -> 18.7 us
  other arithmetic: 0.76 us -> 0.01 us
    ppermute x10, waiting for transfers between devices: 17.3 us -> 4 us  [permute(): return lax.ppermute(x, 'vir', [(n, n ^ flip) for n in range(size)])]
    all_to_all x1, waiting for transfers between devices: 0.01 us -> 12.8 us  [body(): recv = lax.all_to_all(send, 'vir', split_axis=0, concat_axis=0, tiled=True)]
    ppermute x10, starting transfers between devices: 14.9 us -> 12.6 us  [permute(): return lax.ppermute(x, 'vir', [(n, n ^ flip) for n in range(size)])]
    unnamed x18 -> x26, local copies, waits for them, and re-layouts: 2.53 us -> 3.71 us
    all_to_all x1, starting transfers between devices: 5.2 us -> 6.15 us  [body(): recv = lax.all_to_all(send, 'vir', split_axis=0, concat_axis=0, tiled=True)]
    xor x1 -> x0, other arithmetic: 0.76 us -> none  [body(): u = jnp.bitwise_xor(vir_local[:, None], vir_irrep[None, :])]
    dynamic_slice x1 -> x0, local copies, waits for them, and re-layouts: 0.76 us -> none  [body(): lax.dynamic_slice_in_dim(vir_irrep, position * per_device, per_device)]
    pallas_call x3 -> x2, Pallas kernels: 7.78 us -> 7.44 us  [fock_part(): pl.pallas_call(functools.partial(fock_kernel, first), grid=(count // wide...]
  transfers between devices with their start and end apart: 11 -> 11, of which waited for: 2 -> 4; matrix products, arithmetic and copies ran while one was open for 2% -> 0% of each run, Pallas kernels for 29% -> 30%
where the time goes in v8:
time: 68.2 us; the launch traced here: 67.4 us
  Pallas kernels  28 us (41%)
  starting transfers between devices  18.7 us (27%)
  waiting for transfers between devices  16.8 us (25%)
  local copies, waits for them, and re-layouts  3.71 us (5%)
    all_to_all x1, waiting for transfers between devices, body(): recv = lax.all_to_all(send, 'vir', split_axis=0, concat_axis=0, tiled=True)  12.8 us
    ppermute x10, starting transfers between devices, permute(): return lax.ppermute(x, 'vir', [(n, n ^ flip) for n in range(size)])  12.6 us
    pallas_call x1, Pallas kernels, body(): pl.pallas_call(functools.partial(ladder_kernel, parts), grid=(per_device...  7.55 us
    pallas_call x2, Pallas kernels, fock_part(): pl.pallas_call(functools.partial(fock_kernel, first), grid=(count // wide...  7.44 us
    all_to_all x1, starting transfers between devices, body(): recv = lax.all_to_all(send, 'vir', split_axis=0, concat_axis=0, tiled=True)  6.15 us
    pallas_call x1, Pallas kernels, body(): pl.pallas_call(join_kernel, out_shape=jax.ShapeDtypeStruct((occupied, occ...  4.33 us
    ppermute x10, waiting for transfers between devices, permute(): return lax.ppermute(x, 'vir', [(n, n ^ flip) for n in range(size)])  4 us
    unnamed x26, local copies, waits for them, and re-layouts  3.71 us
  transfers between devices with their start and end apart: 11, of which 4 were waited for; matrix products, arithmetic and copies ran while one was open for 0% of the time, Pallas kernels for 30%

profile of v8, /device:TPU:1, one launch (start us, length us, event | category | flops | bytes accessed | tf_op | source)
XLA Modules:
  0.0 67.4 jit_solution(6213785077298127006)
XLA Ops:
  0.0 2.2 %shard_map.74 = (bf16[16,128]{1,0:T(8,128)(2,1)}, bf16[1,2,320,128]{3,2,1,0:T(8,128)(2,1)}) custom-call(bf16[320,128]{1,0:T(8,128)(2,1)} %bitcast.7, bf16[8,8,40,640]{3,2,1,0:T(8,128)(2,1)} %amps_ref.1), custom_call_target="tpu_custom_call" | custom-call | bytes 500000 | tf_op jit(solution)/shard_map/pallas_call | solution.py:375
  2.2 4.2 %collective-permute-start.5 = (bf16[16,128]{1,0:T(8,128)(2,1)}, bf16[16,128]{1,0:T(8,128)(2,1)S(1)}, u32[]{:S(2)}, u32[]{:S(2)}) collective-permute-start(bf16[16,128]{1,0:T(8,128)(2,1)} %get-tuple-element.13.refs_0_), channel_id=1, source_target_pairs={{0,12},{1,13},{2,14},{3,15},{4,8},{5,9},{6,10},{7,11},{8,4},{9,5},... | collective-permute-start | bytes 12296 | tf_op jit(solution)/shard_map/ppermute | solution.py:353
  6.4 0.3 collective-permute-start.3
  6.6 3.3 %collective-permute-start.2 = (bf16[1,2,320,128]{3,2,1,0:T(8,128)(2,1)}, bf16[1,2,320,128]{3,2,1,0:T(8,128)(2,1)S(1)}, u32[]{:S(2)}, u32[]{:S(2)}) collective-permute-start(bf16[1,2,320,128]{3,2,1,0:T(8,128)(2,1)} %get-tuple-element.12.refs_0_), channel_id=1, source_target_pairs={{0,12},{1,13},{2,14},{3,15},{4,8},{5,9},{6,10},{7,11},{8,4},{9,5},... | collective-permute-start | bytes 491528 | tf_op jit(solution)/shard_map/ppermute | solution.py:353
  9.9 0.0 copy-start.7
  9.9 0.7 %copy-done.7 = s32[640]{0:T(1024)S(1)} copy-done((s32[640]{0:T(1024)S(1)}, s32[640]{0:T(1024)}, u32[]{:S(2)}) %copy-start.7) | copy-done | bytes 2584
  10.6 0.7 %copy-done.10 = bf16[8,8]{1,0:T(8,128)(2,1)S(1)} copy-done((bf16[8,8]{1,0:T(8,128)(2,1)S(1)}, bf16[8,8]{1,0:T(8,128)(2,1)}, u32[]{:S(2)}) %copy-start.10) | copy-done | bytes 152
  11.3 1.0 %shard_map.73 = (bf16[320,320]{1,0:T(8,128)(2,1)S(1)}, s32[40,640]{1,0:T(8,128)S(1)}) custom-call(s32[1]{0:T(128)} %bitcast.pos_ref, s32[640]{0:T(1024)S(1)} %copy-done.7, bf16[8,8]{1,0:T(8,128)(2,1)S(1)} %copy-done.10, s32[1,640]{1,0:T(1,128)S(1)} %reshape.13.row_ref), custom_call_target="tpu_custom_call" | custom-call | flops 10000000 | bytes 300000 | tf_op jit(solution)/shard_map/pallas_call | solution.py:392
  12.3 0.3 collective-permute-start
  12.6 1.1 %copy-done.8 = bf16[640,640]{1,0:T(8,128)(2,1)S(1)} copy-done((bf16[640,640]{1,0:T(8,128)(2,1)S(1)}, bf16[640,640]{1,0:T(8,128)(2,1)}, u32[]{:S(2)}) %copy-start.8) | copy-done | bytes 819224
  13.8 3.7 %shard_map.75.refs_4_.refs_0_ = f32[8,40,640]{2,1,0:T(8,128)S(1)} custom-call(s32[8]{0:T(128)S(1)} %copy-done.4, bf16[8,320,640]{2,1,0:T(8,128)(2,1)S(1)} %bitcast.5, bf16[640,640]{1,0:T(8,128)(2,1)S(1)} %copy-done.8, bf16[320,320]{1,0:T(8,128)(2,1)S(1)} %get-tuple-element.14.mix_ref.after_ref, s32[40,640]{1,0:T(8,128)S(1)} %get-tuple-element.11.u_ref.refs_2_, ...), custom_call_target="tpu_custom_call" | custom-call | flops 1572864000 | bytes 2000000 | tf_op jit(solution)/shard_map/pallas_call | solution.py:410
  17.5 0.0 collective-permute-done.3.refs_1_
  17.5 0.8 %shard_map.76.after_ref.a_ref = f32[8,8,128]{2,1,0:T(8,128)S(1)} custom-call(s32[1]{0:T(128)} %bitcast.pos_ref, bf16[16,128]{1,0:T(8,128)(2,1)S(1)} %copy-done.5, bf16[16,128]{1,0:T(8,128)(2,1)} %collective-permute-done.3.refs_1_, bf16[16,128]{1,0:T(8,128)(2,1)S(1)} %collective-permute-done.4.refs_2_, bf16[16,128]{1,0:T(8,128)(2,1)S(1)} %collective-permute-done.5.refs_3_, ...), custom_call_target="tpu_custom_call" | custom-call | bytes 100000 | tf_op jit(solution)/shard_map/pallas_call | solution.py:433
  18.4 0.0 copy-start.3
  18.4 0.0 slice-start.1
  18.4 1.3 %collective-permute-start.6 = (f32[8,8,128]{2,1,0:T(8,128)S(1)}, f32[8,8,128]{2,1,0:T(8,128)S(1)}, u32[]{:S(2)}, u32[]{:S(2)}) collective-permute-start(f32[8,8,128]{2,1,0:T(8,128)S(1)} %shard_map.76.after_ref.a_ref), channel_id=1, source_target_pairs={{0,2},{1,3},{2,0},{3,1},{4,6},{5,7},{6,4},{7,5},{8,10},{9,11},{10,... | collective-permute-start | bytes 98312 | tf_op jit(solution)/shard_map/ppermute | solution.py:353
  19.7 3.7 %shard_map.77.after_ref.refs_1_ = f32[8,40,640]{2,1,0:T(8,128)S(1)} custom-call(s32[8]{0:T(128)S(1)} %copy-done.4, bf16[8,320,640]{2,1,0:T(8,128)(2,1)S(1)} %bitcast.6, bf16[640,640]{1,0:T(8,128)(2,1)S(1)} %copy-done.9, bf16[320,320]{1,0:T(8,128)(2,1)S(1)} %get-tuple-element.14.mix_ref.after_ref, s32[40,640]{1,0:T(8,128)S(1)} %get-tuple-element.11.u_ref.refs_2_, ...), custom_call_target="tpu_custom_call" | custom-call | flops 1572864000 | bytes 2000000 | tf_op jit(solution)/shard_map/pallas_call | solution.py:410
  23.4 0.0 collective-permute-done.6.b_ref
  23.4 0.2 collective-permute-done.1.refs_2_
  23.6 1.0 %shard_map.79.refs_4_.refs_0_ = bf16[4,2,320,128]{3,2,1,0:T(8,128)(2,1)S(1)} custom-call(bf16[1,2,320,128]{3,2,1,0:T(8,128)(2,1)S(1)} %copy-done.3, bf16[1,2,320,128]{3,2,1,0:T(8,128)(2,1)S(1)} %collective-permute-done.refs_1_, bf16[1,2,320,128]{3,2,1,0:T(8,128)(2,1)} %collective-permute-done.1.refs_2_, ...), custom_call_target="tpu_custom_call" | custom-call | bytes 1000000 | tf_op jit(solution)/shard_map/pallas_call | solution.py:152
  24.6 1.3 %collective-permute-start.7 = (bf16[4,2,320,128]{3,2,1,0:T(8,128)(2,1)S(1)}, bf16[4,2,320,128]{3,2,1,0:T(8,128)(2,1)S(1)}, u32[]{:S(2)}, u32[]{:S(2)}) collective-permute-start(bf16[4,2,320,128]{3,2,1,0:T(8,128)(2,1)S(1)} %shard_map.79.refs_4_.refs_0_), channel_id=1, source_target_pairs={{0,2},{1,3},{2,0},{3,1},{4,6},{5,7},{6,4},{7,5},{8,10},{9,11},{10,... | collective-permute-start | bytes 1966088 | tf_op jit(solution)/shard_map/ppermute | solution.py:353
  25.9 1.7 %collective-permute-start.8 = (f32[8,8,128]{2,1,0:T(8,128)S(1)}, f32[8,8,128]{2,1,0:T(8,128)S(1)}, u32[]{:S(2)}, u32[]{:S(2)}) collective-permute-start(f32[8,8,128]{2,1,0:T(8,128)S(1)} %shard_map.78.refs_4_.win0_ref), channel_id=1, source_target_pairs={{0,1},{1,0},{2,3},{3,2},{4,5},{5,4},{6,7},{7,6},{8,9},{9,8},{10,11... | collective-permute-start | bytes 98312 | tf_op jit(solution)/shard_map/ppermute | solution.py:353
  27.6 0.9 %collective-permute-done.8.win1_ref = f32[8,8,128]{2,1,0:T(8,128)S(1)} collective-permute-done((f32[8,8,128]{2,1,0:T(8,128)S(1)}, f32[8,8,128]{2,1,0:T(8,128)S(1)}, u32[]{:S(2)}, u32[]{:S(2)}) %collective-permute-start.8) | collective-permute-done | bytes 32800 | tf_op jit(solution)/shard_map/ppermute | solution.py:353
  28.5 7.6 %shard_map.80 = (f32[16,40,640]{2,1,0:T(8,128)S(1)}, bf16[16,208,128]{2,1,0:T(8,128)(2,1)}) custom-call(s32[8]{0:T(128)S(1)} %copy-done.4, f32[8,8,128]{2,1,0:T(8,128)S(1)} %shard_map.78.refs_4_.win0_ref, f32[8,8,128]{2,1,0:T(8,128)S(1)} %collective-permute-done.8.win1_ref, f32[8,40,640]{2,1,0:T(8,128)S(1)} %shard_map.75.refs_4_.refs_0_, ...), custom_call_target="tpu_custom_call" | custom-call | flops 838860800 | bytes 25000000 | tf_op jit(solution)/shard_map/pallas_call | solution.py:460
  36.1 1.2 %copy-done.1 = f32[16,40,640]{2,1,0:T(8,128)} copy-done((f32[16,40,640]{2,1,0:T(8,128)}, f32[16,40,640]{2,1,0:T(8,128)S(1)}, u32[]{:S(2)}) %copy-start.1) | copy-done | bytes 1638424
  37.2 6.2 %all-to-all-start = ((bf16[16,208,128]{2,1,0:T(8,128)(2,1)}), bf16[16,208,128]{2,1,0:T(8,128)(2,1)S(1)}, u32[]{:S(2)}, u32[]{:S(2)}) async-start(bf16[16,208,128]{2,1,0:T(8,128)(2,1)} %get-tuple-element.15.refs_2_), calls=%async_computation | async-start | bytes 1703936 | tf_op jit(solution)/shard_map/all_to_all | solution.py:484
  43.4 0.1 shard_map.81.own_ref
  43.5 0.2 collective-permute-start.9
  43.7 2.9 %collective-permute-done.9.mate_ref = bf16[8,2,320,128]{3,2,1,0:T(8,128)(2,1)S(1)} collective-permute-done((bf16[8,2,320,128]{3,2,1,0:T(8,128)(2,1)S(1)}, bf16[8,2,320,128]{3,2,1,0:T(8,128)(2,1)S(1)}, u32[]{:S(2)}, u32[]{:S(2)}) %collective-permute-start.9) | collective-permute-done | bytes 1310752 | tf_op jit(solution)/shard_map/ppermute | solution.py:353
  46.6 3.7 %shard_map.82.half_ref = f32[16,40,640]{2,1,0:T(8,128)S(1)} custom-call(s32[1]{0:T(128)} %bitcast.pos_ref, s32[8]{0:T(128)S(1)} %copy-done.4, bf16[8,2,320,128]{3,2,1,0:T(8,128)(2,1)S(1)} %shard_map.81.own_ref, bf16[8,2,320,128]{3,2,1,0:T(8,128)(2,1)S(1)} %collective-permute-done.9.mate_ref, f32[16,40,640]{2,1,0:T(8,128)S(1)} %copy-done.2, ...), custom_call_target="tpu_custom_call" | custom-call | flops 1000 | bytes 1000 | tf_op jit(solution)/shard_map/pallas_call | solution.py:487
  50.2 12.8 %all-to-all-done.recv_ref = bf16[16,208,128]{2,1,0:T(8,128)(2,1)S(1)} async-done(((bf16[16,208,128]{2,1,0:T(8,128)(2,1)}), bf16[16,208,128]{2,1,0:T(8,128)(2,1)S(1)}, u32[]{:S(2)}, u32[]{:S(2)}) %all-to-all-start) | async-done | bytes 852000 | tf_op jit(solution)/shard_map/all_to_all | solution.py:484
  63.1 4.3 %shard_map.83 = f32[8,8,40,640]{3,2,1,0:T(8,128)} custom-call(s32[8]{0:T(128)S(1)} %copy-done.4, s32[40,640]{1,0:T(8,128)S(1)} %get-tuple-element.11.u_ref.refs_2_, f32[16,40,640]{2,1,0:T(8,128)S(1)} %shard_map.82.half_ref, bf16[16,208,128]{2,1,0:T(8,128)(2,1)S(1)} %all-to-all-done.recv_ref), custom_call_target="tpu_custom_call" | custom-call | flops 1000000 | bytes 5000000 | tf_op jit(solution)/shard_map/pallas_call | solution.py:502
  (29 shorter events, 0.1 us)
Async XLA Ops:
  0.0 9.9 %copy-start.6 = (s32[640]{0:T(1024)S(1)}, s32[640]{0:T(1024)}, u32[]{:S(2)}) copy-start(s32[640]{0:T(1024)} %vir_ref.1) | copy-start | bytes 7684
  0.0 12.6 %copy-start = (bf16[8,8,40,640]{3,2,1,0:T(8,128)(2,1)S(1)}, bf16[8,8,40,640]{3,2,1,0:T(8,128)(2,1)}, u32[]{:S(2)}) copy-start(bf16[8,8,40,640]{3,2,1,0:T(8,128)(2,1)} %amps_ref.1) | copy-start | bytes 9830404
  0.0 12.6 %copy-start.4 = (s32[8]{0:T(128)S(1)}, s32[8]{0:T(128)}, u32[]{:S(2)}) copy-start(s32[8]{0:T(128)} %occ_ref.9) | copy-start | bytes 100
  2.2 10.1 %collective-permute-start.5 = (bf16[16,128]{1,0:T(8,128)(2,1)}, bf16[16,128]{1,0:T(8,128)(2,1)S(1)}, u32[]{:S(2)}, u32[]{:S(2)}) collective-permute-start(bf16[16,128]{1,0:T(8,128)(2,1)} %get-tuple-element.13.refs_0_), channel_id=1, source_target_pairs={{0,12},{1,13},{2,14},{3,15},{4,8},{5,9},{6,10},{7,11},{8,4},{9,5},... | collective-permute-start | bytes 12296 | tf_op jit(solution)/shard_map/ppermute | solution.py:353
  6.3 11.2 %collective-permute-start.4 = (bf16[16,128]{1,0:T(8,128)(2,1)}, bf16[16,128]{1,0:T(8,128)(2,1)S(1)}, u32[]{:S(2)}, u32[]{:S(2)}) collective-permute-start(bf16[16,128]{1,0:T(8,128)(2,1)} %get-tuple-element.13.refs_0_), channel_id=1, source_target_pairs={{0,8},{1,9},{2,10},{3,11},{4,12},{5,13},{6,14},{7,15},{8,0},{9,1},... | collective-permute-start | bytes 12296 | tf_op jit(solution)/shard_map/ppermute | solution.py:353
  6.4 11.2 %collective-permute-start.3 = (bf16[16,128]{1,0:T(8,128)(2,1)}, bf16[16,128]{1,0:T(8,128)(2,1)}, u32[]{:S(2)}, u32[]{:S(2)}) collective-permute-start(bf16[16,128]{1,0:T(8,128)(2,1)} %get-tuple-element.13.refs_0_), channel_id=1, source_target_pairs={{0,4},{1,5},{2,6},{3,7},{4,0},{5,1},{6,2},{7,3},{8,12},{9,13},{10,... | collective-permute-start | bytes 12296 | tf_op jit(solution)/shard_map/ppermute | solution.py:353
  6.6 16.8 %collective-permute-start.2 = (bf16[1,2,320,128]{3,2,1,0:T(8,128)(2,1)}, bf16[1,2,320,128]{3,2,1,0:T(8,128)(2,1)S(1)}, u32[]{:S(2)}, u32[]{:S(2)}) collective-permute-start(bf16[1,2,320,128]{3,2,1,0:T(8,128)(2,1)} %get-tuple-element.12.refs_0_), channel_id=1, source_target_pairs={{0,12},{1,13},{2,14},{3,15},{4,8},{5,9},{6,10},{7,11},{8,4},{9,5},... | collective-permute-start | bytes 491528 | tf_op jit(solution)/shard_map/ppermute | solution.py:353
  9.9 13.7 %collective-permute-start.1 = (bf16[1,2,320,128]{3,2,1,0:T(8,128)(2,1)}, bf16[1,2,320,128]{3,2,1,0:T(8,128)(2,1)}, u32[]{:S(2)}, u32[]{:S(2)}) collective-permute-start(bf16[1,2,320,128]{3,2,1,0:T(8,128)(2,1)} %get-tuple-element.12.refs_0_), channel_id=1, source_target_pairs={{0,8},{1,9},{2,10},{3,11},{4,12},{5,13},{6,14},{7,15},{8,0},{9,1},... | collective-permute-start | bytes 491528 | tf_op jit(solution)/shard_map/ppermute | solution.py:353
  9.9 0.7 %copy-start.7 = (s32[640]{0:T(1024)S(1)}, s32[640]{0:T(1024)}, u32[]{:S(2)}) copy-start(s32[640]{0:T(1024)} %vir_ref.1) | copy-start | bytes 7684
  10.6 0.7 %copy-start.10 = (bf16[8,8]{1,0:T(8,128)(2,1)S(1)}, bf16[8,8]{1,0:T(8,128)(2,1)}, u32[]{:S(2)}) copy-start(bf16[8,8]{1,0:T(8,128)(2,1)} %occ_vals_ref.1) | copy-start | bytes 388
  12.3 11.4 %collective-permute-start = (bf16[1,2,320,128]{3,2,1,0:T(8,128)(2,1)}, bf16[1,2,320,128]{3,2,1,0:T(8,128)(2,1)S(1)}, u32[]{:S(2)}, u32[]{:S(2)}) collective-permute-start(bf16[1,2,320,128]{3,2,1,0:T(8,128)(2,1)} %get-tuple-element.12.refs_0_), channel_id=1, source_target_pairs={{0,4},{1,5},{2,6},{3,7},{4,0},{5,1},{6,2},{7,3},{8,12},{9,13},{10,... | collective-permute-start | bytes 491528 | tf_op jit(solution)/shard_map/ppermute | solution.py:353
  12.6 1.1 %copy-start.8 = (bf16[640,640]{1,0:T(8,128)(2,1)S(1)}, bf16[640,640]{1,0:T(8,128)(2,1)}, u32[]{:S(2)}) copy-start(bf16[640,640]{1,0:T(8,128)(2,1)} %fock_ref.3) | copy-start | bytes 2457604
  13.8 3.8 %copy-start.5 = (bf16[16,128]{1,0:T(8,128)(2,1)S(1)}, bf16[16,128]{1,0:T(8,128)(2,1)}, u32[]{:S(2)}) copy-start(bf16[16,128]{1,0:T(8,128)(2,1)} %get-tuple-element.13.refs_0_) | copy-start | bytes 12292
  13.8 5.9 %copy-start.9 = (bf16[640,640]{1,0:T(8,128)(2,1)S(1)}, bf16[640,640]{1,0:T(8,128)(2,1)}, u32[]{:S(2)}) copy-start(bf16[640,640]{1,0:T(8,128)(2,1)} %fock_ref.3) | copy-start | bytes 2457604
  13.8 14.7 %slice-start = ((s8[6553600]{0:T(1024)(128)(4,1)}), s8[4194304]{0:T(1024)(128)(4,1)S(1)}, s32[]{:S(2)}) async-start(s8[6553600]{0:T(1024)(128)(4,1)} %bitcast.3), calls=%async_computation.1 | async-start | bytes 8388608
  18.4 5.3 %copy-start.3 = (bf16[1,2,320,128]{3,2,1,0:T(8,128)(2,1)S(1)}, bf16[1,2,320,128]{3,2,1,0:T(8,128)(2,1)}, u32[]{:S(2)}) copy-start(bf16[1,2,320,128]{3,2,1,0:T(8,128)(2,1)} %get-tuple-element.12.refs_0_) | copy-start | bytes 491524
  18.4 10.1 %slice-start.1 = ((s8[6553600]{0:T(1024)(128)(4,1)}), s8[2359296]{0:T(1024)(128)(4,1)S(1)}, s32[]{:S(2)}) async-start(s8[6553600]{0:T(1024)(128)(4,1)} %bitcast.3), calls=%async_computation.2 | async-start | bytes 4718592
  18.4 5.0 %collective-permute-start.6 = (f32[8,8,128]{2,1,0:T(8,128)S(1)}, f32[8,8,128]{2,1,0:T(8,128)S(1)}, u32[]{:S(2)}, u32[]{:S(2)}) collective-permute-start(f32[8,8,128]{2,1,0:T(8,128)S(1)} %shard_map.76.after_ref.a_ref), channel_id=1, source_target_pairs={{0,2},{1,3},{2,0},{3,1},{4,6},{5,7},{6,4},{7,5},{8,10},{9,11},{10,... | collective-permute-start | bytes 98312 | tf_op jit(solution)/shard_map/ppermute | solution.py:353
  24.6 18.8 %collective-permute-start.7 = (bf16[4,2,320,128]{3,2,1,0:T(8,128)(2,1)S(1)}, bf16[4,2,320,128]{3,2,1,0:T(8,128)(2,1)S(1)}, u32[]{:S(2)}, u32[]{:S(2)}) collective-permute-start(bf16[4,2,320,128]{3,2,1,0:T(8,128)(2,1)S(1)} %shard_map.79.refs_4_.refs_0_), channel_id=1, source_target_pairs={{0,2},{1,3},{2,0},{3,1},{4,6},{5,7},{6,4},{7,5},{8,10},{9,11},{10,... | collective-permute-start | bytes 1966088 | tf_op jit(solution)/shard_map/ppermute | solution.py:353
  25.9 2.6 %collective-permute-start.8 = (f32[8,8,128]{2,1,0:T(8,128)S(1)}, f32[8,8,128]{2,1,0:T(8,128)S(1)}, u32[]{:S(2)}, u32[]{:S(2)}) collective-permute-start(f32[8,8,128]{2,1,0:T(8,128)S(1)} %shard_map.78.refs_4_.win0_ref), channel_id=1, source_target_pairs={{0,1},{1,0},{2,3},{3,2},{4,5},{5,4},{6,7},{7,6},{8,9},{9,8},{10,11... | collective-permute-start | bytes 98312 | tf_op jit(solution)/shard_map/ppermute | solution.py:353
  36.1 1.2 %copy-start.1 = (f32[16,40,640]{2,1,0:T(8,128)}, f32[16,40,640]{2,1,0:T(8,128)S(1)}, u32[]{:S(2)}) copy-start(f32[16,40,640]{2,1,0:T(8,128)S(1)} %get-tuple-element.16.half_ref) | copy-start | bytes 4915204
  37.2 25.8 %all-to-all-start = ((bf16[16,208,128]{2,1,0:T(8,128)(2,1)}), bf16[16,208,128]{2,1,0:T(8,128)(2,1)S(1)}, u32[]{:S(2)}, u32[]{:S(2)}) async-start(bf16[16,208,128]{2,1,0:T(8,128)(2,1)} %get-tuple-element.15.refs_2_), calls=%async_computation | async-start | bytes 1703936 | tf_op jit(solution)/shard_map/all_to_all | solution.py:484
  43.4 3.2 %copy-start.2 = (f32[16,40,640]{2,1,0:T(8,128)S(1)}, f32[16,40,640]{2,1,0:T(8,128)}, u32[]{:S(2)}) copy-start(f32[16,40,640]{2,1,0:T(8,128)} %copy-done.1) | copy-start | bytes 4915204
  43.5 3.1 %collective-permute-start.9 = (bf16[8,2,320,128]{3,2,1,0:T(8,128)(2,1)S(1)}, bf16[8,2,320,128]{3,2,1,0:T(8,128)(2,1)S(1)}, u32[]{:S(2)}, u32[]{:S(2)}) collective-permute-start(bf16[8,2,320,128]{3,2,1,0:T(8,128)(2,1)S(1)} %shard_map.81.own_ref), channel_id=1, source_target_pairs={{0,1},{1,0},{2,3},{3,2},{4,5},{5,4},{6,7},{7,6},{8,9},{9,8},{10,11... | collective-permute-start | bytes 3932168 | tf_op jit(solution)/shard_map/ppermute | solution.py:353

commit v9 on v7

v9 whole, which is shorter than its diff:
```python
import functools

import jax
import jax.numpy as jnp
from jax import lax
from jax.experimental import pallas as pl
from jax.experimental.pallas import tpu as pltpu
from jax.sharding import PartitionSpec as P

DW = 8
CW = 16
LANES = 128
POWER = 9
TOP_EXPONENT = 13


def contract_last(left_side, right_side):
    return lax.dot_general(
        left_side, right_side, (((1,), (1,)), ((), ())), preferred_element_type=jnp.float32
    )


def plain_body(amps, fock_vir, fock_occ, ladder_ints, cycle_ints, occ_irrep, vir_irrep):
    occupied = amps.shape[0]
    per_device = amps.shape[2]
    virtuals = amps.shape[3]
    pair_count = occupied * occupied
    position = lax.axis_index("vir")
    fock_term = jnp.dot(
        amps.reshape(pair_count * per_device, virtuals),
        fock_vir,
        preferred_element_type=jnp.float32,
    ).reshape(occupied, occupied, per_device, virtuals)
    occ_term = jnp.einsum("ikab,kj->ijab", amps, fock_occ, preferred_element_type=jnp.float32)
    flat_ints = ladder_ints.reshape(per_device * virtuals, ladder_ints.shape[2])
    local_window = amps[:, :, 0:1, :DW]
    local_cycle = amps[:, :, :, :CW]
    segment = lax.all_gather(local_window, "vir", axis=2, tiled=True)
    width = segment.shape[2] * DW
    ladder = contract_last(segment.reshape(pair_count, width), flat_ints)
    left_side = jnp.transpose(local_cycle, (0, 2, 1, 3)).reshape(
        occupied * per_device, occupied * CW
    )
    segment = lax.all_gather(cycle_ints, "vir", axis=0, tiled=True)
    right_side = segment.reshape(segment.shape[0] * occupied, occupied * CW)
    cycle_block = contract_last(left_side, right_side).reshape(
        occupied, per_device, segment.shape[0], occupied
    )
    cycle_part = jnp.transpose(cycle_block, (0, 3, 1, 2))
    half_sum = (
        fock_term - occ_term + ladder.reshape(occupied, occupied, per_device, virtuals) + cycle_part
    )
    vir_local = lax.dynamic_slice_in_dim(vir_irrep, position * per_device, per_device)
    occ_pair = jnp.bitwise_xor(occ_irrep[:, None], occ_irrep[None, :])
    vir_pair = jnp.bitwise_xor(vir_local[:, None], vir_irrep[None, :])
    received = lax.all_to_all(half_sum, "vir", split_axis=3, concat_axis=2, tiled=True)
    mirrored = jnp.transpose(received, (1, 0, 3, 2))
    product_irrep = jnp.bitwise_xor(occ_pair[:, :, None, None], vir_pair[None, None, :, :])
    allowed = jnp.where(product_irrep == 0, jnp.float32(1.0), jnp.float32(0.0))
    return allowed * (half_sum + mirrored)


def params(mib):
    return pltpu.CompilerParams(vmem_limit_bytes=mib * 2**20)


def labels_and_copies(occ_ref, occupied):
    labels = [occ_ref[j] for j in range(occupied)]
    copies = []
    for j in range(occupied):
        s = jnp.int32(0)
        for k in range(j):
            s = s + (labels[k] == labels[j]).astype(jnp.int32)
        copies.append(s)
    return labels, copies


def prep_kernel(pos_ref, vir_ref, row_ref, occ_vals_ref, amps_ref, win_ref, mix_ref, u_ref, t_ref, acc_ref):
    dests = win_ref.shape[0]
    occupied, _, per_device, _ = amps_ref.shape
    rows = occupied * per_device
    row = row_ref[...]
    for a in range(per_device):
        u_ref[a : a + 1, :] = row ^ vir_ref[pos_ref[0] * per_device + a]
    at = lax.broadcasted_iota(jnp.int32, (rows, occupied), 0)
    start = lax.broadcasted_iota(jnp.int32, (rows, occupied), 1) * per_device
    in_block = jnp.logical_and(at >= start, at < start + per_device).astype(jnp.bfloat16)
    at = lax.broadcasted_iota(jnp.int32, (rows, per_device), 0)
    col = lax.broadcasted_iota(jnp.int32, (rows, per_device), 1)
    same = at == col
    for n in range(1, occupied):
        same = jnp.logical_or(same, at == col + n * per_device)
    same = same.astype(jnp.bfloat16)
    left = contract_last(in_block, occ_vals_ref[...]).astype(jnp.bfloat16)
    mix = contract_last(left, in_block) * contract_last(same, same)
    mix_ref[...] = mix.astype(jnp.bfloat16)
    lane = lax.broadcasted_iota(jnp.int32, (occupied, LANES), 1)
    packed = jnp.zeros((occupied, LANES), jnp.float32)
    for j in range(occupied):
        w = jnp.where(lane < DW, amps_ref[:, j, 0, :LANES].astype(jnp.float32), 0.0)
        packed = packed + (pltpu.roll(w, j * DW, axis=1) if j else w)
    packed = jnp.concatenate([packed, jnp.zeros_like(packed)], axis=0).astype(jnp.bfloat16)
    for q in range(dests):
        win_ref[q] = packed
    lane = lax.broadcasted_iota(jnp.int32, (per_device, LANES), 1)
    for i in range(occupied):
        acc = jnp.zeros((per_device, LANES), jnp.float32)
        for k in range(occupied):
            piece = jnp.where(lane < CW, amps_ref[i, k, :, :LANES].astype(jnp.float32), 0.0)
            acc = acc + (pltpu.roll(piece, k * CW, axis=1) if k else piece)
        acc_ref[i * per_device : (i + 1) * per_device, :] = acc
    t_ref[0] = acc_ref[...].astype(jnp.bfloat16)


def fock_kernel(occ_ref, amps_ref, fock_ref, mix_ref, u_ref, half_ref, hs_ref):
    wide, rows, virtuals = amps_ref.shape
    _, per_device, _ = half_ref.shape
    occupied = occ_ref.shape[0]
    labels, copies = labels_and_copies(occ_ref, occupied)
    u = u_ref[...]
    h = jnp.dot(
        amps_ref[...].reshape(wide * rows, virtuals),
        fock_ref[...],
        preferred_element_type=jnp.float32,
    )
    for w in range(wide):
        a = amps_ref[w]
        mixed = jnp.dot(mix_ref[...], a, preferred_element_type=jnp.float32)
        hs_ref[...] = (h[w * rows : (w + 1) * rows] - mixed).reshape(hs_ref.shape)
        own = occ_ref[pl.program_id(0) * wide + w]
        for j in range(occupied):
            at = 2 * w + copies[j]
            half_ref[at] = jnp.where(u == (own ^ labels[j]), hs_ref[j], half_ref[at])


def stack(blocks, after):
    count = len(blocks)

    def kernel(*refs):
        out = refs[count + 1]
        at = 0
        for n in range(count):
            head = blocks[n].shape[0]
            out[at : at + head] = refs[n][...]
            at += head

    vmem = pl.BlockSpec(memory_space=pltpu.VMEM)
    shape = (sum(b.shape[0] for b in blocks),) + blocks[0].shape[1:]
    return pl.pallas_call(
        kernel,
        out_shape=jax.ShapeDtypeStruct(shape, blocks[0].dtype),
        in_specs=[vmem] * count + [pl.BlockSpec(memory_space=pl.ANY)],
        out_specs=vmem,
        compiler_params=params(4),
        cost_estimate=pl.CostEstimate(flops=0, bytes_accessed=10**6, transcendentals=0),
    )(*blocks, after)


def payload_pieces(per_device, pairs, dests):
    out = {}
    for q in range(dests):
        for e in range(pairs):
            start = 0
            while start < per_device:
                src = q * per_device + start
                dst = e * per_device + start
                length = min(LANES - src % LANES, LANES - dst % LANES, per_device - start)
                out.setdefault((q, dst // LANES), []).append(
                    (dst % LANES, e, src // LANES, (dst - src) % LANES)
                )
                start += length
    return out


def ladder_kernel(
    groups, occ_ref, win_ref, half_ref, u_ref, lad_ref, _, out_ref, send_ref,
    w1_ref, w2_ref, hs_ref, pay_ref, code_ref, half_sems, send_sems, *ls_refs
):
    occupied = occ_ref.shape[0]
    pairs, per_device, virtuals = hs_ref.shape
    dests = pay_ref.shape[0]
    tiles = virtuals // LANES
    labels, copies = labels_and_copies(occ_ref, occupied)
    lane = lax.broadcasted_iota(jnp.int32, (8, LANES), 1)
    for j in range(occupied):
        total = jnp.zeros((8, LANES), jnp.float32)
        for p in range(dests):
            w = win_ref[p].astype(jnp.float32)[:8]
            w = jnp.where(jnp.logical_and(lane >= j * DW, lane < (j + 1) * DW), w, 0.0)
            shift = (p - j) * DW % LANES
            total = total + (pltpu.roll(w, shift, axis=1) if shift else w)
        w1_ref[j] = total
    for i in range(occupied):
        for j in range(occupied):
            row = (labels[i] ^ labels[j]) * pairs + 2 * i + copies[j]
            w2_ref[pl.ds(row, 1), :] = w1_ref[j, i : i + 1, :]
    w2 = w2_ref[...].astype(jnp.bfloat16)
    pieces_of = payload_pieces(per_device, pairs, dests)
    tops = [jnp.zeros((8, LANES), jnp.float32)]

    def ladder(g, a):
        product = contract_last(w2, lad_ref[8 * g + a])
        ua = u_ref[8 * g + a : 8 * g + a + 1, :]
        sel = product[0:pairs]
        for v in range(1, 4):
            sel = jnp.where(ua == v, product[v * pairs : (v + 1) * pairs], sel)
        for v in range(tiles):
            ls_refs[g][v, pl.ds(a, pairs, stride=8), :] = sel[:, v * LANES : (v + 1) * LANES]

    def payload(g):
        rows = slice(8 * g, 8 * g + 8)
        found = {}
        for t in range(tiles):
            last_e = min(((t + 1) * LANES - 1) // per_device, pairs - 1)
            for e in range(t * LANES // per_device, last_e + 1):
                if (e, 0) in found:
                    continue
                for v in range(tiles):
                    at = slice(v * LANES, (v + 1) * LANES)
                    x = half_ref[e, rows, at] + ls_refs[g][v, 8 * e : 8 * e + 8, :]
                    hs_ref[e, rows, at] = x
                    tops[0] = jnp.maximum(tops[0], jnp.abs(x))
                    found[e, v] = x
            for q in range(dests):
                acc = None
                for first, e, v, shift in pieces_of[q, t]:
                    x = pltpu.roll(found[e, v], shift, axis=1) if shift else found[e, v]
                    acc = x if acc is None else jnp.where(lane >= first, x, acc)
                start = t * per_device + 8 * g
                pay_ref[q, start : start + 8, :] = acc
                if q % 8 == 7:
                    yield

    stores = []
    for g in range(groups + 1):
        before = payload(g - 1) if g else iter(())
        for a in range(8):
            if g < groups:
                ladder(g, a)
            next(before, None)
        for _ in before:
            pass
        if g:
            rows = pl.ds(8 * (g - 1), 8)
            store = pltpu.make_async_copy(
                hs_ref.at[:, rows, :], out_ref.at[:, rows, :], half_sems.at[g - 1]
            )
            store.start()
            stores.append(store)
    most = jnp.max(jnp.max(tops[0], axis=0, keepdims=True), axis=1, keepdims=True)
    k = jnp.floor(TOP_EXPONENT - jnp.log2(jnp.maximum(most, 1e-30)))
    scale = jnp.exp2(k)
    row = lax.broadcasted_iota(jnp.int32, pay_ref.shape[1:], 0)
    for q in range(dests):
        z = pay_ref[q] * scale
        z2 = z * z
        z4 = z2 * z2
        y = jnp.where(row >= tiles * per_device, k, z4 * z4 * z)
        code_ref[q] = y.astype(jnp.bfloat16)
        store = pltpu.make_async_copy(code_ref.at[q], send_ref.at[q], send_sems.at[q])
        store.start()
        stores.append(store)
    for store in stores:
        store.wait()


def cycle_kernel(
    pos_ref, occ_ref, own_ref, mate_ref, half_hbm, u_ref, out_ref, orb_ref, cs_ref, xs_ref, ts_ref,
    half_ref, sems,
):
    occupied = occ_ref.shape[0]
    pairs, per_device, virtuals = half_ref.shape
    dests, rows, _ = own_ref.shape
    load = pltpu.make_async_copy(half_hbm, half_ref, sems.at[0])
    load.start()
    tiles = virtuals // LANES
    labels, copies = labels_and_copies(occ_ref, occupied)
    for j in range(occupied):
        orb_ref[2 * labels[j] + copies[j]] = jnp.int32(j)
    for r in range(dests):
        ref = mate_ref if r & 1 else own_ref
        n = ((r >> 1) & 1) * (dests // 2) + (r >> 2)
        p = pos_ref[0] ^ r
        x = ref[n].astype(jnp.float32).reshape(per_device, occupied, LANES)
        xs_ref[pl.ds(p * per_device, per_device)] = x
        t = ref[n + dests // 4].astype(jnp.float32)
        at = pl.ds(pl.multiple_of(p * per_device, 8), per_device)
        for j in range(occupied):
            ts_ref[j, at, :] = t[j * per_device : (j + 1) * per_device]
    here = pl.ds(pos_ref[0] * per_device, per_device)
    x_left = jnp.concatenate([xs_ref[here, i, :] for i in range(occupied)], axis=0)
    left = jnp.concatenate([own_ref[dests // 4], x_left.astype(jnp.bfloat16)], axis=1)
    for j in range(occupied):
        right = jnp.concatenate([xs_ref[:, j, :], ts_ref[j]], axis=1).astype(jnp.bfloat16)
        cs_ref[j] = contract_last(left, right).reshape(occupied, per_device, virtuals)
    load.wait()
    choices = [
        [orb_ref[2 * (labels[e // 2] ^ n) + e % 2] for n in range(4)] for e in range(pairs)
    ]

    def group(g, carry):
        rows = pl.ds(pl.multiple_of(g * 8, 8), 8)
        for v in range(tiles):
            at = slice(v * LANES, (v + 1) * LANES)
            uv = u_ref[rows, at]
            masks = [uv == n for n in range(1, 4)]
            for e in range(pairs):
                x = cs_ref[choices[e][0], e // 2, rows, at]
                for n in range(1, 4):
                    x = jnp.where(masks[n - 1], cs_ref[choices[e][n], e // 2, rows, at], x)
                out_ref[e, rows, at] = half_ref[e, rows, at] + x
        return carry

    lax.fori_loop(0, per_device // 8, group, 0)


def join_kernel(occ_ref, u_ref, half_ref, recv_ref, out_ref, dec_ref, mir_ref, res_ref, sems):
    occupied = occ_ref.shape[0]
    per_device, virtuals = u_ref.shape
    labels, copies = labels_and_copies(occ_ref, occupied)
    spread = 2 * per_device
    ready = set()

    def decode(t):
        ready.add(t)
        start = t * per_device
        low, high = start // 16 * 16, (start + per_device + 15) // 16 * 16
        end = virtuals // LANES * per_device
        for p in range(recv_ref.shape[0]):
            tail = recv_ref[p, end // 16 * 16 : end // 16 * 16 + 16, :]
            k = tail.astype(jnp.float32)[end % 16 : end % 16 + 1, 0:1]
            y = recv_ref[p, low:high, :].astype(jnp.float32)
            y = y[start - low : start - low + per_device]
            size = jnp.log2(jnp.maximum(jnp.abs(y), 2.0**-126)) * (1.0 / POWER) - k
            size = jnp.exp2(size)
            x = jnp.where(y < 0, -size, jnp.where(y > 0, size, 0.0))
            dec_ref[p * per_device : (p + 1) * per_device, :] = x
        mir_ref[t * LANES : (t + 1) * LANES, :] = dec_ref[...].T

    stores = []
    for j in range(occupied):
        for t in range(j * spread // LANES, ((j + 1) * spread - 1) // LANES + 1):
            if t not in ready:
                decode(t)
        u = u_ref[...]
        for i in range(occupied):
            at = pl.ds(pl.multiple_of((2 * j + copies[i]) * per_device, 8), per_device)
            total = half_ref[2 * i + copies[j]] + mir_ref[at, :]
            n = j * occupied + i
            res_ref[n] = jnp.where(u == (labels[j] ^ labels[i]), total, 0.0)
            store = pltpu.make_async_copy(res_ref.at[n], out_ref.at[i, j], sems.at[n])
            store.start()
            stores.append(store)
    for store in stores:
        store.wait()


def permute(x, flip, size):
    return lax.ppermute(x, "vir", [(n, n ^ flip) for n in range(size)])


def body(dests, amps, fock_vir, fock_occ, ladder_ints, cycle_ints, occ_irrep, vir_irrep):
    occupied, _, per_device, virtuals = amps.shape
    pairs = 2 * occupied
    tiles = virtuals // LANES
    rows = occupied * per_device
    kw = ladder_ints.shape[2]
    f32, bf16 = jnp.float32, jnp.bfloat16
    position = lax.axis_index("vir").astype(jnp.int32)
    pos = position.reshape(1)
    smem = pl.BlockSpec(memory_space=pltpu.SMEM)

    def whole(shape):
        return pl.BlockSpec(shape, lambda n: (0,) * len(shape))

    def cost(flops, size):
        return pl.CostEstimate(flops=flops, bytes_accessed=size, transcendentals=0)

    anywhere = pl.BlockSpec(memory_space=pl.ANY)
    quarter = dests // 4
    vmem = pl.BlockSpec(memory_space=pltpu.VMEM)
    hbm = pl.BlockSpec(memory_space=pltpu.HBM)
    x = cycle_ints.reshape(1, rows, LANES)
    flips = [m << 2 for m in range(1, quarter)]
    x_blocks = [x] + [permute(x, flip, dests) for flip in flips]
    win, mix, u, t = pl.pallas_call(
        prep_kernel,
        out_shape=(
            jax.ShapeDtypeStruct((dests, 16, LANES), bf16),
            jax.ShapeDtypeStruct((rows, rows), bf16),
            jax.ShapeDtypeStruct((per_device, virtuals), jnp.int32),
            jax.ShapeDtypeStruct((1, rows, LANES), bf16),
        ),
        in_specs=[smem, smem, vmem, vmem, vmem],
        out_specs=(vmem,) * 4,
        scratch_shapes=[pltpu.VMEM((rows, LANES), f32)],
        compiler_params=params(12),
        cost_estimate=cost(0, 10**6),
    )(pos, vir_irrep, vir_irrep.reshape(1, virtuals), fock_occ, amps)

    wins = lax.all_to_all(win, "vir", split_axis=0, concat_axis=0, tiled=True)
    t_blocks = [t] + [permute(t, flip, dests) for flip in flips]
    wide = 2
    half = pl.pallas_call(
        fock_kernel,
        grid=(occupied // wide,),
        out_shape=jax.ShapeDtypeStruct((pairs, per_device, virtuals), f32),
        in_specs=[
            smem,
            pl.BlockSpec((wide, rows, virtuals), lambda i: (i, 0, 0)),
            whole(fock_vir.shape),
            whole(mix.shape),
            whole(u.shape),
        ],
        out_specs=pl.BlockSpec((2 * wide, per_device, virtuals), lambda i: (i, 0, 0)),
        scratch_shapes=[pltpu.VMEM((occupied, per_device, virtuals), f32)],
        compiler_params=params(12),
        cost_estimate=cost(3 * occupied * rows * virtuals * virtuals, 8 * 10**6),
    )(occ_irrep, amps.reshape(occupied, rows, virtuals), fock_vir, mix, u)

    near = stack(x_blocks + t_blocks, half)
    near_y = permute(near, 2, dests)
    send_rows = tiles * per_device + 8
    groups = per_device // 8
    half, send = pl.pallas_call(
        functools.partial(ladder_kernel, groups),
        out_shape=(
            jax.ShapeDtypeStruct((pairs, per_device, virtuals), f32),
            jax.ShapeDtypeStruct((dests, send_rows, LANES), bf16),
        ),
        in_specs=[smem] + [vmem] * 4 + [anywhere],
        out_specs=(hbm, hbm),
        scratch_shapes=[
            pltpu.VMEM((occupied, occupied, LANES), f32),
            pltpu.VMEM((occupied * occupied, LANES), f32),
            pltpu.VMEM((pairs, per_device, virtuals), f32),
            pltpu.VMEM((dests, send_rows, LANES), f32),
            pltpu.VMEM((dests, send_rows, LANES), bf16),
            pltpu.SemaphoreType.DMA((groups,)),
            pltpu.SemaphoreType.DMA((dests,)),
        ]
        + [pltpu.VMEM((tiles, 8 * pairs, LANES), f32)] * groups,
        compiler_params=params(24),
        cost_estimate=cost(4 * occupied * rows * virtuals * LANES, 9 * 10**6),
    )(occ_irrep, wins, half, u, ladder_ints, near)

    recv = lax.all_to_all(send, "vir", split_axis=0, concat_axis=0, tiled=True)
    own_blocks = stack([near, near_y], send)
    mate_blocks = permute(own_blocks, 1, dests)
    half = pl.pallas_call(
        cycle_kernel,
        out_shape=jax.ShapeDtypeStruct((pairs, per_device, virtuals), f32),
        in_specs=[smem, smem, vmem, vmem, hbm, vmem],
        out_specs=vmem,
        scratch_shapes=[
            pltpu.SMEM((occupied,), jnp.int32),
            pltpu.VMEM((occupied, occupied, per_device, virtuals), f32),
            pltpu.VMEM((virtuals, occupied, LANES), f32),
            pltpu.VMEM((occupied, virtuals, LANES), f32),
            pltpu.VMEM((pairs, per_device, virtuals), f32),
            pltpu.SemaphoreType.DMA((1,)),
        ],
        compiler_params=params(28),
        cost_estimate=cost(1000, 1000),
    )(pos, occ_irrep, own_blocks, mate_blocks, half, u)

    return pl.pallas_call(
        join_kernel,
        out_shape=jax.ShapeDtypeStruct((occupied, occupied, per_device, virtuals), f32),
        in_specs=[smem, vmem, vmem, vmem],
        out_specs=anywhere,
        scratch_shapes=[
            pltpu.VMEM((virtuals, LANES), f32),
            pltpu.VMEM((tiles * LANES, virtuals), f32),
            pltpu.VMEM((occupied * occupied, per_device, virtuals), f32),
            pltpu.SemaphoreType.DMA((occupied * occupied,)),
        ],
        compiler_params=params(16),
        cost_estimate=cost(10**6, 5 * 10**6),
    )(occ_irrep, u, half, recv)


def solution(mesh):
    dests = mesh.shape["vir"]

    def run(amps, *rest):
        occupied, _, per_device, virtuals = amps.shape
        tiled = (
            dests == 16
            and per_device % 8 == 0
            and virtuals % LANES == 0
            and 2 * occupied * per_device == virtuals
            and rest[2].shape[2] == LANES
            and rest[3].shape[2] == LANES
        )
        return body(dests, amps, *rest) if tiled else plain_body(amps, *rest)

    return jax.shard_map(
        run,
        mesh=mesh,
        in_specs=(
            P("groups", None, "vir", None),
            P("groups", None),
            P("groups", None),
            P("vir", "groups", None),
            P("vir", "groups", None),
            P("groups"),
            P("groups"),
        ),
        out_specs=P("groups", None, "vir", None),
        check_vma=False,
    )
```

time: 71.1 us -> 76.8 us (1.080)
  blocking collectives: 0 us -> 16.2 us
  Pallas kernels: 28.7 us -> 22 us
  starting transfers between devices: 20.1 us -> 15.7 us
  local copies, waits for them, and re-layouts: 3.29 us -> 6.45 us
  waiting for transfers between devices: 17.3 us -> 15.5 us
    all_to_all x0 -> x1, blocking collectives: none -> 16.2 us  [body(): wins = lax.all_to_all(win, 'vir', split_axis=0, concat_axis=0, tiled=True)]
    ppermute x10 -> x8, waiting for transfers between devices: 17.3 us -> 2.95 us  [permute(): return lax.ppermute(x, 'vir', [(n, n ^ flip) for n in range(size)])]
    all_to_all x1, waiting for transfers between devices: 0.01 us -> 12.6 us  [body(): recv = lax.all_to_all(send, 'vir', split_axis=0, concat_axis=0, tiled=True)]
    pallas_call x8 -> x3, Pallas kernels: 19 us -> 13.6 us  [the longest x1 6.84 us: body(): pl.pallas_call(fock_kernel, grid=(occupied // wide,), out_shape=jax.Shape...]
    ppermute x10 -> x8, starting transfers between devices: 14.9 us -> 9.6 us  [permute(): return lax.ppermute(x, 'vir', [(n, n ^ flip) for n in range(size)])]
    unnamed x18 -> x22, local copies, waits for them, and re-layouts: 2.53 us -> 5.76 us
    all_to_all x1, starting transfers between devices: 5.2 us -> 6.15 us  [body(): recv = lax.all_to_all(send, 'vir', split_axis=0, concat_axis=0, tiled=True)]
    pallas_call x2, Pallas kernels: 1.05 us -> 0.13 us  [stack(): pl.pallas_call(kernel, out_shape=jax.ShapeDtypeStruct(shape, blocks[0].dt...]
  transfers between devices with their start and end apart: 11 -> 9, of which waited for: 2 -> 2; matrix products, arithmetic and copies ran while one was open for 2% -> 1% of each run, Pallas kernels for 29% -> 23%
where the time goes in v9:
time: 76.8 us; the launch traced here: 76 us
  Pallas kernels  22 us (29%)
  blocking collectives  16.2 us (21%)
  starting transfers between devices  15.7 us (20%)
  waiting for transfers between devices  15.5 us (20%)
  local copies, waits for them, and re-layouts  6.45 us (8%)
    all_to_all x1, blocking collectives, body(): wins = lax.all_to_all(win, 'vir', split_axis=0, concat_axis=0, tiled=True)  16.2 us
    all_to_all x1, waiting for transfers between devices, body(): recv = lax.all_to_all(send, 'vir', split_axis=0, concat_axis=0, tiled=True)  12.6 us
    ppermute x8, starting transfers between devices, permute(): return lax.ppermute(x, 'vir', [(n, n ^ flip) for n in range(size)])  9.6 us
    pallas_call x1, Pallas kernels, body(): pl.pallas_call(fock_kernel, grid=(occupied // wide,), out_shape=jax.Shape...  6.84 us
    all_to_all x1, starting transfers between devices, body(): recv = lax.all_to_all(send, 'vir', split_axis=0, concat_axis=0, tiled=True)  6.15 us
    unnamed x22, local copies, waits for them, and re-layouts  5.76 us
    pallas_call x1, Pallas kernels, body(): pl.pallas_call(functools.partial(ladder_kernel, groups), out_shape=(jax.S...  5.71 us
    pallas_call x1, Pallas kernels, body(): pl.pallas_call(join_kernel, out_shape=jax.ShapeDtypeStruct((occupied, occ...  4.34 us
  transfers between devices with their start and end apart: 9, of which 2 were waited for; matrix products, arithmetic and copies ran while one was open for 1% of the time, Pallas kernels for 23%

profile of v9, /device:TPU:1, one launch (start us, length us, event | category | flops | bytes accessed | tf_op | source)
XLA Modules:
  0.0 76.0 jit_solution(17939721730667890680)
XLA Ops:
  0.0 4.2 %collective-permute-start.2 = (bf16[1,320,128]{2,1,0:T(8,128)(2,1)}, bf16[1,320,128]{2,1,0:T(8,128)(2,1)S(1)}, u32[]{:S(2)}, u32[]{:S(2)}) collective-permute-start(bf16[1,320,128]{2,1,0:T(8,128)(2,1)} %bitcast.6), channel_id=1, source_target_pairs={{0,12},{1,13},{2,14},{3,15},{4,8},{5,9},{6,10},{7,11},{8,4},{9,5},... | collective-permute-start | bytes 245768 | tf_op jit(solution)/shard_map/ppermute | solution.py:359
  4.2 0.0 collective-permute-start.1
  4.2 0.3 collective-permute-start
  4.4 0.7 reshape.13.row_ref
  5.1 1.9 %copy-done = bf16[8,8,40,640]{3,2,1,0:T(8,128)(2,1)S(1)} copy-done((bf16[8,8,40,640]{3,2,1,0:T(8,128)(2,1)S(1)}, bf16[8,8,40,640]{3,2,1,0:T(8,128)(2,1)}, u32[]{:S(2)}) %copy-start) | copy-done | bytes 3276824
  7.1 0.7 copy-done.5
  7.7 0.7 copy-done.7
  8.4 1.0 %shard_map.73 = (bf16[16,16,128]{2,1,0:T(8,128)(2,1)S(1)}, bf16[320,320]{1,0:T(8,128)(2,1)S(1)}, s32[40,640]{1,0:T(8,128)S(1)}, bf16[1,320,128]{2,1,0:T(8,128)(2,1)S(1)}) custom-call(s32[1]{0:T(128)} %bitcast.pos_ref, s32[640]{0:T(1024)S(1)} %copy-done.5, s32[1,640]{1,0:T(1,128)S(1)} %reshape.13.row_ref, bf16[8,8]{1,0:T(8,128)(2,1)S(1)} %copy-done.7, ...), custom_call_target="tpu_custom_call" | custom-call | bytes 1000000 | tf_op jit(solution)/shard_map/pallas_call | solution.py:386
  9.5 3.3 %collective-permute-start.5 = (bf16[1,320,128]{2,1,0:T(8,128)(2,1)S(1)}, bf16[1,320,128]{2,1,0:T(8,128)(2,1)S(1)}, u32[]{:S(2)}, u32[]{:S(2)}) collective-permute-start(bf16[1,320,128]{2,1,0:T(8,128)(2,1)S(1)} %get-tuple-element.12.refs_4_), channel_id=1, source_target_pairs={{0,12},{1,13},{2,14},{3,15},{4,8},{5,9},{6,10},{7,11},{8,4},{9,5},... | collective-permute-start | bytes 245768 | tf_op jit(solution)/shard_map/ppermute | solution.py:359
  12.8 0.0 collective-permute-start.4
  12.8 0.0 collective-permute-done.2.refs_3_
  12.8 0.4 collective-permute-start.3
  13.2 1.3 %copy-done.8 = bf16[640,640]{1,0:T(8,128)(2,1)S(1)} copy-done((bf16[640,640]{1,0:T(8,128)(2,1)S(1)}, bf16[640,640]{1,0:T(8,128)(2,1)}, u32[]{:S(2)}) %copy-start.8) | copy-done | bytes 819224
  14.5 6.8 %shard_map.74.refs_8_.half_ref = f32[16,40,640]{2,1,0:T(8,128)S(1)} custom-call(s32[8]{0:T(128)S(1)} %copy-done.6, bf16[8,320,640]{2,1,0:T(8,128)(2,1)S(1)} %bitcast.5, bf16[640,640]{1,0:T(8,128)(2,1)S(1)} %copy-done.8, bf16[320,320]{1,0:T(8,128)(2,1)S(1)} %get-tuple-element.13.mix_ref, s32[40,640]{1,0:T(8,128)S(1)} %get-tuple-element.11.u_ref), custom_call_target="tpu_custom_call" | custom-call | flops 3145728000 | bytes 8000000 | tf_op jit(solution)/shard_map/pallas_call | solution.py:404
  21.3 0.0 collective-permute-done.1.refs_2_
  21.3 0.0 collective-permute-done.refs_1_
  21.3 0.0 collective-permute-done.5.refs_7_
  21.4 0.0 collective-permute-done.4.refs_6_
  21.4 0.0 collective-permute-done.3.refs_5_
  21.4 1.3 %collective-permute-start.6 = (bf16[8,320,128]{2,1,0:T(8,128)(2,1)S(1)}, bf16[8,320,128]{2,1,0:T(8,128)(2,1)S(1)}, u32[]{:S(2)}, u32[]{:S(2)}) collective-permute-start(bf16[8,320,128]{2,1,0:T(8,128)(2,1)S(1)} %shard_map.75._.refs_0_), channel_id=1, source_target_pairs={{0,2},{1,3},{2,0},{3,1},{4,6},{5,7},{6,4},{7,5},{8,10},{9,11},{10,... | collective-permute-start | bytes 1966088 | tf_op jit(solution)/shard_map/ppermute | solution.py:359
  22.7 16.2 %all_to_all.10.win_ref = bf16[16,16,128]{2,1,0:T(8,128)(2,1)S(1)} all-to-all(bf16[16,16,128]{2,1,0:T(8,128)(2,1)S(1)} %get-tuple-element.14), channel_id=1, replica_groups=mesh['groups'=2,'vir'=16] {'vir'}, dimensions={0} | all-to-all | bytes 131072 | tf_op jit(solution)/shard_map/all_to_all | solution.py:401
  38.9 5.7 %shard_map.76 = (f32[16,40,640]{2,1,0:T(8,128)S(1)}, bf16[16,208,128]{2,1,0:T(8,128)(2,1)}) custom-call(s32[8]{0:T(128)S(1)} %copy-done.6, bf16[16,16,128]{2,1,0:T(8,128)(2,1)S(1)} %all_to_all.10.win_ref, f32[16,40,640]{2,1,0:T(8,128)S(1)} %shard_map.74.refs_8_.half_ref, s32[40,640]{1,0:T(8,128)S(1)} %get-tuple-element.11.u_ref, ...), custom_call_target="tpu_custom_call" | custom-call | flops 838860800 | bytes 9000000 | tf_op jit(solution)/shard_map/pallas_call | solution.py:425
  44.6 0.0 copy-start.2
  44.7 1.2 %copy-done.2 = f32[16,40,640]{2,1,0:T(8,128)} copy-done((f32[16,40,640]{2,1,0:T(8,128)}, f32[16,40,640]{2,1,0:T(8,128)S(1)}, u32[]{:S(2)}) %copy-start.2) | copy-done | bytes 1638424
  45.8 6.2 %all-to-all-start.1 = ((bf16[16,208,128]{2,1,0:T(8,128)(2,1)}), bf16[16,208,128]{2,1,0:T(8,128)(2,1)S(1)}, u32[]{:S(2)}, u32[]{:S(2)}) async-start(bf16[16,208,128]{2,1,0:T(8,128)(2,1)} %get-tuple-element.15.refs_2_), calls=%async_computation.1 | async-start | bytes 1703936 | tf_op jit(solution)/shard_map/all_to_all | solution.py:447
  52.0 0.0 collective-permute-done.6.refs_1_
  52.0 0.1 shard_map.77.own_ref
  52.1 0.2 collective-permute-start.7
  52.2 2.9 %collective-permute-done.7.mate_ref = bf16[16,320,128]{2,1,0:T(8,128)(2,1)S(1)} collective-permute-done((bf16[16,320,128]{2,1,0:T(8,128)(2,1)S(1)}, bf16[16,320,128]{2,1,0:T(8,128)(2,1)S(1)}, u32[]{:S(2)}, u32[]{:S(2)}) %collective-permute-start.7) | collective-permute-done | bytes 1310752 | tf_op jit(solution)/shard_map/ppermute | solution.py:359
  55.2 3.9 %shard_map.78.half_ref = f32[16,40,640]{2,1,0:T(8,128)S(1)} custom-call(s32[1]{0:T(128)} %bitcast.pos_ref, s32[8]{0:T(128)S(1)} %copy-done.6, bf16[16,320,128]{2,1,0:T(8,128)(2,1)S(1)} %shard_map.77.own_ref, bf16[16,320,128]{2,1,0:T(8,128)(2,1)S(1)} %collective-permute-done.7.mate_ref, f32[16,40,640]{2,1,0:T(8,128)S(1)} %copy-done.3, ...), custom_call_target="tpu_custom_call" | custom-call | flops 1000 | bytes 1000 | tf_op jit(solution)/shard_map/pallas_call | solution.py:450
  59.1 12.6 %all-to-all-done.1.recv_ref = bf16[16,208,128]{2,1,0:T(8,128)(2,1)S(1)} async-done(((bf16[16,208,128]{2,1,0:T(8,128)(2,1)}), bf16[16,208,128]{2,1,0:T(8,128)(2,1)S(1)}, u32[]{:S(2)}, u32[]{:S(2)}) %all-to-all-start.1) | async-done | bytes 852000 | tf_op jit(solution)/shard_map/all_to_all | solution.py:447
  71.7 4.3 %shard_map.79 = f32[8,8,40,640]{3,2,1,0:T(8,128)} custom-call(s32[8]{0:T(128)S(1)} %copy-done.6, s32[40,640]{1,0:T(8,128)S(1)} %get-tuple-element.11.u_ref, f32[16,40,640]{2,1,0:T(8,128)S(1)} %shard_map.78.half_ref, bf16[16,208,128]{2,1,0:T(8,128)(2,1)S(1)} %all-to-all-done.1.recv_ref), custom_call_target="tpu_custom_call" | custom-call | flops 1000000 | bytes 5000000 | tf_op jit(solution)/shard_map/pallas_call | solution.py:467
  (18 shorter events, 0.1 us)
Async XLA Ops:
  0.0 12.8 %collective-permute-start.2 = (bf16[1,320,128]{2,1,0:T(8,128)(2,1)}, bf16[1,320,128]{2,1,0:T(8,128)(2,1)S(1)}, u32[]{:S(2)}, u32[]{:S(2)}) collective-permute-start(bf16[1,320,128]{2,1,0:T(8,128)(2,1)} %bitcast.6), channel_id=1, source_target_pairs={{0,12},{1,13},{2,14},{3,15},{4,8},{5,9},{6,10},{7,11},{8,4},{9,5},... | collective-permute-start | bytes 245768 | tf_op jit(solution)/shard_map/ppermute | solution.py:359
  4.2 17.2 %collective-permute-start.1 = (bf16[1,320,128]{2,1,0:T(8,128)(2,1)}, bf16[1,320,128]{2,1,0:T(8,128)(2,1)S(1)}, u32[]{:S(2)}, u32[]{:S(2)}) collective-permute-start(bf16[1,320,128]{2,1,0:T(8,128)(2,1)} %bitcast.7), channel_id=1, source_target_pairs={{0,8},{1,9},{2,10},{3,11},{4,12},{5,13},{6,14},{7,15},{8,0},{9,1},... | collective-permute-start | bytes 245768 | tf_op jit(solution)/shard_map/ppermute | solution.py:359
  4.2 17.2 %collective-permute-start = (bf16[1,320,128]{2,1,0:T(8,128)(2,1)}, bf16[1,320,128]{2,1,0:T(8,128)(2,1)S(1)}, u32[]{:S(2)}, u32[]{:S(2)}) collective-permute-start(bf16[1,320,128]{2,1,0:T(8,128)(2,1)} %bitcast.8), channel_id=1, source_target_pairs={{0,4},{1,5},{2,6},{3,7},{4,0},{5,1},{6,2},{7,3},{8,12},{9,13},{10,... | collective-permute-start | bytes 245768 | tf_op jit(solution)/shard_map/ppermute | solution.py:359
  5.1 1.9 %copy-start = (bf16[8,8,40,640]{3,2,1,0:T(8,128)(2,1)S(1)}, bf16[8,8,40,640]{3,2,1,0:T(8,128)(2,1)}, u32[]{:S(2)}) copy-start(bf16[8,8,40,640]{3,2,1,0:T(8,128)(2,1)} %amps_ref.1) | copy-start | bytes 9830404
  7.1 0.7 copy-start.5
  7.7 0.7 copy-start.7
  8.4 4.7 %copy-start.1 = (bf16[8,8,40,640]{3,2,1,0:T(8,128)(2,1)S(1)}, bf16[8,8,40,640]{3,2,1,0:T(8,128)(2,1)}, u32[]{:S(2)}) copy-start(bf16[8,8,40,640]{3,2,1,0:T(8,128)(2,1)} %amps_ref.1) | copy-start | bytes 9830404
  8.4 4.7 %copy-start.6 = (s32[8]{0:T(128)S(1)}, s32[8]{0:T(128)}, u32[]{:S(2)}) copy-start(s32[8]{0:T(128)} %occ_ref.7) | copy-start | bytes 100
  9.5 11.9 %collective-permute-start.5 = (bf16[1,320,128]{2,1,0:T(8,128)(2,1)S(1)}, bf16[1,320,128]{2,1,0:T(8,128)(2,1)S(1)}, u32[]{:S(2)}, u32[]{:S(2)}) collective-permute-start(bf16[1,320,128]{2,1,0:T(8,128)(2,1)S(1)} %get-tuple-element.12.refs_4_), channel_id=1, source_target_pairs={{0,12},{1,13},{2,14},{3,15},{4,8},{5,9},{6,10},{7,11},{8,4},{9,5},... | collective-permute-start | bytes 245768 | tf_op jit(solution)/shard_map/ppermute | solution.py:359
  12.8 8.6 %collective-permute-start.4 = (bf16[1,320,128]{2,1,0:T(8,128)(2,1)S(1)}, bf16[1,320,128]{2,1,0:T(8,128)(2,1)S(1)}, u32[]{:S(2)}, u32[]{:S(2)}) collective-permute-start(bf16[1,320,128]{2,1,0:T(8,128)(2,1)S(1)} %get-tuple-element.12.refs_4_), channel_id=1, source_target_pairs={{0,8},{1,9},{2,10},{3,11},{4,12},{5,13},{6,14},{7,15},{8,0},{9,1},... | collective-permute-start | bytes 245768 | tf_op jit(solution)/shard_map/ppermute | solution.py:359
  12.8 8.6 %collective-permute-start.3 = (bf16[1,320,128]{2,1,0:T(8,128)(2,1)S(1)}, bf16[1,320,128]{2,1,0:T(8,128)(2,1)S(1)}, u32[]{:S(2)}, u32[]{:S(2)}) collective-permute-start(bf16[1,320,128]{2,1,0:T(8,128)(2,1)S(1)} %get-tuple-element.12.refs_4_), channel_id=1, source_target_pairs={{0,4},{1,5},{2,6},{3,7},{4,0},{5,1},{6,2},{7,3},{8,12},{9,13},{10,... | collective-permute-start | bytes 245768 | tf_op jit(solution)/shard_map/ppermute | solution.py:359
  13.2 25.8 %slice-start = ((s8[6553600]{0:T(1024)(128)(4,1)}), s8[4194304]{0:T(1024)(128)(4,1)S(1)}, s32[]{:S(2)}) async-start(s8[6553600]{0:T(1024)(128)(4,1)} %bitcast.3), calls=%async_computation.2 | async-start | bytes 8388608
  13.2 1.3 %copy-start.8 = (bf16[640,640]{1,0:T(8,128)(2,1)S(1)}, bf16[640,640]{1,0:T(8,128)(2,1)}, u32[]{:S(2)}) copy-start(bf16[640,640]{1,0:T(8,128)(2,1)} %fock_ref.1) | copy-start | bytes 2457604
  14.5 6.9 %copy-start.4 = (bf16[40,8,128]{2,1,0:T(8,128)(2,1)S(1)}, bf16[40,8,128]{2,1,0:T(8,128)(2,1)}, u32[]{:S(2)}) copy-start(bf16[40,8,128]{2,1,0:T(8,128)(2,1)} %param.11) | copy-start | bytes 245764
  14.5 24.4 %slice-start.1 = ((s8[6553600]{0:T(1024)(128)(4,1)}), s8[2359296]{0:T(1024)(128)(4,1)S(1)}, s32[]{:S(2)}) async-start(s8[6553600]{0:T(1024)(128)(4,1)} %bitcast.3), calls=%async_computation.3 | async-start | bytes 4718592
  21.4 30.5 %collective-permute-start.6 = (bf16[8,320,128]{2,1,0:T(8,128)(2,1)S(1)}, bf16[8,320,128]{2,1,0:T(8,128)(2,1)S(1)}, u32[]{:S(2)}, u32[]{:S(2)}) collective-permute-start(bf16[8,320,128]{2,1,0:T(8,128)(2,1)S(1)} %shard_map.75._.refs_0_), channel_id=1, source_target_pairs={{0,2},{1,3},{2,0},{3,1},{4,6},{5,7},{6,4},{7,5},{8,10},{9,11},{10,... | collective-permute-start | bytes 1966088 | tf_op jit(solution)/shard_map/ppermute | solution.py:359
  44.6 1.2 %copy-start.2 = (f32[16,40,640]{2,1,0:T(8,128)}, f32[16,40,640]{2,1,0:T(8,128)S(1)}, u32[]{:S(2)}) copy-start(f32[16,40,640]{2,1,0:T(8,128)S(1)} %get-tuple-element.16.half_hbm) | copy-start | bytes 4915204
  45.8 25.8 %all-to-all-start.1 = ((bf16[16,208,128]{2,1,0:T(8,128)(2,1)}), bf16[16,208,128]{2,1,0:T(8,128)(2,1)S(1)}, u32[]{:S(2)}, u32[]{:S(2)}) async-start(bf16[16,208,128]{2,1,0:T(8,128)(2,1)} %get-tuple-element.15.refs_2_), calls=%async_computation.1 | async-start | bytes 1703936 | tf_op jit(solution)/shard_map/all_to_all | solution.py:447
  52.0 3.2 %copy-start.3 = (f32[16,40,640]{2,1,0:T(8,128)S(1)}, f32[16,40,640]{2,1,0:T(8,128)}, u32[]{:S(2)}) copy-start(f32[16,40,640]{2,1,0:T(8,128)} %copy-done.2) | copy-start | bytes 4915204
  52.1 3.1 %collective-permute-start.7 = (bf16[16,320,128]{2,1,0:T(8,128)(2,1)S(1)}, bf16[16,320,128]{2,1,0:T(8,128)(2,1)S(1)}, u32[]{:S(2)}, u32[]{:S(2)}) collective-permute-start(bf16[16,320,128]{2,1,0:T(8,128)(2,1)S(1)} %shard_map.77.own_ref), channel_id=1, source_target_pairs={{0,1},{1,0},{2,3},{3,2},{4,5},{5,4},{6,7},{7,6},{8,9},{9,8},{10,11... | collective-permute-start | bytes 3932168 | tf_op jit(solution)/shard_map/ppermute | solution.py:359

commit v10 on v9

--- a/solution.py
+++ b/solution.py
@@ -75,13 +75,28 @@
     return labels, copies
 
 
-def prep_kernel(pos_ref, vir_ref, row_ref, occ_vals_ref, amps_ref, win_ref, mix_ref, u_ref, t_ref, acc_ref):
-    dests = win_ref.shape[0]
+def prep_kernel(
+    pos_ref, cyc_ref, amps_ref, vir_ref, occ_vals_ref,
+    win_ref, xt_ref, mix_ref, u_ref,
+    corner_ref, acc_ref, vals_ref, row_ref, vir_smem, sems,
+):
     occupied, _, per_device, _ = amps_ref.shape
     rows = occupied * per_device
-    row = row_ref[...]
+    moves = [
+        (amps_ref.at[:, :, :, :LANES], corner_ref),
+        (occ_vals_ref, vals_ref),
+        (vir_ref, row_ref),
+        (vir_ref, vir_smem),
+        (cyc_ref, xt_ref.at[0, 0]),
+    ]
+    copies = [pltpu.make_async_copy(s, d, sems.at[n]) for n, (s, d) in enumerate(moves)]
+    for copy in copies:
+        copy.start()
+    for copy in copies[1:4]:
+        copy.wait()
+    row = row_ref[...].reshape(1, u_ref.shape[1])
     for a in range(per_device):
-        u_ref[a : a + 1, :] = row ^ vir_ref[pos_ref[0] * per_device + a]
+        u_ref[a : a + 1, :] = row ^ vir_smem[pos_ref[0] * per_device + a]
     at = lax.broadcasted_iota(jnp.int32, (rows, occupied), 0)
     start = lax.broadcasted_iota(jnp.int32, (rows, occupied), 1) * per_device
     in_block = jnp.logical_and(at >= start, at < start + per_device).astype(jnp.bfloat16)
@@ -91,28 +106,29 @@
     for n in range(1, occupied):
         same = jnp.logical_or(same, at == col + n * per_device)
     same = same.astype(jnp.bfloat16)
-    left = contract_last(in_block, occ_vals_ref[...]).astype(jnp.bfloat16)
+    left = contract_last(in_block, vals_ref[...]).astype(jnp.bfloat16)
     mix = contract_last(left, in_block) * contract_last(same, same)
     mix_ref[...] = mix.astype(jnp.bfloat16)
+    copies[0].wait()
     lane = lax.broadcasted_iota(jnp.int32, (occupied, LANES), 1)
     packed = jnp.zeros((occupied, LANES), jnp.float32)
     for j in range(occupied):
-        w = jnp.where(lane < DW, amps_ref[:, j, 0, :LANES].astype(jnp.float32), 0.0)
+        w = jnp.where(lane < DW, corner_ref[:, j, 0, :].astype(jnp.float32), 0.0)
         packed = packed + (pltpu.roll(w, j * DW, axis=1) if j else w)
     packed = jnp.concatenate([packed, jnp.zeros_like(packed)], axis=0).astype(jnp.bfloat16)
-    for q in range(dests):
-        win_ref[q] = packed
+    win_ref[...] = packed
     lane = lax.broadcasted_iota(jnp.int32, (per_device, LANES), 1)
     for i in range(occupied):
         acc = jnp.zeros((per_device, LANES), jnp.float32)
         for k in range(occupied):
-            piece = jnp.where(lane < CW, amps_ref[i, k, :, :LANES].astype(jnp.float32), 0.0)
+            piece = jnp.where(lane < CW, corner_ref[i, k].astype(jnp.float32), 0.0)
             acc = acc + (pltpu.roll(piece, k * CW, axis=1) if k else piece)
         acc_ref[i * per_device : (i + 1) * per_device, :] = acc
-    t_ref[0] = acc_ref[...].astype(jnp.bfloat16)
-
-
-def fock_kernel(occ_ref, amps_ref, fock_ref, mix_ref, u_ref, half_ref, hs_ref):
+    xt_ref[0, 1] = acc_ref[...].astype(jnp.bfloat16)
+    copies[4].wait()
+
+
+def fock_kernel(occ_ref, amps_ref, fock_ref, mix_ref, u_ref, _0, _1, _2, half_ref, hs_ref):
     wide, rows, virtuals = amps_ref.shape
     _, per_device, _ = half_ref.shape
     occupied = occ_ref.shape[0]
@@ -151,9 +167,23 @@
         out_shape=jax.ShapeDtypeStruct(shape, blocks[0].dtype),
         in_specs=[vmem] * count + [pl.BlockSpec(memory_space=pl.ANY)],
         out_specs=vmem,
-        compiler_params=params(4),
+        compiler_params=params(60),
         cost_estimate=pl.CostEstimate(flops=0, bytes_accessed=10**6, transcendentals=0),
     )(*blocks, after)
+
+
+def unpack_kernel(pos_ref, *refs):
+    blocks, win_ref = refs[:-1], refs[-1]
+    occupied, _, lanes = win_ref.shape
+    lane = lax.broadcasted_iota(jnp.int32, (8, lanes), 1)
+    for j in range(occupied):
+        total = jnp.zeros((8, lanes), jnp.float32)
+        for m, block in enumerate(blocks):
+            p = pos_ref[0] ^ (m << 2)
+            w = block[...].astype(jnp.float32)[:8]
+            w = jnp.where(jnp.logical_and(lane >= j * DW, lane < (j + 1) * DW), w, 0.0)
+            total = total + pltpu.roll(w, lax.rem(p * DW - j * DW + lanes, lanes), axis=1)
+        win_ref[j] = total
 
 
 def payload_pieces(per_device, pairs, dests):
@@ -173,27 +203,31 @@
 
 
 def ladder_kernel(
-    groups, occ_ref, win_ref, half_ref, u_ref, lad_ref, _, out_ref, send_ref,
-    w1_ref, w2_ref, hs_ref, pay_ref, code_ref, half_sems, send_sems, *ls_refs
+    groups, occ_ref, win0, win1, win2, win3, half_hbm, u_hbm, lad_hbm, _, out_ref, send_ref,
+    win_ref, half_ref, u_ref, lad_ref, w2_ref, hs_ref, pay_ref, code_ref,
+    in_sems, half_sems, send_sems, *ls_refs
 ):
     occupied = occ_ref.shape[0]
     pairs, per_device, virtuals = hs_ref.shape
     dests = pay_ref.shape[0]
     tiles = virtuals // LANES
+    moves = [(w, win_ref.at[n]) for n, w in enumerate((win0, win1, win2, win3))]
+    moves.append((u_hbm, u_ref))
+    moves.extend((lad_hbm.at[pl.ds(8 * g, 8)], lad_ref.at[pl.ds(8 * g, 8)]) for g in range(groups))
+    moves.append((half_hbm, half_ref))
+    loads = [pltpu.make_async_copy(s, d, in_sems.at[n]) for n, (s, d) in enumerate(moves)]
+    for load in loads:
+        load.start()
+    for load in loads[:5]:
+        load.wait()
     labels, copies = labels_and_copies(occ_ref, occupied)
     lane = lax.broadcasted_iota(jnp.int32, (8, LANES), 1)
-    for j in range(occupied):
-        total = jnp.zeros((8, LANES), jnp.float32)
-        for p in range(dests):
-            w = win_ref[p].astype(jnp.float32)[:8]
-            w = jnp.where(jnp.logical_and(lane >= j * DW, lane < (j + 1) * DW), w, 0.0)
-            shift = (p - j) * DW % LANES
-            total = total + (pltpu.roll(w, shift, axis=1) if shift else w)
-        w1_ref[j] = total
     for i in range(occupied):
         for j in range(occupied):
             row = (labels[i] ^ labels[j]) * pairs + 2 * i + copies[j]
-            w2_ref[pl.ds(row, 1), :] = w1_ref[j, i : i + 1, :]
+            at = slice(i, i + 1)
+            w = win_ref[0, j, at, :] + win_ref[1, j, at, :]
+            w2_ref[pl.ds(row, 1), :] = w + (win_ref[2, j, at, :] + win_ref[3, j, at, :])
     w2 = w2_ref[...].astype(jnp.bfloat16)
     pieces_of = payload_pieces(per_device, pairs, dests)
     tops = [jnp.zeros((8, LANES), jnp.float32)]
@@ -234,6 +268,10 @@
     stores = []
     for g in range(groups + 1):
         before = payload(g - 1) if g else iter(())
+        if g < groups:
+            loads[5 + g].wait()
+        if g == 1:
+            loads[-1].wait()
         for a in range(8):
             if g < groups:
                 ladder(g, a)
@@ -270,7 +308,7 @@
 ):
     occupied = occ_ref.shape[0]
     pairs, per_device, virtuals = half_ref.shape
-    dests, rows, _ = own_ref.shape
+    dests, rows = 2 * own_ref.shape[0], own_ref.shape[2]
     load = pltpu.make_async_copy(half_hbm, half_ref, sems.at[0])
     load.start()
     tiles = virtuals // LANES
@@ -279,17 +317,17 @@
         orb_ref[2 * labels[j] + copies[j]] = jnp.int32(j)
     for r in range(dests):
         ref = mate_ref if r & 1 else own_ref
-        n = ((r >> 1) & 1) * (dests // 2) + (r >> 2)
+        n = ((r >> 1) & 1) * (dests // 4) + (r >> 2)
         p = pos_ref[0] ^ r
-        x = ref[n].astype(jnp.float32).reshape(per_device, occupied, LANES)
+        x = ref[n, 0].astype(jnp.float32).reshape(per_device, occupied, LANES)
         xs_ref[pl.ds(p * per_device, per_device)] = x
-        t = ref[n + dests // 4].astype(jnp.float32)
+        t = ref[n, 1].astype(jnp.float32)
         at = pl.ds(pl.multiple_of(p * per_device, 8), per_device)
         for j in range(occupied):
             ts_ref[j, at, :] = t[j * per_device : (j + 1) * per_device]
     here = pl.ds(pos_ref[0] * per_device, per_device)
     x_left = jnp.concatenate([xs_ref[here, i, :] for i in range(occupied)], axis=0)
-    left = jnp.concatenate([own_ref[dests // 4], x_left.astype(jnp.bfloat16)], axis=1)
+    left = jnp.concatenate([own_ref[0, 1], x_left.astype(jnp.bfloat16)], axis=1)
     for j in range(occupied):
         right = jnp.concatenate([xs_ref[:, j, :], ts_ref[j]], axis=1).astype(jnp.bfloat16)
         cs_ref[j] = contract_last(left, right).reshape(occupied, per_device, virtuals)
@@ -380,26 +418,41 @@
     quarter = dests // 4
     vmem = pl.BlockSpec(memory_space=pltpu.VMEM)
     hbm = pl.BlockSpec(memory_space=pltpu.HBM)
-    x = cycle_ints.reshape(1, rows, LANES)
-    flips = [m << 2 for m in range(1, quarter)]
-    x_blocks = [x] + [permute(x, flip, dests) for flip in flips]
-    win, mix, u, t = pl.pallas_call(
+    win, xt, mix, u = pl.pallas_call(
         prep_kernel,
         out_shape=(
-            jax.ShapeDtypeStruct((dests, 16, LANES), bf16),
+            jax.ShapeDtypeStruct((16, LANES), bf16),
+            jax.ShapeDtypeStruct((1, 2, rows, LANES), bf16),
             jax.ShapeDtypeStruct((rows, rows), bf16),
             jax.ShapeDtypeStruct((per_device, virtuals), jnp.int32),
-            jax.ShapeDtypeStruct((1, rows, LANES), bf16),
         ),
-        in_specs=[smem, smem, vmem, vmem, vmem],
+        in_specs=[smem] + [anywhere] * 4,
         out_specs=(vmem,) * 4,
-        scratch_shapes=[pltpu.VMEM((rows, LANES), f32)],
-        compiler_params=params(12),
+        scratch_shapes=[
+            pltpu.VMEM((occupied, occupied, per_device, LANES), bf16),
+            pltpu.VMEM((rows, LANES), f32),
+            pltpu.VMEM(fock_occ.shape, bf16),
+            pltpu.VMEM(vir_irrep.shape, jnp.int32),
+            pltpu.SMEM(vir_irrep.shape, jnp.int32),
+            pltpu.SemaphoreType.DMA((5,)),
+        ],
+        compiler_params=params(60),
         cost_estimate=cost(0, 10**6),
-    )(pos, vir_irrep, vir_irrep.reshape(1, virtuals), fock_occ, amps)
-
-    wins = lax.all_to_all(win, "vir", split_axis=0, concat_axis=0, tiled=True)
-    t_blocks = [t] + [permute(t, flip, dests) for flip in flips]
+    )(pos, cycle_ints.reshape(rows, LANES), amps, vir_irrep, fock_occ)
+
+    flips = [m << 2 for m in range(1, quarter)]
+    wins = [win] + [permute(win, flip, dests) for flip in flips]
+    blocks = [xt] + [permute(xt, flip, dests) for flip in flips]
+    win = pl.pallas_call(
+        unpack_kernel,
+        out_shape=jax.ShapeDtypeStruct((occupied, occupied, LANES), f32),
+        in_specs=[smem] + [vmem] * quarter,
+        out_specs=vmem,
+        compiler_params=params(60),
+        cost_estimate=cost(0, 10**5),
+    )(pos, *wins)
+    wins = [win] + [permute(win, flip, dests) for flip in (1, 2, 3)]
+
     wide = 2
     half = pl.pallas_call(
         fock_kernel,
@@ -411,14 +464,15 @@
             whole(fock_vir.shape),
             whole(mix.shape),
             whole(u.shape),
-        ],
+        ]
+        + [anywhere] * 3,
         out_specs=pl.BlockSpec((2 * wide, per_device, virtuals), lambda i: (i, 0, 0)),
         scratch_shapes=[pltpu.VMEM((occupied, per_device, virtuals), f32)],
-        compiler_params=params(12),
+        compiler_params=params(60),
         cost_estimate=cost(3 * occupied * rows * virtuals * virtuals, 8 * 10**6),
-    )(occ_irrep, amps.reshape(occupied, rows, virtuals), fock_vir, mix, u)
-
-    near = stack(x_blocks + t_blocks, half)
+    )(occ_irrep, amps.reshape(occupied, rows, virtuals), fock_vir, mix, u, *wins[1:])
+
+    near = stack(blocks, half)
     near_y = permute(near, 2, dests)
     send_rows = tiles * per_device + 8
     groups = per_device // 8
@@ -428,21 +482,25 @@
             jax.ShapeDtypeStruct((pairs, per_device, virtuals), f32),
             jax.ShapeDtypeStruct((dests, send_rows, LANES), bf16),
         ),
-        in_specs=[smem] + [vmem] * 4 + [anywhere],
-        out_specs=(hbm, hbm),
+        in_specs=[smem] + [anywhere] * 8,
+        out_specs=(anywhere, anywhere),
         scratch_shapes=[
-            pltpu.VMEM((occupied, occupied, LANES), f32),
+            pltpu.VMEM((4,) + win.shape, f32),
+            pltpu.VMEM((pairs, per_device, virtuals), f32),
+            pltpu.VMEM((per_device, virtuals), jnp.int32),
+            pltpu.VMEM(ladder_ints.shape, bf16),
             pltpu.VMEM((occupied * occupied, LANES), f32),
             pltpu.VMEM((pairs, per_device, virtuals), f32),
             pltpu.VMEM((dests, send_rows, LANES), f32),
             pltpu.VMEM((dests, send_rows, LANES), bf16),
+            pltpu.SemaphoreType.DMA((groups + 6,)),
             pltpu.SemaphoreType.DMA((groups,)),
             pltpu.SemaphoreType.DMA((dests,)),
         ]
         + [pltpu.VMEM((tiles, 8 * pairs, LANES), f32)] * groups,
-        compiler_params=params(24),
-        cost_estimate=cost(4 * occupied * rows * virtuals * LANES, 9 * 10**6),
-    )(occ_irrep, wins, half, u, ladder_ints, near)
+        compiler_params=params(60),
+        cost_estimate=cost(4 * occupied * rows * virtuals * LANES, 25 * 10**6),
+    )(occ_irrep, *wins, half, u, ladder_ints, near)
 
     recv = lax.all_to_all(send, "vir", split_axis=0, concat_axis=0, tiled=True)
     own_blocks = stack([near, near_y], send)

time: 76.8 us -> 76.2 us (level)
  blocking collectives: 16.2 us -> 0 us
  Pallas kernels: 22 us -> 33.9 us
  starting transfers between devices: 15.7 us -> 19 us
    all_to_all x1 -> x0, blocking collectives: 16.2 us -> none  [body(): wins = lax.all_to_all(win, 'vir', split_axis=0, concat_axis=0, tiled=True)]
    ppermute x8 -> x11, waiting for transfers between devices: 2.95 us -> 10.9 us  [permute(): return lax.ppermute(x, 'vir', [(n, n ^ flip) for n in range(size)])]
    all_to_all x1, waiting for transfers between devices: 12.6 us -> 4.74 us  [body(): recv = lax.all_to_all(send, 'vir', split_axis=0, concat_axis=0, tiled=True)]
    pallas_call x2, Pallas kernels: 0.13 us -> 4.46 us  [stack(): pl.pallas_call(kernel, out_shape=jax.ShapeDtypeStruct(shape, blocks[0].dt...]
    ppermute x8 -> x11, starting transfers between devices: 9.6 us -> 13.6 us  [permute(): return lax.ppermute(x, 'vir', [(n, n ^ flip) for n in range(size)])]
    pallas_call x1, Pallas kernels: 5.71 us -> 8.95 us  [body(): pl.pallas_call(functools.partial(ladder_kernel, groups), out_shape=(jax.S...]
    pallas_call x1 -> x2, Pallas kernels: 1.03 us -> 3.83 us  [the longest x1 2.38 us: body(): pl.pallas_call(prep_kernel, out_shape=(jax.ShapeDtypeStruct((16, LANES),...]
    pallas_call x1, Pallas kernels: 6.84 us -> 8.35 us  [body(): pl.pallas_call(fock_kernel, grid=(occupied // wide,), out_shape=jax.Shape...]
  transfers between devices with their start and end apart: 9 -> 12, of which waited for: 2 -> 7; matrix products, arithmetic and copies ran while one was open for 1% -> 0% of each run, Pallas kernels for 23% -> 31%
where the time goes in v10:
time: 76.2 us; the launch traced here: 75.3 us
  Pallas kernels  33.9 us (44%)
  starting transfers between devices  19 us (25%)
  waiting for transfers between devices  15.7 us (21%)
  local copies, waits for them, and re-layouts  6.7 us (9%)
    ppermute x11, starting transfers between devices, permute(): return lax.ppermute(x, 'vir', [(n, n ^ flip) for n in range(size)])  13.6 us
    ppermute x11, waiting for transfers between devices, permute(): return lax.ppermute(x, 'vir', [(n, n ^ flip) for n in range(size)])  10.9 us
    pallas_call x1, Pallas kernels, body(): pl.pallas_call(functools.partial(ladder_kernel, groups), out_shape=(jax.S...  8.95 us
    pallas_call x1, Pallas kernels, body(): pl.pallas_call(fock_kernel, grid=(occupied // wide,), out_shape=jax.Shape...  8.35 us
    unnamed x28, local copies, waits for them, and re-layouts  6.7 us
    all_to_all x1, starting transfers between devices, body(): recv = lax.all_to_all(send, 'vir', split_axis=0, concat_axis=0, tiled=True)  5.4 us
    all_to_all x1, waiting for transfers between devices, body(): recv = lax.all_to_all(send, 'vir', split_axis=0, concat_axis=0, tiled=True)  4.74 us
    pallas_call x2, Pallas kernels, stack(): pl.pallas_call(kernel, out_shape=jax.ShapeDtypeStruct(shape, blocks[0].dt...  4.46 us
  transfers between devices with their start and end apart: 12, of which 7 were waited for; matrix products, arithmetic and copies ran while one was open for 0% of the time, Pallas kernels for 31%

profile of v10, /device:TPU:1, one launch (start us, length us, event | category | flops | bytes accessed | tf_op | source)
XLA Modules:
  0.0 75.3 jit_solution(1516639870343867233)
XLA Ops:
  0.0 2.4 %shard_map.73 = (bf16[16,128]{1,0:T(8,128)(2,1)}, bf16[1,2,320,128]{3,2,1,0:T(8,128)(2,1)}, bf16[320,320]{1,0:T(8,128)(2,1)}, s32[40,640]{1,0:T(8,128)}) custom-call(s32[1]{0:T(128)} %bitcast.pos_ref, bf16[320,128]{1,0:T(8,128)(2,1)} %bitcast.4, bf16[8,8,40,640]{3,2,1,0:T(8,128)(2,1)} %amps_ref.1, s32[640]{0:T(1024)} %vir_ref.1, bf16[8,8]{1,0:T(8,128)(2,1)} %occ_vals_ref.1), custom_call_target="tpu_custom_call" | custom-call | bytes 1000000 | tf_op jit(solution)/shard_map/pallas_call | solution.py:421
  2.4 4.2 %collective-permute-start.5 = (bf16[16,128]{1,0:T(8,128)(2,1)}, bf16[16,128]{1,0:T(8,128)(2,1)S(1)}, u32[]{:S(2)}, u32[]{:S(2)}) collective-permute-start(bf16[16,128]{1,0:T(8,128)(2,1)} %get-tuple-element.14.refs_0_), channel_id=1, source_target_pairs={{0,12},{1,13},{2,14},{3,15},{4,8},{5,9},{6,10},{7,11},{8,4},{9,5},... | collective-permute-start | bytes 12296 | tf_op jit(solution)/shard_map/ppermute | solution.py:397
  6.6 0.4 collective-permute-start.3
  7.0 0.8 %collective-permute-done.5.refs_3_ = bf16[16,128]{1,0:T(8,128)(2,1)S(1)} collective-permute-done((bf16[16,128]{1,0:T(8,128)(2,1)}, bf16[16,128]{1,0:T(8,128)(2,1)S(1)}, u32[]{:S(2)}, u32[]{:S(2)}) %collective-permute-start.5) | collective-permute-done | bytes 4128 | tf_op jit(solution)/shard_map/ppermute | solution.py:397
  7.8 2.4 %collective-permute-done.4.refs_2_ = bf16[16,128]{1,0:T(8,128)(2,1)S(1)} collective-permute-done((bf16[16,128]{1,0:T(8,128)(2,1)}, bf16[16,128]{1,0:T(8,128)(2,1)S(1)}, u32[]{:S(2)}, u32[]{:S(2)}) %collective-permute-start.4) | collective-permute-done | bytes 4128 | tf_op jit(solution)/shard_map/ppermute | solution.py:397
  10.2 0.6 copy-done.12
  10.8 0.6 copy-done.13
  11.4 1.4 %shard_map.74.win0 = f32[8,8,128]{2,1,0:T(8,128)} custom-call(s32[1]{0:T(128)} %bitcast.pos_ref, bf16[16,128]{1,0:T(8,128)(2,1)} %get-tuple-element.14.refs_0_, bf16[16,128]{1,0:T(8,128)(2,1)} %copy-done.13, bf16[16,128]{1,0:T(8,128)(2,1)} %copy-done.12, bf16[16,128]{1,0:T(8,128)(2,1)} %copy-done.11), custom_call_target="tpu_custom_call" | custom-call | bytes 100000 | tf_op jit(solution)/shard_map/pallas_call | solution.py:446
  12.8 3.2 %collective-permute-start.8 = (f32[8,8,128]{2,1,0:T(8,128)}, f32[8,8,128]{2,1,0:T(8,128)S(1)}, u32[]{:S(2)}, u32[]{:S(2)}) collective-permute-start(f32[8,8,128]{2,1,0:T(8,128)} %shard_map.74.win0), channel_id=1, source_target_pairs={{0,3},{1,2},{2,1},{3,0},{4,7},{5,6},{6,5},{7,4},{8,11},{9,10},{10,... | collective-permute-start | bytes 98312 | tf_op jit(solution)/shard_map/ppermute | solution.py:397
  16.5 0.6 collective-permute-start.2
  17.1 0.5 collective-permute-start.1
  17.6 0.7 collective-permute-done.8._2.win3
  18.3 1.7 %collective-permute-start = (bf16[1,2,320,128]{3,2,1,0:T(8,128)(2,1)}, bf16[1,2,320,128]{3,2,1,0:T(8,128)(2,1)S(1)}, u32[]{:S(2)}, u32[]{:S(2)}) collective-permute-start(bf16[1,2,320,128]{3,2,1,0:T(8,128)(2,1)} %get-tuple-element.12.refs_0_), channel_id=1, source_target_pairs={{0,4},{1,5},{2,6},{3,7},{4,0},{5,1},{6,2},{7,3},{8,12},{9,13},{10,... | collective-permute-start | bytes 491528 | tf_op jit(solution)/shard_map/ppermute | solution.py:397
  20.0 0.6 copy-done.9
  20.6 8.4 %shard_map.75.refs_4_.half_hbm = f32[16,40,640]{2,1,0:T(8,128)} custom-call(s32[8]{0:T(128)} %occ_ref.7, bf16[8,320,640]{2,1,0:T(8,128)(2,1)} %bitcast.3, bf16[640,640]{1,0:T(8,128)(2,1)} %fock_ref.1, bf16[320,320]{1,0:T(8,128)(2,1)} %get-tuple-element.13.mix_ref, s32[40,640]{1,0:T(8,128)} %get-tuple-element.11.u_ref.u_hbm, f32[8,8,128]{2,1,0:T(8,128)} %copy-done.10, ...), custom_call_target="tpu_custom_call" | custom-call | flops 3145728000 | bytes 8000000 | tf_op jit(solution)/shard_map/pallas_call | solution.py:457
  29.0 3.7 %collective-permute-done.1.refs_2_ = bf16[1,2,320,128]{3,2,1,0:T(8,128)(2,1)S(1)} collective-permute-done((bf16[1,2,320,128]{3,2,1,0:T(8,128)(2,1)}, bf16[1,2,320,128]{3,2,1,0:T(8,128)(2,1)S(1)}, u32[]{:S(2)}, u32[]{:S(2)}) %collective-permute-start.1) | collective-permute-done | bytes 163872 | tf_op jit(solution)/shard_map/ppermute | solution.py:397
  32.7 0.7 copy-done.6
  33.4 0.7 copy-done.7
  34.0 2.0 %shard_map.76._.refs_0_ = bf16[4,2,320,128]{3,2,1,0:T(8,128)(2,1)} custom-call(bf16[1,2,320,128]{3,2,1,0:T(8,128)(2,1)} %get-tuple-element.12.refs_0_, bf16[1,2,320,128]{3,2,1,0:T(8,128)(2,1)} %copy-done.7, bf16[1,2,320,128]{3,2,1,0:T(8,128)(2,1)} %copy-done.6, bf16[1,2,320,128]{3,2,1,0:T(8,128)(2,1)} %copy-done.5, f32[16,40,640]{2,1,0:T(8,128)} %shard_map.75.refs_4_.half_hbm), custom_call_target="tpu_custom_call" | custom-call | bytes 1000000 | tf_op jit(solution)/shard_map/pallas_call | solution.py:165
  36.1 0.8 %collective-permute-start.9 = (bf16[4,2,320,128]{3,2,1,0:T(8,128)(2,1)}, bf16[4,2,320,128]{3,2,1,0:T(8,128)(2,1)S(1)}, u32[]{:S(2)}, u32[]{:S(2)}) collective-permute-start(bf16[4,2,320,128]{3,2,1,0:T(8,128)(2,1)} %shard_map.76._.refs_0_), channel_id=1, source_target_pairs={{0,2},{1,3},{2,0},{3,1},{4,6},{5,7},{6,4},{7,5},{8,10},{9,11},{10,... | collective-permute-start | bytes 1966088 | tf_op jit(solution)/shard_map/ppermute | solution.py:397
  36.9 9.0 %shard_map.77 = (f32[16,40,640]{2,1,0:T(8,128)}, bf16[16,208,128]{2,1,0:T(8,128)(2,1)}) custom-call(s32[8]{0:T(128)} %occ_ref.7, f32[8,8,128]{2,1,0:T(8,128)} %shard_map.74.win0, f32[8,8,128]{2,1,0:T(8,128)} %copy-done.10, f32[8,8,128]{2,1,0:T(8,128)} %copy-done.9, f32[8,8,128]{2,1,0:T(8,128)} %copy-done.8, f32[16,40,640]{2,1,0:T(8,128)} %shard_map.75.refs_4_.half_hbm, ...), custom_call_target="tpu_custom_call" | custom-call | flops 838860800 | bytes 25000000 | tf_op jit(solution)/shard_map/pallas_call | solution.py:479
  45.9 5.4 %all-to-all-start = ((bf16[16,208,128]{2,1,0:T(8,128)(2,1)}), bf16[16,208,128]{2,1,0:T(8,128)(2,1)S(1)}, u32[]{:S(2)}, u32[]{:S(2)}) async-start(bf16[16,208,128]{2,1,0:T(8,128)(2,1)} %get-tuple-element.15.refs_2_), calls=%async_computation | async-start | bytes 1703936 | tf_op jit(solution)/shard_map/all_to_all | solution.py:505
  51.3 0.5 collective-permute-done.9.refs_1_
  51.7 0.8 %copy-done.4 = bf16[4,2,320,128]{3,2,1,0:T(8,128)(2,1)} copy-done((bf16[4,2,320,128]{3,2,1,0:T(8,128)(2,1)}, bf16[4,2,320,128]{3,2,1,0:T(8,128)(2,1)S(1)}, u32[]{:S(2)}) %copy-start.4) | copy-done | bytes 655384
  52.6 2.4 %shard_map.78.own_ref = bf16[8,2,320,128]{3,2,1,0:T(8,128)(2,1)} custom-call(bf16[4,2,320,128]{3,2,1,0:T(8,128)(2,1)} %shard_map.76._.refs_0_, bf16[4,2,320,128]{3,2,1,0:T(8,128)(2,1)} %copy-done.4, bf16[16,208,128]{2,1,0:T(8,128)(2,1)} %get-tuple-element.15.refs_2_), custom_call_target="tpu_custom_call" | custom-call | bytes 1000000 | tf_op jit(solution)/shard_map/pallas_call | solution.py:165
  55.0 1.7 %collective-permute-start.10 = (bf16[8,2,320,128]{3,2,1,0:T(8,128)(2,1)}, bf16[8,2,320,128]{3,2,1,0:T(8,128)(2,1)S(1)}, u32[]{:S(2)}, u32[]{:S(2)}) collective-permute-start(bf16[8,2,320,128]{3,2,1,0:T(8,128)(2,1)} %shard_map.78.own_ref), channel_id=1, source_target_pairs={{0,1},{1,0},{2,3},{3,2},{4,5},{5,4},{6,7},{7,6},{8,9},{9,8},{10,11... | collective-permute-start | bytes 3932168 | tf_op jit(solution)/shard_map/ppermute | solution.py:397
  56.7 2.9 %collective-permute-done.10.mate_ref = bf16[8,2,320,128]{3,2,1,0:T(8,128)(2,1)S(1)} collective-permute-done((bf16[8,2,320,128]{3,2,1,0:T(8,128)(2,1)}, bf16[8,2,320,128]{3,2,1,0:T(8,128)(2,1)S(1)}, u32[]{:S(2)}, u32[]{:S(2)}) %collective-permute-start.10) | collective-permute-done | bytes 1310752 | tf_op jit(solution)/shard_map/ppermute | solution.py:397
  59.6 1.3 %copy-done = bf16[8,2,320,128]{3,2,1,0:T(8,128)(2,1)S(1)} copy-done((bf16[8,2,320,128]{3,2,1,0:T(8,128)(2,1)S(1)}, bf16[8,2,320,128]{3,2,1,0:T(8,128)(2,1)}, u32[]{:S(2)}) %copy-start) | copy-done | bytes 1310744
  60.9 1.4 %copy-done.1 = f32[16,40,640]{2,1,0:T(8,128)S(1)} copy-done((f32[16,40,640]{2,1,0:T(8,128)S(1)}, f32[16,40,640]{2,1,0:T(8,128)}, u32[]{:S(2)}) %copy-start.1) | copy-done | bytes 1638424
  62.3 3.9 %shard_map.79.half_ref = f32[16,40,640]{2,1,0:T(8,128)S(1)} custom-call(s32[1]{0:T(128)} %bitcast.pos_ref, s32[8]{0:T(128)S(1)} %copy-done.3, bf16[8,2,320,128]{3,2,1,0:T(8,128)(2,1)S(1)} %copy-done, bf16[8,2,320,128]{3,2,1,0:T(8,128)(2,1)S(1)} %collective-permute-done.10.mate_ref, f32[16,40,640]{2,1,0:T(8,128)S(1)} %copy-done.1, s32[40,640]{1,0:T(8,128)S(1)} %copy-done.2), custom_call_target="tpu_custom_call" | custom-call | flops 1000 | bytes 1000 | tf_op jit(solution)/shard_map/pallas_call | solution.py:508
  66.2 4.7 %all-to-all-done.recv_ref = bf16[16,208,128]{2,1,0:T(8,128)(2,1)S(1)} async-done(((bf16[16,208,128]{2,1,0:T(8,128)(2,1)}), bf16[16,208,128]{2,1,0:T(8,128)(2,1)S(1)}, u32[]{:S(2)}, u32[]{:S(2)}) %all-to-all-start) | async-done | bytes 852000 | tf_op jit(solution)/shard_map/all_to_all | solution.py:505
  71.0 4.4 %shard_map.80 = f32[8,8,40,640]{3,2,1,0:T(8,128)} custom-call(s32[8]{0:T(128)S(1)} %copy-done.3, s32[40,640]{1,0:T(8,128)S(1)} %copy-done.2, f32[16,40,640]{2,1,0:T(8,128)S(1)} %shard_map.79.half_ref, bf16[16,208,128]{2,1,0:T(8,128)(2,1)S(1)} %all-to-all-done.recv_ref), custom_call_target="tpu_custom_call" | custom-call | flops 1000000 | bytes 5000000 | tf_op jit(solution)/shard_map/pallas_call | solution.py:525
  (28 shorter events, 0.5 us)
Async XLA Ops:
  2.4 5.4 %collective-permute-start.5 = (bf16[16,128]{1,0:T(8,128)(2,1)}, bf16[16,128]{1,0:T(8,128)(2,1)S(1)}, u32[]{:S(2)}, u32[]{:S(2)}) collective-permute-start(bf16[16,128]{1,0:T(8,128)(2,1)} %get-tuple-element.14.refs_0_), channel_id=1, source_target_pairs={{0,12},{1,13},{2,14},{3,15},{4,8},{5,9},{6,10},{7,11},{8,4},{9,5},... | collective-permute-start | bytes 12296 | tf_op jit(solution)/shard_map/ppermute | solution.py:397
  6.6 3.6 %collective-permute-start.4 = (bf16[16,128]{1,0:T(8,128)(2,1)}, bf16[16,128]{1,0:T(8,128)(2,1)S(1)}, u32[]{:S(2)}, u32[]{:S(2)}) collective-permute-start(bf16[16,128]{1,0:T(8,128)(2,1)} %get-tuple-element.14.refs_0_), channel_id=1, source_target_pairs={{0,8},{1,9},{2,10},{3,11},{4,12},{5,13},{6,14},{7,15},{8,0},{9,1},... | collective-permute-start | bytes 12296 | tf_op jit(solution)/shard_map/ppermute | solution.py:397
  6.6 3.6 %collective-permute-start.3 = (bf16[16,128]{1,0:T(8,128)(2,1)}, bf16[16,128]{1,0:T(8,128)(2,1)S(1)}, u32[]{:S(2)}, u32[]{:S(2)}) collective-permute-start(bf16[16,128]{1,0:T(8,128)(2,1)} %get-tuple-element.14.refs_0_), channel_id=1, source_target_pairs={{0,4},{1,5},{2,6},{3,7},{4,0},{5,1},{6,2},{7,3},{8,12},{9,13},{10,... | collective-permute-start | bytes 12296 | tf_op jit(solution)/shard_map/ppermute | solution.py:397
  7.8 2.4 %copy-start.11 = (bf16[16,128]{1,0:T(8,128)(2,1)}, bf16[16,128]{1,0:T(8,128)(2,1)S(1)}, u32[]{:S(2)}) copy-start(bf16[16,128]{1,0:T(8,128)(2,1)S(1)} %collective-permute-done.5.refs_3_) | copy-start | bytes 12292
  10.2 0.6 copy-start.12
  10.8 0.6 copy-start.13
  12.8 5.5 %collective-permute-start.8 = (f32[8,8,128]{2,1,0:T(8,128)}, f32[8,8,128]{2,1,0:T(8,128)S(1)}, u32[]{:S(2)}, u32[]{:S(2)}) collective-permute-start(f32[8,8,128]{2,1,0:T(8,128)} %shard_map.74.win0), channel_id=1, source_target_pairs={{0,3},{1,2},{2,1},{3,0},{4,7},{5,6},{6,5},{7,4},{8,11},{9,10},{10,... | collective-permute-start | bytes 98312 | tf_op jit(solution)/shard_map/ppermute | solution.py:397
  16.0 4.0 %collective-permute-start.7 = (f32[8,8,128]{2,1,0:T(8,128)}, f32[8,8,128]{2,1,0:T(8,128)S(1)}, u32[]{:S(2)}, u32[]{:S(2)}) collective-permute-start(f32[8,8,128]{2,1,0:T(8,128)} %shard_map.74.win0), channel_id=1, source_target_pairs={{0,2},{1,3},{2,0},{3,1},{4,6},{5,7},{6,4},{7,5},{8,10},{9,11},{10,... | collective-permute-start | bytes 98312 | tf_op jit(solution)/shard_map/ppermute | solution.py:397
  16.3 3.8 %collective-permute-start.6 = (f32[8,8,128]{2,1,0:T(8,128)}, f32[8,8,128]{2,1,0:T(8,128)S(1)}, u32[]{:S(2)}, u32[]{:S(2)}) collective-permute-start(f32[8,8,128]{2,1,0:T(8,128)} %shard_map.74.win0), channel_id=1, source_target_pairs={{0,1},{1,0},{2,3},{3,2},{4,5},{5,4},{6,7},{7,6},{8,9},{9,8},{10,11... | collective-permute-start | bytes 98312 | tf_op jit(solution)/shard_map/ppermute | solution.py:397
  16.5 12.5 %collective-permute-start.2 = (bf16[1,2,320,128]{3,2,1,0:T(8,128)(2,1)}, bf16[1,2,320,128]{3,2,1,0:T(8,128)(2,1)S(1)}, u32[]{:S(2)}, u32[]{:S(2)}) collective-permute-start(bf16[1,2,320,128]{3,2,1,0:T(8,128)(2,1)} %get-tuple-element.12.refs_0_), channel_id=1, source_target_pairs={{0,12},{1,13},{2,14},{3,15},{4,8},{5,9},{6,10},{7,11},{8,4},{9,5},... | collective-permute-start | bytes 491528 | tf_op jit(solution)/shard_map/ppermute | solution.py:397
  17.1 15.6 %collective-permute-start.1 = (bf16[1,2,320,128]{3,2,1,0:T(8,128)(2,1)}, bf16[1,2,320,128]{3,2,1,0:T(8,128)(2,1)S(1)}, u32[]{:S(2)}, u32[]{:S(2)}) collective-permute-start(bf16[1,2,320,128]{3,2,1,0:T(8,128)(2,1)} %get-tuple-element.12.refs_0_), channel_id=1, source_target_pairs={{0,8},{1,9},{2,10},{3,11},{4,12},{5,13},{6,14},{7,15},{8,0},{9,1},... | collective-permute-start | bytes 491528 | tf_op jit(solution)/shard_map/ppermute | solution.py:397
  18.3 1.7 %copy-start.8 = (f32[8,8,128]{2,1,0:T(8,128)}, f32[8,8,128]{2,1,0:T(8,128)S(1)}, u32[]{:S(2)}) copy-start(f32[8,8,128]{2,1,0:T(8,128)S(1)} %collective-permute-done.8._2.win3) | copy-start | bytes 98308
  18.3 14.4 %collective-permute-start = (bf16[1,2,320,128]{3,2,1,0:T(8,128)(2,1)}, bf16[1,2,320,128]{3,2,1,0:T(8,128)(2,1)S(1)}, u32[]{:S(2)}, u32[]{:S(2)}) collective-permute-start(bf16[1,2,320,128]{3,2,1,0:T(8,128)(2,1)} %get-tuple-element.12.refs_0_), channel_id=1, source_target_pairs={{0,4},{1,5},{2,6},{3,7},{4,0},{5,1},{6,2},{7,3},{8,12},{9,13},{10,... | collective-permute-start | bytes 491528 | tf_op jit(solution)/shard_map/ppermute | solution.py:397
  20.0 0.6 copy-start.9
  20.0 0.6 copy-start.10
  29.0 3.7 %copy-start.5 = (bf16[1,2,320,128]{3,2,1,0:T(8,128)(2,1)}, bf16[1,2,320,128]{3,2,1,0:T(8,128)(2,1)S(1)}, u32[]{:S(2)}) copy-start(bf16[1,2,320,128]{3,2,1,0:T(8,128)(2,1)S(1)} %collective-permute-done.2.refs_3_) | copy-start | bytes 491524
  32.7 0.7 copy-start.6
  33.4 0.7 copy-start.7
  36.1 15.7 %collective-permute-start.9 = (bf16[4,2,320,128]{3,2,1,0:T(8,128)(2,1)}, bf16[4,2,320,128]{3,2,1,0:T(8,128)(2,1)S(1)}, u32[]{:S(2)}, u32[]{:S(2)}) collective-permute-start(bf16[4,2,320,128]{3,2,1,0:T(8,128)(2,1)} %shard_map.76._.refs_0_), channel_id=1, source_target_pairs={{0,2},{1,3},{2,0},{3,1},{4,6},{5,7},{6,4},{7,5},{8,10},{9,11},{10,... | collective-permute-start | bytes 1966088 | tf_op jit(solution)/shard_map/ppermute | solution.py:397
  45.9 25.1 %all-to-all-start = ((bf16[16,208,128]{2,1,0:T(8,128)(2,1)}), bf16[16,208,128]{2,1,0:T(8,128)(2,1)S(1)}, u32[]{:S(2)}, u32[]{:S(2)}) async-start(bf16[16,208,128]{2,1,0:T(8,128)(2,1)} %get-tuple-element.15.refs_2_), calls=%async_computation | async-start | bytes 1703936 | tf_op jit(solution)/shard_map/all_to_all | solution.py:505
  51.3 8.3 %copy-start.2 = (s32[40,640]{1,0:T(8,128)S(1)}, s32[40,640]{1,0:T(8,128)}, u32[]{:S(2)}) copy-start(s32[40,640]{1,0:T(8,128)} %get-tuple-element.11.u_ref.u_hbm) | copy-start | bytes 307204
  51.3 8.3 %copy-start.3 = (s32[8]{0:T(128)S(1)}, s32[8]{0:T(128)}, u32[]{:S(2)}) copy-start(s32[8]{0:T(128)} %occ_ref.7) | copy-start | bytes 100
  51.7 0.8 %copy-start.4 = (bf16[4,2,320,128]{3,2,1,0:T(8,128)(2,1)}, bf16[4,2,320,128]{3,2,1,0:T(8,128)(2,1)S(1)}, u32[]{:S(2)}) copy-start(bf16[4,2,320,128]{3,2,1,0:T(8,128)(2,1)S(1)} %collective-permute-done.9.refs_1_) | copy-start | bytes 1966084
  55.0 4.6 %collective-permute-start.10 = (bf16[8,2,320,128]{3,2,1,0:T(8,128)(2,1)}, bf16[8,2,320,128]{3,2,1,0:T(8,128)(2,1)S(1)}, u32[]{:S(2)}, u32[]{:S(2)}) collective-permute-start(bf16[8,2,320,128]{3,2,1,0:T(8,128)(2,1)} %shard_map.78.own_ref), channel_id=1, source_target_pairs={{0,1},{1,0},{2,3},{3,2},{4,5},{5,4},{6,7},{7,6},{8,9},{9,8},{10,11... | collective-permute-start | bytes 3932168 | tf_op jit(solution)/shard_map/ppermute | solution.py:397
  59.6 1.3 %copy-start = (bf16[8,2,320,128]{3,2,1,0:T(8,128)(2,1)S(1)}, bf16[8,2,320,128]{3,2,1,0:T(8,128)(2,1)}, u32[]{:S(2)}) copy-start(bf16[8,2,320,128]{3,2,1,0:T(8,128)(2,1)} %shard_map.78.own_ref) | copy-start | bytes 3932164
  60.9 1.4 %copy-start.1 = (f32[16,40,640]{2,1,0:T(8,128)S(1)}, f32[16,40,640]{2,1,0:T(8,128)}, u32[]{:S(2)}) copy-start(f32[16,40,640]{2,1,0:T(8,128)} %get-tuple-element.16.half_hbm) | copy-start | bytes 4915204

commit v11 on v8

--- a/solution.py
+++ b/solution.py
@@ -136,11 +136,11 @@
             half_ref[at] = jnp.where(u == (own ^ labels[j]), hs_ref[j], half_ref[at])
 
 
-def stack(blocks, after):
+def stack(blocks, *after):
     count = len(blocks)
 
     def kernel(*refs):
-        out = refs[count + 1]
+        out = refs[-1]
         at = 0
         for n in range(count):
             head = blocks[n].shape[0]
@@ -152,11 +152,11 @@
     return pl.pallas_call(
         kernel,
         out_shape=jax.ShapeDtypeStruct(shape, blocks[0].dtype),
-        in_specs=[vmem] * count + [pl.BlockSpec(memory_space=pl.ANY)],
+        in_specs=[vmem] * count + [pl.BlockSpec(memory_space=pl.ANY)] * len(after),
         out_specs=vmem,
         compiler_params=params(4),
         cost_estimate=pl.CostEstimate(flops=0, bytes_accessed=10**6, transcendentals=0),
-    )(*blocks, after)
+    )(*blocks, *after)
 
 
 def unpack_kernel(pos_ref, *refs):
@@ -171,10 +171,6 @@
             w = jnp.where(jnp.logical_and(lane >= j * DW, lane < (j + 1) * DW), w, 0.0)
             total = total + pltpu.roll(w, lax.rem(p * DW - j * DW + lanes, lanes), axis=1)
         win_ref[j] = total
-
-
-def add_kernel(a_ref, b_ref, after_ref, out_ref):
-    out_ref[...] = a_ref[...] + b_ref[...]
 
 
 def payload_pieces(per_device, pairs, dests):
@@ -193,74 +189,91 @@
     return out
 
 
-def ladder_kernel(parts, occ_ref, win0_ref, win1_ref, *refs):
-    halves = refs[: len(parts)]
-    u_ref, lad_ref, _, out_ref, send_ref, w2_ref, ls_ref, pay_ref, max_ref = refs[len(parts) :]
-    step = pl.program_id(0)
+def ladder_kernel(
+    groups, occ_ref, win0, win1, win2, win3, part0, part1, u_ref, lad_ref, _, out_ref, send_ref,
+    w2_ref, hs_ref, pay_ref, code_ref, half_sems, send_sems, *ls_refs
+):
     occupied = occ_ref.shape[0]
-    pairs, _, virtuals = out_ref.shape
-    per_device = u_ref.shape[0]
-    dests = send_ref.shape[0]
+    pairs, per_device, virtuals = hs_ref.shape
+    dests = pay_ref.shape[0]
     tiles = virtuals // LANES
     labels, copies = labels_and_copies(occ_ref, occupied)
-
-    @pl.when(step == 0)
-    def _():
-        for i in range(occupied):
-            for j in range(occupied):
-                row = (labels[i] ^ labels[j]) * pairs + 2 * i + copies[j]
-                w = win0_ref[j, i : i + 1, :].astype(jnp.float32)
-                w2_ref[pl.ds(row, 1), :] = w + win1_ref[j, i : i + 1, :].astype(jnp.float32)
-        max_ref[...] = jnp.zeros_like(max_ref)
-
+    lane = lax.broadcasted_iota(jnp.int32, (8, LANES), 1)
+    for i in range(occupied):
+        for j in range(occupied):
+            row = (labels[i] ^ labels[j]) * pairs + 2 * i + copies[j]
+            at = slice(i, i + 1)
+            w = (win0[j, at, :] + win1[j, at, :]) + (win2[j, at, :] + win3[j, at, :])
+            w2_ref[pl.ds(row, 1), :] = w
     w2 = w2_ref[...].astype(jnp.bfloat16)
-    u8 = u_ref[pl.ds(pl.multiple_of(step * 8, 8), 8), :]
-    for a in range(8):
-        ladder = contract_last(w2, lad_ref[a])
-        ua = u8[a : a + 1, :]
-        sel = ladder[0:pairs]
+    sources = [(part, n) for part in (part0, part1) for n in range(part.shape[0])]
+    pieces_of = payload_pieces(per_device, pairs, dests)
+    tops = [jnp.zeros((8, LANES), jnp.float32)]
+
+    def ladder(g, a):
+        product = contract_last(w2, lad_ref[8 * g + a])
+        ua = u_ref[8 * g + a : 8 * g + a + 1, :]
+        sel = product[0:pairs]
         for v in range(1, 4):
-            sel = jnp.where(ua == v, ladder[v * pairs : (v + 1) * pairs], sel)
+            sel = jnp.where(ua == v, product[v * pairs : (v + 1) * pairs], sel)
         for v in range(tiles):
-            ls_ref[v, pl.ds(a, pairs, stride=8), :] = sel[:, v * LANES : (v + 1) * LANES]
-    sources = [(part, n) for part, count in zip(halves, parts) for n in range(2 * count)]
-    pieces_of = payload_pieces(per_device, pairs, dests)
-    lane = lax.broadcasted_iota(jnp.int32, (8, LANES), 1)
-    top = max_ref[...]
-    found = {}
-    for t in range(tiles):
-        last_e = min(((t + 1) * LANES - 1) // per_device, pairs - 1)
-        for e in range(t * LANES // per_device, last_e + 1):
-            if (e, 0) in found:
-                continue
-            part, n = sources[e]
-            for v in range(tiles):
-                at = slice(v * LANES, (v + 1) * LANES)
-                x = part[n, :, at] + ls_ref[v, 8 * e : 8 * e + 8, :]
-                out_ref[e, :, at] = x
-                top = jnp.maximum(top, jnp.abs(x))
-                found[e, v] = x
-        for q in range(dests):
-            acc = None
-            for first, e, v, shift in pieces_of[q, t]:
-                x = pltpu.roll(found[e, v], shift, axis=1) if shift else found[e, v]
-                acc = x if acc is None else jnp.where(lane >= first, x, acc)
-            at = pl.ds(pl.multiple_of(t * per_device + step * 8, 8), 8)
-            pay_ref[q, at, :] = acc
-    max_ref[...] = top
-
-    @pl.when(step == pl.num_programs(0) - 1)
-    def _():
-        most = jnp.max(jnp.max(max_ref[...], axis=0, keepdims=True), axis=1, keepdims=True)
-        k = jnp.floor(TOP_EXPONENT - jnp.log2(jnp.maximum(most, 1e-30)))
-        scale = jnp.exp2(k)
-        row = lax.broadcasted_iota(jnp.int32, pay_ref.shape[1:], 0)
-        for q in range(dests):
-            z = pay_ref[q] * scale
-            z2 = z * z
-            z4 = z2 * z2
-            y = jnp.where(row >= tiles * per_device, k, z4 * z4 * z)
-            send_ref[q] = y.astype(jnp.bfloat16)
+            ls_refs[g][v, pl.ds(a, pairs, stride=8), :] = sel[:, v * LANES : (v + 1) * LANES]
+
+    def payload(g):
+        rows = slice(8 * g, 8 * g + 8)
+        found = {}
+        for t in range(tiles):
+            last_e = min(((t + 1) * LANES - 1) // per_device, pairs - 1)
+            for e in range(t * LANES // per_device, last_e + 1):
+                if (e, 0) in found:
+                    continue
+                for v in range(tiles):
+                    at = slice(v * LANES, (v + 1) * LANES)
+                    x = sources[e][0][sources[e][1], rows, at] + ls_refs[g][v, 8 * e : 8 * e + 8, :]
+                    hs_ref[e, rows, at] = x
+                    tops[0] = jnp.maximum(tops[0], jnp.abs(x))
+                    found[e, v] = x
+            for q in range(dests):
+                acc = None
+                for first, e, v, shift in pieces_of[q, t]:
+                    x = pltpu.roll(found[e, v], shift, axis=1) if shift else found[e, v]
+                    acc = x if acc is None else jnp.where(lane >= first, x, acc)
+                start = t * per_device + 8 * g
+                pay_ref[q, start : start + 8, :] = acc
+                if q % 8 == 7:
+                    yield
+
+    stores = []
+    for g in range(groups + 1):
+        before = payload(g - 1) if g else iter(())
+        for a in range(8):
+            if g < groups:
+                ladder(g, a)
+            next(before, None)
+        for _ in before:
+            pass
+        if g:
+            rows = pl.ds(8 * (g - 1), 8)
+            store = pltpu.make_async_copy(
+                hs_ref.at[:, rows, :], out_ref.at[:, rows, :], half_sems.at[g - 1]
+            )
+            store.start()
+            stores.append(store)
+    most = jnp.max(jnp.max(tops[0], axis=0, keepdims=True), axis=1, keepdims=True)
+    k = jnp.floor(TOP_EXPONENT - jnp.log2(jnp.maximum(most, 1e-30)))
+    scale = jnp.exp2(k)
+    row = lax.broadcasted_iota(jnp.int32, pay_ref.shape[1:], 0)
+    for q in range(dests):
+        z = pay_ref[q] * scale
+        z2 = z * z
+        z4 = z2 * z2
+        y = jnp.where(row >= tiles * per_device, k, z4 * z4 * z)
+        code_ref[q] = y.astype(jnp.bfloat16)
+        store = pltpu.make_async_copy(code_ref.at[q], send_ref.at[q], send_sems.at[q])
+        store.start()
+        stores.append(store)
+    for store in stores:
+        store.wait()
 
 
 def cycle_kernel(pos_ref, occ_ref, own_ref, mate_ref, half_ref, u_ref, out_ref, orb_ref, cs_ref, xs_ref, ts_ref):
@@ -385,7 +398,7 @@
         ],
         out_specs=(whole((16, LANES)), whole((1, 2, rows, LANES))),
         scratch_shapes=[pltpu.VMEM((rows, LANES), f32)],
-        compiler_params=params(60),
+        compiler_params=params(58),
         cost_estimate=cost(0, 500000),
     )(cycle_ints.reshape(rows, LANES), amps)
     vmem = pl.BlockSpec(memory_space=pltpu.VMEM)
@@ -439,47 +452,33 @@
         cost_estimate=cost(0, 10**5),
     )(pos, *wins, half0)
 
-    def add(a, b, after):
-        return pl.pallas_call(
-            add_kernel,
-            out_shape=jax.ShapeDtypeStruct(a.shape, a.dtype),
-            in_specs=[vmem, vmem, anywhere],
-            out_specs=vmem,
-            compiler_params=params(4),
-            cost_estimate=cost(0, 10**5),
-        )(a, b, after)
-
-    win_y = permute(win, 2, dests)
+    wins = [win] + [permute(win, flip, dests) for flip in (1, 2, 3)]
     half1 = fock_part(1, win)
-    win = add(win, win_y, half1)
-    win_mate = permute(win, 1, dests)
-    near = stack(blocks, win)
+    near = stack(blocks, half1)
     near_y = permute(near, 2, dests)
 
     send_rows = tiles * per_device + 8
+    groups = per_device // 8
     half, send = pl.pallas_call(
-        functools.partial(ladder_kernel, parts),
-        grid=(per_device // 8,),
+        functools.partial(ladder_kernel, groups),
         out_shape=(
             jax.ShapeDtypeStruct((pairs, per_device, virtuals), f32),
             jax.ShapeDtypeStruct((dests, send_rows, LANES), bf16),
         ),
-        in_specs=[smem, whole(win_shape), whole(win_shape)]
-        + [pl.BlockSpec((2 * count, 8, virtuals), lambda n: (0, n, 0)) for count in parts]
-        + [whole((per_device, virtuals)), pl.BlockSpec((8, virtuals, kw), lambda n: (n, 0, 0)), anywhere],
-        out_specs=(
-            pl.BlockSpec((pairs, 8, virtuals), lambda n: (0, n, 0)),
-            whole((dests, send_rows, LANES)),
-        ),
+        in_specs=[smem] + [vmem] * 8 + [anywhere],
+        out_specs=(anywhere, anywhere),
         scratch_shapes=[
             pltpu.VMEM((occupied * occupied, LANES), f32),
-            pltpu.VMEM((tiles, 8 * pairs, LANES), f32),
+            pltpu.VMEM((pairs, per_device, virtuals), f32),
             pltpu.VMEM((dests, send_rows, LANES), f32),
-            pltpu.VMEM((8, LANES), f32),
-        ],
-        compiler_params=params(16),
+            pltpu.VMEM((dests, send_rows, LANES), bf16),
+            pltpu.SemaphoreType.DMA((groups,)),
+            pltpu.SemaphoreType.DMA((dests,)),
+        ]
+        + [pltpu.VMEM((tiles, 8 * pairs, LANES), f32)] * groups,
+        compiler_params=params(24),
         cost_estimate=cost(4 * occupied * rows * virtuals * LANES, 25 * 10**6),
-    )(occ_irrep, win, win_mate, half0, half1, u, ladder_ints, near)
+    )(occ_irrep, *wins, half0, half1, u, ladder_ints, near)
 
     recv = lax.all_to_all(send, "vir", split_axis=0, concat_axis=0, tiled=True)
     own_blocks = stack([near, near_y], send)

time: 68.2 us -> 79.3 us (1.16)
  waiting for transfers between devices: 16.8 us -> 30.5 us
  Pallas kernels: 28 us -> 26 us
  starting transfers between devices: 18.7 us -> 17.9 us
    ppermute x10 -> x11, waiting for transfers between devices: 4 us -> 17.7 us  [permute(): return lax.ppermute(x, 'vir', [(n, n ^ flip) for n in range(size)])]
    pallas_call x2 -> x1, Pallas kernels: 7.56 us -> 5.62 us  [body(): pl.pallas_call(functools.partial(ladder_kernel, groups), out_shape=(jax.S...]
    all_to_all x1, starting transfers between devices: 6.15 us -> 5.3 us  [body(): recv = lax.all_to_all(send, 'vir', split_axis=0, concat_axis=0, tiled=True)]
    ppermute x10 -> x11, starting transfers between devices: 12.6 us -> 12.6 us  [permute(): return lax.ppermute(x, 'vir', [(n, n ^ flip) for n in range(size)])]
  transfers between devices with their start and end apart: 11 -> 12, of which waited for: 4 -> 4; matrix products, arithmetic and copies ran while one was open for 0% -> 0% of each run, Pallas kernels for 30% -> 24%
where the time goes in v11:
time: 79.3 us; the launch traced here: 78.5 us
  waiting for transfers between devices  30.5 us (38%)
  Pallas kernels  26 us (33%)
  starting transfers between devices  17.9 us (23%)
  local copies, waits for them, and re-layouts  3.71 us (5%)
    ppermute x11, waiting for transfers between devices, permute(): return lax.ppermute(x, 'vir', [(n, n ^ flip) for n in range(size)])  17.7 us
    all_to_all x1, waiting for transfers between devices, body(): recv = lax.all_to_all(send, 'vir', split_axis=0, concat_axis=0, tiled=True)  12.8 us
    ppermute x11, starting transfers between devices, permute(): return lax.ppermute(x, 'vir', [(n, n ^ flip) for n in range(size)])  12.6 us
    pallas_call x2, Pallas kernels, fock_part(): pl.pallas_call(functools.partial(fock_kernel, first), grid=(count // wide...  7.42 us
    pallas_call x1, Pallas kernels, body(): pl.pallas_call(functools.partial(ladder_kernel, groups), out_shape=(jax.S...  5.62 us
    all_to_all x1, starting transfers between devices, body(): recv = lax.all_to_all(send, 'vir', split_axis=0, concat_axis=0, tiled=True)  5.3 us
    pallas_call x1, Pallas kernels, body(): pl.pallas_call(join_kernel, out_shape=jax.ShapeDtypeStruct((occupied, occ...  4.32 us
    unnamed x26, local copies, waits for them, and re-layouts  3.71 us
  transfers between devices with their start and end apart: 12, of which 4 were waited for; matrix products, arithmetic and copies ran while one was open for 0% of the time, Pallas kernels for 24%

profile of v11, /device:TPU:1, one launch (start us, length us, event | category | flops | bytes accessed | tf_op | source)
XLA Modules:
  0.0 78.5 jit_solution(4679380707288724147)
XLA Ops:
  0.0 2.2 %shard_map.74 = (bf16[16,128]{1,0:T(8,128)(2,1)}, bf16[1,2,320,128]{3,2,1,0:T(8,128)(2,1)}) custom-call(bf16[320,128]{1,0:T(8,128)(2,1)} %bitcast.7, bf16[8,8,40,640]{3,2,1,0:T(8,128)(2,1)} %amps_ref.1), custom_call_target="tpu_custom_call" | custom-call | bytes 500000 | tf_op jit(solution)/shard_map/pallas_call | solution.py:388
  2.2 4.2 %collective-permute-start.5 = (bf16[16,128]{1,0:T(8,128)(2,1)}, bf16[16,128]{1,0:T(8,128)(2,1)S(1)}, u32[]{:S(2)}, u32[]{:S(2)}) collective-permute-start(bf16[16,128]{1,0:T(8,128)(2,1)} %get-tuple-element.14.refs_0_), channel_id=1, source_target_pairs={{0,12},{1,13},{2,14},{3,15},{4,8},{5,9},{6,10},{7,11},{8,4},{9,5},... | collective-permute-start | bytes 12296 | tf_op jit(solution)/shard_map/ppermute | solution.py:366
  6.3 0.0 collective-permute-start.4
  6.4 0.3 collective-permute-start.3
  6.6 3.3 %collective-permute-start.2 = (bf16[1,2,320,128]{3,2,1,0:T(8,128)(2,1)}, bf16[1,2,320,128]{3,2,1,0:T(8,128)(2,1)S(1)}, u32[]{:S(2)}, u32[]{:S(2)}) collective-permute-start(bf16[1,2,320,128]{3,2,1,0:T(8,128)(2,1)} %get-tuple-element.12.refs_0_), channel_id=1, source_target_pairs={{0,12},{1,13},{2,14},{3,15},{4,8},{5,9},{6,10},{7,11},{8,4},{9,5},... | collective-permute-start | bytes 491528 | tf_op jit(solution)/shard_map/ppermute | solution.py:366
  9.9 0.0 copy-start.7
  9.9 0.7 copy-done.7
  10.6 0.7 copy-done.10
  11.3 1.0 %shard_map.73 = (bf16[320,320]{1,0:T(8,128)(2,1)S(1)}, s32[40,640]{1,0:T(8,128)S(1)}) custom-call(s32[1]{0:T(128)} %bitcast.pos_ref, s32[640]{0:T(1024)S(1)} %copy-done.7, bf16[8,8]{1,0:T(8,128)(2,1)S(1)} %copy-done.10, s32[1,640]{1,0:T(1,128)S(1)} %reshape.13.row_ref), custom_call_target="tpu_custom_call" | custom-call | flops 10000000 | bytes 300000 | tf_op jit(solution)/shard_map/pallas_call | solution.py:405
  12.3 0.3 collective-permute-start
  12.6 1.1 %copy-done.8 = bf16[640,640]{1,0:T(8,128)(2,1)S(1)} copy-done((bf16[640,640]{1,0:T(8,128)(2,1)S(1)}, bf16[640,640]{1,0:T(8,128)(2,1)}, u32[]{:S(2)}) %copy-start.8) | copy-done | bytes 819224
  13.8 3.7 %shard_map.75.refs_4_.part0 = f32[8,40,640]{2,1,0:T(8,128)S(1)} custom-call(s32[8]{0:T(128)S(1)} %copy-done.4, bf16[8,320,640]{2,1,0:T(8,128)(2,1)S(1)} %bitcast.5, bf16[640,640]{1,0:T(8,128)(2,1)S(1)} %copy-done.8, bf16[320,320]{1,0:T(8,128)(2,1)S(1)} %get-tuple-element.13.mix_ref.after_ref, s32[40,640]{1,0:T(8,128)S(1)} %get-tuple-element.11.u_ref, ...), custom_call_target="tpu_custom_call" | custom-call | flops 1572864000 | bytes 2000000 | tf_op jit(solution)/shard_map/pallas_call | solution.py:423
  17.5 0.8 %shard_map.76.after_ref.win0 = f32[8,8,128]{2,1,0:T(8,128)S(1)} custom-call(s32[1]{0:T(128)} %bitcast.pos_ref, bf16[16,128]{1,0:T(8,128)(2,1)S(1)} %copy-done.5, bf16[16,128]{1,0:T(8,128)(2,1)} %collective-permute-done.3.refs_1_, bf16[16,128]{1,0:T(8,128)(2,1)S(1)} %collective-permute-done.4.refs_2_, bf16[16,128]{1,0:T(8,128)(2,1)S(1)} %collective-permute-done.5.refs_3_, ...), custom_call_target="tpu_custom_call" | custom-call | bytes 100000 | tf_op jit(solution)/shard_map/pallas_call | solution.py:446
  18.3 0.0 copy-start.3
  18.3 0.0 slice-start.1
  18.4 3.7 %shard_map.77.refs_4_.part1 = f32[8,40,640]{2,1,0:T(8,128)S(1)} custom-call(s32[8]{0:T(128)S(1)} %copy-done.4, bf16[8,320,640]{2,1,0:T(8,128)(2,1)S(1)} %bitcast.6, bf16[640,640]{1,0:T(8,128)(2,1)S(1)} %copy-done.9, bf16[320,320]{1,0:T(8,128)(2,1)S(1)} %get-tuple-element.13.mix_ref.after_ref, s32[40,640]{1,0:T(8,128)S(1)} %get-tuple-element.11.u_ref, ...), custom_call_target="tpu_custom_call" | custom-call | flops 1572864000 | bytes 2000000 | tf_op jit(solution)/shard_map/pallas_call | solution.py:423
  22.1 1.5 %collective-permute-done.1.refs_2_ = bf16[1,2,320,128]{3,2,1,0:T(8,128)(2,1)} collective-permute-done((bf16[1,2,320,128]{3,2,1,0:T(8,128)(2,1)}, bf16[1,2,320,128]{3,2,1,0:T(8,128)(2,1)}, u32[]{:S(2)}, u32[]{:S(2)}) %collective-permute-start.1) | collective-permute-done | bytes 163872 | tf_op jit(solution)/shard_map/ppermute | solution.py:366
  23.6 1.0 %shard_map.78._.refs_0_ = bf16[4,2,320,128]{3,2,1,0:T(8,128)(2,1)S(1)} custom-call(bf16[1,2,320,128]{3,2,1,0:T(8,128)(2,1)S(1)} %copy-done.3, bf16[1,2,320,128]{3,2,1,0:T(8,128)(2,1)S(1)} %collective-permute-done.refs_1_, bf16[1,2,320,128]{3,2,1,0:T(8,128)(2,1)} %collective-permute-done.1.refs_2_, ...), custom_call_target="tpu_custom_call" | custom-call | bytes 1000000 | tf_op jit(solution)/shard_map/pallas_call | solution.py:152
  24.6 1.3 %collective-permute-start.6 = (bf16[4,2,320,128]{3,2,1,0:T(8,128)(2,1)S(1)}, bf16[4,2,320,128]{3,2,1,0:T(8,128)(2,1)S(1)}, u32[]{:S(2)}, u32[]{:S(2)}) collective-permute-start(bf16[4,2,320,128]{3,2,1,0:T(8,128)(2,1)S(1)} %shard_map.78._.refs_0_), channel_id=1, source_target_pairs={{0,2},{1,3},{2,0},{3,1},{4,6},{5,7},{6,4},{7,5},{8,10},{9,11},{10,... | collective-permute-start | bytes 1966088 | tf_op jit(solution)/shard_map/ppermute | solution.py:366
  25.9 1.8 %collective-permute-start.9 = (f32[8,8,128]{2,1,0:T(8,128)S(1)}, f32[8,8,128]{2,1,0:T(8,128)S(1)}, u32[]{:S(2)}, u32[]{:S(2)}) collective-permute-start(f32[8,8,128]{2,1,0:T(8,128)S(1)} %shard_map.76.after_ref.win0), channel_id=1, source_target_pairs={{0,3},{1,2},{2,1},{3,0},{4,7},{5,6},{6,5},{7,4},{8,11},{9,10},{10,... | collective-permute-start | bytes 98312 | tf_op jit(solution)/shard_map/ppermute | solution.py:366
  27.8 1.2 %collective-permute-start.8 = (f32[8,8,128]{2,1,0:T(8,128)S(1)}, f32[8,8,128]{2,1,0:T(8,128)S(1)}, u32[]{:S(2)}, u32[]{:S(2)}) collective-permute-start(f32[8,8,128]{2,1,0:T(8,128)S(1)} %shard_map.76.after_ref.win0), channel_id=1, source_target_pairs={{0,2},{1,3},{2,0},{3,1},{4,6},{5,7},{6,4},{7,5},{8,10},{9,11},{10,... | collective-permute-start | bytes 98312 | tf_op jit(solution)/shard_map/ppermute | solution.py:366
  29.0 13.2 %collective-permute-done.9.win3 = f32[8,8,128]{2,1,0:T(8,128)S(1)} collective-permute-done((f32[8,8,128]{2,1,0:T(8,128)S(1)}, f32[8,8,128]{2,1,0:T(8,128)S(1)}, u32[]{:S(2)}, u32[]{:S(2)}) %collective-permute-start.9) | collective-permute-done | bytes 32800 | tf_op jit(solution)/shard_map/ppermute | solution.py:366
  42.2 5.6 %shard_map.79 = (f32[16,40,640]{2,1,0:T(8,128)S(1)}, bf16[16,208,128]{2,1,0:T(8,128)(2,1)}) custom-call(s32[8]{0:T(128)S(1)} %copy-done.4, f32[8,8,128]{2,1,0:T(8,128)S(1)} %shard_map.76.after_ref.win0, f32[8,8,128]{2,1,0:T(8,128)S(1)} %collective-permute-done.7.win1, f32[8,8,128]{2,1,0:T(8,128)S(1)} %collective-permute-done.8.win2, ...), custom_call_target="tpu_custom_call" | custom-call | flops 838860800 | bytes 25000000 | tf_op jit(solution)/shard_map/pallas_call | solution.py:462
  47.8 0.0 copy-start.1
  47.9 1.2 %copy-done.1 = f32[16,40,640]{2,1,0:T(8,128)} copy-done((f32[16,40,640]{2,1,0:T(8,128)}, f32[16,40,640]{2,1,0:T(8,128)S(1)}, u32[]{:S(2)}) %copy-start.1) | copy-done | bytes 1638424
  49.0 5.3 %all-to-all-start = ((bf16[16,208,128]{2,1,0:T(8,128)(2,1)}), bf16[16,208,128]{2,1,0:T(8,128)(2,1)S(1)}, u32[]{:S(2)}, u32[]{:S(2)}) async-start(bf16[16,208,128]{2,1,0:T(8,128)(2,1)} %get-tuple-element.15.refs_2_), calls=%async_computation | async-start | bytes 1703936 | tf_op jit(solution)/shard_map/all_to_all | solution.py:483
  54.3 0.1 shard_map.80.own_ref
  54.4 0.2 collective-permute-start.10
  54.6 2.9 %collective-permute-done.10.mate_ref = bf16[8,2,320,128]{3,2,1,0:T(8,128)(2,1)S(1)} collective-permute-done((bf16[8,2,320,128]{3,2,1,0:T(8,128)(2,1)S(1)}, bf16[8,2,320,128]{3,2,1,0:T(8,128)(2,1)S(1)}, u32[]{:S(2)}, u32[]{:S(2)}) %collective-permute-start.10) | collective-permute-done | bytes 1310752 | tf_op jit(solution)/shard_map/ppermute | solution.py:366
  57.5 3.6 %shard_map.81.half_ref = f32[16,40,640]{2,1,0:T(8,128)S(1)} custom-call(s32[1]{0:T(128)} %bitcast.pos_ref, s32[8]{0:T(128)S(1)} %copy-done.4, bf16[8,2,320,128]{3,2,1,0:T(8,128)(2,1)S(1)} %shard_map.80.own_ref, bf16[8,2,320,128]{3,2,1,0:T(8,128)(2,1)S(1)} %collective-permute-done.10.mate_ref, f32[16,40,640]{2,1,0:T(8,128)S(1)} %copy-done.2, ...), custom_call_target="tpu_custom_call" | custom-call | flops 1000 | bytes 1000 | tf_op jit(solution)/shard_map/pallas_call | solution.py:486
  61.2 12.8 %all-to-all-done.recv_ref = bf16[16,208,128]{2,1,0:T(8,128)(2,1)S(1)} async-done(((bf16[16,208,128]{2,1,0:T(8,128)(2,1)}), bf16[16,208,128]{2,1,0:T(8,128)(2,1)S(1)}, u32[]{:S(2)}, u32[]{:S(2)}) %all-to-all-start) | async-done | bytes 852000 | tf_op jit(solution)/shard_map/all_to_all | solution.py:483
  74.0 4.3 %shard_map.82 = f32[8,8,40,640]{3,2,1,0:T(8,128)} custom-call(s32[8]{0:T(128)S(1)} %copy-done.4, s32[40,640]{1,0:T(8,128)S(1)} %get-tuple-element.11.u_ref, f32[16,40,640]{2,1,0:T(8,128)S(1)} %shard_map.81.half_ref, bf16[16,208,128]{2,1,0:T(8,128)(2,1)S(1)} %all-to-all-done.recv_ref), custom_call_target="tpu_custom_call" | custom-call | flops 1000000 | bytes 5000000 | tf_op jit(solution)/shard_map/pallas_call | solution.py:501
  (30 shorter events, 0.1 us)
Async XLA Ops:
  0.0 9.9 %copy-start.6 = (s32[640]{0:T(1024)S(1)}, s32[640]{0:T(1024)}, u32[]{:S(2)}) copy-start(s32[640]{0:T(1024)} %vir_ref.1) | copy-start | bytes 7684
  0.0 12.6 %copy-start = (bf16[8,8,40,640]{3,2,1,0:T(8,128)(2,1)S(1)}, bf16[8,8,40,640]{3,2,1,0:T(8,128)(2,1)}, u32[]{:S(2)}) copy-start(bf16[8,8,40,640]{3,2,1,0:T(8,128)(2,1)} %amps_ref.1) | copy-start | bytes 9830404
  0.0 12.6 %copy-start.4 = (s32[8]{0:T(128)S(1)}, s32[8]{0:T(128)}, u32[]{:S(2)}) copy-start(s32[8]{0:T(128)} %occ_ref.9) | copy-start | bytes 100
  2.2 10.1 %collective-permute-start.5 = (bf16[16,128]{1,0:T(8,128)(2,1)}, bf16[16,128]{1,0:T(8,128)(2,1)S(1)}, u32[]{:S(2)}, u32[]{:S(2)}) collective-permute-start(bf16[16,128]{1,0:T(8,128)(2,1)} %get-tuple-element.14.refs_0_), channel_id=1, source_target_pairs={{0,12},{1,13},{2,14},{3,15},{4,8},{5,9},{6,10},{7,11},{8,4},{9,5},... | collective-permute-start | bytes 12296 | tf_op jit(solution)/shard_map/ppermute | solution.py:366
  6.3 11.1 %collective-permute-start.4 = (bf16[16,128]{1,0:T(8,128)(2,1)}, bf16[16,128]{1,0:T(8,128)(2,1)S(1)}, u32[]{:S(2)}, u32[]{:S(2)}) collective-permute-start(bf16[16,128]{1,0:T(8,128)(2,1)} %get-tuple-element.14.refs_0_), channel_id=1, source_target_pairs={{0,8},{1,9},{2,10},{3,11},{4,12},{5,13},{6,14},{7,15},{8,0},{9,1},... | collective-permute-start | bytes 12296 | tf_op jit(solution)/shard_map/ppermute | solution.py:366
  6.4 11.1 %collective-permute-start.3 = (bf16[16,128]{1,0:T(8,128)(2,1)}, bf16[16,128]{1,0:T(8,128)(2,1)}, u32[]{:S(2)}, u32[]{:S(2)}) collective-permute-start(bf16[16,128]{1,0:T(8,128)(2,1)} %get-tuple-element.14.refs_0_), channel_id=1, source_target_pairs={{0,4},{1,5},{2,6},{3,7},{4,0},{5,1},{6,2},{7,3},{8,12},{9,13},{10,... | collective-permute-start | bytes 12296 | tf_op jit(solution)/shard_map/ppermute | solution.py:366
  6.6 15.4 %collective-permute-start.2 = (bf16[1,2,320,128]{3,2,1,0:T(8,128)(2,1)}, bf16[1,2,320,128]{3,2,1,0:T(8,128)(2,1)S(1)}, u32[]{:S(2)}, u32[]{:S(2)}) collective-permute-start(bf16[1,2,320,128]{3,2,1,0:T(8,128)(2,1)} %get-tuple-element.12.refs_0_), channel_id=1, source_target_pairs={{0,12},{1,13},{2,14},{3,15},{4,8},{5,9},{6,10},{7,11},{8,4},{9,5},... | collective-permute-start | bytes 491528 | tf_op jit(solution)/shard_map/ppermute | solution.py:366
  9.9 13.7 %collective-permute-start.1 = (bf16[1,2,320,128]{3,2,1,0:T(8,128)(2,1)}, bf16[1,2,320,128]{3,2,1,0:T(8,128)(2,1)}, u32[]{:S(2)}, u32[]{:S(2)}) collective-permute-start(bf16[1,2,320,128]{3,2,1,0:T(8,128)(2,1)} %get-tuple-element.12.refs_0_), channel_id=1, source_target_pairs={{0,8},{1,9},{2,10},{3,11},{4,12},{5,13},{6,14},{7,15},{8,0},{9,1},... | collective-permute-start | bytes 491528 | tf_op jit(solution)/shard_map/ppermute | solution.py:366
  9.9 0.7 copy-start.7
  10.6 0.7 copy-start.10
  12.3 11.4 %collective-permute-start = (bf16[1,2,320,128]{3,2,1,0:T(8,128)(2,1)}, bf16[1,2,320,128]{3,2,1,0:T(8,128)(2,1)S(1)}, u32[]{:S(2)}, u32[]{:S(2)}) collective-permute-start(bf16[1,2,320,128]{3,2,1,0:T(8,128)(2,1)} %get-tuple-element.12.refs_0_), channel_id=1, source_target_pairs={{0,4},{1,5},{2,6},{3,7},{4,0},{5,1},{6,2},{7,3},{8,12},{9,13},{10,... | collective-permute-start | bytes 491528 | tf_op jit(solution)/shard_map/ppermute | solution.py:366
  12.6 1.1 %copy-start.8 = (bf16[640,640]{1,0:T(8,128)(2,1)S(1)}, bf16[640,640]{1,0:T(8,128)(2,1)}, u32[]{:S(2)}) copy-start(bf16[640,640]{1,0:T(8,128)(2,1)} %fock_ref.3) | copy-start | bytes 2457604
  13.8 3.7 %copy-start.5 = (bf16[16,128]{1,0:T(8,128)(2,1)S(1)}, bf16[16,128]{1,0:T(8,128)(2,1)}, u32[]{:S(2)}) copy-start(bf16[16,128]{1,0:T(8,128)(2,1)} %get-tuple-element.14.refs_0_) | copy-start | bytes 12292
  13.8 4.5 %copy-start.9 = (bf16[640,640]{1,0:T(8,128)(2,1)S(1)}, bf16[640,640]{1,0:T(8,128)(2,1)}, u32[]{:S(2)}) copy-start(bf16[640,640]{1,0:T(8,128)(2,1)} %fock_ref.3) | copy-start | bytes 2457604
  13.8 28.4 %slice-start = ((s8[6553600]{0:T(1024)(128)(4,1)}), s8[4194304]{0:T(1024)(128)(4,1)S(1)}, s32[]{:S(2)}) async-start(s8[6553600]{0:T(1024)(128)(4,1)} %bitcast.3), calls=%async_computation.1 | async-start | bytes 8388608
  18.3 5.3 %copy-start.3 = (bf16[1,2,320,128]{3,2,1,0:T(8,128)(2,1)S(1)}, bf16[1,2,320,128]{3,2,1,0:T(8,128)(2,1)}, u32[]{:S(2)}) copy-start(bf16[1,2,320,128]{3,2,1,0:T(8,128)(2,1)} %get-tuple-element.12.refs_0_) | copy-start | bytes 491524
  18.3 23.9 %slice-start.1 = ((s8[6553600]{0:T(1024)(128)(4,1)}), s8[2359296]{0:T(1024)(128)(4,1)S(1)}, s32[]{:S(2)}) async-start(s8[6553600]{0:T(1024)(128)(4,1)} %bitcast.3), calls=%async_computation.2 | async-start | bytes 4718592
  24.6 29.7 %collective-permute-start.6 = (bf16[4,2,320,128]{3,2,1,0:T(8,128)(2,1)S(1)}, bf16[4,2,320,128]{3,2,1,0:T(8,128)(2,1)S(1)}, u32[]{:S(2)}, u32[]{:S(2)}) collective-permute-start(bf16[4,2,320,128]{3,2,1,0:T(8,128)(2,1)S(1)} %shard_map.78._.refs_0_), channel_id=1, source_target_pairs={{0,2},{1,3},{2,0},{3,1},{4,6},{5,7},{6,4},{7,5},{8,10},{9,11},{10,... | collective-permute-start | bytes 1966088 | tf_op jit(solution)/shard_map/ppermute | solution.py:366
  25.9 16.3 %collective-permute-start.9 = (f32[8,8,128]{2,1,0:T(8,128)S(1)}, f32[8,8,128]{2,1,0:T(8,128)S(1)}, u32[]{:S(2)}, u32[]{:S(2)}) collective-permute-start(f32[8,8,128]{2,1,0:T(8,128)S(1)} %shard_map.76.after_ref.win0), channel_id=1, source_target_pairs={{0,3},{1,2},{2,1},{3,0},{4,7},{5,6},{6,5},{7,4},{8,11},{9,10},{10,... | collective-permute-start | bytes 98312 | tf_op jit(solution)/shard_map/ppermute | solution.py:366
  27.8 14.4 %collective-permute-start.8 = (f32[8,8,128]{2,1,0:T(8,128)S(1)}, f32[8,8,128]{2,1,0:T(8,128)S(1)}, u32[]{:S(2)}, u32[]{:S(2)}) collective-permute-start(f32[8,8,128]{2,1,0:T(8,128)S(1)} %shard_map.76.after_ref.win0), channel_id=1, source_target_pairs={{0,2},{1,3},{2,0},{3,1},{4,6},{5,7},{6,4},{7,5},{8,10},{9,11},{10,... | collective-permute-start | bytes 98312 | tf_op jit(solution)/shard_map/ppermute | solution.py:366
  29.0 13.2 %collective-permute-start.7 = (f32[8,8,128]{2,1,0:T(8,128)S(1)}, f32[8,8,128]{2,1,0:T(8,128)S(1)}, u32[]{:S(2)}, u32[]{:S(2)}) collective-permute-start(f32[8,8,128]{2,1,0:T(8,128)S(1)} %shard_map.76.after_ref.win0), channel_id=1, source_target_pairs={{0,1},{1,0},{2,3},{3,2},{4,5},{5,4},{6,7},{7,6},{8,9},{9,8},{10,11... | collective-permute-start | bytes 98312 | tf_op jit(solution)/shard_map/ppermute | solution.py:366
  47.8 1.2 %copy-start.1 = (f32[16,40,640]{2,1,0:T(8,128)}, f32[16,40,640]{2,1,0:T(8,128)S(1)}, u32[]{:S(2)}) copy-start(f32[16,40,640]{2,1,0:T(8,128)S(1)} %get-tuple-element.16.half_ref) | copy-start | bytes 4915204
  49.0 25.0 %all-to-all-start = ((bf16[16,208,128]{2,1,0:T(8,128)(2,1)}), bf16[16,208,128]{2,1,0:T(8,128)(2,1)S(1)}, u32[]{:S(2)}, u32[]{:S(2)}) async-start(bf16[16,208,128]{2,1,0:T(8,128)(2,1)} %get-tuple-element.15.refs_2_), calls=%async_computation | async-start | bytes 1703936 | tf_op jit(solution)/shard_map/all_to_all | solution.py:483
  54.3 3.2 %copy-start.2 = (f32[16,40,640]{2,1,0:T(8,128)S(1)}, f32[16,40,640]{2,1,0:T(8,128)}, u32[]{:S(2)}) copy-start(f32[16,40,640]{2,1,0:T(8,128)} %copy-done.1) | copy-start | bytes 4915204
  54.4 3.1 %collective-permute-start.10 = (bf16[8,2,320,128]{3,2,1,0:T(8,128)(2,1)S(1)}, bf16[8,2,320,128]{3,2,1,0:T(8,128)(2,1)S(1)}, u32[]{:S(2)}, u32[]{:S(2)}) collective-permute-start(bf16[8,2,320,128]{3,2,1,0:T(8,128)(2,1)S(1)} %shard_map.80.own_ref), channel_id=1, source_target_pairs={{0,1},{1,0},{2,3},{3,2},{4,5},{5,4},{6,7},{7,6},{8,9},{9,8},{10,11... | collective-permute-start | bytes 3932168 | tf_op jit(solution)/shard_map/ppermute | solution.py:366

commit v12 on v11

--- a/solution.py
+++ b/solution.py
@@ -75,29 +75,20 @@
     return labels, copies
 
 
-def prep_kernel(cyc_ref, amps_ref, win_ref, xt_ref, t_ref):
-    occupied, _, per_device, _ = amps_ref.shape
-    xt_ref[0, 0] = cyc_ref[...]
+def prep_kernel(cyc_ref, amps_ref, block_ref):
+    occupied = amps_ref.shape[0]
+    rows = cyc_ref.shape[0]
+    block_ref[:rows, :] = cyc_ref[...]
     lane = lax.broadcasted_iota(jnp.int32, (occupied, LANES), 1)
     packed = jnp.zeros((occupied, LANES), jnp.float32)
     for j in range(occupied):
         w = jnp.where(lane < DW, amps_ref[:, j, 0, :].astype(jnp.float32), 0.0)
         packed = packed + (pltpu.roll(w, j * DW, axis=1) if j else w)
     packed = jnp.concatenate([packed, jnp.zeros_like(packed)], axis=0)
-    win_ref[...] = packed.astype(jnp.bfloat16)
-    lane = lax.broadcasted_iota(jnp.int32, (per_device, LANES), 1)
-    for i in range(occupied):
-        acc = jnp.zeros((per_device, LANES), jnp.float32)
-        for k in range(occupied):
-            piece = jnp.where(lane < CW, amps_ref[i, k].astype(jnp.float32), 0.0)
-            acc = acc + (pltpu.roll(piece, k * CW, axis=1) if k else piece)
-        t_ref[i * per_device : (i + 1) * per_device, :] = acc
-    xt_ref[0, 1] = t_ref[...].astype(jnp.bfloat16)
-
-
-def setup_kernel(pos_ref, vir_ref, occ_vals_ref, row_ref, mix_ref, u_ref):
-    for a in range(u_ref.shape[0]):
-        u_ref[a : a + 1, :] = row_ref[...] ^ vir_ref[pos_ref[0] * u_ref.shape[0] + a]
+    block_ref[rows:, :] = packed.astype(jnp.bfloat16)
+
+
+def mix_kernel(occ_vals_ref, mix_ref):
     rows = mix_ref.shape[0]
     occupied = occ_vals_ref.shape[0]
     per_device = rows // occupied
@@ -115,7 +106,7 @@
     mix_ref[...] = mix.astype(jnp.bfloat16)
 
 
-def fock_kernel(first, occ_ref, amps_ref, fock_ref, mix_ref, u_ref, after_ref, half_ref, hs_ref):
+def fock_kernel(first, occ_ref, amps_ref, fock_ref, mix_ref, u_ref, after_ref, half_ref, cyc_ref, hs_ref):
     wide, rows, virtuals = amps_ref.shape
     _, per_device, _ = half_ref.shape
     occupied = occ_ref.shape[0]
@@ -134,13 +125,20 @@
         for j in range(occupied):
             at = 2 * w + copies[j]
             half_ref[at] = jnp.where(u == (own ^ labels[j]), hs_ref[j], half_ref[at])
-
-
-def stack(blocks, *after):
+        head = a[:, :LANES].astype(jnp.float32)
+        lane = lax.broadcasted_iota(jnp.int32, (per_device, LANES), 1)
+        acc = jnp.zeros((per_device, LANES), jnp.float32)
+        for k in range(occupied):
+            piece = jnp.where(lane < CW, head[k * per_device : (k + 1) * per_device], 0.0)
+            acc = acc + (pltpu.roll(piece, k * CW, axis=1) if k else piece)
+        cyc_ref[w] = acc.astype(jnp.bfloat16)
+
+
+def stack(blocks, after):
     count = len(blocks)
 
     def kernel(*refs):
-        out = refs[-1]
+        out = refs[count + 1]
         at = 0
         for n in range(count):
             head = blocks[n].shape[0]
@@ -152,25 +150,11 @@
     return pl.pallas_call(
         kernel,
         out_shape=jax.ShapeDtypeStruct(shape, blocks[0].dtype),
-        in_specs=[vmem] * count + [pl.BlockSpec(memory_space=pl.ANY)] * len(after),
+        in_specs=[vmem] * count + [pl.BlockSpec(memory_space=pl.ANY)],
         out_specs=vmem,
         compiler_params=params(4),
         cost_estimate=pl.CostEstimate(flops=0, bytes_accessed=10**6, transcendentals=0),
-    )(*blocks, *after)
-
-
-def unpack_kernel(pos_ref, *refs):
-    blocks, win_ref = refs[:-2], refs[-1]
-    occupied, _, lanes = win_ref.shape
-    lane = lax.broadcasted_iota(jnp.int32, (8, lanes), 1)
-    for j in range(occupied):
-        total = jnp.zeros((8, lanes), jnp.float32)
-        for m, block in enumerate(blocks):
-            p = pos_ref[0] ^ (m << 2)
-            w = block[...].astype(jnp.float32)[:8]
-            w = jnp.where(jnp.logical_and(lane >= j * DW, lane < (j + 1) * DW), w, 0.0)
-            total = total + pltpu.roll(w, lax.rem(p * DW - j * DW + lanes, lanes), axis=1)
-        win_ref[j] = total
+    )(*blocks, after)
 
 
 def payload_pieces(per_device, pairs, dests):
@@ -189,24 +173,41 @@
     return out
 
 
-def ladder_kernel(
-    groups, occ_ref, win0, win1, win2, win3, part0, part1, u_ref, lad_ref, _, out_ref, send_ref,
-    w2_ref, hs_ref, pay_ref, code_ref, half_sems, send_sems, *ls_refs
-):
+def half_kernel(groups, parts, pos_ref, occ_ref, own_ref, mate_ref, *refs):
+    halves, refs = refs[: len(parts)], refs[len(parts) :]
+    cycs, refs = refs[: len(parts)], refs[len(parts) :]
+    u_ref, lad_ref, out_ref, send_ref, orb_ref, w2_ref, xs_ref, cs_ref, pay_ref = refs[:9]
+    ls_refs = refs[9:]
     occupied = occ_ref.shape[0]
-    pairs, per_device, virtuals = hs_ref.shape
+    pairs, per_device, virtuals = out_ref.shape
     dests = pay_ref.shape[0]
     tiles = virtuals // LANES
+    rows = occupied * per_device
     labels, copies = labels_and_copies(occ_ref, occupied)
     lane = lax.broadcasted_iota(jnp.int32, (8, LANES), 1)
-    for i in range(occupied):
-        for j in range(occupied):
+
+    def block_of(r):
+        ref = mate_ref if r & 1 else own_ref
+        return ref[((r >> 1) & 1) * (dests // 4) + (r >> 2)]
+
+    packed = [block_of(r)[rows:].astype(jnp.float32)[:8] for r in range(dests)]
+    for j in range(occupied):
+        orb_ref[2 * labels[j] + copies[j]] = jnp.int32(j)
+        window = jnp.zeros((8, LANES), jnp.float32)
+        for r in range(dests):
+            w = jnp.where(jnp.logical_and(lane >= j * DW, lane < (j + 1) * DW), packed[r], 0.0)
+            shift = lax.rem((pos_ref[0] ^ r) * DW - j * DW + LANES, LANES)
+            window = window + pltpu.roll(w, shift, axis=1)
+        for i in range(occupied):
             row = (labels[i] ^ labels[j]) * pairs + 2 * i + copies[j]
-            at = slice(i, i + 1)
-            w = (win0[j, at, :] + win1[j, at, :]) + (win2[j, at, :] + win3[j, at, :])
-            w2_ref[pl.ds(row, 1), :] = w
+            w2_ref[pl.ds(row, 1), :] = window[i : i + 1, :]
     w2 = w2_ref[...].astype(jnp.bfloat16)
-    sources = [(part, n) for part in (part0, part1) for n in range(part.shape[0])]
+    left = jnp.concatenate([ref[...].astype(jnp.float32) for ref in cycs], axis=0)
+    left = left.reshape(rows, LANES).astype(jnp.bfloat16)
+    choices = [
+        [orb_ref[2 * (labels[e // 2] ^ n) + e % 2] for n in range(4)] for e in range(pairs)
+    ]
+    sources = [(part, n) for part in halves for n in range(part.shape[0])]
     pieces_of = payload_pieces(per_device, pairs, dests)
     tops = [jnp.zeros((8, LANES), jnp.float32)]
 
@@ -219,18 +220,36 @@
         for v in range(tiles):
             ls_refs[g][v, pl.ds(a, pairs, stride=8), :] = sel[:, v * LANES : (v + 1) * LANES]
 
+    def gathered():
+        for r in range(dests):
+            x = block_of(r)[:rows].astype(jnp.float32).reshape(per_device, occupied, LANES)
+            xs_ref[pl.ds((pos_ref[0] ^ r) * per_device, per_device)] = x
+            if r % 2:
+                yield
+
+    def cycle():
+        for j in range(occupied):
+            c = contract_last(left, xs_ref[:, j, :].astype(jnp.bfloat16))
+            cs_ref[j] = c.reshape(occupied, per_device, virtuals)
+            yield
+
     def payload(g):
-        rows = slice(8 * g, 8 * g + 8)
+        group = slice(8 * g, 8 * g + 8)
         found = {}
         for t in range(tiles):
             last_e = min(((t + 1) * LANES - 1) // per_device, pairs - 1)
             for e in range(t * LANES // per_device, last_e + 1):
                 if (e, 0) in found:
                     continue
+                part, n = sources[e]
                 for v in range(tiles):
                     at = slice(v * LANES, (v + 1) * LANES)
-                    x = sources[e][0][sources[e][1], rows, at] + ls_refs[g][v, 8 * e : 8 * e + 8, :]
-                    hs_ref[e, rows, at] = x
+                    uv = u_ref[group, at]
+                    x = cs_ref[choices[e][0], e // 2, group, at]
+                    for m in range(1, 4):
+                        x = jnp.where(uv == m, cs_ref[choices[e][m], e // 2, group, at], x)
+                    x = x + (part[n, group, at] + ls_refs[g][v, 8 * e : 8 * e + 8, :])
+                    out_ref[e, group, at] = x
                     tops[0] = jnp.maximum(tops[0], jnp.abs(x))
                     found[e, v] = x
             for q in range(dests):
@@ -243,22 +262,14 @@
                 if q % 8 == 7:
                     yield
 
-    stores = []
-    for g in range(groups + 1):
-        before = payload(g - 1) if g else iter(())
+    others = [gathered(), cycle()] + [payload(g) for g in range(groups)]
+    for g, other in enumerate(others):
         for a in range(8):
             if g < groups:
                 ladder(g, a)
-            next(before, None)
-        for _ in before:
+            next(other, None)
+        for _ in other:
             pass
-        if g:
-            rows = pl.ds(8 * (g - 1), 8)
-            store = pltpu.make_async_copy(
-                hs_ref.at[:, rows, :], out_ref.at[:, rows, :], half_sems.at[g - 1]
-            )
-            store.start()
-            stores.append(store)
     most = jnp.max(jnp.max(tops[0], axis=0, keepdims=True), axis=1, keepdims=True)
     k = jnp.floor(TOP_EXPONENT - jnp.log2(jnp.maximum(most, 1e-30)))
     scale = jnp.exp2(k)
@@ -268,57 +279,7 @@
         z2 = z * z
         z4 = z2 * z2
         y = jnp.where(row >= tiles * per_device, k, z4 * z4 * z)
-        code_ref[q] = y.astype(jnp.bfloat16)
-        store = pltpu.make_async_copy(code_ref.at[q], send_ref.at[q], send_sems.at[q])
-        store.start()
-        stores.append(store)
-    for store in stores:
-        store.wait()
-
-
-def cycle_kernel(pos_ref, occ_ref, own_ref, mate_ref, half_ref, u_ref, out_ref, orb_ref, cs_ref, xs_ref, ts_ref):
-    occupied = occ_ref.shape[0]
-    pairs, per_device, virtuals = half_ref.shape
-    quads, _, rows, _ = own_ref.shape
-    dests = 2 * quads
-    tiles = virtuals // LANES
-    labels, copies = labels_and_copies(occ_ref, occupied)
-    for j in range(occupied):
-        orb_ref[2 * labels[j] + copies[j]] = jnp.int32(j)
-    for r in range(dests):
-        ref = mate_ref if r & 1 else own_ref
-        n = ((r >> 1) & 1) * (dests // 4) + (r >> 2)
-        p = pos_ref[0] ^ r
-        x = ref[n, 0].astype(jnp.float32).reshape(per_device, occupied, LANES)
-        xs_ref[pl.ds(p * per_device, per_device)] = x
-        t = ref[n, 1].astype(jnp.float32)
-        at = pl.ds(pl.multiple_of(p * per_device, 8), per_device)
-        for j in range(occupied):
-            ts_ref[j, at, :] = t[j * per_device : (j + 1) * per_device]
-    here = pl.ds(pos_ref[0] * per_device, per_device)
-    x_left = jnp.concatenate([xs_ref[here, i, :] for i in range(occupied)], axis=0)
-    left = jnp.concatenate([own_ref[0, 1], x_left.astype(jnp.bfloat16)], axis=1)
-    for j in range(occupied):
-        right = jnp.concatenate([xs_ref[:, j, :], ts_ref[j]], axis=1).astype(jnp.bfloat16)
-        cs_ref[j] = contract_last(left, right).reshape(occupied, per_device, virtuals)
-    choices = [
-        [orb_ref[2 * (labels[e // 2] ^ n) + e % 2] for n in range(4)] for e in range(pairs)
-    ]
-
-    def group(g, carry):
-        rows = pl.ds(pl.multiple_of(g * 8, 8), 8)
-        for v in range(tiles):
-            at = slice(v * LANES, (v + 1) * LANES)
-            uv = u_ref[rows, at]
-            masks = [uv == n for n in range(1, 4)]
-            for e in range(pairs):
-                x = cs_ref[choices[e][0], e // 2, rows, at]
-                for n in range(1, 4):
-                    x = jnp.where(masks[n - 1], cs_ref[choices[e][n], e // 2, rows, at], x)
-                out_ref[e, rows, at] = half_ref[e, rows, at] + x
-        return carry
-
-    lax.fori_loop(0, per_device // 8, group, 0)
+        send_ref[q] = y.astype(jnp.bfloat16)
 
 
 def join_kernel(occ_ref, u_ref, half_ref, recv_ref, out_ref, dec_ref, mir_ref, res_ref, sems):
@@ -375,6 +336,8 @@
     f32, bf16 = jnp.float32, jnp.bfloat16
     position = lax.axis_index("vir").astype(jnp.int32)
     pos = position.reshape(1)
+    vir_local = lax.dynamic_slice_in_dim(vir_irrep, position * per_device, per_device)
+    u = jnp.bitwise_xor(vir_local[:, None], vir_irrep[None, :])
     smem = pl.BlockSpec(memory_space=pltpu.SMEM)
 
     def whole(shape):
@@ -385,37 +348,32 @@
 
     anywhere = pl.BlockSpec(memory_space=pl.ANY)
     quarter = dests // 4
-    win, xt = pl.pallas_call(
+    block_rows = rows + 16
+    block = pl.pallas_call(
         prep_kernel,
         grid=(1,),
-        out_shape=(
-            jax.ShapeDtypeStruct((16, LANES), bf16),
-            jax.ShapeDtypeStruct((1, 2, rows, LANES), bf16),
-        ),
+        out_shape=jax.ShapeDtypeStruct((block_rows, LANES), bf16),
         in_specs=[
             whole((rows, LANES)),
-            pl.BlockSpec((occupied, occupied, per_device, LANES), lambda n: (0, 0, 0, 0)),
+            pl.BlockSpec((occupied, occupied, 16, LANES), lambda n: (0, 0, 0, 0)),
         ],
-        out_specs=(whole((16, LANES)), whole((1, 2, rows, LANES))),
-        scratch_shapes=[pltpu.VMEM((rows, LANES), f32)],
-        compiler_params=params(58),
+        out_specs=whole((block_rows, LANES)),
+        compiler_params=params(60),
         cost_estimate=cost(0, 500000),
     )(cycle_ints.reshape(rows, LANES), amps)
+    block = block.reshape(1, block_rows, LANES)
     vmem = pl.BlockSpec(memory_space=pltpu.VMEM)
-    mix, u = pl.pallas_call(
-        setup_kernel,
-        out_shape=(
-            jax.ShapeDtypeStruct((rows, rows), bf16),
-            jax.ShapeDtypeStruct((per_device, virtuals), jnp.int32),
-        ),
-        in_specs=[smem, smem, vmem, vmem],
-        out_specs=(vmem, vmem),
+    mix = pl.pallas_call(
+        mix_kernel,
+        out_shape=jax.ShapeDtypeStruct((rows, rows), bf16),
+        in_specs=[vmem],
+        out_specs=vmem,
         compiler_params=params(4),
         cost_estimate=cost(10**7, 300000),
-    )(pos, vir_irrep, fock_occ, vir_irrep.reshape(1, virtuals))
+    )(fock_occ)
 
     flat_amps = amps.reshape(occupied, rows, virtuals)
-    parts = (4, 4)
+    parts = (2, 2, 2, 2)
     wide = 2
 
     def fock_part(n, after):
@@ -423,80 +381,65 @@
         return pl.pallas_call(
             functools.partial(fock_kernel, first),
             grid=(count // wide,),
-            out_shape=jax.ShapeDtypeStruct((2 * count, per_device, virtuals), f32),
+            out_shape=(
+                jax.ShapeDtypeStruct((2 * count, per_device, virtuals), f32),
+                jax.ShapeDtypeStruct((count, per_device, LANES), bf16),
+            ),
             in_specs=[
                 smem,
                 pl.BlockSpec((wide, rows, virtuals), lambda i: (i + first // wide, 0, 0)),
                 whole(fock_vir.shape),
                 whole(mix.shape),
-                whole((per_device, virtuals)),
+                whole(u.shape),
                 anywhere,
             ],
-            out_specs=pl.BlockSpec((2 * wide, per_device, virtuals), lambda i: (i, 0, 0)),
+            out_specs=(
+                pl.BlockSpec((2 * wide, per_device, virtuals), lambda i: (i, 0, 0)),
+                pl.BlockSpec((wide, per_device, LANES), lambda i: (i, 0, 0)),
+            ),
             scratch_shapes=[pltpu.VMEM((occupied, per_device, virtuals), f32)],
             compiler_params=params(12),
             cost_estimate=cost(3 * count * rows * virtuals * virtuals, 2 * 10**6),
         )(occ_irrep, flat_amps, fock_vir, mix, u, after)
 
-    flips = [m << 2 for m in range(1, quarter)]
-    win_shape = (occupied, occupied, LANES)
-    wins = [win] + [permute(win, flip, dests) for flip in flips]
-    blocks = [xt] + [permute(xt, flip, dests) for flip in flips]
-    half0 = fock_part(0, mix)
-    win = pl.pallas_call(
-        unpack_kernel,
-        out_shape=jax.ShapeDtypeStruct(win_shape, f32),
-        in_specs=[smem] + [vmem] * quarter + [anywhere],
-        out_specs=vmem,
-        compiler_params=params(4),
-        cost_estimate=cost(0, 10**5),
-    )(pos, *wins, half0)
-
-    wins = [win] + [permute(win, flip, dests) for flip in (1, 2, 3)]
-    half1 = fock_part(1, win)
-    near = stack(blocks, half1)
+    z1, z2, z3 = [permute(block, m << 2, dests) for m in range(1, quarter)]
+    half0, cyc0 = fock_part(0, mix)
+    near = stack([block, z1], half0)
     near_y = permute(near, 2, dests)
+    half1, cyc1 = fock_part(1, near)
+    far = stack([z2, z3], half1)
+    far_y = permute(far, 2, dests)
+    half2, cyc2 = fock_part(2, far)
+    own_blocks = stack([near, far, near_y, far_y], half2)
+    mate_blocks = permute(own_blocks, 1, dests)
+    half3, cyc3 = fock_part(3, own_blocks)
 
     send_rows = tiles * per_device + 8
     groups = per_device // 8
     half, send = pl.pallas_call(
-        functools.partial(ladder_kernel, groups),
+        functools.partial(half_kernel, groups, parts),
         out_shape=(
             jax.ShapeDtypeStruct((pairs, per_device, virtuals), f32),
             jax.ShapeDtypeStruct((dests, send_rows, LANES), bf16),
         ),
-        in_specs=[smem] + [vmem] * 8 + [anywhere],
-        out_specs=(anywhere, anywhere),
+        in_specs=[smem, smem] + [vmem] * (4 + 2 * len(parts)),
+        out_specs=(vmem, vmem),
         scratch_shapes=[
+            pltpu.SMEM((occupied,), jnp.int32),
             pltpu.VMEM((occupied * occupied, LANES), f32),
-            pltpu.VMEM((pairs, per_device, virtuals), f32),
+            pltpu.VMEM((virtuals, occupied, LANES), f32),
+            pltpu.VMEM((occupied, occupied, per_device, virtuals), f32),
             pltpu.VMEM((dests, send_rows, LANES), f32),
-            pltpu.VMEM((dests, send_rows, LANES), bf16),
-            pltpu.SemaphoreType.DMA((groups,)),
-            pltpu.SemaphoreType.DMA((dests,)),
         ]
         + [pltpu.VMEM((tiles, 8 * pairs, LANES), f32)] * groups,
-        compiler_params=params(24),
-        cost_estimate=cost(4 * occupied * rows * virtuals * LANES, 25 * 10**6),
-    )(occ_irrep, *wins, half0, half1, u, ladder_ints, near)
+        compiler_params=params(28),
+        cost_estimate=cost(6 * occupied * rows * virtuals * LANES, 15 * 10**6),
+    )(
+        pos, occ_irrep, own_blocks, mate_blocks, half0, half1, half2, half3,
+        cyc0, cyc1, cyc2, cyc3, u, ladder_ints,
+    )
 
     recv = lax.all_to_all(send, "vir", split_axis=0, concat_axis=0, tiled=True)
-    own_blocks = stack([near, near_y], send)
-    mate_blocks = permute(own_blocks, 1, dests)
-    half = pl.pallas_call(
-        cycle_kernel,
-        out_shape=jax.ShapeDtypeStruct((pairs, per_device, virtuals), f32),
-        in_specs=[smem, smem] + [vmem] * 4,
-        out_specs=vmem,
-        scratch_shapes=[
-            pltpu.SMEM((occupied,), jnp.int32),
-            pltpu.VMEM((occupied, occupied, per_device, virtuals), f32),
-            pltpu.VMEM((virtuals, occupied, LANES), f32),
-            pltpu.VMEM((occupied, virtuals, LANES), f32),
-        ],
-        compiler_params=params(28),
-        cost_estimate=cost(1000, 1000),
-    )(pos, occ_irrep, own_blocks, mate_blocks, half, u)
 
     return pl.pallas_call(
         join_kernel,

time: 79.3 us -> 67.6 us (0.85)
  waiting for transfers between devices: 30.5 us -> 2.27 us
  blocking collectives: 0 us -> 27.5 us
  starting transfers between devices: 17.9 us -> 8.7 us
  Pallas kernels: 26 us -> 21.8 us
  local copies, waits for them, and re-layouts: 3.71 us -> 6.05 us
    all_to_all x0 -> x1, blocking collectives: none -> 27.5 us  [body(): recv = lax.all_to_all(send, 'vir', split_axis=0, concat_axis=0, tiled=True)]
    ppermute x11 -> x6, waiting for transfers between devices: 17.7 us -> 2.27 us  [permute(): return lax.ppermute(x, 'vir', [(n, n ^ flip) for n in range(size)])]
    all_to_all x1 -> x0, waiting for transfers between devices: 12.8 us -> none  [body(): recv = lax.all_to_all(send, 'vir', split_axis=0, concat_axis=0, tiled=True)]
    all_to_all x1 -> x0, starting transfers between devices: 5.3 us -> none  [body(): recv = lax.all_to_all(send, 'vir', split_axis=0, concat_axis=0, tiled=True)]
    pallas_call x5 -> x3, Pallas kernels: 13.2 us -> 9.2 us  [the longest x1 7.04 us: body(): pl.pallas_call(functools.partial(half_kernel, groups, parts), out_shape=(...]
    ppermute x11 -> x6, starting transfers between devices: 12.6 us -> 8.7 us  [permute(): return lax.ppermute(x, 'vir', [(n, n ^ flip) for n in range(size)])]
    unnamed x26 -> x16, local copies, waits for them, and re-layouts: 3.71 us -> 5.3 us
    pallas_call x2 -> x3, Pallas kernels: 1.05 us -> 0.07 us  [stack(): pl.pallas_call(kernel, out_shape=jax.ShapeDtypeStruct(shape, blocks[0].dt...]
  transfers between devices with their start and end apart: 12 -> 6, of which waited for: 4 -> 1; matrix products, arithmetic and copies ran while one was open for 0% -> 2% of each run, Pallas kernels for 24% -> 13%
where the time goes in v12:
time: 67.6 us; the launch traced here: 67.3 us
  blocking collectives  27.5 us (41%)
  Pallas kernels  21.8 us (32%)
  starting transfers between devices  8.7 us (13%)
  local copies, waits for them, and re-layouts  6.05 us (9%)
  waiting for transfers between devices  2.27 us (3%)
  other arithmetic  0.76 us (1%)
    all_to_all x1, blocking collectives, body(): recv = lax.all_to_all(send, 'vir', split_axis=0, concat_axis=0, tiled=True)  27.5 us
    ppermute x6, starting transfers between devices, permute(): return lax.ppermute(x, 'vir', [(n, n ^ flip) for n in range(size)])  8.7 us
    pallas_call x4, Pallas kernels, fock_part(): pl.pallas_call(functools.partial(fock_kernel, first), grid=(count // wide...  8.14 us
    pallas_call x1, Pallas kernels, body(): pl.pallas_call(functools.partial(half_kernel, groups, parts), out_shape=(...  7.04 us
    unnamed x16, local copies, waits for them, and re-layouts  5.3 us
    pallas_call x1, Pallas kernels, body(): pl.pallas_call(join_kernel, out_shape=jax.ShapeDtypeStruct((occupied, occ...  4.4 us
    ppermute x6, waiting for transfers between devices, permute(): return lax.ppermute(x, 'vir', [(n, n ^ flip) for n in range(size)])  2.27 us
    pallas_call x1, Pallas kernels, body(): pl.pallas_call(prep_kernel, grid=(1,), out_shape=jax.ShapeDtypeStruct((bl...  1.75 us
  transfers between devices with their start and end apart: 6, of which 1 were waited for; matrix products, arithmetic and copies ran while one was open for 2% of the time, Pallas kernels for 13%

profile of v12, /device:TPU:1, one launch (start us, length us, event | category | flops | bytes accessed | tf_op | source)
XLA Modules:
  0.0 67.3 jit_solution(5159361979394787720)
XLA Ops:
  0.0 1.8 %shard_map.73 = bf16[336,128]{1,0:T(8,128)(2,1)} custom-call(bf16[320,128]{1,0:T(8,128)(2,1)} %bitcast.14, bf16[8,8,40,640]{3,2,1,0:T(8,128)(2,1)} %amps_ref.1), custom_call_target="tpu_custom_call" | custom-call | bytes 500000 | tf_op jit(solution)/shard_map/pallas_call | solution.py:352
  1.8 4.2 %collective-permute-start.2 = (bf16[1,336,128]{2,1,0:T(8,128)(2,1)}, bf16[1,336,128]{2,1,0:T(8,128)(2,1)S(1)}, u32[]{:S(2)}, u32[]{:S(2)}) collective-permute-start(bf16[1,336,128]{2,1,0:T(8,128)(2,1)} %bitcast.10), channel_id=1, source_target_pairs={{0,12},{1,13},{2,14},{3,15},{4,8},{5,9},{6,10},{7,11},{8,4},{9,5},... | collective-permute-start | bytes 258056 | tf_op jit(solution)/shard_map/ppermute | solution.py:327
  5.9 0.0 collective-permute-start.1
  5.9 0.3 collective-permute-start
  6.2 0.8 %dynamic_slice.3 = s32[40]{0:T(128)S(1)} dynamic-slice(s32[640]{0:T(1024)} %param.13, s32[]{:T(128)S(6)} %select_n.3), dynamic_slice_sizes={40} | dynamic-slice | bytes 324 | tf_op jit(solution)/shard_map/dynamic_slice | solution.py:339
  7.0 0.8 %broadcast_xor_fusion.u_ref.refs_8_ = s32[40,640]{1,0:T(8,128)S(1)} fusion(s32[640]{0:T(1024)} %param.13, s32[40]{0:T(128)S(1)} %dynamic_slice.3), kind=kLoop, calls=%fused_computation | loop fusion | flops 25600 | bytes 105120 | tf_op jit(solution)/shard_map/xor | solution.py:340
  7.7 0.0 copy-start.5
  7.7 0.7 %copy-done.5 = bf16[8,8]{1,0:T(8,128)(2,1)S(1)} copy-done((bf16[8,8]{1,0:T(8,128)(2,1)S(1)}, bf16[8,8]{1,0:T(8,128)(2,1)}, u32[]{:S(2)}) %copy-start.5) | copy-done | bytes 152
  8.4 0.4 shard_map.74.mix_ref.after_ref
  8.8 0.0 copy-start
  8.8 1.9 %copy-done = bf16[8,8,40,640]{3,2,1,0:T(8,128)(2,1)S(1)} copy-done((bf16[8,8,40,640]{3,2,1,0:T(8,128)(2,1)S(1)}, bf16[8,8,40,640]{3,2,1,0:T(8,128)(2,1)}, u32[]{:S(2)}) %copy-start) | copy-done | bytes 3276824
  10.7 1.1 %copy-done.1 = bf16[640,640]{1,0:T(8,128)(2,1)S(1)} copy-done((bf16[640,640]{1,0:T(8,128)(2,1)S(1)}, bf16[640,640]{1,0:T(8,128)(2,1)}, u32[]{:S(2)}) %copy-start.1) | copy-done | bytes 819224
  11.9 0.7 copy-done.3
  12.5 2.0 %shard_map.75 = (f32[4,40,640]{2,1,0:T(8,128)S(1)}, bf16[2,40,128]{2,1,0:T(8,128)(2,1)S(1)}) custom-call(s32[8]{0:T(128)S(1)} %copy-done.3, bf16[8,320,640]{2,1,0:T(8,128)(2,1)S(1)} %bitcast.4, bf16[640,640]{1,0:T(8,128)(2,1)S(1)} %copy-done.1, bf16[320,320]{1,0:T(8,128)(2,1)S(1)} %shard_map.74.mix_ref.after_ref, ...), custom_call_target="tpu_custom_call" | custom-call | flops 786432000 | bytes 2000000 | tf_op jit(solution)/shard_map/pallas_call | solution.py:381
  14.6 0.0 collective-permute-done.refs_1_
  14.6 0.0 copy-start.2
  14.6 0.9 %copy-done.2 = bf16[336,128]{1,0:T(8,128)(2,1)S(1)} copy-done((bf16[336,128]{1,0:T(8,128)(2,1)S(1)}, bf16[336,128]{1,0:T(8,128)(2,1)}, u32[]{:S(2)}) %copy-start.2) | copy-done | bytes 86040
  15.5 1.3 %collective-permute-start.3 = (bf16[2,336,128]{2,1,0:T(8,128)(2,1)S(1)}, bf16[2,336,128]{2,1,0:T(8,128)(2,1)S(1)}, u32[]{:S(2)}, u32[]{:S(2)}) collective-permute-start(bf16[2,336,128]{2,1,0:T(8,128)(2,1)S(1)} %shard_map.76.after_ref.refs_0_), channel_id=1, source_target_pairs={{0,2},{1,3},{2,0},{3,1},{4,6},{5,7},{6,4},{7,5},{8,10},{9,11},{10,... | collective-permute-start | bytes 516104 | tf_op jit(solution)/shard_map/ppermute | solution.py:327
  16.8 2.0 %shard_map.77 = (f32[4,40,640]{2,1,0:T(8,128)S(1)}, bf16[2,40,128]{2,1,0:T(8,128)(2,1)S(1)}) custom-call(s32[8]{0:T(128)S(1)} %copy-done.3, bf16[8,320,640]{2,1,0:T(8,128)(2,1)S(1)} %bitcast.5, bf16[640,640]{1,0:T(8,128)(2,1)S(1)} %copy-done.1, bf16[320,320]{1,0:T(8,128)(2,1)S(1)} %shard_map.74.mix_ref.after_ref, ...), custom_call_target="tpu_custom_call" | custom-call | flops 786432000 | bytes 2000000 | tf_op jit(solution)/shard_map/pallas_call | solution.py:381
  18.8 0.0 collective-permute-done.2.refs_1_
  18.8 0.0 collective-permute-done.1.refs_0_
  18.9 0.0 slice-start.1
  18.9 0.3 collective-permute-start.4
  19.2 2.0 %shard_map.79 = (f32[4,40,640]{2,1,0:T(8,128)S(1)}, bf16[2,40,128]{2,1,0:T(8,128)(2,1)S(1)}) custom-call(s32[8]{0:T(128)S(1)} %copy-done.4, bf16[8,320,640]{2,1,0:T(8,128)(2,1)S(1)} %bitcast.6, bf16[640,640]{1,0:T(8,128)(2,1)S(1)} %copy-done.1, bf16[320,320]{1,0:T(8,128)(2,1)S(1)} %shard_map.74.mix_ref.after_ref, ...), custom_call_target="tpu_custom_call" | custom-call | flops 786432000 | bytes 2000000 | tf_op jit(solution)/shard_map/pallas_call | solution.py:381
  21.2 0.0 collective-permute-done.3.refs_2_
  21.2 2.3 %collective-permute-done.4.refs_3_ = bf16[2,336,128]{2,1,0:T(8,128)(2,1)S(1)} collective-permute-done((bf16[2,336,128]{2,1,0:T(8,128)(2,1)S(1)}, bf16[2,336,128]{2,1,0:T(8,128)(2,1)S(1)}, u32[]{:S(2)}, u32[]{:S(2)}) %collective-permute-start.4) | collective-permute-done | bytes 172064 | tf_op jit(solution)/shard_map/ppermute | solution.py:327
  23.5 2.7 %collective-permute-start.5 = (bf16[8,336,128]{2,1,0:T(8,128)(2,1)S(1)}, bf16[8,336,128]{2,1,0:T(8,128)(2,1)S(1)}, u32[]{:S(2)}, u32[]{:S(2)}) collective-permute-start(bf16[8,336,128]{2,1,0:T(8,128)(2,1)S(1)} %shard_map.80.after_ref.own_ref), channel_id=1, source_target_pairs={{0,1},{1,0},{2,3},{3,2},{4,5},{5,4},{6,7},{7,6},{8,9},{9,8},{10,11... | collective-permute-start | bytes 2064392 | tf_op jit(solution)/shard_map/ppermute | solution.py:327
  26.2 2.0 %shard_map.81 = (f32[4,40,640]{2,1,0:T(8,128)S(1)}, bf16[2,40,128]{2,1,0:T(8,128)(2,1)S(1)}) custom-call(s32[8]{0:T(128)S(1)} %copy-done.4, bf16[8,320,640]{2,1,0:T(8,128)(2,1)S(1)} %bitcast.7, bf16[640,640]{1,0:T(8,128)(2,1)S(1)} %copy-done.1, bf16[320,320]{1,0:T(8,128)(2,1)S(1)} %shard_map.74.mix_ref.after_ref, ...), custom_call_target="tpu_custom_call" | custom-call | flops 786432000 | bytes 2000000 | tf_op jit(solution)/shard_map/pallas_call | solution.py:381
  28.2 0.0 collective-permute-done.5.mate_ref
  28.3 7.0 %shard_map.82 = (f32[16,40,640]{2,1,0:T(8,128)S(1)}, bf16[16,208,128]{2,1,0:T(8,128)(2,1)S(1)}) custom-call(s32[1]{0:T(128)} %bitcast.pos_ref, s32[8]{0:T(128)S(1)} %copy-done.4, bf16[8,336,128]{2,1,0:T(8,128)(2,1)S(1)} %shard_map.80.after_ref.own_ref, bf16[8,336,128]{2,1,0:T(8,128)(2,1)S(1)} %collective-permute-done.5.mate_ref, ...), custom_call_target="tpu_custom_call" | custom-call | flops 1258291200 | bytes 15000000 | tf_op jit(solution)/shard_map/pallas_call | solution.py:419
  35.3 27.5 %all_to_all.5.recv_ref = bf16[16,208,128]{2,1,0:T(8,128)(2,1)S(1)} all-to-all(bf16[16,208,128]{2,1,0:T(8,128)(2,1)S(1)} %get-tuple-element.24), channel_id=1, replica_groups=mesh['groups'=2,'vir'=16] {'vir'}, dimensions={0} | all-to-all | bytes 1703936 | tf_op jit(solution)/shard_map/all_to_all | solution.py:442
  62.9 4.4 %shard_map.83 = f32[8,8,40,640]{3,2,1,0:T(8,128)} custom-call(s32[8]{0:T(128)S(1)} %copy-done.4, s32[40,640]{1,0:T(8,128)S(1)} %broadcast_xor_fusion.u_ref.refs_8_, f32[16,40,640]{2,1,0:T(8,128)S(1)} %get-tuple-element.23.half_ref, bf16[16,208,128]{2,1,0:T(8,128)(2,1)S(1)} %all_to_all.5.recv_ref), custom_call_target="tpu_custom_call" | custom-call | flops 1000000 | bytes 5000000 | tf_op jit(solution)/shard_map/pallas_call | solution.py:444
  (11 shorter events, 0.1 us)
Async XLA Ops:
  0.0 19.2 %copy-start.4 = (s32[8]{0:T(128)S(1)}, s32[8]{0:T(128)}, u32[]{:S(2)}) copy-start(s32[8]{0:T(128)} %occ_ref.11) | copy-start | bytes 100
  1.8 17.1 %collective-permute-start.2 = (bf16[1,336,128]{2,1,0:T(8,128)(2,1)}, bf16[1,336,128]{2,1,0:T(8,128)(2,1)S(1)}, u32[]{:S(2)}, u32[]{:S(2)}) collective-permute-start(bf16[1,336,128]{2,1,0:T(8,128)(2,1)} %bitcast.10), channel_id=1, source_target_pairs={{0,12},{1,13},{2,14},{3,15},{4,8},{5,9},{6,10},{7,11},{8,4},{9,5},... | collective-permute-start | bytes 258056 | tf_op jit(solution)/shard_map/ppermute | solution.py:327
  5.9 12.9 %collective-permute-start.1 = (bf16[1,336,128]{2,1,0:T(8,128)(2,1)}, bf16[1,336,128]{2,1,0:T(8,128)(2,1)S(1)}, u32[]{:S(2)}, u32[]{:S(2)}) collective-permute-start(bf16[1,336,128]{2,1,0:T(8,128)(2,1)} %bitcast.11), channel_id=1, source_target_pairs={{0,8},{1,9},{2,10},{3,11},{4,12},{5,13},{6,14},{7,15},{8,0},{9,1},... | collective-permute-start | bytes 258056 | tf_op jit(solution)/shard_map/ppermute | solution.py:327
  5.9 8.7 %collective-permute-start = (bf16[1,336,128]{2,1,0:T(8,128)(2,1)}, bf16[1,336,128]{2,1,0:T(8,128)(2,1)S(1)}, u32[]{:S(2)}, u32[]{:S(2)}) collective-permute-start(bf16[1,336,128]{2,1,0:T(8,128)(2,1)} %bitcast.12), channel_id=1, source_target_pairs={{0,4},{1,5},{2,6},{3,7},{4,0},{5,1},{6,2},{7,3},{8,12},{9,13},{10,... | collective-permute-start | bytes 258056 | tf_op jit(solution)/shard_map/ppermute | solution.py:327
  7.7 0.7 %copy-start.5 = (bf16[8,8]{1,0:T(8,128)(2,1)S(1)}, bf16[8,8]{1,0:T(8,128)(2,1)}, u32[]{:S(2)}) copy-start(bf16[8,8]{1,0:T(8,128)(2,1)} %occ_vals_ref.1) | copy-start | bytes 388
  8.8 1.9 %copy-start = (bf16[8,8,40,640]{3,2,1,0:T(8,128)(2,1)S(1)}, bf16[8,8,40,640]{3,2,1,0:T(8,128)(2,1)}, u32[]{:S(2)}) copy-start(bf16[8,8,40,640]{3,2,1,0:T(8,128)(2,1)} %amps_ref.1) | copy-start | bytes 9830404
  10.7 1.1 %copy-start.1 = (bf16[640,640]{1,0:T(8,128)(2,1)S(1)}, bf16[640,640]{1,0:T(8,128)(2,1)}, u32[]{:S(2)}) copy-start(bf16[640,640]{1,0:T(8,128)(2,1)} %fock_ref.7) | copy-start | bytes 2457604
  11.9 0.7 copy-start.3
  14.6 0.9 %copy-start.2 = (bf16[336,128]{1,0:T(8,128)(2,1)S(1)}, bf16[336,128]{1,0:T(8,128)(2,1)}, u32[]{:S(2)}) copy-start(bf16[336,128]{1,0:T(8,128)(2,1)} %shard_map.73) | copy-start | bytes 258052
  15.5 5.7 %collective-permute-start.3 = (bf16[2,336,128]{2,1,0:T(8,128)(2,1)S(1)}, bf16[2,336,128]{2,1,0:T(8,128)(2,1)S(1)}, u32[]{:S(2)}, u32[]{:S(2)}) collective-permute-start(bf16[2,336,128]{2,1,0:T(8,128)(2,1)S(1)} %shard_map.76.after_ref.refs_0_), channel_id=1, source_target_pairs={{0,2},{1,3},{2,0},{3,1},{4,6},{5,7},{6,4},{7,5},{8,10},{9,11},{10,... | collective-permute-start | bytes 516104 | tf_op jit(solution)/shard_map/ppermute | solution.py:327
  16.8 11.5 %slice-start = ((s8[6553600]{0:T(1024)(128)(4,1)}), s8[4194304]{0:T(1024)(128)(4,1)S(1)}, s32[]{:S(2)}) async-start(s8[6553600]{0:T(1024)(128)(4,1)} %bitcast.8), calls=%async_computation.1 | async-start | bytes 8388608
  18.9 9.4 %slice-start.1 = ((s8[6553600]{0:T(1024)(128)(4,1)}), s8[2359296]{0:T(1024)(128)(4,1)S(1)}, s32[]{:S(2)}) async-start(s8[6553600]{0:T(1024)(128)(4,1)} %bitcast.8), calls=%async_computation.2 | async-start | bytes 4718592
  18.9 4.6 %collective-permute-start.4 = (bf16[2,336,128]{2,1,0:T(8,128)(2,1)S(1)}, bf16[2,336,128]{2,1,0:T(8,128)(2,1)S(1)}, u32[]{:S(2)}, u32[]{:S(2)}) collective-permute-start(bf16[2,336,128]{2,1,0:T(8,128)(2,1)S(1)} %shard_map.78.after_ref.refs_1_), channel_id=1, source_target_pairs={{0,2},{1,3},{2,0},{3,1},{4,6},{5,7},{6,4},{7,5},{8,10},{9,11},{10,... | collective-permute-start | bytes 516104 | tf_op jit(solution)/shard_map/ppermute | solution.py:327
  23.5 4.7 %collective-permute-start.5 = (bf16[8,336,128]{2,1,0:T(8,128)(2,1)S(1)}, bf16[8,336,128]{2,1,0:T(8,128)(2,1)S(1)}, u32[]{:S(2)}, u32[]{:S(2)}) collective-permute-start(bf16[8,336,128]{2,1,0:T(8,128)(2,1)S(1)} %shard_map.80.after_ref.own_ref), channel_id=1, source_target_pairs={{0,1},{1,0},{2,3},{3,2},{4,5},{5,4},{6,7},{7,6},{8,9},{9,8},{10,11... | collective-permute-start | bytes 2064392 | tf_op jit(solution)/shard_map/ppermute | solution.py:327

commit v13 on v12

--- a/solution.py
+++ b/solution.py
@@ -88,7 +88,7 @@
     block_ref[rows:, :] = packed.astype(jnp.bfloat16)
 
 
-def mix_kernel(occ_vals_ref, mix_ref):
+def mix_kernel(occ_vals_ref, after_ref, mix_ref):
     rows = mix_ref.shape[0]
     occupied = occ_vals_ref.shape[0]
     per_device = rows // occupied
@@ -366,11 +366,11 @@
     mix = pl.pallas_call(
         mix_kernel,
         out_shape=jax.ShapeDtypeStruct((rows, rows), bf16),
-        in_specs=[vmem],
+        in_specs=[vmem, anywhere],
         out_specs=vmem,
         compiler_params=params(4),
         cost_estimate=cost(10**7, 300000),
-    )(fock_occ)
+    )(fock_occ, block)
 
     flat_amps = amps.reshape(occupied, rows, virtuals)
     parts = (2, 2, 2, 2)

time: 67.6 us -> 68.6 us (1.015)
  local copies, waits for them, and re-layouts: 6.05 us -> 6.94 us
    unnamed x16 -> x18, local copies, waits for them, and re-layouts: 5.3 us -> 6.18 us
where the time goes in v13:
time: 68.6 us; the launch traced here: 68.1 us
  blocking collectives  27.5 us (40%)
  Pallas kernels  21.8 us (32%)
  starting transfers between devices  8.71 us (13%)
  local copies, waits for them, and re-layouts  6.94 us (10%)
  waiting for transfers between devices  2.27 us (3%)
  other arithmetic  0.76 us (1%)
    all_to_all x1, blocking collectives, body(): recv = lax.all_to_all(send, 'vir', split_axis=0, concat_axis=0, tiled=True)  27.5 us
    ppermute x6, starting transfers between devices, permute(): return lax.ppermute(x, 'vir', [(n, n ^ flip) for n in range(size)])  8.71 us
    pallas_call x4, Pallas kernels, fock_part(): pl.pallas_call(functools.partial(fock_kernel, first), grid=(count // wide...  8.12 us
    pallas_call x1, Pallas kernels, body(): pl.pallas_call(functools.partial(half_kernel, groups, parts), out_shape=(...  7.05 us
    unnamed x18, local copies, waits for them, and re-layouts  6.18 us
    pallas_call x1, Pallas kernels, body(): pl.pallas_call(join_kernel, out_shape=jax.ShapeDtypeStruct((occupied, occ...  4.38 us
    ppermute x6, waiting for transfers between devices, permute(): return lax.ppermute(x, 'vir', [(n, n ^ flip) for n in range(size)])  2.27 us
    pallas_call x1, Pallas kernels, body(): pl.pallas_call(prep_kernel, grid=(1,), out_shape=jax.ShapeDtypeStruct((bl...  1.75 us
  transfers between devices with their start and end apart: 6, of which 1 were waited for; matrix products, arithmetic and copies ran while one was open for 2% of the time, Pallas kernels for 13%

profile of v13, /device:TPU:1, one launch (start us, length us, event | category | flops | bytes accessed | tf_op | source)
XLA Modules:
  0.0 68.1 jit_solution(11739060758053672175)
XLA Ops:
  0.0 1.8 %shard_map.73 = bf16[336,128]{1,0:T(8,128)(2,1)} custom-call(bf16[320,128]{1,0:T(8,128)(2,1)} %bitcast.15, bf16[8,8,40,640]{3,2,1,0:T(8,128)(2,1)} %amps_ref.1), custom_call_target="tpu_custom_call" | custom-call | bytes 500000 | tf_op jit(solution)/shard_map/pallas_call | solution.py:352
  1.8 4.2 %collective-permute-start.2 = (bf16[1,336,128]{2,1,0:T(8,128)(2,1)}, bf16[1,336,128]{2,1,0:T(8,128)(2,1)S(1)}, u32[]{:S(2)}, u32[]{:S(2)}) collective-permute-start(bf16[1,336,128]{2,1,0:T(8,128)(2,1)} %bitcast.10), channel_id=1, source_target_pairs={{0,12},{1,13},{2,14},{3,15},{4,8},{5,9},{6,10},{7,11},{8,4},{9,5},... | collective-permute-start | bytes 258056 | tf_op jit(solution)/shard_map/ppermute | solution.py:327
  5.9 0.0 collective-permute-start.1
  5.9 0.3 collective-permute-start
  6.2 0.8 %dynamic_slice.3 = s32[40]{0:T(128)S(1)} dynamic-slice(s32[640]{0:T(1024)} %param.13, s32[]{:T(128)S(6)} %select_n.3), dynamic_slice_sizes={40} | dynamic-slice | bytes 324 | tf_op jit(solution)/shard_map/dynamic_slice | solution.py:339
  7.0 0.8 %broadcast_xor_fusion.u_ref.refs_8_ = s32[40,640]{1,0:T(8,128)S(1)} fusion(s32[640]{0:T(1024)} %param.13, s32[40]{0:T(128)S(1)} %dynamic_slice.3), kind=kLoop, calls=%fused_computation | loop fusion | flops 25600 | bytes 105120 | tf_op jit(solution)/shard_map/xor | solution.py:340
  7.7 0.9 %copy-done.2 = bf16[336,128]{1,0:T(8,128)(2,1)S(1)} copy-done((bf16[336,128]{1,0:T(8,128)(2,1)S(1)}, bf16[336,128]{1,0:T(8,128)(2,1)}, u32[]{:S(2)}) %copy-start.2) | copy-done | bytes 86040
  8.6 0.7 copy-done.6
  9.3 0.4 shard_map.74.mix_ref.after_ref
  9.7 0.0 copy-start
  9.7 1.9 %copy-done = bf16[8,8,40,640]{3,2,1,0:T(8,128)(2,1)S(1)} copy-done((bf16[8,8,40,640]{3,2,1,0:T(8,128)(2,1)S(1)}, bf16[8,8,40,640]{3,2,1,0:T(8,128)(2,1)}, u32[]{:S(2)}) %copy-start) | copy-done | bytes 3276824
  11.6 1.1 %copy-done.1 = bf16[640,640]{1,0:T(8,128)(2,1)S(1)} copy-done((bf16[640,640]{1,0:T(8,128)(2,1)S(1)}, bf16[640,640]{1,0:T(8,128)(2,1)}, u32[]{:S(2)}) %copy-start.1) | copy-done | bytes 819224
  12.8 0.7 copy-done.4
  13.4 2.0 %shard_map.75 = (f32[4,40,640]{2,1,0:T(8,128)S(1)}, bf16[2,40,128]{2,1,0:T(8,128)(2,1)S(1)}) custom-call(s32[8]{0:T(128)S(1)} %copy-done.4, bf16[8,320,640]{2,1,0:T(8,128)(2,1)S(1)} %bitcast.4, bf16[640,640]{1,0:T(8,128)(2,1)S(1)} %copy-done.1, bf16[320,320]{1,0:T(8,128)(2,1)S(1)} %shard_map.74.mix_ref.after_ref, ...), custom_call_target="tpu_custom_call" | custom-call | flops 786432000 | bytes 2000000 | tf_op jit(solution)/shard_map/pallas_call | solution.py:381
  15.5 0.0 collective-permute-done.refs_1_
  15.5 0.0 copy-start.3
  15.5 0.9 %copy-done.3 = bf16[336,128]{1,0:T(8,128)(2,1)S(1)} copy-done((bf16[336,128]{1,0:T(8,128)(2,1)S(1)}, bf16[336,128]{1,0:T(8,128)(2,1)}, u32[]{:S(2)}) %copy-start.3) | copy-done | bytes 86040
  16.4 1.3 %collective-permute-start.3 = (bf16[2,336,128]{2,1,0:T(8,128)(2,1)S(1)}, bf16[2,336,128]{2,1,0:T(8,128)(2,1)S(1)}, u32[]{:S(2)}, u32[]{:S(2)}) collective-permute-start(bf16[2,336,128]{2,1,0:T(8,128)(2,1)S(1)} %shard_map.76.after_ref.refs_0_), channel_id=1, source_target_pairs={{0,2},{1,3},{2,0},{3,1},{4,6},{5,7},{6,4},{7,5},{8,10},{9,11},{10,... | collective-permute-start | bytes 516104 | tf_op jit(solution)/shard_map/ppermute | solution.py:327
  17.7 2.0 %shard_map.77 = (f32[4,40,640]{2,1,0:T(8,128)S(1)}, bf16[2,40,128]{2,1,0:T(8,128)(2,1)S(1)}) custom-call(s32[8]{0:T(128)S(1)} %copy-done.4, bf16[8,320,640]{2,1,0:T(8,128)(2,1)S(1)} %bitcast.5, bf16[640,640]{1,0:T(8,128)(2,1)S(1)} %copy-done.1, bf16[320,320]{1,0:T(8,128)(2,1)S(1)} %shard_map.74.mix_ref.after_ref, ...), custom_call_target="tpu_custom_call" | custom-call | flops 786432000 | bytes 2000000 | tf_op jit(solution)/shard_map/pallas_call | solution.py:381
  19.7 0.0 collective-permute-done.2.refs_1_
  19.7 0.0 collective-permute-done.1.refs_0_
  19.8 0.0 slice-start.1
  19.8 0.3 collective-permute-start.4
  20.1 2.0 %shard_map.79 = (f32[4,40,640]{2,1,0:T(8,128)S(1)}, bf16[2,40,128]{2,1,0:T(8,128)(2,1)S(1)}) custom-call(s32[8]{0:T(128)S(1)} %copy-done.5, bf16[8,320,640]{2,1,0:T(8,128)(2,1)S(1)} %bitcast.6, bf16[640,640]{1,0:T(8,128)(2,1)S(1)} %copy-done.1, bf16[320,320]{1,0:T(8,128)(2,1)S(1)} %shard_map.74.mix_ref.after_ref, ...), custom_call_target="tpu_custom_call" | custom-call | flops 786432000 | bytes 2000000 | tf_op jit(solution)/shard_map/pallas_call | solution.py:381
  22.1 0.0 collective-permute-done.3.refs_2_
  22.1 2.3 %collective-permute-done.4.refs_3_ = bf16[2,336,128]{2,1,0:T(8,128)(2,1)S(1)} collective-permute-done((bf16[2,336,128]{2,1,0:T(8,128)(2,1)S(1)}, bf16[2,336,128]{2,1,0:T(8,128)(2,1)S(1)}, u32[]{:S(2)}, u32[]{:S(2)}) %collective-permute-start.4) | collective-permute-done | bytes 172064 | tf_op jit(solution)/shard_map/ppermute | solution.py:327
  24.4 2.7 %collective-permute-start.5 = (bf16[8,336,128]{2,1,0:T(8,128)(2,1)S(1)}, bf16[8,336,128]{2,1,0:T(8,128)(2,1)S(1)}, u32[]{:S(2)}, u32[]{:S(2)}) collective-permute-start(bf16[8,336,128]{2,1,0:T(8,128)(2,1)S(1)} %shard_map.80.after_ref.own_ref), channel_id=1, source_target_pairs={{0,1},{1,0},{2,3},{3,2},{4,5},{5,4},{6,7},{7,6},{8,9},{9,8},{10,11... | collective-permute-start | bytes 2064392 | tf_op jit(solution)/shard_map/ppermute | solution.py:327
  27.1 2.0 %shard_map.81 = (f32[4,40,640]{2,1,0:T(8,128)S(1)}, bf16[2,40,128]{2,1,0:T(8,128)(2,1)S(1)}) custom-call(s32[8]{0:T(128)S(1)} %copy-done.5, bf16[8,320,640]{2,1,0:T(8,128)(2,1)S(1)} %bitcast.7, bf16[640,640]{1,0:T(8,128)(2,1)S(1)} %copy-done.1, bf16[320,320]{1,0:T(8,128)(2,1)S(1)} %shard_map.74.mix_ref.after_ref, ...), custom_call_target="tpu_custom_call" | custom-call | flops 786432000 | bytes 2000000 | tf_op jit(solution)/shard_map/pallas_call | solution.py:381
  29.1 0.0 collective-permute-done.5.mate_ref
  29.2 7.0 %shard_map.82 = (f32[16,40,640]{2,1,0:T(8,128)S(1)}, bf16[16,208,128]{2,1,0:T(8,128)(2,1)S(1)}) custom-call(s32[1]{0:T(128)} %bitcast.pos_ref, s32[8]{0:T(128)S(1)} %copy-done.5, bf16[8,336,128]{2,1,0:T(8,128)(2,1)S(1)} %shard_map.80.after_ref.own_ref, bf16[8,336,128]{2,1,0:T(8,128)(2,1)S(1)} %collective-permute-done.5.mate_ref, ...), custom_call_target="tpu_custom_call" | custom-call | flops 1258291200 | bytes 15000000 | tf_op jit(solution)/shard_map/pallas_call | solution.py:419
  36.2 27.5 %all_to_all.5.recv_ref = bf16[16,208,128]{2,1,0:T(8,128)(2,1)S(1)} all-to-all(bf16[16,208,128]{2,1,0:T(8,128)(2,1)S(1)} %get-tuple-element.24), channel_id=1, replica_groups=mesh['groups'=2,'vir'=16] {'vir'}, dimensions={0} | all-to-all | bytes 1703936 | tf_op jit(solution)/shard_map/all_to_all | solution.py:442
  63.7 4.4 %shard_map.83 = f32[8,8,40,640]{3,2,1,0:T(8,128)} custom-call(s32[8]{0:T(128)S(1)} %copy-done.5, s32[40,640]{1,0:T(8,128)S(1)} %broadcast_xor_fusion.u_ref.refs_8_, f32[16,40,640]{2,1,0:T(8,128)S(1)} %get-tuple-element.23.half_ref, bf16[16,208,128]{2,1,0:T(8,128)(2,1)S(1)} %all_to_all.5.recv_ref), custom_call_target="tpu_custom_call" | custom-call | flops 1000000 | bytes 5000000 | tf_op jit(solution)/shard_map/pallas_call | solution.py:444
  (13 shorter events, 0.1 us)
Async XLA Ops:
  0.0 20.1 %copy-start.5 = (s32[8]{0:T(128)S(1)}, s32[8]{0:T(128)}, u32[]{:S(2)}) copy-start(s32[8]{0:T(128)} %occ_ref.11) | copy-start | bytes 100
  1.8 18.0 %collective-permute-start.2 = (bf16[1,336,128]{2,1,0:T(8,128)(2,1)}, bf16[1,336,128]{2,1,0:T(8,128)(2,1)S(1)}, u32[]{:S(2)}, u32[]{:S(2)}) collective-permute-start(bf16[1,336,128]{2,1,0:T(8,128)(2,1)} %bitcast.10), channel_id=1, source_target_pairs={{0,12},{1,13},{2,14},{3,15},{4,8},{5,9},{6,10},{7,11},{8,4},{9,5},... | collective-permute-start | bytes 258056 | tf_op jit(solution)/shard_map/ppermute | solution.py:327
  5.9 13.8 %collective-permute-start.1 = (bf16[1,336,128]{2,1,0:T(8,128)(2,1)}, bf16[1,336,128]{2,1,0:T(8,128)(2,1)S(1)}, u32[]{:S(2)}, u32[]{:S(2)}) collective-permute-start(bf16[1,336,128]{2,1,0:T(8,128)(2,1)} %bitcast.11), channel_id=1, source_target_pairs={{0,8},{1,9},{2,10},{3,11},{4,12},{5,13},{6,14},{7,15},{8,0},{9,1},... | collective-permute-start | bytes 258056 | tf_op jit(solution)/shard_map/ppermute | solution.py:327
  5.9 9.6 %collective-permute-start = (bf16[1,336,128]{2,1,0:T(8,128)(2,1)}, bf16[1,336,128]{2,1,0:T(8,128)(2,1)S(1)}, u32[]{:S(2)}, u32[]{:S(2)}) collective-permute-start(bf16[1,336,128]{2,1,0:T(8,128)(2,1)} %bitcast.12), channel_id=1, source_target_pairs={{0,4},{1,5},{2,6},{3,7},{4,0},{5,1},{6,2},{7,3},{8,12},{9,13},{10,... | collective-permute-start | bytes 258056 | tf_op jit(solution)/shard_map/ppermute | solution.py:327
  7.7 0.9 %copy-start.2 = (bf16[336,128]{1,0:T(8,128)(2,1)S(1)}, bf16[336,128]{1,0:T(8,128)(2,1)}, u32[]{:S(2)}) copy-start(bf16[336,128]{1,0:T(8,128)(2,1)} %shard_map.73) | copy-start | bytes 258052
  8.6 0.7 %copy-start.6 = (bf16[8,8]{1,0:T(8,128)(2,1)S(1)}, bf16[8,8]{1,0:T(8,128)(2,1)}, u32[]{:S(2)}) copy-start(bf16[8,8]{1,0:T(8,128)(2,1)} %occ_vals_ref.1) | copy-start | bytes 388
  9.7 1.9 %copy-start = (bf16[8,8,40,640]{3,2,1,0:T(8,128)(2,1)S(1)}, bf16[8,8,40,640]{3,2,1,0:T(8,128)(2,1)}, u32[]{:S(2)}) copy-start(bf16[8,8,40,640]{3,2,1,0:T(8,128)(2,1)} %amps_ref.1) | copy-start | bytes 9830404
  11.6 1.1 %copy-start.1 = (bf16[640,640]{1,0:T(8,128)(2,1)S(1)}, bf16[640,640]{1,0:T(8,128)(2,1)}, u32[]{:S(2)}) copy-start(bf16[640,640]{1,0:T(8,128)(2,1)} %fock_ref.7) | copy-start | bytes 2457604
  12.8 0.7 copy-start.4
  15.5 0.9 %copy-start.3 = (bf16[336,128]{1,0:T(8,128)(2,1)S(1)}, bf16[336,128]{1,0:T(8,128)(2,1)}, u32[]{:S(2)}) copy-start(bf16[336,128]{1,0:T(8,128)(2,1)} %shard_map.73) | copy-start | bytes 258052
  16.4 5.7 %collective-permute-start.3 = (bf16[2,336,128]{2,1,0:T(8,128)(2,1)S(1)}, bf16[2,336,128]{2,1,0:T(8,128)(2,1)S(1)}, u32[]{:S(2)}, u32[]{:S(2)}) collective-permute-start(bf16[2,336,128]{2,1,0:T(8,128)(2,1)S(1)} %shard_map.76.after_ref.refs_0_), channel_id=1, source_target_pairs={{0,2},{1,3},{2,0},{3,1},{4,6},{5,7},{6,4},{7,5},{8,10},{9,11},{10,... | collective-permute-start | bytes 516104 | tf_op jit(solution)/shard_map/ppermute | solution.py:327
  17.7 11.5 %slice-start = ((s8[6553600]{0:T(1024)(128)(4,1)}), s8[4194304]{0:T(1024)(128)(4,1)S(1)}, s32[]{:S(2)}) async-start(s8[6553600]{0:T(1024)(128)(4,1)} %bitcast.8), calls=%async_computation.1 | async-start | bytes 8388608
  19.8 9.4 %slice-start.1 = ((s8[6553600]{0:T(1024)(128)(4,1)}), s8[2359296]{0:T(1024)(128)(4,1)S(1)}, s32[]{:S(2)}) async-start(s8[6553600]{0:T(1024)(128)(4,1)} %bitcast.8), calls=%async_computation.2 | async-start | bytes 4718592
  19.8 4.6 %collective-permute-start.4 = (bf16[2,336,128]{2,1,0:T(8,128)(2,1)S(1)}, bf16[2,336,128]{2,1,0:T(8,128)(2,1)S(1)}, u32[]{:S(2)}, u32[]{:S(2)}) collective-permute-start(bf16[2,336,128]{2,1,0:T(8,128)(2,1)S(1)} %shard_map.78.after_ref.refs_1_), channel_id=1, source_target_pairs={{0,2},{1,3},{2,0},{3,1},{4,6},{5,7},{6,4},{7,5},{8,10},{9,11},{10,... | collective-permute-start | bytes 516104 | tf_op jit(solution)/shard_map/ppermute | solution.py:327
  24.4 4.7 %collective-permute-start.5 = (bf16[8,336,128]{2,1,0:T(8,128)(2,1)S(1)}, bf16[8,336,128]{2,1,0:T(8,128)(2,1)S(1)}, u32[]{:S(2)}, u32[]{:S(2)}) collective-permute-start(bf16[8,336,128]{2,1,0:T(8,128)(2,1)S(1)} %shard_map.80.after_ref.own_ref), channel_id=1, source_target_pairs={{0,1},{1,0},{2,3},{3,2},{4,5},{5,4},{6,7},{7,6},{8,9},{9,8},{10,11... | collective-permute-start | bytes 2064392 | tf_op jit(solution)/shard_map/ppermute | solution.py:327

commit v14 on v12

--- a/solution.py
+++ b/solution.py
@@ -373,7 +373,7 @@
     )(fock_occ)
 
     flat_amps = amps.reshape(occupied, rows, virtuals)
-    parts = (2, 2, 2, 2)
+    parts = (6, 2)
     wide = 2
 
     def fock_part(n, after):
@@ -403,16 +403,12 @@
         )(occ_irrep, flat_amps, fock_vir, mix, u, after)
 
     z1, z2, z3 = [permute(block, m << 2, dests) for m in range(1, quarter)]
-    half0, cyc0 = fock_part(0, mix)
-    near = stack([block, z1], half0)
-    near_y = permute(near, 2, dests)
-    half1, cyc1 = fock_part(1, near)
-    far = stack([z2, z3], half1)
-    far_y = permute(far, 2, dests)
-    half2, cyc2 = fock_part(2, far)
-    own_blocks = stack([near, far, near_y, far_y], half2)
+    column = stack([block, z1, z2, z3], mix)
+    column_y = permute(column, 2, dests)
+    half0, cyc0 = fock_part(0, column)
+    own_blocks = stack([column, column_y], half0)
     mate_blocks = permute(own_blocks, 1, dests)
-    half3, cyc3 = fock_part(3, own_blocks)
+    half1, cyc1 = fock_part(1, own_blocks)
 
     send_rows = tiles * per_device + 8
     groups = per_device // 8
@@ -435,8 +431,7 @@
         compiler_params=params(28),
         cost_estimate=cost(6 * occupied * rows * virtuals * LANES, 15 * 10**6),
     )(
-        pos, occ_irrep, own_blocks, mate_blocks, half0, half1, half2, half3,
-        cyc0, cyc1, cyc2, cyc3, u, ladder_ints,
+        pos, occ_irrep, own_blocks, mate_blocks, half0, half1, cyc0, cyc1, u, ladder_ints,
     )
 
     recv = lax.all_to_all(send, "vir", split_axis=0, concat_axis=0, tiled=True)

time: 67.6 us -> 64.2 us (0.950)
  waiting for transfers between devices: 2.27 us -> 6.54 us
  local copies, waits for them, and re-layouts: 6.05 us -> 2.28 us
  blocking collectives: 27.5 us -> 25.7 us
  Pallas kernels: 21.8 us -> 21.1 us
  other arithmetic: 0.76 us -> 0.07 us
    ppermute x6 -> x5, waiting for transfers between devices: 2.27 us -> 6.54 us  [permute(): return lax.ppermute(x, 'vir', [(n, n ^ flip) for n in range(size)])]
    unnamed x16, local copies, waits for them, and re-layouts: 5.3 us -> 2.2 us
    all_to_all x1, blocking collectives: 27.5 us -> 25.7 us  [body(): recv = lax.all_to_all(send, 'vir', split_axis=0, concat_axis=0, tiled=True)]
    pallas_call x4 -> x2, Pallas kernels: 8.14 us -> 7.33 us  [fock_part(): pl.pallas_call(functools.partial(fock_kernel, first), grid=(count // wide...]
    xor x1, other arithmetic: 0.76 us -> 0.07 us  [body(): u = jnp.bitwise_xor(vir_local[:, None], vir_irrep[None, :])]
    dynamic_slice x1, local copies, waits for them, and re-layouts: 0.76 us -> 0.07 us  [body(): lax.dynamic_slice_in_dim(vir_irrep, position * per_device, per_device)]
    ppermute x6 -> x5, starting transfers between devices: 8.7 us -> 8.13 us  [permute(): return lax.ppermute(x, 'vir', [(n, n ^ flip) for n in range(size)])]
  transfers between devices with their start and end apart: 6 -> 5, of which waited for: 1 -> 3; matrix products, arithmetic and copies ran while one was open for 2% -> 0% of each run, Pallas kernels for 13% -> 12%
where the time goes in v14:
time: 64.2 us; the launch traced here: 64 us
  blocking collectives  25.7 us (40%)
  Pallas kernels  21.1 us (33%)
  starting transfers between devices  8.13 us (13%)
  waiting for transfers between devices  6.54 us (10%)
  local copies, waits for them, and re-layouts  2.28 us (4%)
    all_to_all x1, blocking collectives, body(): recv = lax.all_to_all(send, 'vir', split_axis=0, concat_axis=0, tiled=True)  25.7 us
    ppermute x5, starting transfers between devices, permute(): return lax.ppermute(x, 'vir', [(n, n ^ flip) for n in range(size)])  8.13 us
    pallas_call x2, Pallas kernels, fock_part(): pl.pallas_call(functools.partial(fock_kernel, first), grid=(count // wide...  7.33 us
    pallas_call x1, Pallas kernels, body(): pl.pallas_call(functools.partial(half_kernel, groups, parts), out_shape=(...  7.06 us
    ppermute x5, waiting for transfers between devices, permute(): return lax.ppermute(x, 'vir', [(n, n ^ flip) for n in range(size)])  6.54 us
    pallas_call x1, Pallas kernels, body(): pl.pallas_call(join_kernel, out_shape=jax.ShapeDtypeStruct((occupied, occ...  4.39 us
    unnamed x16, local copies, waits for them, and re-layouts  2.2 us
    pallas_call x1, Pallas kernels, body(): pl.pallas_call(prep_kernel, grid=(1,), out_shape=jax.ShapeDtypeStruct((bl...  1.89 us
  transfers between devices with their start and end apart: 5, of which 3 were waited for; matrix products, arithmetic and copies ran while one was open for 0% of the time, Pallas kernels for 12%

profile of v14, /device:TPU:1, one launch (start us, length us, event | category | flops | bytes accessed | tf_op | source)
XLA Modules:
  0.0 64.0 jit_solution(12741562120625879291)
XLA Ops:
  0.0 0.0 copy-start
  0.0 0.0 copy-start.4
  0.0 0.0 copy-start.3
  0.0 1.9 %shard_map.73 = bf16[336,128]{1,0:T(8,128)(2,1)} custom-call(bf16[320,128]{1,0:T(8,128)(2,1)} %bitcast.12, bf16[8,8,40,640]{3,2,1,0:T(8,128)(2,1)} %amps_ref.1), custom_call_target="tpu_custom_call" | custom-call | bytes 500000 | tf_op jit(solution)/shard_map/pallas_call | solution.py:352
  1.9 4.2 %collective-permute-start.2 = (bf16[1,336,128]{2,1,0:T(8,128)(2,1)}, bf16[1,336,128]{2,1,0:T(8,128)(2,1)S(1)}, u32[]{:S(2)}, u32[]{:S(2)}) collective-permute-start(bf16[1,336,128]{2,1,0:T(8,128)(2,1)} %bitcast.8), channel_id=1, source_target_pairs={{0,12},{1,13},{2,14},{3,15},{4,8},{5,9},{6,10},{7,11},{8,4},{9,5},... | collective-permute-start | bytes 258056 | tf_op jit(solution)/shard_map/ppermute | solution.py:327
  6.1 0.0 collective-permute-start.1
  6.1 0.3 collective-permute-start
  6.3 0.0 copy-done.5
  6.4 0.1 dynamic_slice.3
  6.4 0.0 copy-done.4
  6.4 0.4 shard_map.74.refs_4_.mix_ref
  6.8 1.7 %collective-permute-done.2.refs_3_ = bf16[1,336,128]{2,1,0:T(8,128)(2,1)S(1)} collective-permute-done((bf16[1,336,128]{2,1,0:T(8,128)(2,1)}, bf16[1,336,128]{2,1,0:T(8,128)(2,1)S(1)}, u32[]{:S(2)}, u32[]{:S(2)}) %collective-permute-start.2) | collective-permute-done | bytes 86048 | tf_op jit(solution)/shard_map/ppermute | solution.py:327
  8.5 4.6 %collective-permute-done.1.refs_2_ = bf16[1,336,128]{2,1,0:T(8,128)(2,1)S(1)} collective-permute-done((bf16[1,336,128]{2,1,0:T(8,128)(2,1)}, bf16[1,336,128]{2,1,0:T(8,128)(2,1)S(1)}, u32[]{:S(2)}, u32[]{:S(2)}) %collective-permute-start.1) | collective-permute-done | bytes 86048 | tf_op jit(solution)/shard_map/ppermute | solution.py:327
  13.1 0.0 collective-permute-done.refs_1_
  13.1 0.0 copy-start.2
  13.1 0.9 %copy-done.2 = bf16[336,128]{1,0:T(8,128)(2,1)S(1)} copy-done((bf16[336,128]{1,0:T(8,128)(2,1)S(1)}, bf16[336,128]{1,0:T(8,128)(2,1)}, u32[]{:S(2)}) %copy-start.2) | copy-done | bytes 86040
  14.1 1.4 %collective-permute-start.3 = (bf16[4,336,128]{2,1,0:T(8,128)(2,1)S(1)}, bf16[4,336,128]{2,1,0:T(8,128)(2,1)S(1)}, u32[]{:S(2)}, u32[]{:S(2)}) collective-permute-start(bf16[4,336,128]{2,1,0:T(8,128)(2,1)S(1)} %shard_map.75.after_ref.refs_0_), channel_id=1, source_target_pairs={{0,2},{1,3},{2,0},{3,1},{4,6},{5,7},{6,4},{7,5},{8,10},{9,11},{10,... | collective-permute-start | bytes 1032200 | tf_op jit(solution)/shard_map/ppermute | solution.py:327
  15.5 0.1 broadcast_xor_fusion.u_ref.refs_4_
  15.6 0.0 copy-done
  15.6 0.0 copy-done.3
  15.6 0.0 copy-start.1
  15.6 1.3 %copy-done.1 = bf16[640,640]{1,0:T(8,128)(2,1)S(1)} copy-done((bf16[640,640]{1,0:T(8,128)(2,1)S(1)}, bf16[640,640]{1,0:T(8,128)(2,1)}, u32[]{:S(2)}) %copy-start.1) | copy-done | bytes 819224
  16.9 5.3 %shard_map.76 = (f32[12,40,640]{2,1,0:T(8,128)S(1)}, bf16[6,40,128]{2,1,0:T(8,128)(2,1)S(1)}) custom-call(s32[8]{0:T(128)S(1)} %copy-done.3, bf16[8,320,640]{2,1,0:T(8,128)(2,1)S(1)} %bitcast.4, bf16[640,640]{1,0:T(8,128)(2,1)S(1)} %copy-done.1, bf16[320,320]{1,0:T(8,128)(2,1)S(1)} %shard_map.74.refs_4_.mix_ref, ...), custom_call_target="tpu_custom_call" | custom-call | flops 2359296000 | bytes 2000000 | tf_op jit(solution)/shard_map/pallas_call | solution.py:381
  22.2 0.2 collective-permute-done.3.refs_1_
  22.4 2.3 %collective-permute-start.4 = (bf16[8,336,128]{2,1,0:T(8,128)(2,1)S(1)}, bf16[8,336,128]{2,1,0:T(8,128)(2,1)S(1)}, u32[]{:S(2)}, u32[]{:S(2)}) collective-permute-start(bf16[8,336,128]{2,1,0:T(8,128)(2,1)S(1)} %shard_map.77.after_ref.own_ref), channel_id=1, source_target_pairs={{0,1},{1,0},{2,3},{3,2},{4,5},{5,4},{6,7},{7,6},{8,9},{9,8},{10,11... | collective-permute-start | bytes 2064392 | tf_op jit(solution)/shard_map/ppermute | solution.py:327
  24.7 2.0 %shard_map.78 = (f32[4,40,640]{2,1,0:T(8,128)S(1)}, bf16[2,40,128]{2,1,0:T(8,128)(2,1)S(1)}) custom-call(s32[8]{0:T(128)S(1)} %copy-done.3, bf16[8,320,640]{2,1,0:T(8,128)(2,1)S(1)} %bitcast.5, bf16[640,640]{1,0:T(8,128)(2,1)S(1)} %copy-done.1, bf16[320,320]{1,0:T(8,128)(2,1)S(1)} %shard_map.74.refs_4_.mix_ref, ...), custom_call_target="tpu_custom_call" | custom-call | flops 786432000 | bytes 2000000 | tf_op jit(solution)/shard_map/pallas_call | solution.py:381
  26.8 0.0 collective-permute-done.4.mate_ref
  26.8 0.0 slice-done
  26.8 0.0 slice-done.1
  26.8 7.1 %shard_map.79 = (f32[16,40,640]{2,1,0:T(8,128)S(1)}, bf16[16,208,128]{2,1,0:T(8,128)(2,1)S(1)}) custom-call(s32[1]{0:T(128)} %bitcast.pos_ref, s32[8]{0:T(128)S(1)} %copy-done.3, bf16[8,336,128]{2,1,0:T(8,128)(2,1)S(1)} %shard_map.77.after_ref.own_ref, bf16[8,336,128]{2,1,0:T(8,128)(2,1)S(1)} %collective-permute-done.4.mate_ref, ...), custom_call_target="tpu_custom_call" | custom-call | flops 1258291200 | bytes 15000000 | tf_op jit(solution)/shard_map/pallas_call | solution.py:415
  33.9 25.7 %all_to_all.5.recv_ref = bf16[16,208,128]{2,1,0:T(8,128)(2,1)S(1)} all-to-all(bf16[16,208,128]{2,1,0:T(8,128)(2,1)S(1)} %get-tuple-element.16), channel_id=1, replica_groups=mesh['groups'=2,'vir'=16] {'vir'}, dimensions={0} | all-to-all | bytes 1703936 | tf_op jit(solution)/shard_map/all_to_all | solution.py:437
  59.6 4.4 %shard_map.80 = f32[8,8,40,640]{3,2,1,0:T(8,128)} custom-call(s32[8]{0:T(128)S(1)} %copy-done.3, s32[40,640]{1,0:T(8,128)S(1)} %broadcast_xor_fusion.u_ref.refs_4_, f32[16,40,640]{2,1,0:T(8,128)S(1)} %get-tuple-element.15.half_ref, bf16[16,208,128]{2,1,0:T(8,128)(2,1)S(1)} %all_to_all.5.recv_ref), custom_call_target="tpu_custom_call" | custom-call | flops 1000000 | bytes 5000000 | tf_op jit(solution)/shard_map/pallas_call | solution.py:439
  (6 shorter events, 0.1 us)
Async XLA Ops:
  0.0 15.6 %copy-start = (bf16[8,8,40,640]{3,2,1,0:T(8,128)(2,1)S(1)}, bf16[8,8,40,640]{3,2,1,0:T(8,128)(2,1)}, u32[]{:S(2)}) copy-start(bf16[8,8,40,640]{3,2,1,0:T(8,128)(2,1)} %amps_ref.1) | copy-start | bytes 9830404
  0.0 6.3 %copy-start.5 = (s32[640]{0:T(1024)S(1)}, s32[640]{0:T(1024)}, u32[]{:S(2)}) copy-start(s32[640]{0:T(1024)} %param.13) | copy-start | bytes 7684
  0.0 6.4 %copy-start.4 = (bf16[8,8]{1,0:T(8,128)(2,1)S(1)}, bf16[8,8]{1,0:T(8,128)(2,1)}, u32[]{:S(2)}) copy-start(bf16[8,8]{1,0:T(8,128)(2,1)} %occ_vals_ref.1) | copy-start | bytes 388
  0.0 15.6 %copy-start.3 = (s32[8]{0:T(128)S(1)}, s32[8]{0:T(128)}, u32[]{:S(2)}) copy-start(s32[8]{0:T(128)} %occ_ref.7) | copy-start | bytes 100
  1.9 6.6 %collective-permute-start.2 = (bf16[1,336,128]{2,1,0:T(8,128)(2,1)}, bf16[1,336,128]{2,1,0:T(8,128)(2,1)S(1)}, u32[]{:S(2)}, u32[]{:S(2)}) collective-permute-start(bf16[1,336,128]{2,1,0:T(8,128)(2,1)} %bitcast.8), channel_id=1, source_target_pairs={{0,12},{1,13},{2,14},{3,15},{4,8},{5,9},{6,10},{7,11},{8,4},{9,5},... | collective-permute-start | bytes 258056 | tf_op jit(solution)/shard_map/ppermute | solution.py:327
  6.1 7.1 %collective-permute-start.1 = (bf16[1,336,128]{2,1,0:T(8,128)(2,1)}, bf16[1,336,128]{2,1,0:T(8,128)(2,1)S(1)}, u32[]{:S(2)}, u32[]{:S(2)}) collective-permute-start(bf16[1,336,128]{2,1,0:T(8,128)(2,1)} %bitcast.9), channel_id=1, source_target_pairs={{0,8},{1,9},{2,10},{3,11},{4,12},{5,13},{6,14},{7,15},{8,0},{9,1},... | collective-permute-start | bytes 258056 | tf_op jit(solution)/shard_map/ppermute | solution.py:327
  6.1 7.1 %collective-permute-start = (bf16[1,336,128]{2,1,0:T(8,128)(2,1)}, bf16[1,336,128]{2,1,0:T(8,128)(2,1)S(1)}, u32[]{:S(2)}, u32[]{:S(2)}) collective-permute-start(bf16[1,336,128]{2,1,0:T(8,128)(2,1)} %bitcast.10), channel_id=1, source_target_pairs={{0,4},{1,5},{2,6},{3,7},{4,0},{5,1},{6,2},{7,3},{8,12},{9,13},{10,... | collective-permute-start | bytes 258056 | tf_op jit(solution)/shard_map/ppermute | solution.py:327
  13.1 0.9 %copy-start.2 = (bf16[336,128]{1,0:T(8,128)(2,1)S(1)}, bf16[336,128]{1,0:T(8,128)(2,1)}, u32[]{:S(2)}) copy-start(bf16[336,128]{1,0:T(8,128)(2,1)} %shard_map.73) | copy-start | bytes 258052
  14.1 8.3 %collective-permute-start.3 = (bf16[4,336,128]{2,1,0:T(8,128)(2,1)S(1)}, bf16[4,336,128]{2,1,0:T(8,128)(2,1)S(1)}, u32[]{:S(2)}, u32[]{:S(2)}) collective-permute-start(bf16[4,336,128]{2,1,0:T(8,128)(2,1)S(1)} %shard_map.75.after_ref.refs_0_), channel_id=1, source_target_pairs={{0,2},{1,3},{2,0},{3,1},{4,6},{5,7},{6,4},{7,5},{8,10},{9,11},{10,... | collective-permute-start | bytes 1032200 | tf_op jit(solution)/shard_map/ppermute | solution.py:327
  15.5 11.2 %slice-start = ((s8[6553600]{0:T(1024)(128)(4,1)}), s8[4194304]{0:T(1024)(128)(4,1)S(1)}, s32[]{:S(2)}) async-start(s8[6553600]{0:T(1024)(128)(4,1)} %bitcast.6), calls=%async_computation.1 | async-start | bytes 8388608
  15.6 1.3 %copy-start.1 = (bf16[640,640]{1,0:T(8,128)(2,1)S(1)}, bf16[640,640]{1,0:T(8,128)(2,1)}, u32[]{:S(2)}) copy-start(bf16[640,640]{1,0:T(8,128)(2,1)} %fock_ref.3) | copy-start | bytes 2457604
  16.9 9.9 %slice-start.1 = ((s8[6553600]{0:T(1024)(128)(4,1)}), s8[2359296]{0:T(1024)(128)(4,1)S(1)}, s32[]{:S(2)}) async-start(s8[6553600]{0:T(1024)(128)(4,1)} %bitcast.6), calls=%async_computation.2 | async-start | bytes 4718592
  22.4 4.3 %collective-permute-start.4 = (bf16[8,336,128]{2,1,0:T(8,128)(2,1)S(1)}, bf16[8,336,128]{2,1,0:T(8,128)(2,1)S(1)}, u32[]{:S(2)}, u32[]{:S(2)}) collective-permute-start(bf16[8,336,128]{2,1,0:T(8,128)(2,1)S(1)} %shard_map.77.after_ref.own_ref), channel_id=1, source_target_pairs={{0,1},{1,0},{2,3},{3,2},{4,5},{5,4},{6,7},{7,6},{8,9},{9,8},{10,11... | collective-permute-start | bytes 2064392 | tf_op jit(solution)/shard_map/ppermute | solution.py:327

commit v15 on v14

--- a/solution.py
+++ b/solution.py
@@ -88,7 +88,8 @@
     block_ref[rows:, :] = packed.astype(jnp.bfloat16)
 
 
-def mix_kernel(occ_vals_ref, mix_ref):
+def mix_kernel(occ_vals_ref, fock_ref, mix_ref, fock_out_ref):
+    fock_out_ref[...] = fock_ref[...]
     rows = mix_ref.shape[0]
     occupied = occ_vals_ref.shape[0]
     per_device = rows // occupied
@@ -363,14 +364,17 @@
     )(cycle_ints.reshape(rows, LANES), amps)
     block = block.reshape(1, block_rows, LANES)
     vmem = pl.BlockSpec(memory_space=pltpu.VMEM)
-    mix = pl.pallas_call(
+    mix, fock = pl.pallas_call(
         mix_kernel,
-        out_shape=jax.ShapeDtypeStruct((rows, rows), bf16),
-        in_specs=[vmem],
-        out_specs=vmem,
-        compiler_params=params(4),
-        cost_estimate=cost(10**7, 300000),
-    )(fock_occ)
+        out_shape=(
+            jax.ShapeDtypeStruct((rows, rows), bf16),
+            jax.ShapeDtypeStruct(fock_vir.shape, bf16),
+        ),
+        in_specs=[vmem, vmem],
+        out_specs=(vmem, vmem),
+        compiler_params=params(6),
+        cost_estimate=cost(10**7, 2 * 10**6),
+    )(fock_occ, fock_vir)
 
     flat_amps = amps.reshape(occupied, rows, virtuals)
     parts = (6, 2)
@@ -400,13 +404,14 @@
             scratch_shapes=[pltpu.VMEM((occupied, per_device, virtuals), f32)],
             compiler_params=params(12),
             cost_estimate=cost(3 * count * rows * virtuals * virtuals, 2 * 10**6),
-        )(occ_irrep, flat_amps, fock_vir, mix, u, after)
+        )(occ_irrep, flat_amps, fock, mix, u, after)
 
     z1, z2, z3 = [permute(block, m << 2, dests) for m in range(1, quarter)]
-    column = stack([block, z1, z2, z3], mix)
+    block_y = permute(block, 2, dests)
+    column = stack([z1, z2, z3], mix)
     column_y = permute(column, 2, dests)
     half0, cyc0 = fock_part(0, column)
-    own_blocks = stack([column, column_y], half0)
+    own_blocks = stack([block, column, block_y, column_y], half0)
     mate_blocks = permute(own_blocks, 1, dests)
     half1, cyc1 = fock_part(1, own_blocks)
 

time: 64.2 us -> 62.4 us (0.972)
  waiting for transfers between devices: 6.54 us -> 3.86 us
  local copies, waits for them, and re-layouts: 2.28 us -> 1.25 us
  Pallas kernels: 21.1 us -> 22.1 us
  starting transfers between devices: 8.13 us -> 8.98 us
    ppermute x5 -> x6, waiting for transfers between devices: 6.54 us -> 3.86 us  [permute(): return lax.ppermute(x, 'vir', [(n, n ^ flip) for n in range(size)])]
    unnamed x16, local copies, waits for them, and re-layouts: 2.2 us -> 1.18 us
    pallas_call x2, Pallas kernels: 0.07 us -> 0.95 us  [stack(): pl.pallas_call(kernel, out_shape=jax.ShapeDtypeStruct(shape, blocks[0].dt...]
    ppermute x5 -> x6, starting transfers between devices: 8.13 us -> 8.98 us  [permute(): return lax.ppermute(x, 'vir', [(n, n ^ flip) for n in range(size)])]
  transfers between devices with their start and end apart: 5 -> 6, of which waited for: 3 -> 1; matrix products, arithmetic and copies ran while one was open for 0% -> 0% of each run, Pallas kernels for 12% -> 14%
where the time goes in v15:
time: 62.4 us; the launch traced here: 62.2 us
  blocking collectives  25.7 us (41%)
  Pallas kernels  22.1 us (35%)
  starting transfers between devices  8.98 us (14%)
  waiting for transfers between devices  3.86 us (6%)
  local copies, waits for them, and re-layouts  1.25 us (2%)
    all_to_all x1, blocking collectives, body(): recv = lax.all_to_all(send, 'vir', split_axis=0, concat_axis=0, tiled=True)  25.7 us
    ppermute x6, starting transfers between devices, permute(): return lax.ppermute(x, 'vir', [(n, n ^ flip) for n in range(size)])  8.98 us
    pallas_call x2, Pallas kernels, fock_part(): pl.pallas_call(functools.partial(fock_kernel, first), grid=(count // wide...  7.35 us
    pallas_call x1, Pallas kernels, body(): pl.pallas_call(functools.partial(half_kernel, groups, parts), out_shape=(...  7.07 us
    pallas_call x1, Pallas kernels, body(): pl.pallas_call(join_kernel, out_shape=jax.ShapeDtypeStruct((occupied, occ...  4.38 us
    ppermute x6, waiting for transfers between devices, permute(): return lax.ppermute(x, 'vir', [(n, n ^ flip) for n in range(size)])  3.86 us
    pallas_call x1, Pallas kernels, body(): pl.pallas_call(prep_kernel, grid=(1,), out_shape=jax.ShapeDtypeStruct((bl...  1.89 us
  transfers between devices with their start and end apart: 6, of which 1 were waited for; matrix products, arithmetic and copies ran while one was open for 0% of the time, Pallas kernels for 14%

profile of v15, /device:TPU:1, one launch (start us, length us, event | category | flops | bytes accessed | tf_op | source)
XLA Modules:
  0.0 62.2 jit_solution(6120986552080800966)
XLA Ops:
  0.0 0.0 copy-start.3
  0.0 1.9 %shard_map.73 = bf16[336,128]{1,0:T(8,128)(2,1)} custom-call(bf16[320,128]{1,0:T(8,128)(2,1)} %bitcast.13, bf16[8,8,40,640]{3,2,1,0:T(8,128)(2,1)} %amps_ref.1), custom_call_target="tpu_custom_call" | custom-call | bytes 500000 | tf_op jit(solution)/shard_map/pallas_call | solution.py:353
  1.9 4.2 %collective-permute-start.2 = (bf16[1,336,128]{2,1,0:T(8,128)(2,1)}, bf16[1,336,128]{2,1,0:T(8,128)(2,1)S(1)}, u32[]{:S(2)}, u32[]{:S(2)}) collective-permute-start(bf16[1,336,128]{2,1,0:T(8,128)(2,1)} %bitcast.8), channel_id=1, source_target_pairs={{0,12},{1,13},{2,14},{3,15},{4,8},{5,9},{6,10},{7,11},{8,4},{9,5},... | collective-permute-start | bytes 258056 | tf_op jit(solution)/shard_map/ppermute | solution.py:328
  6.1 0.0 collective-permute-start.1
  6.1 0.3 collective-permute-start
  6.3 1.2 %collective-permute-start.3 = (bf16[1,336,128]{2,1,0:T(8,128)(2,1)}, bf16[1,336,128]{2,1,0:T(8,128)(2,1)S(1)}, u32[]{:S(2)}, u32[]{:S(2)}) collective-permute-start(bf16[1,336,128]{2,1,0:T(8,128)(2,1)} %bitcast.11), channel_id=1, source_target_pairs={{0,2},{1,3},{2,0},{3,1},{4,6},{5,7},{6,4},{7,5},{8,10},{9,11},{10,... | collective-permute-start | bytes 258056 | tf_op jit(solution)/shard_map/ppermute | solution.py:328
  7.6 0.0 copy-done.5
  7.6 0.1 dynamic_slice.3
  7.7 0.0 copy-done.4
  7.7 1.1 %copy-done.1 = bf16[640,640]{1,0:T(8,128)(2,1)S(1)} copy-done((bf16[640,640]{1,0:T(8,128)(2,1)S(1)}, bf16[640,640]{1,0:T(8,128)(2,1)}, u32[]{:S(2)}) %copy-start.1) | copy-done | bytes 819224
  8.8 0.5 shard_map.74
  9.3 0.0 collective-permute-done.2.refs_2_
  9.3 3.8 %collective-permute-done.1.refs_1_ = bf16[1,336,128]{2,1,0:T(8,128)(2,1)S(1)} collective-permute-done((bf16[1,336,128]{2,1,0:T(8,128)(2,1)}, bf16[1,336,128]{2,1,0:T(8,128)(2,1)S(1)}, u32[]{:S(2)}, u32[]{:S(2)}) %collective-permute-start.1) | collective-permute-done | bytes 86048 | tf_op jit(solution)/shard_map/ppermute | solution.py:328
  13.1 0.0 collective-permute-done.refs_0_
  13.1 0.9 %shard_map.75.after_ref.refs_1_ = bf16[3,336,128]{2,1,0:T(8,128)(2,1)S(1)} custom-call(bf16[1,336,128]{2,1,0:T(8,128)(2,1)} %collective-permute-done.refs_0_, bf16[1,336,128]{2,1,0:T(8,128)(2,1)S(1)} %collective-permute-done.1.refs_1_, bf16[1,336,128]{2,1,0:T(8,128)(2,1)S(1)} %collective-permute-done.2.refs_2_, ...), custom_call_target="tpu_custom_call" | custom-call | bytes 1000000 | tf_op jit(solution)/shard_map/pallas_call | solution.py:151
  14.1 1.4 %collective-permute-start.4 = (bf16[3,336,128]{2,1,0:T(8,128)(2,1)S(1)}, bf16[3,336,128]{2,1,0:T(8,128)(2,1)S(1)}, u32[]{:S(2)}, u32[]{:S(2)}) collective-permute-start(bf16[3,336,128]{2,1,0:T(8,128)(2,1)S(1)} %shard_map.75.after_ref.refs_1_), channel_id=1, source_target_pairs={{0,2},{1,3},{2,0},{3,1},{4,6},{5,7},{6,4},{7,5},{8,10},{9,11},{10,... | collective-permute-start | bytes 774152 | tf_op jit(solution)/shard_map/ppermute | solution.py:328
  15.5 0.1 broadcast_xor_fusion.u_ref.refs_4_
  15.5 0.0 copy-done
  15.6 0.0 copy-done.3
  15.6 0.0 copy-start.2
  15.6 0.0 slice-start.1
  15.6 5.3 %shard_map.76 = (f32[12,40,640]{2,1,0:T(8,128)S(1)}, bf16[6,40,128]{2,1,0:T(8,128)(2,1)S(1)}) custom-call(s32[8]{0:T(128)S(1)} %copy-done.3, bf16[8,320,640]{2,1,0:T(8,128)(2,1)S(1)} %bitcast.4, bf16[640,640]{1,0:T(8,128)(2,1)S(1)} %get-tuple-element.14.fock_ref, bf16[320,320]{1,0:T(8,128)(2,1)S(1)} %get-tuple-element.13.refs_3_.mix_ref, ...), custom_call_target="tpu_custom_call" | custom-call | flops 2359296000 | bytes 2000000 | tf_op jit(solution)/shard_map/pallas_call | solution.py:385
  20.9 0.0 collective-permute-done.3.refs_2_
  20.9 0.0 collective-permute-done.4.refs_3_
  20.9 0.0 copy-done.2
  21.0 1.9 %collective-permute-start.5 = (bf16[8,336,128]{2,1,0:T(8,128)(2,1)S(1)}, bf16[8,336,128]{2,1,0:T(8,128)(2,1)S(1)}, u32[]{:S(2)}, u32[]{:S(2)}) collective-permute-start(bf16[8,336,128]{2,1,0:T(8,128)(2,1)S(1)} %shard_map.77.after_ref.own_ref), channel_id=1, source_target_pairs={{0,1},{1,0},{2,3},{3,2},{4,5},{5,4},{6,7},{7,6},{8,9},{9,8},{10,11... | collective-permute-start | bytes 2064392 | tf_op jit(solution)/shard_map/ppermute | solution.py:328
  22.9 2.1 %shard_map.78 = (f32[4,40,640]{2,1,0:T(8,128)S(1)}, bf16[2,40,128]{2,1,0:T(8,128)(2,1)S(1)}) custom-call(s32[8]{0:T(128)S(1)} %copy-done.3, bf16[8,320,640]{2,1,0:T(8,128)(2,1)S(1)} %bitcast.5, bf16[640,640]{1,0:T(8,128)(2,1)S(1)} %get-tuple-element.14.fock_ref, bf16[320,320]{1,0:T(8,128)(2,1)S(1)} %get-tuple-element.13.refs_3_.mix_ref, ...), custom_call_target="tpu_custom_call" | custom-call | flops 786432000 | bytes 2000000 | tf_op jit(solution)/shard_map/pallas_call | solution.py:385
  24.9 0.0 collective-permute-done.5.mate_ref
  24.9 0.0 slice-done
  25.0 7.1 %shard_map.79 = (f32[16,40,640]{2,1,0:T(8,128)S(1)}, bf16[16,208,128]{2,1,0:T(8,128)(2,1)S(1)}) custom-call(s32[1]{0:T(128)} %bitcast.pos_ref, s32[8]{0:T(128)S(1)} %copy-done.3, bf16[8,336,128]{2,1,0:T(8,128)(2,1)S(1)} %shard_map.77.after_ref.own_ref, bf16[8,336,128]{2,1,0:T(8,128)(2,1)S(1)} %collective-permute-done.5.mate_ref, ...), custom_call_target="tpu_custom_call" | custom-call | flops 1258291200 | bytes 15000000 | tf_op jit(solution)/shard_map/pallas_call | solution.py:420
  32.0 25.7 %all_to_all.5.recv_ref = bf16[16,208,128]{2,1,0:T(8,128)(2,1)S(1)} all-to-all(bf16[16,208,128]{2,1,0:T(8,128)(2,1)S(1)} %get-tuple-element.20), channel_id=1, replica_groups=mesh['groups'=2,'vir'=16] {'vir'}, dimensions={0} | all-to-all | bytes 1703936 | tf_op jit(solution)/shard_map/all_to_all | solution.py:442
  57.8 4.4 %shard_map.80 = f32[8,8,40,640]{3,2,1,0:T(8,128)} custom-call(s32[8]{0:T(128)S(1)} %copy-done.3, s32[40,640]{1,0:T(8,128)S(1)} %broadcast_xor_fusion.u_ref.refs_4_, f32[16,40,640]{2,1,0:T(8,128)S(1)} %get-tuple-element.19.half_ref, bf16[16,208,128]{2,1,0:T(8,128)(2,1)S(1)} %all_to_all.5.recv_ref), custom_call_target="tpu_custom_call" | custom-call | flops 1000000 | bytes 5000000 | tf_op jit(solution)/shard_map/pallas_call | solution.py:444
  (8 shorter events, 0.1 us)
Async XLA Ops:
  0.0 15.6 %copy-start = (bf16[8,8,40,640]{3,2,1,0:T(8,128)(2,1)S(1)}, bf16[8,8,40,640]{3,2,1,0:T(8,128)(2,1)}, u32[]{:S(2)}) copy-start(bf16[8,8,40,640]{3,2,1,0:T(8,128)(2,1)} %amps_ref.1) | copy-start | bytes 9830404
  0.0 7.6 %copy-start.5 = (s32[640]{0:T(1024)S(1)}, s32[640]{0:T(1024)}, u32[]{:S(2)}) copy-start(s32[640]{0:T(1024)} %param.13) | copy-start | bytes 7684
  0.0 7.7 %copy-start.4 = (bf16[8,8]{1,0:T(8,128)(2,1)S(1)}, bf16[8,8]{1,0:T(8,128)(2,1)}, u32[]{:S(2)}) copy-start(bf16[8,8]{1,0:T(8,128)(2,1)} %occ_vals_ref.1) | copy-start | bytes 388
  0.0 15.6 %copy-start.3 = (s32[8]{0:T(128)S(1)}, s32[8]{0:T(128)}, u32[]{:S(2)}) copy-start(s32[8]{0:T(128)} %occ_ref.7) | copy-start | bytes 100
  1.9 7.4 %collective-permute-start.2 = (bf16[1,336,128]{2,1,0:T(8,128)(2,1)}, bf16[1,336,128]{2,1,0:T(8,128)(2,1)S(1)}, u32[]{:S(2)}, u32[]{:S(2)}) collective-permute-start(bf16[1,336,128]{2,1,0:T(8,128)(2,1)} %bitcast.8), channel_id=1, source_target_pairs={{0,12},{1,13},{2,14},{3,15},{4,8},{5,9},{6,10},{7,11},{8,4},{9,5},... | collective-permute-start | bytes 258056 | tf_op jit(solution)/shard_map/ppermute | solution.py:328
  6.1 7.1 %collective-permute-start.1 = (bf16[1,336,128]{2,1,0:T(8,128)(2,1)}, bf16[1,336,128]{2,1,0:T(8,128)(2,1)S(1)}, u32[]{:S(2)}, u32[]{:S(2)}) collective-permute-start(bf16[1,336,128]{2,1,0:T(8,128)(2,1)} %bitcast.9), channel_id=1, source_target_pairs={{0,8},{1,9},{2,10},{3,11},{4,12},{5,13},{6,14},{7,15},{8,0},{9,1},... | collective-permute-start | bytes 258056 | tf_op jit(solution)/shard_map/ppermute | solution.py:328
  6.1 7.1 %collective-permute-start = (bf16[1,336,128]{2,1,0:T(8,128)(2,1)}, bf16[1,336,128]{2,1,0:T(8,128)(2,1)}, u32[]{:S(2)}, u32[]{:S(2)}) collective-permute-start(bf16[1,336,128]{2,1,0:T(8,128)(2,1)} %bitcast.10), channel_id=1, source_target_pairs={{0,4},{1,5},{2,6},{3,7},{4,0},{5,1},{6,2},{7,3},{8,12},{9,13},{10,... | collective-permute-start | bytes 258056 | tf_op jit(solution)/shard_map/ppermute | solution.py:328
  6.3 14.5 %collective-permute-start.3 = (bf16[1,336,128]{2,1,0:T(8,128)(2,1)}, bf16[1,336,128]{2,1,0:T(8,128)(2,1)S(1)}, u32[]{:S(2)}, u32[]{:S(2)}) collective-permute-start(bf16[1,336,128]{2,1,0:T(8,128)(2,1)} %bitcast.11), channel_id=1, source_target_pairs={{0,2},{1,3},{2,0},{3,1},{4,6},{5,7},{6,4},{7,5},{8,10},{9,11},{10,... | collective-permute-start | bytes 258056 | tf_op jit(solution)/shard_map/ppermute | solution.py:328
  7.7 1.1 %copy-start.1 = (bf16[640,640]{1,0:T(8,128)(2,1)S(1)}, bf16[640,640]{1,0:T(8,128)(2,1)}, u32[]{:S(2)}) copy-start(bf16[640,640]{1,0:T(8,128)(2,1)} %fock_ref.1) | copy-start | bytes 2457604
  14.1 6.8 %collective-permute-start.4 = (bf16[3,336,128]{2,1,0:T(8,128)(2,1)S(1)}, bf16[3,336,128]{2,1,0:T(8,128)(2,1)S(1)}, u32[]{:S(2)}, u32[]{:S(2)}) collective-permute-start(bf16[3,336,128]{2,1,0:T(8,128)(2,1)S(1)} %shard_map.75.after_ref.refs_1_), channel_id=1, source_target_pairs={{0,2},{1,3},{2,0},{3,1},{4,6},{5,7},{6,4},{7,5},{8,10},{9,11},{10,... | collective-permute-start | bytes 774152 | tf_op jit(solution)/shard_map/ppermute | solution.py:328
  15.5 9.4 %slice-start = ((s8[6553600]{0:T(1024)(128)(4,1)}), s8[4194304]{0:T(1024)(128)(4,1)S(1)}, s32[]{:S(2)}) async-start(s8[6553600]{0:T(1024)(128)(4,1)} %bitcast.6), calls=%async_computation.1 | async-start | bytes 8388608
  15.6 5.3 %copy-start.2 = (bf16[336,128]{1,0:T(8,128)(2,1)S(1)}, bf16[336,128]{1,0:T(8,128)(2,1)}, u32[]{:S(2)}) copy-start(bf16[336,128]{1,0:T(8,128)(2,1)} %shard_map.73) | copy-start | bytes 258052
  15.6 9.4 %slice-start.1 = ((s8[6553600]{0:T(1024)(128)(4,1)}), s8[2359296]{0:T(1024)(128)(4,1)S(1)}, s32[]{:S(2)}) async-start(s8[6553600]{0:T(1024)(128)(4,1)} %bitcast.6), calls=%async_computation.2 | async-start | bytes 4718592
  21.0 4.0 %collective-permute-start.5 = (bf16[8,336,128]{2,1,0:T(8,128)(2,1)S(1)}, bf16[8,336,128]{2,1,0:T(8,128)(2,1)S(1)}, u32[]{:S(2)}, u32[]{:S(2)}) collective-permute-start(bf16[8,336,128]{2,1,0:T(8,128)(2,1)S(1)} %shard_map.77.after_ref.own_ref), channel_id=1, source_target_pairs={{0,1},{1,0},{2,3},{3,2},{4,5},{5,4},{6,7},{7,6},{8,9},{9,8},{10,11... | collective-permute-start | bytes 2064392 | tf_op jit(solution)/shard_map/ppermute | solution.py:328

commit v16 on v15

--- a/solution.py
+++ b/solution.py
@@ -202,7 +202,11 @@
         for i in range(occupied):
             row = (labels[i] ^ labels[j]) * pairs + 2 * i + copies[j]
             w2_ref[pl.ds(row, 1), :] = window[i : i + 1, :]
-    w2 = w2_ref[...].astype(jnp.bfloat16)
+    w2 = w2_ref[...]
+    zero = jnp.zeros_like(w2)
+    w2 = jnp.concatenate(
+        [jnp.concatenate([w2, zero], axis=1), jnp.concatenate([zero, w2], axis=1)], axis=0
+    ).astype(jnp.bfloat16)
     left = jnp.concatenate([ref[...].astype(jnp.float32) for ref in cycs], axis=0)
     left = left.reshape(rows, LANES).astype(jnp.bfloat16)
     choices = [
@@ -213,13 +217,18 @@
     tops = [jnp.zeros((8, LANES), jnp.float32)]
 
     def ladder(g, a):
-        product = contract_last(w2, lad_ref[8 * g + a])
-        ua = u_ref[8 * g + a : 8 * g + a + 1, :]
-        sel = product[0:pairs]
-        for v in range(1, 4):
-            sel = jnp.where(ua == v, product[v * pairs : (v + 1) * pairs], sel)
-        for v in range(tiles):
-            ls_refs[g][v, pl.ds(a, pairs, stride=8), :] = sel[:, v * LANES : (v + 1) * LANES]
+        first = 8 * g + a
+        product = contract_last(w2, jnp.concatenate([lad_ref[first], lad_ref[first + 1]], axis=1))
+        for n in range(2):
+            ua = u_ref[first + n : first + n + 1, :]
+            start = n * occupied * occupied
+            sel = product[start : start + pairs]
+            for v in range(1, 4):
+                at = start + v * pairs
+                sel = jnp.where(ua == v, product[at : at + pairs], sel)
+            for v in range(tiles):
+                to = pl.ds(a + n, pairs, stride=8)
+                ls_refs[g][v, to, :] = sel[:, v * LANES : (v + 1) * LANES]
 
     def gathered():
         for r in range(dests):
@@ -266,7 +275,7 @@
     others = [gathered(), cycle()] + [payload(g) for g in range(groups)]
     for g, other in enumerate(others):
         for a in range(8):
-            if g < groups:
+            if g < groups and a % 2 == 0:
                 ladder(g, a)
             next(other, None)
         for _ in other:

time: 62.4 us -> 62.3 us (level)
  no operation moved by 1% of the time
where the time goes in v16:
time: 62.3 us; the launch traced here: 62.1 us
  blocking collectives  25.7 us (41%)
  Pallas kernels  22.1 us (35%)
  starting transfers between devices  8.98 us (14%)
  waiting for transfers between devices  3.86 us (6%)
  local copies, waits for them, and re-layouts  1.25 us (2%)
    all_to_all x1, blocking collectives, body(): recv = lax.all_to_all(send, 'vir', split_axis=0, concat_axis=0, tiled=True)  25.7 us
    ppermute x6, starting transfers between devices, permute(): return lax.ppermute(x, 'vir', [(n, n ^ flip) for n in range(size)])  8.98 us
    pallas_call x2, Pallas kernels, fock_part(): pl.pallas_call(functools.partial(fock_kernel, first), grid=(count // wide...  7.35 us
    pallas_call x1, Pallas kernels, body(): pl.pallas_call(functools.partial(half_kernel, groups, parts), out_shape=(...  7.05 us
    pallas_call x1, Pallas kernels, body(): pl.pallas_call(join_kernel, out_shape=jax.ShapeDtypeStruct((occupied, occ...  4.38 us
    ppermute x6, waiting for transfers between devices, permute(): return lax.ppermute(x, 'vir', [(n, n ^ flip) for n in range(size)])  3.86 us
    pallas_call x1, Pallas kernels, body(): pl.pallas_call(prep_kernel, grid=(1,), out_shape=jax.ShapeDtypeStruct((bl...  1.89 us
  transfers between devices with their start and end apart: 6, of which 1 were waited for; matrix products, arithmetic and copies ran while one was open for 0% of the time, Pallas kernels for 14%

profile of v16, /device:TPU:1, one launch (start us, length us, event | category | flops | bytes accessed | tf_op | source)
XLA Modules:
  0.0 62.1 jit_solution(19645261746881407)
XLA Ops:
  0.0 0.0 copy-start.3
  0.0 1.9 %shard_map.73 = bf16[336,128]{1,0:T(8,128)(2,1)} custom-call(bf16[320,128]{1,0:T(8,128)(2,1)} %bitcast.13, bf16[8,8,40,640]{3,2,1,0:T(8,128)(2,1)} %amps_ref.1), custom_call_target="tpu_custom_call" | custom-call | bytes 500000 | tf_op jit(solution)/shard_map/pallas_call | solution.py:362
  1.9 4.2 %collective-permute-start.2 = (bf16[1,336,128]{2,1,0:T(8,128)(2,1)}, bf16[1,336,128]{2,1,0:T(8,128)(2,1)S(1)}, u32[]{:S(2)}, u32[]{:S(2)}) collective-permute-start(bf16[1,336,128]{2,1,0:T(8,128)(2,1)} %bitcast.8), channel_id=1, source_target_pairs={{0,12},{1,13},{2,14},{3,15},{4,8},{5,9},{6,10},{7,11},{8,4},{9,5},... | collective-permute-start | bytes 258056 | tf_op jit(solution)/shard_map/ppermute | solution.py:337
  6.1 0.0 collective-permute-start.1
  6.1 0.3 collective-permute-start
  6.3 1.2 %collective-permute-start.3 = (bf16[1,336,128]{2,1,0:T(8,128)(2,1)}, bf16[1,336,128]{2,1,0:T(8,128)(2,1)S(1)}, u32[]{:S(2)}, u32[]{:S(2)}) collective-permute-start(bf16[1,336,128]{2,1,0:T(8,128)(2,1)} %bitcast.11), channel_id=1, source_target_pairs={{0,2},{1,3},{2,0},{3,1},{4,6},{5,7},{6,4},{7,5},{8,10},{9,11},{10,... | collective-permute-start | bytes 258056 | tf_op jit(solution)/shard_map/ppermute | solution.py:337
  7.6 0.0 copy-done.5
  7.6 0.1 dynamic_slice.3
  7.7 0.0 copy-done.4
  7.7 1.1 %copy-done.1 = bf16[640,640]{1,0:T(8,128)(2,1)S(1)} copy-done((bf16[640,640]{1,0:T(8,128)(2,1)S(1)}, bf16[640,640]{1,0:T(8,128)(2,1)}, u32[]{:S(2)}) %copy-start.1) | copy-done | bytes 819224
  8.8 0.5 shard_map.74
  9.3 0.0 collective-permute-done.2.refs_2_
  9.3 3.8 %collective-permute-done.1.refs_1_ = bf16[1,336,128]{2,1,0:T(8,128)(2,1)S(1)} collective-permute-done((bf16[1,336,128]{2,1,0:T(8,128)(2,1)}, bf16[1,336,128]{2,1,0:T(8,128)(2,1)S(1)}, u32[]{:S(2)}, u32[]{:S(2)}) %collective-permute-start.1) | collective-permute-done | bytes 86048 | tf_op jit(solution)/shard_map/ppermute | solution.py:337
  13.1 0.0 collective-permute-done.refs_0_
  13.1 0.9 %shard_map.75.after_ref.refs_1_ = bf16[3,336,128]{2,1,0:T(8,128)(2,1)S(1)} custom-call(bf16[1,336,128]{2,1,0:T(8,128)(2,1)} %collective-permute-done.refs_0_, bf16[1,336,128]{2,1,0:T(8,128)(2,1)S(1)} %collective-permute-done.1.refs_1_, bf16[1,336,128]{2,1,0:T(8,128)(2,1)S(1)} %collective-permute-done.2.refs_2_, ...), custom_call_target="tpu_custom_call" | custom-call | bytes 1000000 | tf_op jit(solution)/shard_map/pallas_call | solution.py:151
  14.1 1.4 %collective-permute-start.4 = (bf16[3,336,128]{2,1,0:T(8,128)(2,1)S(1)}, bf16[3,336,128]{2,1,0:T(8,128)(2,1)S(1)}, u32[]{:S(2)}, u32[]{:S(2)}) collective-permute-start(bf16[3,336,128]{2,1,0:T(8,128)(2,1)S(1)} %shard_map.75.after_ref.refs_1_), channel_id=1, source_target_pairs={{0,2},{1,3},{2,0},{3,1},{4,6},{5,7},{6,4},{7,5},{8,10},{9,11},{10,... | collective-permute-start | bytes 774152 | tf_op jit(solution)/shard_map/ppermute | solution.py:337
  15.5 0.1 broadcast_xor_fusion.u_ref.refs_4_
  15.5 0.0 copy-done
  15.6 0.0 copy-done.3
  15.6 0.0 copy-start.2
  15.6 0.0 slice-start.1
  15.6 5.3 %shard_map.76 = (f32[12,40,640]{2,1,0:T(8,128)S(1)}, bf16[6,40,128]{2,1,0:T(8,128)(2,1)S(1)}) custom-call(s32[8]{0:T(128)S(1)} %copy-done.3, bf16[8,320,640]{2,1,0:T(8,128)(2,1)S(1)} %bitcast.4, bf16[640,640]{1,0:T(8,128)(2,1)S(1)} %get-tuple-element.14.fock_ref, bf16[320,320]{1,0:T(8,128)(2,1)S(1)} %get-tuple-element.13.refs_3_.mix_ref, ...), custom_call_target="tpu_custom_call" | custom-call | flops 2359296000 | bytes 2000000 | tf_op jit(solution)/shard_map/pallas_call | solution.py:394
  20.9 0.0 collective-permute-done.3.refs_2_
  20.9 0.0 collective-permute-done.4.refs_3_
  20.9 0.0 copy-done.2
  21.0 1.9 %collective-permute-start.5 = (bf16[8,336,128]{2,1,0:T(8,128)(2,1)S(1)}, bf16[8,336,128]{2,1,0:T(8,128)(2,1)S(1)}, u32[]{:S(2)}, u32[]{:S(2)}) collective-permute-start(bf16[8,336,128]{2,1,0:T(8,128)(2,1)S(1)} %shard_map.77.after_ref.own_ref), channel_id=1, source_target_pairs={{0,1},{1,0},{2,3},{3,2},{4,5},{5,4},{6,7},{7,6},{8,9},{9,8},{10,11... | collective-permute-start | bytes 2064392 | tf_op jit(solution)/shard_map/ppermute | solution.py:337
  22.9 2.1 %shard_map.78 = (f32[4,40,640]{2,1,0:T(8,128)S(1)}, bf16[2,40,128]{2,1,0:T(8,128)(2,1)S(1)}) custom-call(s32[8]{0:T(128)S(1)} %copy-done.3, bf16[8,320,640]{2,1,0:T(8,128)(2,1)S(1)} %bitcast.5, bf16[640,640]{1,0:T(8,128)(2,1)S(1)} %get-tuple-element.14.fock_ref, bf16[320,320]{1,0:T(8,128)(2,1)S(1)} %get-tuple-element.13.refs_3_.mix_ref, ...), custom_call_target="tpu_custom_call" | custom-call | flops 786432000 | bytes 2000000 | tf_op jit(solution)/shard_map/pallas_call | solution.py:394
  24.9 0.0 collective-permute-done.5.mate_ref
  24.9 0.0 slice-done
  25.0 7.0 %shard_map.79 = (f32[16,40,640]{2,1,0:T(8,128)S(1)}, bf16[16,208,128]{2,1,0:T(8,128)(2,1)S(1)}) custom-call(s32[1]{0:T(128)} %bitcast.pos_ref, s32[8]{0:T(128)S(1)} %copy-done.3, bf16[8,336,128]{2,1,0:T(8,128)(2,1)S(1)} %shard_map.77.after_ref.own_ref, bf16[8,336,128]{2,1,0:T(8,128)(2,1)S(1)} %collective-permute-done.5.mate_ref, ...), custom_call_target="tpu_custom_call" | custom-call | flops 1258291200 | bytes 15000000 | tf_op jit(solution)/shard_map/pallas_call | solution.py:429
  32.0 25.7 %all_to_all.5.recv_ref = bf16[16,208,128]{2,1,0:T(8,128)(2,1)S(1)} all-to-all(bf16[16,208,128]{2,1,0:T(8,128)(2,1)S(1)} %get-tuple-element.20), channel_id=1, replica_groups=mesh['groups'=2,'vir'=16] {'vir'}, dimensions={0} | all-to-all | bytes 1703936 | tf_op jit(solution)/shard_map/all_to_all | solution.py:451
  57.7 4.4 %shard_map.80 = f32[8,8,40,640]{3,2,1,0:T(8,128)} custom-call(s32[8]{0:T(128)S(1)} %copy-done.3, s32[40,640]{1,0:T(8,128)S(1)} %broadcast_xor_fusion.u_ref.refs_4_, f32[16,40,640]{2,1,0:T(8,128)S(1)} %get-tuple-element.19.half_ref, bf16[16,208,128]{2,1,0:T(8,128)(2,1)S(1)} %all_to_all.5.recv_ref), custom_call_target="tpu_custom_call" | custom-call | flops 1000000 | bytes 5000000 | tf_op jit(solution)/shard_map/pallas_call | solution.py:453
  (8 shorter events, 0.1 us)
Async XLA Ops:
  0.0 15.6 %copy-start = (bf16[8,8,40,640]{3,2,1,0:T(8,128)(2,1)S(1)}, bf16[8,8,40,640]{3,2,1,0:T(8,128)(2,1)}, u32[]{:S(2)}) copy-start(bf16[8,8,40,640]{3,2,1,0:T(8,128)(2,1)} %amps_ref.1) | copy-start | bytes 9830404
  0.0 7.6 %copy-start.5 = (s32[640]{0:T(1024)S(1)}, s32[640]{0:T(1024)}, u32[]{:S(2)}) copy-start(s32[640]{0:T(1024)} %param.13) | copy-start | bytes 7684
  0.0 7.7 %copy-start.4 = (bf16[8,8]{1,0:T(8,128)(2,1)S(1)}, bf16[8,8]{1,0:T(8,128)(2,1)}, u32[]{:S(2)}) copy-start(bf16[8,8]{1,0:T(8,128)(2,1)} %occ_vals_ref.1) | copy-start | bytes 388
  0.0 15.6 %copy-start.3 = (s32[8]{0:T(128)S(1)}, s32[8]{0:T(128)}, u32[]{:S(2)}) copy-start(s32[8]{0:T(128)} %occ_ref.7) | copy-start | bytes 100
  1.9 7.4 %collective-permute-start.2 = (bf16[1,336,128]{2,1,0:T(8,128)(2,1)}, bf16[1,336,128]{2,1,0:T(8,128)(2,1)S(1)}, u32[]{:S(2)}, u32[]{:S(2)}) collective-permute-start(bf16[1,336,128]{2,1,0:T(8,128)(2,1)} %bitcast.8), channel_id=1, source_target_pairs={{0,12},{1,13},{2,14},{3,15},{4,8},{5,9},{6,10},{7,11},{8,4},{9,5},... | collective-permute-start | bytes 258056 | tf_op jit(solution)/shard_map/ppermute | solution.py:337
  6.1 7.1 %collective-permute-start.1 = (bf16[1,336,128]{2,1,0:T(8,128)(2,1)}, bf16[1,336,128]{2,1,0:T(8,128)(2,1)S(1)}, u32[]{:S(2)}, u32[]{:S(2)}) collective-permute-start(bf16[1,336,128]{2,1,0:T(8,128)(2,1)} %bitcast.9), channel_id=1, source_target_pairs={{0,8},{1,9},{2,10},{3,11},{4,12},{5,13},{6,14},{7,15},{8,0},{9,1},... | collective-permute-start | bytes 258056 | tf_op jit(solution)/shard_map/ppermute | solution.py:337
  6.1 7.1 %collective-permute-start = (bf16[1,336,128]{2,1,0:T(8,128)(2,1)}, bf16[1,336,128]{2,1,0:T(8,128)(2,1)}, u32[]{:S(2)}, u32[]{:S(2)}) collective-permute-start(bf16[1,336,128]{2,1,0:T(8,128)(2,1)} %bitcast.10), channel_id=1, source_target_pairs={{0,4},{1,5},{2,6},{3,7},{4,0},{5,1},{6,2},{7,3},{8,12},{9,13},{10,... | collective-permute-start | bytes 258056 | tf_op jit(solution)/shard_map/ppermute | solution.py:337
  6.3 14.5 %collective-permute-start.3 = (bf16[1,336,128]{2,1,0:T(8,128)(2,1)}, bf16[1,336,128]{2,1,0:T(8,128)(2,1)S(1)}, u32[]{:S(2)}, u32[]{:S(2)}) collective-permute-start(bf16[1,336,128]{2,1,0:T(8,128)(2,1)} %bitcast.11), channel_id=1, source_target_pairs={{0,2},{1,3},{2,0},{3,1},{4,6},{5,7},{6,4},{7,5},{8,10},{9,11},{10,... | collective-permute-start | bytes 258056 | tf_op jit(solution)/shard_map/ppermute | solution.py:337
  7.7 1.1 %copy-start.1 = (bf16[640,640]{1,0:T(8,128)(2,1)S(1)}, bf16[640,640]{1,0:T(8,128)(2,1)}, u32[]{:S(2)}) copy-start(bf16[640,640]{1,0:T(8,128)(2,1)} %fock_ref.1) | copy-start | bytes 2457604
  14.1 6.8 %collective-permute-start.4 = (bf16[3,336,128]{2,1,0:T(8,128)(2,1)S(1)}, bf16[3,336,128]{2,1,0:T(8,128)(2,1)S(1)}, u32[]{:S(2)}, u32[]{:S(2)}) collective-permute-start(bf16[3,336,128]{2,1,0:T(8,128)(2,1)S(1)} %shard_map.75.after_ref.refs_1_), channel_id=1, source_target_pairs={{0,2},{1,3},{2,0},{3,1},{4,6},{5,7},{6,4},{7,5},{8,10},{9,11},{10,... | collective-permute-start | bytes 774152 | tf_op jit(solution)/shard_map/ppermute | solution.py:337
  15.5 9.4 %slice-start = ((s8[6553600]{0:T(1024)(128)(4,1)}), s8[4194304]{0:T(1024)(128)(4,1)S(1)}, s32[]{:S(2)}) async-start(s8[6553600]{0:T(1024)(128)(4,1)} %bitcast.6), calls=%async_computation.1 | async-start | bytes 8388608
  15.6 5.3 %copy-start.2 = (bf16[336,128]{1,0:T(8,128)(2,1)S(1)}, bf16[336,128]{1,0:T(8,128)(2,1)}, u32[]{:S(2)}) copy-start(bf16[336,128]{1,0:T(8,128)(2,1)} %shard_map.73) | copy-start | bytes 258052
  15.6 9.4 %slice-start.1 = ((s8[6553600]{0:T(1024)(128)(4,1)}), s8[2359296]{0:T(1024)(128)(4,1)S(1)}, s32[]{:S(2)}) async-start(s8[6553600]{0:T(1024)(128)(4,1)} %bitcast.6), calls=%async_computation.2 | async-start | bytes 4718592
  21.0 4.0 %collective-permute-start.5 = (bf16[8,336,128]{2,1,0:T(8,128)(2,1)S(1)}, bf16[8,336,128]{2,1,0:T(8,128)(2,1)S(1)}, u32[]{:S(2)}, u32[]{:S(2)}) collective-permute-start(bf16[8,336,128]{2,1,0:T(8,128)(2,1)S(1)} %shard_map.77.after_ref.own_ref), channel_id=1, source_target_pairs={{0,1},{1,0},{2,3},{3,2},{4,5},{5,4},{6,7},{7,6},{8,9},{9,8},{10,11... | collective-permute-start | bytes 2064392 | tf_op jit(solution)/shard_map/ppermute | solution.py:337

commit v17 on v15

--- a/solution.py
+++ b/solution.py
@@ -237,6 +237,7 @@
     def payload(g):
         group = slice(8 * g, 8 * g + 8)
         found = {}
+        rolled = {}
         for t in range(tiles):
             last_e = min(((t + 1) * LANES - 1) // per_device, pairs - 1)
             for e in range(t * LANES // per_device, last_e + 1):
@@ -256,7 +257,10 @@
             for q in range(dests):
                 acc = None
                 for first, e, v, shift in pieces_of[q, t]:
-                    x = pltpu.roll(found[e, v], shift, axis=1) if shift else found[e, v]
+                    if (e, v, shift) not in rolled:
+                        x = found[e, v]
+                        rolled[e, v, shift] = pltpu.roll(x, shift, axis=1) if shift else x
+                    x = rolled[e, v, shift]
                     acc = x if acc is None else jnp.where(lane >= first, x, acc)
                 start = t * per_device + 8 * g
                 pay_ref[q, start : start + 8, :] = acc
@@ -408,10 +412,11 @@
 
     z1, z2, z3 = [permute(block, m << 2, dests) for m in range(1, quarter)]
     block_y = permute(block, 2, dests)
-    column = stack([z1, z2, z3], mix)
+    diagonal = permute(block_y, 4, dests)
+    column = stack([z2, z3], mix)
     column_y = permute(column, 2, dests)
     half0, cyc0 = fock_part(0, column)
-    own_blocks = stack([block, column, block_y, column_y], half0)
+    own_blocks = stack([block, z1, column, block_y, diagonal, column_y], half0)
     mate_blocks = permute(own_blocks, 1, dests)
     half1, cyc1 = fock_part(1, own_blocks)
 

time: 62.4 us -> 63.6 us (1.019)
  starting transfers between devices: 8.98 us -> 7.16 us
  waiting for transfers between devices: 3.86 us -> 5.57 us
  blocking collectives: 25.7 us -> 27 us
    ppermute x6 -> x7, starting transfers between devices: 8.98 us -> 7.16 us  [permute(): return lax.ppermute(x, 'vir', [(n, n ^ flip) for n in range(size)])]
    ppermute x6 -> x7, waiting for transfers between devices: 3.86 us -> 5.57 us  [permute(): return lax.ppermute(x, 'vir', [(n, n ^ flip) for n in range(size)])]
    all_to_all x1, blocking collectives: 25.7 us -> 27 us  [body(): recv = lax.all_to_all(send, 'vir', split_axis=0, concat_axis=0, tiled=True)]
  transfers between devices with their start and end apart: 6 -> 7, of which waited for: 1 -> 2; matrix products, arithmetic and copies ran while one was open for 0% -> 0% of each run, Pallas kernels for 14% -> 14%
where the time goes in v17:
time: 63.6 us; the launch traced here: 63.4 us
  blocking collectives  27 us (42%)
  Pallas kernels  22.1 us (35%)
  starting transfers between devices  7.16 us (11%)
  waiting for transfers between devices  5.57 us (9%)
  local copies, waits for them, and re-layouts  1.25 us (2%)
    all_to_all x1, blocking collectives, body(): recv = lax.all_to_all(send, 'vir', split_axis=0, concat_axis=0, tiled=True)  27 us
    pallas_call x2, Pallas kernels, fock_part(): pl.pallas_call(functools.partial(fock_kernel, first), grid=(count // wide...  7.37 us
    ppermute x7, starting transfers between devices, permute(): return lax.ppermute(x, 'vir', [(n, n ^ flip) for n in range(size)])  7.16 us
    pallas_call x1, Pallas kernels, body(): pl.pallas_call(functools.partial(half_kernel, groups, parts), out_shape=(...  7.07 us
    ppermute x7, waiting for transfers between devices, permute(): return lax.ppermute(x, 'vir', [(n, n ^ flip) for n in range(size)])  5.57 us
    pallas_call x1, Pallas kernels, body(): pl.pallas_call(join_kernel, out_shape=jax.ShapeDtypeStruct((occupied, occ...  4.38 us
    pallas_call x1, Pallas kernels, body(): pl.pallas_call(prep_kernel, grid=(1,), out_shape=jax.ShapeDtypeStruct((bl...  1.89 us
  transfers between devices with their start and end apart: 7, of which 2 were waited for; matrix products, arithmetic and copies ran while one was open for 0% of the time, Pallas kernels for 14%

profile of v17, /device:TPU:1, one launch (start us, length us, event | category | flops | bytes accessed | tf_op | source)
XLA Modules:
  0.0 63.4 jit_solution(7932117879252254600)
XLA Ops:
  0.0 1.9 %shard_map.73 = bf16[336,128]{1,0:T(8,128)(2,1)} custom-call(bf16[320,128]{1,0:T(8,128)(2,1)} %bitcast.13, bf16[8,8,40,640]{3,2,1,0:T(8,128)(2,1)} %amps_ref.1), custom_call_target="tpu_custom_call" | custom-call | bytes 500000 | tf_op jit(solution)/shard_map/pallas_call | solution.py:357
  1.9 2.1 %collective-permute-start.3 = (bf16[1,336,128]{2,1,0:T(8,128)(2,1)}, bf16[1,336,128]{2,1,0:T(8,128)(2,1)S(1)}, u32[]{:S(2)}, u32[]{:S(2)}) collective-permute-start(bf16[1,336,128]{2,1,0:T(8,128)(2,1)} %bitcast.8), channel_id=1, source_target_pairs={{0,2},{1,3},{2,0},{3,1},{4,6},{5,7},{6,4},{7,5},{8,10},{9,11},{10,... | collective-permute-start | bytes 258056 | tf_op jit(solution)/shard_map/ppermute | solution.py:332
  4.0 3.3 %collective-permute-start.2 = (bf16[1,336,128]{2,1,0:T(8,128)(2,1)}, bf16[1,336,128]{2,1,0:T(8,128)(2,1)S(1)}, u32[]{:S(2)}, u32[]{:S(2)}) collective-permute-start(bf16[1,336,128]{2,1,0:T(8,128)(2,1)} %bitcast.9), channel_id=1, source_target_pairs={{0,12},{1,13},{2,14},{3,15},{4,8},{5,9},{6,10},{7,11},{8,4},{9,5},... | collective-permute-start | bytes 258056 | tf_op jit(solution)/shard_map/ppermute | solution.py:332
  7.3 0.0 collective-permute-start.1
  7.3 0.3 collective-permute-start
  7.6 0.1 dynamic_slice.3
  7.7 0.1 broadcast_xor_fusion.u_ref.refs_4_
  7.8 0.0 copy-start.1
  7.8 1.1 %copy-done.1 = bf16[640,640]{1,0:T(8,128)(2,1)S(1)} copy-done((bf16[640,640]{1,0:T(8,128)(2,1)S(1)}, bf16[640,640]{1,0:T(8,128)(2,1)}, u32[]{:S(2)}) %copy-start.1) | copy-done | bytes 819224
  8.9 0.5 shard_map.74
  9.4 0.1 collective-permute-done.2.refs_1_
  9.5 5.4 %collective-permute-done.1.refs_0_ = bf16[1,336,128]{2,1,0:T(8,128)(2,1)} collective-permute-done((bf16[1,336,128]{2,1,0:T(8,128)(2,1)}, bf16[1,336,128]{2,1,0:T(8,128)(2,1)}, u32[]{:S(2)}, u32[]{:S(2)}) %collective-permute-start.1) | collective-permute-done | bytes 86048 | tf_op jit(solution)/shard_map/ppermute | solution.py:332
  14.9 0.9 %shard_map.75.after_ref.refs_2_ = bf16[2,336,128]{2,1,0:T(8,128)(2,1)S(1)} custom-call(bf16[1,336,128]{2,1,0:T(8,128)(2,1)} %collective-permute-done.1.refs_0_, bf16[1,336,128]{2,1,0:T(8,128)(2,1)S(1)} %collective-permute-done.2.refs_1_, bf16[320,320]{1,0:T(8,128)(2,1)S(1)} %get-tuple-element.13.refs_2_.mix_ref), custom_call_target="tpu_custom_call" | custom-call | bytes 1000000 | tf_op jit(solution)/shard_map/pallas_call | solution.py:151
  15.8 0.1 collective-permute-start.5
  15.9 0.0 collective-permute-done.3.refs_3_
  15.9 0.1 collective-permute-start.4
  16.0 0.0 slice-start
  16.0 0.0 copy-done
  16.0 0.0 copy-done.3
  16.0 0.0 copy-start.2
  16.1 0.0 slice-start.1
  16.1 5.3 %shard_map.76 = (f32[12,40,640]{2,1,0:T(8,128)S(1)}, bf16[6,40,128]{2,1,0:T(8,128)(2,1)S(1)}) custom-call(s32[8]{0:T(128)S(1)} %copy-done.3, bf16[8,320,640]{2,1,0:T(8,128)(2,1)S(1)} %bitcast.4, bf16[640,640]{1,0:T(8,128)(2,1)S(1)} %get-tuple-element.14.fock_ref, bf16[320,320]{1,0:T(8,128)(2,1)S(1)} %get-tuple-element.13.refs_2_.mix_ref, ...), custom_call_target="tpu_custom_call" | custom-call | flops 2359296000 | bytes 2000000 | tf_op jit(solution)/shard_map/pallas_call | solution.py:389
  21.4 0.0 collective-permute-done.refs_1_
  21.4 0.0 collective-permute-done.4.refs_4_
  21.4 0.0 collective-permute-done.5.refs_5_
  21.4 0.0 copy-done.2
  21.5 1.3 %collective-permute-start.6 = (bf16[8,336,128]{2,1,0:T(8,128)(2,1)S(1)}, bf16[8,336,128]{2,1,0:T(8,128)(2,1)S(1)}, u32[]{:S(2)}, u32[]{:S(2)}) collective-permute-start(bf16[8,336,128]{2,1,0:T(8,128)(2,1)S(1)} %shard_map.77.after_ref.own_ref), channel_id=1, source_target_pairs={{0,1},{1,0},{2,3},{3,2},{4,5},{5,4},{6,7},{7,6},{8,9},{9,8},{10,11... | collective-permute-start | bytes 2064392 | tf_op jit(solution)/shard_map/ppermute | solution.py:332
  22.8 2.1 %shard_map.78 = (f32[4,40,640]{2,1,0:T(8,128)S(1)}, bf16[2,40,128]{2,1,0:T(8,128)(2,1)S(1)}) custom-call(s32[8]{0:T(128)S(1)} %copy-done.3, bf16[8,320,640]{2,1,0:T(8,128)(2,1)S(1)} %bitcast.5, bf16[640,640]{1,0:T(8,128)(2,1)S(1)} %get-tuple-element.14.fock_ref, bf16[320,320]{1,0:T(8,128)(2,1)S(1)} %get-tuple-element.13.refs_2_.mix_ref, ...), custom_call_target="tpu_custom_call" | custom-call | flops 786432000 | bytes 2000000 | tf_op jit(solution)/shard_map/pallas_call | solution.py:389
  24.9 0.0 collective-permute-done.6.mate_ref
  24.9 7.1 %shard_map.79 = (f32[16,40,640]{2,1,0:T(8,128)S(1)}, bf16[16,208,128]{2,1,0:T(8,128)(2,1)S(1)}) custom-call(s32[1]{0:T(128)} %bitcast.pos_ref, s32[8]{0:T(128)S(1)} %copy-done.3, bf16[8,336,128]{2,1,0:T(8,128)(2,1)S(1)} %shard_map.77.after_ref.own_ref, bf16[8,336,128]{2,1,0:T(8,128)(2,1)S(1)} %collective-permute-done.6.mate_ref, ...), custom_call_target="tpu_custom_call" | custom-call | flops 1258291200 | bytes 15000000 | tf_op jit(solution)/shard_map/pallas_call | solution.py:425
  32.0 27.0 %all_to_all.5.recv_ref = bf16[16,208,128]{2,1,0:T(8,128)(2,1)S(1)} all-to-all(bf16[16,208,128]{2,1,0:T(8,128)(2,1)S(1)} %get-tuple-element.20), channel_id=1, replica_groups=mesh['groups'=2,'vir'=16] {'vir'}, dimensions={0} | all-to-all | bytes 1703936 | tf_op jit(solution)/shard_map/all_to_all | solution.py:447
  59.0 4.4 %shard_map.80 = f32[8,8,40,640]{3,2,1,0:T(8,128)} custom-call(s32[8]{0:T(128)S(1)} %copy-done.3, s32[40,640]{1,0:T(8,128)S(1)} %broadcast_xor_fusion.u_ref.refs_4_, f32[16,40,640]{2,1,0:T(8,128)S(1)} %get-tuple-element.19.half_ref, bf16[16,208,128]{2,1,0:T(8,128)(2,1)S(1)} %all_to_all.5.recv_ref), custom_call_target="tpu_custom_call" | custom-call | flops 1000000 | bytes 5000000 | tf_op jit(solution)/shard_map/pallas_call | solution.py:449
  (10 shorter events, 0.1 us)
Async XLA Ops:
  0.0 16.0 %copy-start = (bf16[8,8,40,640]{3,2,1,0:T(8,128)(2,1)S(1)}, bf16[8,8,40,640]{3,2,1,0:T(8,128)(2,1)}, u32[]{:S(2)}) copy-start(bf16[8,8,40,640]{3,2,1,0:T(8,128)(2,1)} %amps_ref.1) | copy-start | bytes 9830404
  0.0 7.6 %copy-start.5 = (s32[640]{0:T(1024)S(1)}, s32[640]{0:T(1024)}, u32[]{:S(2)}) copy-start(s32[640]{0:T(1024)} %param.13) | copy-start | bytes 7684
  0.0 7.7 %copy-start.4 = (bf16[8,8]{1,0:T(8,128)(2,1)S(1)}, bf16[8,8]{1,0:T(8,128)(2,1)}, u32[]{:S(2)}) copy-start(bf16[8,8]{1,0:T(8,128)(2,1)} %occ_vals_ref.1) | copy-start | bytes 388
  0.0 16.0 %copy-start.3 = (s32[8]{0:T(128)S(1)}, s32[8]{0:T(128)}, u32[]{:S(2)}) copy-start(s32[8]{0:T(128)} %occ_ref.7) | copy-start | bytes 100
  1.9 14.0 %collective-permute-start.3 = (bf16[1,336,128]{2,1,0:T(8,128)(2,1)}, bf16[1,336,128]{2,1,0:T(8,128)(2,1)S(1)}, u32[]{:S(2)}, u32[]{:S(2)}) collective-permute-start(bf16[1,336,128]{2,1,0:T(8,128)(2,1)} %bitcast.8), channel_id=1, source_target_pairs={{0,2},{1,3},{2,0},{3,1},{4,6},{5,7},{6,4},{7,5},{8,10},{9,11},{10,... | collective-permute-start | bytes 258056 | tf_op jit(solution)/shard_map/ppermute | solution.py:332
  4.0 5.5 %collective-permute-start.2 = (bf16[1,336,128]{2,1,0:T(8,128)(2,1)}, bf16[1,336,128]{2,1,0:T(8,128)(2,1)S(1)}, u32[]{:S(2)}, u32[]{:S(2)}) collective-permute-start(bf16[1,336,128]{2,1,0:T(8,128)(2,1)} %bitcast.9), channel_id=1, source_target_pairs={{0,12},{1,13},{2,14},{3,15},{4,8},{5,9},{6,10},{7,11},{8,4},{9,5},... | collective-permute-start | bytes 258056 | tf_op jit(solution)/shard_map/ppermute | solution.py:332
  7.3 7.6 %collective-permute-start.1 = (bf16[1,336,128]{2,1,0:T(8,128)(2,1)}, bf16[1,336,128]{2,1,0:T(8,128)(2,1)}, u32[]{:S(2)}, u32[]{:S(2)}) collective-permute-start(bf16[1,336,128]{2,1,0:T(8,128)(2,1)} %bitcast.10), channel_id=1, source_target_pairs={{0,8},{1,9},{2,10},{3,11},{4,12},{5,13},{6,14},{7,15},{8,0},{9,1},... | collective-permute-start | bytes 258056 | tf_op jit(solution)/shard_map/ppermute | solution.py:332
  7.3 14.1 %collective-permute-start = (bf16[1,336,128]{2,1,0:T(8,128)(2,1)}, bf16[1,336,128]{2,1,0:T(8,128)(2,1)S(1)}, u32[]{:S(2)}, u32[]{:S(2)}) collective-permute-start(bf16[1,336,128]{2,1,0:T(8,128)(2,1)} %bitcast.11), channel_id=1, source_target_pairs={{0,4},{1,5},{2,6},{3,7},{4,0},{5,1},{6,2},{7,3},{8,12},{9,13},{10,... | collective-permute-start | bytes 258056 | tf_op jit(solution)/shard_map/ppermute | solution.py:332
  7.8 1.1 %copy-start.1 = (bf16[640,640]{1,0:T(8,128)(2,1)S(1)}, bf16[640,640]{1,0:T(8,128)(2,1)}, u32[]{:S(2)}) copy-start(bf16[640,640]{1,0:T(8,128)(2,1)} %fock_ref.1) | copy-start | bytes 2457604
  15.8 5.6 %collective-permute-start.5 = (bf16[2,336,128]{2,1,0:T(8,128)(2,1)S(1)}, bf16[2,336,128]{2,1,0:T(8,128)(2,1)S(1)}, u32[]{:S(2)}, u32[]{:S(2)}) collective-permute-start(bf16[2,336,128]{2,1,0:T(8,128)(2,1)S(1)} %shard_map.75.after_ref.refs_2_), channel_id=1, source_target_pairs={{0,2},{1,3},{2,0},{3,1},{4,6},{5,7},{6,4},{7,5},{8,10},{9,11},{10,... | collective-permute-start | bytes 516104 | tf_op jit(solution)/shard_map/ppermute | solution.py:332
  15.9 5.5 %collective-permute-start.4 = (bf16[1,336,128]{2,1,0:T(8,128)(2,1)S(1)}, bf16[1,336,128]{2,1,0:T(8,128)(2,1)S(1)}, u32[]{:S(2)}, u32[]{:S(2)}) collective-permute-start(bf16[1,336,128]{2,1,0:T(8,128)(2,1)S(1)} %collective-permute-done.3.refs_3_), channel_id=1, source_target_pairs={{0,4},{1,5},{2,6},{3,7},{4,0},{5,1},{6,2},{7,3},{8,12},{9,13},{10,... | collective-permute-start | bytes 258056 | tf_op jit(solution)/shard_map/ppermute | solution.py:332
  16.0 8.9 %slice-start = ((s8[6553600]{0:T(1024)(128)(4,1)}), s8[4194304]{0:T(1024)(128)(4,1)S(1)}, s32[]{:S(2)}) async-start(s8[6553600]{0:T(1024)(128)(4,1)} %bitcast.6), calls=%async_computation.1 | async-start | bytes 8388608
  16.0 5.4 %copy-start.2 = (bf16[336,128]{1,0:T(8,128)(2,1)S(1)}, bf16[336,128]{1,0:T(8,128)(2,1)}, u32[]{:S(2)}) copy-start(bf16[336,128]{1,0:T(8,128)(2,1)} %shard_map.73) | copy-start | bytes 258052
  16.1 8.8 %slice-start.1 = ((s8[6553600]{0:T(1024)(128)(4,1)}), s8[2359296]{0:T(1024)(128)(4,1)S(1)}, s32[]{:S(2)}) async-start(s8[6553600]{0:T(1024)(128)(4,1)} %bitcast.6), calls=%async_computation.2 | async-start | bytes 4718592
  21.5 3.4 %collective-permute-start.6 = (bf16[8,336,128]{2,1,0:T(8,128)(2,1)S(1)}, bf16[8,336,128]{2,1,0:T(8,128)(2,1)S(1)}, u32[]{:S(2)}, u32[]{:S(2)}) collective-permute-start(bf16[8,336,128]{2,1,0:T(8,128)(2,1)S(1)} %shard_map.77.after_ref.own_ref), channel_id=1, source_target_pairs={{0,1},{1,0},{2,3},{3,2},{4,5},{5,4},{6,7},{7,6},{8,9},{9,8},{10,11... | collective-permute-start | bytes 2064392 | tf_op jit(solution)/shard_map/ppermute | solution.py:332

commit v18 on v15

--- a/solution.py
+++ b/solution.py
@@ -378,10 +378,10 @@
 
     flat_amps = amps.reshape(occupied, rows, virtuals)
     parts = (6, 2)
-    wide = 2
 
     def fock_part(n, after):
         first, count = sum(parts[:n]), parts[n]
+        wide = 3 if count % 3 == 0 else 2
         return pl.pallas_call(
             functools.partial(fock_kernel, first),
             grid=(count // wide,),
@@ -402,7 +402,7 @@
                 pl.BlockSpec((wide, per_device, LANES), lambda i: (i, 0, 0)),
             ),
             scratch_shapes=[pltpu.VMEM((occupied, per_device, virtuals), f32)],
-            compiler_params=params(12),
+            compiler_params=params(16),
             cost_estimate=cost(3 * count * rows * virtuals * virtuals, 2 * 10**6),
         )(occ_irrep, flat_amps, fock, mix, u, after)
 

time: 62.4 us -> 62.4 us (level)
  no operation moved by 1% of the time
where the time goes in v18:
time: 62.4 us; the launch traced here: 62.2 us
  blocking collectives  25.7 us (41%)
  Pallas kernels  22 us (35%)
  starting transfers between devices  9.15 us (15%)
  waiting for transfers between devices  3.86 us (6%)
  local copies, waits for them, and re-layouts  1.25 us (2%)
    all_to_all x1, blocking collectives, body(): recv = lax.all_to_all(send, 'vir', split_axis=0, concat_axis=0, tiled=True)  25.7 us
    ppermute x6, starting transfers between devices, permute(): return lax.ppermute(x, 'vir', [(n, n ^ flip) for n in range(size)])  9.15 us
    pallas_call x2, Pallas kernels, fock_part(): pl.pallas_call(functools.partial(fock_kernel, first), grid=(count // wide...  7.17 us
    pallas_call x1, Pallas kernels, body(): pl.pallas_call(functools.partial(half_kernel, groups, parts), out_shape=(...  7.07 us
    pallas_call x1, Pallas kernels, body(): pl.pallas_call(join_kernel, out_shape=jax.ShapeDtypeStruct((occupied, occ...  4.4 us
    ppermute x6, waiting for transfers between devices, permute(): return lax.ppermute(x, 'vir', [(n, n ^ flip) for n in range(size)])  3.86 us
    pallas_call x1, Pallas kernels, body(): pl.pallas_call(prep_kernel, grid=(1,), out_shape=jax.ShapeDtypeStruct((bl...  1.89 us
  transfers between devices with their start and end apart: 6, of which 1 were waited for; matrix products, arithmetic and copies ran while one was open for 0% of the time, Pallas kernels for 14%

profile of v18, /device:TPU:1, one launch (start us, length us, event | category | flops | bytes accessed | tf_op | source)
XLA Modules:
  0.0 62.2 jit_solution(16198878496636219053)
XLA Ops:
  0.0 0.0 copy-start.3
  0.0 1.9 %shard_map.73 = bf16[336,128]{1,0:T(8,128)(2,1)} custom-call(bf16[320,128]{1,0:T(8,128)(2,1)} %bitcast.13, bf16[8,8,40,640]{3,2,1,0:T(8,128)(2,1)} %amps_ref.1), custom_call_target="tpu_custom_call" | custom-call | bytes 500000 | tf_op jit(solution)/shard_map/pallas_call | solution.py:353
  1.9 4.2 %collective-permute-start.2 = (bf16[1,336,128]{2,1,0:T(8,128)(2,1)}, bf16[1,336,128]{2,1,0:T(8,128)(2,1)S(1)}, u32[]{:S(2)}, u32[]{:S(2)}) collective-permute-start(bf16[1,336,128]{2,1,0:T(8,128)(2,1)} %bitcast.8), channel_id=1, source_target_pairs={{0,12},{1,13},{2,14},{3,15},{4,8},{5,9},{6,10},{7,11},{8,4},{9,5},... | collective-permute-start | bytes 258056 | tf_op jit(solution)/shard_map/ppermute | solution.py:328
  6.1 0.0 collective-permute-start.1
  6.1 0.3 collective-permute-start
  6.3 1.2 %collective-permute-start.3 = (bf16[1,336,128]{2,1,0:T(8,128)(2,1)}, bf16[1,336,128]{2,1,0:T(8,128)(2,1)S(1)}, u32[]{:S(2)}, u32[]{:S(2)}) collective-permute-start(bf16[1,336,128]{2,1,0:T(8,128)(2,1)} %bitcast.11), channel_id=1, source_target_pairs={{0,2},{1,3},{2,0},{3,1},{4,6},{5,7},{6,4},{7,5},{8,10},{9,11},{10,... | collective-permute-start | bytes 258056 | tf_op jit(solution)/shard_map/ppermute | solution.py:328
  7.6 0.0 copy-done.5
  7.6 0.1 dynamic_slice.3
  7.7 0.0 copy-done.4
  7.7 1.1 %copy-done.1 = bf16[640,640]{1,0:T(8,128)(2,1)S(1)} copy-done((bf16[640,640]{1,0:T(8,128)(2,1)S(1)}, bf16[640,640]{1,0:T(8,128)(2,1)}, u32[]{:S(2)}) %copy-start.1) | copy-done | bytes 819224
  8.8 0.5 shard_map.74
  9.3 0.0 collective-permute-done.2.refs_2_
  9.3 3.8 %collective-permute-done.1.refs_1_ = bf16[1,336,128]{2,1,0:T(8,128)(2,1)S(1)} collective-permute-done((bf16[1,336,128]{2,1,0:T(8,128)(2,1)}, bf16[1,336,128]{2,1,0:T(8,128)(2,1)S(1)}, u32[]{:S(2)}, u32[]{:S(2)}) %collective-permute-start.1) | collective-permute-done | bytes 86048 | tf_op jit(solution)/shard_map/ppermute | solution.py:328
  13.1 0.0 collective-permute-done.refs_0_
  13.1 0.9 %shard_map.75.after_ref.refs_1_ = bf16[3,336,128]{2,1,0:T(8,128)(2,1)S(1)} custom-call(bf16[1,336,128]{2,1,0:T(8,128)(2,1)} %collective-permute-done.refs_0_, bf16[1,336,128]{2,1,0:T(8,128)(2,1)S(1)} %collective-permute-done.1.refs_1_, bf16[1,336,128]{2,1,0:T(8,128)(2,1)S(1)} %collective-permute-done.2.refs_2_, ...), custom_call_target="tpu_custom_call" | custom-call | bytes 1000000 | tf_op jit(solution)/shard_map/pallas_call | solution.py:151
  14.1 1.4 %collective-permute-start.4 = (bf16[3,336,128]{2,1,0:T(8,128)(2,1)S(1)}, bf16[3,336,128]{2,1,0:T(8,128)(2,1)S(1)}, u32[]{:S(2)}, u32[]{:S(2)}) collective-permute-start(bf16[3,336,128]{2,1,0:T(8,128)(2,1)S(1)} %shard_map.75.after_ref.refs_1_), channel_id=1, source_target_pairs={{0,2},{1,3},{2,0},{3,1},{4,6},{5,7},{6,4},{7,5},{8,10},{9,11},{10,... | collective-permute-start | bytes 774152 | tf_op jit(solution)/shard_map/ppermute | solution.py:328
  15.5 0.1 broadcast_xor_fusion.u_ref.refs_4_
  15.5 0.0 copy-done
  15.6 0.0 copy-done.3
  15.6 0.0 copy-start.2
  15.6 0.0 slice-start.1
  15.6 5.1 %shard_map.76 = (f32[12,40,640]{2,1,0:T(8,128)S(1)}, bf16[6,40,128]{2,1,0:T(8,128)(2,1)S(1)}) custom-call(s32[8]{0:T(128)S(1)} %copy-done.3, bf16[8,320,640]{2,1,0:T(8,128)(2,1)S(1)} %bitcast.4, bf16[640,640]{1,0:T(8,128)(2,1)S(1)} %get-tuple-element.14.fock_ref, bf16[320,320]{1,0:T(8,128)(2,1)S(1)} %get-tuple-element.13.refs_3_.mix_ref, ...), custom_call_target="tpu_custom_call" | custom-call | flops 2359296000 | bytes 2000000 | tf_op jit(solution)/shard_map/pallas_call | solution.py:385
  20.7 0.0 collective-permute-done.3.refs_2_
  20.7 0.0 collective-permute-done.4.refs_3_
  20.7 0.0 copy-done.2
  20.8 2.1 %collective-permute-start.5 = (bf16[8,336,128]{2,1,0:T(8,128)(2,1)S(1)}, bf16[8,336,128]{2,1,0:T(8,128)(2,1)S(1)}, u32[]{:S(2)}, u32[]{:S(2)}) collective-permute-start(bf16[8,336,128]{2,1,0:T(8,128)(2,1)S(1)} %shard_map.77.after_ref.own_ref), channel_id=1, source_target_pairs={{0,1},{1,0},{2,3},{3,2},{4,5},{5,4},{6,7},{7,6},{8,9},{9,8},{10,11... | collective-permute-start | bytes 2064392 | tf_op jit(solution)/shard_map/ppermute | solution.py:328
  22.9 2.0 %shard_map.78 = (f32[4,40,640]{2,1,0:T(8,128)S(1)}, bf16[2,40,128]{2,1,0:T(8,128)(2,1)S(1)}) custom-call(s32[8]{0:T(128)S(1)} %copy-done.3, bf16[8,320,640]{2,1,0:T(8,128)(2,1)S(1)} %bitcast.5, bf16[640,640]{1,0:T(8,128)(2,1)S(1)} %get-tuple-element.14.fock_ref, bf16[320,320]{1,0:T(8,128)(2,1)S(1)} %get-tuple-element.13.refs_3_.mix_ref, ...), custom_call_target="tpu_custom_call" | custom-call | flops 786432000 | bytes 2000000 | tf_op jit(solution)/shard_map/pallas_call | solution.py:385
  24.9 0.0 collective-permute-done.5.mate_ref
  24.9 0.0 slice-done
  25.0 7.1 %shard_map.79 = (f32[16,40,640]{2,1,0:T(8,128)S(1)}, bf16[16,208,128]{2,1,0:T(8,128)(2,1)S(1)}) custom-call(s32[1]{0:T(128)} %bitcast.pos_ref, s32[8]{0:T(128)S(1)} %copy-done.3, bf16[8,336,128]{2,1,0:T(8,128)(2,1)S(1)} %shard_map.77.after_ref.own_ref, bf16[8,336,128]{2,1,0:T(8,128)(2,1)S(1)} %collective-permute-done.5.mate_ref, ...), custom_call_target="tpu_custom_call" | custom-call | flops 1258291200 | bytes 15000000 | tf_op jit(solution)/shard_map/pallas_call | solution.py:420
  32.0 25.7 %all_to_all.5.recv_ref = bf16[16,208,128]{2,1,0:T(8,128)(2,1)S(1)} all-to-all(bf16[16,208,128]{2,1,0:T(8,128)(2,1)S(1)} %get-tuple-element.20), channel_id=1, replica_groups=mesh['groups'=2,'vir'=16] {'vir'}, dimensions={0} | all-to-all | bytes 1703936 | tf_op jit(solution)/shard_map/all_to_all | solution.py:442
  57.8 4.4 %shard_map.80 = f32[8,8,40,640]{3,2,1,0:T(8,128)} custom-call(s32[8]{0:T(128)S(1)} %copy-done.3, s32[40,640]{1,0:T(8,128)S(1)} %broadcast_xor_fusion.u_ref.refs_4_, f32[16,40,640]{2,1,0:T(8,128)S(1)} %get-tuple-element.19.half_ref, bf16[16,208,128]{2,1,0:T(8,128)(2,1)S(1)} %all_to_all.5.recv_ref), custom_call_target="tpu_custom_call" | custom-call | flops 1000000 | bytes 5000000 | tf_op jit(solution)/shard_map/pallas_call | solution.py:444
  (8 shorter events, 0.1 us)
Async XLA Ops:
  0.0 15.6 %copy-start = (bf16[8,8,40,640]{3,2,1,0:T(8,128)(2,1)S(1)}, bf16[8,8,40,640]{3,2,1,0:T(8,128)(2,1)}, u32[]{:S(2)}) copy-start(bf16[8,8,40,640]{3,2,1,0:T(8,128)(2,1)} %amps_ref.1) | copy-start | bytes 9830404
  0.0 7.6 %copy-start.5 = (s32[640]{0:T(1024)S(1)}, s32[640]{0:T(1024)}, u32[]{:S(2)}) copy-start(s32[640]{0:T(1024)} %param.13) | copy-start | bytes 7684
  0.0 7.7 %copy-start.4 = (bf16[8,8]{1,0:T(8,128)(2,1)S(1)}, bf16[8,8]{1,0:T(8,128)(2,1)}, u32[]{:S(2)}) copy-start(bf16[8,8]{1,0:T(8,128)(2,1)} %occ_vals_ref.1) | copy-start | bytes 388
  0.0 15.6 %copy-start.3 = (s32[8]{0:T(128)S(1)}, s32[8]{0:T(128)}, u32[]{:S(2)}) copy-start(s32[8]{0:T(128)} %occ_ref.7) | copy-start | bytes 100
  1.9 7.4 %collective-permute-start.2 = (bf16[1,336,128]{2,1,0:T(8,128)(2,1)}, bf16[1,336,128]{2,1,0:T(8,128)(2,1)S(1)}, u32[]{:S(2)}, u32[]{:S(2)}) collective-permute-start(bf16[1,336,128]{2,1,0:T(8,128)(2,1)} %bitcast.8), channel_id=1, source_target_pairs={{0,12},{1,13},{2,14},{3,15},{4,8},{5,9},{6,10},{7,11},{8,4},{9,5},... | collective-permute-start | bytes 258056 | tf_op jit(solution)/shard_map/ppermute | solution.py:328
  6.1 7.1 %collective-permute-start.1 = (bf16[1,336,128]{2,1,0:T(8,128)(2,1)}, bf16[1,336,128]{2,1,0:T(8,128)(2,1)S(1)}, u32[]{:S(2)}, u32[]{:S(2)}) collective-permute-start(bf16[1,336,128]{2,1,0:T(8,128)(2,1)} %bitcast.9), channel_id=1, source_target_pairs={{0,8},{1,9},{2,10},{3,11},{4,12},{5,13},{6,14},{7,15},{8,0},{9,1},... | collective-permute-start | bytes 258056 | tf_op jit(solution)/shard_map/ppermute | solution.py:328
  6.1 7.1 %collective-permute-start = (bf16[1,336,128]{2,1,0:T(8,128)(2,1)}, bf16[1,336,128]{2,1,0:T(8,128)(2,1)}, u32[]{:S(2)}, u32[]{:S(2)}) collective-permute-start(bf16[1,336,128]{2,1,0:T(8,128)(2,1)} %bitcast.10), channel_id=1, source_target_pairs={{0,4},{1,5},{2,6},{3,7},{4,0},{5,1},{6,2},{7,3},{8,12},{9,13},{10,... | collective-permute-start | bytes 258056 | tf_op jit(solution)/shard_map/ppermute | solution.py:328
  6.3 14.4 %collective-permute-start.3 = (bf16[1,336,128]{2,1,0:T(8,128)(2,1)}, bf16[1,336,128]{2,1,0:T(8,128)(2,1)S(1)}, u32[]{:S(2)}, u32[]{:S(2)}) collective-permute-start(bf16[1,336,128]{2,1,0:T(8,128)(2,1)} %bitcast.11), channel_id=1, source_target_pairs={{0,2},{1,3},{2,0},{3,1},{4,6},{5,7},{6,4},{7,5},{8,10},{9,11},{10,... | collective-permute-start | bytes 258056 | tf_op jit(solution)/shard_map/ppermute | solution.py:328
  7.7 1.1 %copy-start.1 = (bf16[640,640]{1,0:T(8,128)(2,1)S(1)}, bf16[640,640]{1,0:T(8,128)(2,1)}, u32[]{:S(2)}) copy-start(bf16[640,640]{1,0:T(8,128)(2,1)} %fock_ref.1) | copy-start | bytes 2457604
  14.1 6.7 %collective-permute-start.4 = (bf16[3,336,128]{2,1,0:T(8,128)(2,1)S(1)}, bf16[3,336,128]{2,1,0:T(8,128)(2,1)S(1)}, u32[]{:S(2)}, u32[]{:S(2)}) collective-permute-start(bf16[3,336,128]{2,1,0:T(8,128)(2,1)S(1)} %shard_map.75.after_ref.refs_1_), channel_id=1, source_target_pairs={{0,2},{1,3},{2,0},{3,1},{4,6},{5,7},{6,4},{7,5},{8,10},{9,11},{10,... | collective-permute-start | bytes 774152 | tf_op jit(solution)/shard_map/ppermute | solution.py:328
  15.5 9.4 %slice-start = ((s8[6553600]{0:T(1024)(128)(4,1)}), s8[4194304]{0:T(1024)(128)(4,1)S(1)}, s32[]{:S(2)}) async-start(s8[6553600]{0:T(1024)(128)(4,1)} %bitcast.6), calls=%async_computation.1 | async-start | bytes 8388608
  15.6 5.2 %copy-start.2 = (bf16[336,128]{1,0:T(8,128)(2,1)S(1)}, bf16[336,128]{1,0:T(8,128)(2,1)}, u32[]{:S(2)}) copy-start(bf16[336,128]{1,0:T(8,128)(2,1)} %shard_map.73) | copy-start | bytes 258052
  15.6 9.4 %slice-start.1 = ((s8[6553600]{0:T(1024)(128)(4,1)}), s8[2359296]{0:T(1024)(128)(4,1)S(1)}, s32[]{:S(2)}) async-start(s8[6553600]{0:T(1024)(128)(4,1)} %bitcast.6), calls=%async_computation.2 | async-start | bytes 4718592
  20.8 4.1 %collective-permute-start.5 = (bf16[8,336,128]{2,1,0:T(8,128)(2,1)S(1)}, bf16[8,336,128]{2,1,0:T(8,128)(2,1)S(1)}, u32[]{:S(2)}, u32[]{:S(2)}) collective-permute-start(bf16[8,336,128]{2,1,0:T(8,128)(2,1)S(1)} %shard_map.77.after_ref.own_ref), channel_id=1, source_target_pairs={{0,1},{1,0},{2,3},{3,2},{4,5},{5,4},{6,7},{7,6},{8,9},{9,8},{10,11... | collective-permute-start | bytes 2064392 | tf_op jit(solution)/shard_map/ppermute | solution.py:328
